TPU v7x, 32 devices: a whole 2x2x4 slice. The times are simulated.
32 devices in a mesh: groups: 2 (over x), surf: 16 (over z, y, core).
Axes of the slice: x: 2, y: 2, z: 4, core: 2. Of those that a mesh axis runs over, the one named last changes fastest.
Arguments:
- currents: bfloat16 [32, 65536], P(None, ('groups', 'surf')), parts along dimension 1, may hold values from -6 to 6
- near_tiles: bfloat16 [1536, 256, 256], P(('groups', 'surf')), parts along dimension 0, may hold values from -0.15625 to 0.15625
- near_target: int32 [1536], P(('groups', 'surf')), parts along dimension 0, may hold values from 0 to 7
- near_source: int32 [1536], P(('groups', 'surf')), parts along dimension 0, may hold values from 0 to 127, as said below
- primal_compress: bfloat16 [256, 32, 256], P(('groups', 'surf')), parts along dimension 0, may hold values from -0.375 to 0.375
- primal_expand: bfloat16 [256, 32, 256], P(('groups', 'surf')), parts along dimension 0, may hold values from -1 to 1
- primal_coupling: bfloat16 [4096, 1024], P(('groups', 'surf')), parts along dimension 0, may hold values from -0.25 to 0.25
- far_source: int32 [4096], P(('groups', 'surf')), parts along dimension 0, may hold values from 0 to 7
- far_owner: int32 [4096, 1], P(('groups', 'surf')), parts along dimension 0, may hold values from 0 to 15; in each aligned block of 128 rows (0 to 127, 128 to 255, ...) at most 16 rows name the same one
- far_block: int32 [4096], P(('groups', 'surf')), parts along dimension 0, may hold values from 0 to 7
- gram_inverse: bfloat16 [256, 256, 256], P(('groups', 'surf')), parts along dimension 0, may hold values from -0.5 to 1.5
- gram_lower: bfloat16 [256, 256, 256], P(('groups', 'surf')), parts along dimension 0, may hold values from -0.15625 to 0.15625
- gram_upper: bfloat16 [256, 256, 256], P(('groups', 'surf')), parts along dimension 0, may hold values from -0.15625 to 0.15625
- refine_weight: float32 [65536], P(('groups', 'surf')), parts along dimension 0, may hold values from 0.5 to 2
- dual_owner: int32 [65536, 1], P(('groups', 'surf')), parts along dimension 0, may hold values from 0 to 15; in each aligned block of 2048 rows (0 to 2047, 2048 to 4095, ...) at most 256 rows name the same one
- dual_index: int32 [65536], P(('groups', 'surf')), parts along dimension 0, may hold values from 0 to 2047
- dual_self: bfloat16 [256, 256, 256], P(('groups', 'surf')), parts along dimension 0, may hold values from -0.375 to 0.375
- dual_compress: bfloat16 [256, 32, 256], P(('groups', 'surf')), parts along dimension 0, may hold values from -0.375 to 0.375
- dual_expand: bfloat16 [256, 32, 256], P(('groups', 'surf')), parts along dimension 0, may hold values from -1 to 1
- dual_coupling: bfloat16 [4096, 1024], P(('groups', 'surf')), parts along dimension 0, may hold values from -0.25 to 0.25
Outputs:
- response: bfloat16 [32, 65536], P(None, ('groups', 'surf')), parts along dimension 1
There are 2 independent parts, one for each index of `groups`. A program takes and returns all parts, laid end to end along the dimension named above; each array names one. Nothing has to cross between parts.
Inputs may be any that keep to these rules, and one draw needn't show every extreme that they name: `near_source`: tiles of device d (rows d * 48 to (d + 1) * 48 - 1) take sources among blocks d * 8 - 1 to (d + 1) * 8 + 1 - 1 that exist. `far_owner`: of the far tiles of one device, at most 16 name the same owner. `dual_owner`: of the unknowns of one device, at most 256 name the same dual owner.
All inputs are finite; a program needn't handle non-finite values.
Results may differ from a plain program's by a relative error of at most 0.015.
Values may be sent and summed in bfloat16 or wider, within the bound.
No kernel may reach another device: no remote copies, remote signals or barrier semaphores. Data moves between devices by JAX's collectives and lax.ppermute only.
A program may use at most 64 MiB of HBM per device.

v0:
```python
import jax
import jax.numpy as jnp
from jax import lax
from jax.sharding import PartitionSpec as P

TILE = 256
INC = 32
HALO = 1
SWEEPS = 4
BLK_DEV = 8
NP_DEV = 2048


def with_halo(cells, sides, width):
    for axis, dim in sides:
        count = lax.axis_size(axis)
        ends = count - 1
        head = lax.slice_in_dim(cells, 0, width, axis=dim)
        tail = lax.slice_in_dim(cells, cells.shape[dim] - width, cells.shape[dim], axis=dim)
        cells = jnp.concatenate(
            [
                lax.ppermute(tail, axis, [(i, (i + 1) % count) for i in range(ends)]),
                cells,
                lax.ppermute(head, axis, [((i + 1) % count, i) for i in range(ends)]),
            ],
            axis=dim,
        )
    return cells


def arrival_slots(owners, surf_count):
    onehot = (owners[:, None] == jnp.arange(surf_count, dtype=jnp.int32)[None, :]).astype(jnp.int32)
    before = jnp.cumsum(onehot, axis=0) - onehot
    return jnp.sum(before * onehot, axis=1)


def far_field(blocks, compress, expand, coupling, far_source, far_owner, far_block, surf_count):
    block_count = blocks.shape[1]
    rank_size = compress.shape[1]
    tile_count = far_source.shape[0]
    coefficients = jnp.einsum(
        "ibt,brt->ibr", blocks, compress, preferred_element_type=jnp.float32
    ).astype(jnp.bfloat16)
    picked = jnp.take(coefficients, far_source, axis=1)
    far_terms = jnp.einsum(
        "ifr,frs->fis",
        picked,
        coupling.reshape(tile_count, rank_size, rank_size),
        preferred_element_type=jnp.float32,
    )
    term_rows = far_terms.reshape(tile_count, -1)
    row_width = term_rows.shape[1]
    owners = far_owner[:, 0]
    dense = (
        jnp.zeros((surf_count * block_count, row_width), jnp.float32)
        .at[owners * block_count + far_block]
        .add(term_rows)
    )
    summed = lax.psum_scatter(dense, "surf", scatter_dimension=0, tiled=True)
    summed = summed.astype(jnp.bfloat16).reshape(block_count, blocks.shape[0], rank_size)
    return jnp.einsum("bir,brt->ibt", summed, expand, preferred_element_type=jnp.float32)


def shards(
    currents,
    near_tiles,
    near_target,
    near_source,
    primal_compress,
    primal_expand,
    primal_coupling,
    far_source,
    far_owner,
    far_block,
    gram_inverse,
    gram_lower,
    gram_upper,
    refine_weight,
    dual_owner,
    dual_index,
    dual_self,
    dual_compress,
    dual_expand,
    dual_coupling,
):
    surf_count = lax.axis_size("surf")
    position = lax.axis_index("surf")
    blocks = currents.reshape(INC, BLK_DEV, TILE)
    extended = with_halo(currents, (("surf", 1),), HALO * TILE)
    extended = extended.reshape(INC, BLK_DEV + 2 * HALO, TILE)
    relative = near_source - (position * BLK_DEV - HALO)
    picked = jnp.take(extended, relative, axis=1)
    product = jnp.einsum("ikt,kts->iks", picked, near_tiles, preferred_element_type=jnp.float32)
    select = (near_target[:, None] == jnp.arange(BLK_DEV, dtype=jnp.int32)[None, :]).astype(
        jnp.float32
    )
    near_part = jnp.einsum("iks,kb->ibs", product, select, precision=lax.Precision.HIGHEST)
    far_part = far_field(
        blocks,
        primal_compress,
        primal_expand,
        primal_coupling,
        far_source,
        far_owner,
        far_block,
        surf_count,
    )
    primal_field = (near_part + far_part).astype(jnp.bfloat16)
    primal_wide = primal_field.astype(jnp.float32)
    iterate = jnp.einsum(
        "ibt,bts->ibs", primal_field, gram_inverse, preferred_element_type=jnp.float32
    ).astype(jnp.bfloat16)
    for sweep_number in range(SWEEPS - 1):
        padded = with_halo(iterate.reshape(INC, NP_DEV), (("surf", 1),), TILE)
        padded = padded.reshape(INC, BLK_DEV + 2, TILE)
        residue = primal_wide - jnp.einsum(
            "ibt,bts->ibs", padded[:, :-2], gram_lower, preferred_element_type=jnp.float32
        )
        residue = residue - jnp.einsum(
            "ibt,bts->ibs", padded[:, 2:], gram_upper, preferred_element_type=jnp.float32
        )
        iterate = jnp.einsum(
            "ibt,bts->ibs",
            residue.astype(jnp.bfloat16),
            gram_inverse,
            preferred_element_type=jnp.float32,
        ).astype(jnp.bfloat16)
    shares = (iterate.reshape(INC, NP_DEV).astype(jnp.float32) * refine_weight[None, :]).astype(
        jnp.bfloat16
    )
    share_rows = shares.T
    owners = dual_owner[:, 0]
    capacity = max(2, 2 * NP_DEV // surf_count)
    slot_index = arrival_slots(owners, surf_count)
    send_rows = (
        jnp.zeros((surf_count, capacity, INC), jnp.bfloat16).at[owners, slot_index].set(share_rows)
    )
    send_rows = send_rows.reshape(surf_count, capacity * INC)
    send_index = jnp.zeros((surf_count, capacity), jnp.int32).at[owners, slot_index].set(dual_index)
    arrived, arrived_index = (
        lax.all_to_all(send_rows, "surf", split_axis=0, concat_axis=0, tiled=True),
        lax.all_to_all(send_index, "surf", split_axis=0, concat_axis=0, tiled=True),
    )
    gathered = (
        jnp.zeros((NP_DEV, INC), jnp.float32)
        .at[arrived_index.reshape(-1)]
        .add(arrived.reshape(-1, INC).astype(jnp.float32))
    )
    dual_field = gathered.T.astype(jnp.bfloat16)
    dual_blocks = dual_field.reshape(INC, BLK_DEV, TILE)
    near_dual = jnp.einsum(
        "ibt,bts->ibs", dual_blocks, dual_self, preferred_element_type=jnp.float32
    )
    far_dual = far_field(
        dual_blocks,
        dual_compress,
        dual_expand,
        dual_coupling,
        far_source,
        far_owner,
        far_block,
        surf_count,
    )
    return (near_dual + far_dual).reshape(INC, NP_DEV).astype(jnp.bfloat16)


def solution(mesh):
    return jax.shard_map(
        shards,
        mesh=mesh,
        in_specs=(
            P(None, ("groups", "surf")),
            P(("groups", "surf"), None, None),
            P(("groups", "surf")),
            P(("groups", "surf")),
            P(("groups", "surf"), None, None),
            P(("groups", "surf"), None, None),
            P(("groups", "surf"), None),
            P(("groups", "surf")),
            P(("groups", "surf"), None),
            P(("groups", "surf")),
            P(("groups", "surf"), None, None),
            P(("groups", "surf"), None, None),
            P(("groups", "surf"), None, None),
            P(("groups", "surf")),
            P(("groups", "surf"), None),
            P(("groups", "surf")),
            P(("groups", "surf"), None, None),
            P(("groups", "surf"), None, None),
            P(("groups", "surf"), None, None),
            P(("groups", "surf"), None),
        ),
        out_specs=P(None, ("groups", "surf")),
        check_vma=False,
    )
```

profile of v0, /device:TPU:0, one launch (start us, length us, event | category | flops | bytes accessed | tf_op | source)
XLA Modules:
  0.0 272.9 jit_solution(6038161003227852639)
XLA Ops:
  6.5 0.8 fusion.85
  7.4 2.3 collective-permute-start
  9.7 1.3 collective-permute-start.1
  12.4 1.1 fusion.18
  13.6 1.1 copy.87
  14.7 2.3 copy.88
  17.0 1.7 gather_fusion.1
  18.8 2.0 fusion.22
  20.8 2.1 copy.89
  22.9 1.3 copy.90
  24.2 2.4 scatter_custom_fusion
  26.7 4.5 %reduce-window.6 = s32[16,16,128]{2,1,0:T(8,128)S(1)} reduce-window(s32[16,16,128]{2,1,0:T(8,128)S(1)} %fusion.70, s32[]{:T(128)} %constant.22.clone.1), window={size=1x1x128 pad=0_0x0_0x127_0}, to_apply=%region_0.1 | reduce-window | flops 4161536 | bytes 262148 | tf_op jit(solution)/shard_map/reduce-window
  32.8 5.2 %convolution_bitcast_fusion = f32[32,48,256]{2,0,1:T(8,128)} fusion(bf16[48,256,256]{2,1,0:T(8,128)(2,1)} %param.23, bf16[48,32,256]{2,1,0:T(8,128)(2,1)S(1)} %gather_fusion, pred[48]{0:T(512)(128)(4,1)S(1)} %get-tuple-element.6), kind=kOutput, calls=%fused_computation.10 | convolution fusion | flops 201719808 | bytes 8650800 | tf_op jit(solution)/shard_map/ikt,kts->iks/dot_general | solution.py:93
  38.0 49.2 %reduce-scatter.3.cloned.1.call-done = f32[8,1024]{1,0:T(8,128)} async-done(((f32[128,1024]{1,0:T(8,128)}), f32[8,1024]{1,0:T(8,128)}) %reduce-scatter.3.cloned.1.call-update) | async-done | bytes 32784 | tf_op jit(solution)/shard_map/reduce_scatter | solution.py:59
  87.2 0.8 convert_element_type.103
  88.2 3.0 %fusion.15 = bf16[32,8,256]{2,1,0:T(8,128)(2,1)S(1)} fusion(f32[32,48,256]{2,0,1:T(8,128)} %convolution_bitcast_fusion, f32[8,32,256]{2,1,0:T(8,128)S(1)} %fusion.86, s32[48]{0:T(128)S(1)} %copy-done.19), kind=kOutput, calls=%fused_computation.25 | convolution fusion | flops 37880192 | bytes 1966272 | tf_op jit(solution)/shard_map/iks,kb->ibs/dot_general | solution.py:97
  91.5 1.3 collective-permute-start.2
  92.8 1.3 collective-permute-start.3
  94.8 2.7 %collective-permute-done.3 = bf16[32,256]{1,0:T(8,128)(2,1)S(1)} collective-permute-done((bf16[32,256]{1,0:T(8,128)(2,1)S(1)}, bf16[32,256]{1,0:T(8,128)(2,1)S(1)}, u32[]{:S(2)}, u32[]{:S(2)}) %collective-permute-start.3) | collective-permute-done | bytes 16416 | tf_op jit(solution)/shard_map/ppermute | solution.py:24
  98.2 1.0 reshape.143
  100.5 4.4 %collective-permute-start.4 = (bf16[32,256]{1,0:T(8,128)(2,1)S(1)}, bf16[32,256]{1,0:T(8,128)(2,1)S(1)}, u32[]{:S(2)}, u32[]{:S(2)}) collective-permute-start(bf16[32,256]{1,0:T(8,128)(2,1)S(1)} %get-tuple-element.16), channel_id=1, source_target_pairs={{0,1},{1,2},{2,3},{3,4},{4,5},{5,6},{6,7},{7,8},{8,9},{9,10},{10,1... | collective-permute-start | bytes 49160 | tf_op jit(solution)/shard_map/ppermute | solution.py:22
  104.9 1.3 collective-permute-start.5
  106.9 1.1 collective-permute-done.5
  108.6 1.0 reshape.145
  112.1 5.2 %collective-permute-start.6 = (bf16[32,256]{1,0:T(8,128)(2,1)}, bf16[32,256]{1,0:T(8,128)(2,1)}, u32[]{:S(2)}, u32[]{:S(2)}) collective-permute-start(bf16[32,256]{1,0:T(8,128)(2,1)} %get-tuple-element.14), channel_id=1, source_target_pairs={{0,1},{1,2},{2,3},{3,4},{4,5},{5,6},{6,7},{7,8},{8,9},{9,10},{10,1... | collective-permute-start | bytes 49160 | tf_op jit(solution)/shard_map/ppermute | solution.py:22
  117.3 1.5 collective-permute-start.7
  118.8 8.8 %scatter_custom_fusion.3 = s32[4096]{0:T(1024)} fusion(s32[2048]{0:T(1024)S(1)} %broadcast_select_fusion, s32[2048]{0:T(1024)} %param.37, s32[]{:T(128)} %constant.22.clone.1), kind=kCustom, calls=%fused_computation.102 | custom fusion | bytes 16896
  127.6 6.0 %all-to-all-start = ((s32[16,1,256]{2,1,0:T(1,128)}), s32[16,1,256]{2,1,0:T(1,128)S(1)}, u32[]{:S(2)}, u32[]{:S(2)}) async-start(s32[16,1,256]{2,1,0:T(1,128)} %bitcast.4), calls=%async_computation | async-start | bytes 32768 | tf_op jit(solution)/shard_map/all_to_all | solution.py:142
  133.6 1.1 copy.117
  134.8 2.3 copy.118
  137.1 1.6 pad_maximum_fusion.3
  138.7 1.0 reshape.147
  141.2 6.2 %scatter_custom_fusion.4 = bf16[4096,32]{1,0:T(8,128)(2,1)S(1)} fusion(s32[2048]{0:T(1024)} %copy-done.15, bf16[2048,32]{1,0:T(8,128)(2,1)S(1)} %copy.112, bf16[]{:T(256)} %constant.14.clone.1), kind=kCustom, calls=%fused_computation.44 | custom fusion | bytes 262656
  148.6 2.2 reduce.10
  150.8 0.9 reshape.246
  151.6 6.0 %all-to-all-start.1 = ((bf16[16,2,4096]{2,1,0:T(2,128)(2,1)}), bf16[16,2,4096]{2,1,0:T(2,128)(2,1)S(1)}, u32[]{:S(2)}, u32[]{:S(2)}) async-start(bf16[16,2,4096]{2,1,0:T(2,128)(2,1)} %reshape.246), calls=%async_computation.2 | async-start | bytes 524288 | tf_op jit(solution)/shard_map/all_to_all | solution.py:141
  158.0 9.7 %all-to-all-done.1 = bf16[16,2,4096]{2,1,0:T(2,128)(2,1)S(1)} async-done(((bf16[16,2,4096]{2,1,0:T(2,128)(2,1)}), bf16[16,2,4096]{2,1,0:T(2,128)(2,1)S(1)}, u32[]{:S(2)}, u32[]{:S(2)}) %all-to-all-start.1) | async-done | bytes 262176 | tf_op jit(solution)/shard_map/all_to_all | solution.py:141
  168.0 1.5 convert_reduce_fusion
  169.5 2.0 reshape.200
  171.5 27.2 %scatter_custom_fusion.1 = f32[2048,32]{1,0:T(8,128)S(1)} fusion(s32[4096]{0:T(1024)S(1)} %bitcast.141, f32[4096,32]{1,0:T(8,128)} %reshape.200, f32[]{:T(128)} %constant.21.clone.1), kind=kCustom, calls=%fused_computation.46 | custom fusion | flops 131072 | bytes 262656 | tf_op jit(solution)/shard_map/scatter-add | solution.py:147
  198.7 0.8 copy-done.3
  199.9 1.8 gather_fusion.2
  201.7 2.0 fusion.20
  203.7 2.1 copy.119
  205.8 1.4 copy.120
  207.2 2.5 scatter_custom_fusion.2
  210.0 54.3 %reduce-scatter.5.cloned.1.call-done = f32[8,1024]{1,0:T(8,128)} async-done(((f32[128,1024]{1,0:T(8,128)}), f32[8,1024]{1,0:T(8,128)}) %reduce-scatter.5.cloned.1.call-update) | async-done | bytes 32784 | tf_op jit(solution)/shard_map/reduce_scatter | solution.py:59
  264.3 0.8 convert_element_type.127
  (120 shorter events, 14.7 us)
Async XLA Ops:
  6.5 84.7 %copy-start = (bf16[8,256,256]{2,1,0:T(8,128)(2,1)S(1)}, bf16[8,256,256]{2,1,0:T(8,128)(2,1)}, u32[]{:S(2)}) copy-start(bf16[8,256,256]{2,1,0:T(8,128)(2,1)} %param.32) | copy-start | bytes 3145732
  6.5 80.6 %reduce-scatter.3.cloned.1.call-start = ((), (), s32[]{:S(2)}) async-start(), calls=%async_computation.4 | async-start | bytes 557056 | tf_op jit(solution)/shard_map/reduce_scatter | solution.py:59
  7.4 24.7 %collective-permute-start = (bf16[32,256]{1,0:T(8,128)(2,1)S(1)}, bf16[32,256]{1,0:T(8,128)(2,1)S(1)}, u32[]{:S(2)}, u32[]{:S(2)}) collective-permute-start(bf16[32,256]{1,0:T(8,128)(2,1)S(1)} %get-tuple-element.20), channel_id=1, source_target_pairs={{0,1},{1,2},{2,3},{3,4},{4,5},{5,6},{6,7},{7,8},{8,9},{9,10},{10,1... | collective-permute-start | bytes 49160 | tf_op jit(solution)/shard_map/ppermute | solution.py:22
  9.7 22.4 %collective-permute-start.1 = (bf16[32,256]{1,0:T(8,128)(2,1)S(1)}, bf16[32,256]{1,0:T(8,128)(2,1)S(1)}, u32[]{:S(2)}, u32[]{:S(2)}) collective-permute-start(bf16[32,256]{1,0:T(8,128)(2,1)S(1)} %get-tuple-element.21), channel_id=1, source_target_pairs={{1,0},{2,1},{3,2},{4,3},{5,4},{6,5},{7,6},{8,7},{9,8},{10,9},{11,1... | collective-permute-start | bytes 49160 | tf_op jit(solution)/shard_map/ppermute | solution.py:24
  12.3 6.4 %copy-start.17 = (pred[128]{0:T(512)(128)(4,1)}, pred[128]{0:T(512)(128)(4,1)S(1)}, u32[]{:S(2)}) copy-start(pred[128]{0:T(512)(128)(4,1)S(1)} %compare_and_fusion) | copy-start | bytes 388
  12.4 4.7 %copy-start.16 = (s32[1024]{0:T(1024)}, s32[1024]{0:T(1024)S(1)}, u32[]{:S(2)}) copy-start(s32[1024]{0:T(1024)S(1)} %pad_clamp_fusion) | copy-start | bytes 12292
  20.8 3.4 %copy-start.23 = (s32[128]{0:T(128)S(1)}, s32[128]{0:T(128)}, u32[]{:S(2)}) copy-start(s32[128]{0:T(128)} %param.31) | copy-start | bytes 1540
  20.8 3.4 %copy-start.24 = (s32[128,1]{0,1:T(1,128)S(1)}, s32[128,1]{0,1:T(1,128)}, u32[]{:S(2)}) copy-start(s32[128,1]{0,1:T(1,128)} %param.30) | copy-start | bytes 1540
  20.8 5.8 %copy-start.11 = (s32[2048,1]{0,1:T(1,128)S(1)}, s32[2048,1]{0,1:T(1,128)}, u32[]{:S(2)}) copy-start(s32[2048,1]{0,1:T(1,128)} %param.36) | copy-start | bytes 24580
  22.9 9.2 %copy-start.22 = (s32[48]{0:T(128)S(1)}, s32[48]{0:T(128)}, u32[]{:S(2)}) copy-start(s32[48]{0:T(128)} %param.25) | copy-start | bytes 580
  22.9 9.2 %copy-start.6 = (bf16[32,2048]{1,0:T(8,128)(2,1)S(1)}, bf16[32,2048]{1,0:T(8,128)(2,1)}, u32[]{:S(2)}) copy-start(bf16[32,2048]{1,0:T(8,128)(2,1)} %param.22) | copy-start | bytes 393220
  24.2 2.4 copy-start.25
  32.8 55.3 %copy-start.8 = (bf16[8,32,256]{2,1,0:T(8,128)(2,1)S(1)}, bf16[8,32,256]{2,1,0:T(8,128)(2,1)}, u32[]{:S(2)}) copy-start(bf16[8,32,256]{2,1,0:T(8,128)(2,1)} %param.27) | copy-start | bytes 393220
  32.8 55.4 %copy-start.19 = (s32[48]{0:T(128)S(1)}, s32[48]{0:T(128)}, u32[]{:S(2)}) copy-start(s32[48]{0:T(128)} %param.24) | copy-start | bytes 580
  38.0 56.1 %copy-start.21 = (s32[2]{0:T(128)S(1)}, s32[2]{0:T(128)}, u32[]{:S(2)}) copy-start(s32[2]{0:T(128)} %constant.72) | copy-start | bytes 28
  88.2 11.1 %copy-start.1 = (bf16[8,256,256]{2,1,0:T(8,128)(2,1)S(1)}, bf16[8,256,256]{2,1,0:T(8,128)(2,1)}, u32[]{:S(2)}) copy-start(bf16[8,256,256]{2,1,0:T(8,128)(2,1)} %param.34) | copy-start | bytes 3145732
  91.2 8.4 %copy-start.2 = (bf16[8,256,256]{2,1,0:T(8,128)(2,1)S(1)}, bf16[8,256,256]{2,1,0:T(8,128)(2,1)}, u32[]{:S(2)}) copy-start(bf16[8,256,256]{2,1,0:T(8,128)(2,1)} %param.33) | copy-start | bytes 3145732
  91.5 3.3 %collective-permute-start.2 = (bf16[32,256]{1,0:T(8,128)(2,1)S(1)}, bf16[32,256]{1,0:T(8,128)(2,1)S(1)}, u32[]{:S(2)}, u32[]{:S(2)}) collective-permute-start(bf16[32,256]{1,0:T(8,128)(2,1)S(1)} %get-tuple-element.18), channel_id=1, source_target_pairs={{0,1},{1,2},{2,3},{3,4},{4,5},{5,6},{6,7},{7,8},{8,9},{9,10},{10,1... | collective-permute-start | bytes 49160 | tf_op jit(solution)/shard_map/ppermute | solution.py:22
  92.8 4.8 %collective-permute-start.3 = (bf16[32,256]{1,0:T(8,128)(2,1)S(1)}, bf16[32,256]{1,0:T(8,128)(2,1)S(1)}, u32[]{:S(2)}, u32[]{:S(2)}) collective-permute-start(bf16[32,256]{1,0:T(8,128)(2,1)S(1)} %get-tuple-element.19), channel_id=1, source_target_pairs={{1,0},{2,1},{3,2},{4,3},{5,4},{6,5},{7,6},{8,7},{9,8},{10,9},{11,1... | collective-permute-start | bytes 49160 | tf_op jit(solution)/shard_map/ppermute | solution.py:24
  99.6 6.6 %copy-start.20 = (s32[2]{0:T(128)S(1)}, s32[2]{0:T(128)}, u32[]{:S(2)}) copy-start(s32[2]{0:T(128)} %constant.69) | copy-start | bytes 28
  100.5 6.4 %collective-permute-start.4 = (bf16[32,256]{1,0:T(8,128)(2,1)S(1)}, bf16[32,256]{1,0:T(8,128)(2,1)S(1)}, u32[]{:S(2)}, u32[]{:S(2)}) collective-permute-start(bf16[32,256]{1,0:T(8,128)(2,1)S(1)} %get-tuple-element.16), channel_id=1, source_target_pairs={{0,1},{1,2},{2,3},{3,4},{4,5},{5,6},{6,7},{7,8},{8,9},{9,10},{10,1... | collective-permute-start | bytes 49160 | tf_op jit(solution)/shard_map/ppermute | solution.py:22
  104.9 3.1 %collective-permute-start.5 = (bf16[32,256]{1,0:T(8,128)(2,1)S(1)}, bf16[32,256]{1,0:T(8,128)(2,1)S(1)}, u32[]{:S(2)}, u32[]{:S(2)}) collective-permute-start(bf16[32,256]{1,0:T(8,128)(2,1)S(1)} %get-tuple-element.17), channel_id=1, source_target_pairs={{1,0},{2,1},{3,2},{4,3},{5,4},{6,5},{7,6},{8,7},{9,8},{10,9},{11,1... | collective-permute-start | bytes 49160 | tf_op jit(solution)/shard_map/ppermute | solution.py:24
  110.0 8.8 %copy-start.12 = (s32[2048]{0:T(1024)S(1)}, s32[2048]{0:T(1024)}, u32[]{:S(2)}) copy-start(s32[2048]{0:T(1024)} %multiply_reduce_fusion) | copy-start | bytes 24580
  110.0 8.8 %copy-start.14 = (pred[2048]{0:T(1024)(128)(4,1)S(1)}, pred[2048]{0:T(1024)(128)(4,1)}, u32[]{:S(2)}) copy-start(pred[2048]{0:T(1024)(128)(4,1)} %and_reduce_fusion) | copy-start | bytes 6148
  110.9 0.7 copy-start.7
  112.1 25.0 %collective-permute-start.6 = (bf16[32,256]{1,0:T(8,128)(2,1)}, bf16[32,256]{1,0:T(8,128)(2,1)}, u32[]{:S(2)}, u32[]{:S(2)}) collective-permute-start(bf16[32,256]{1,0:T(8,128)(2,1)} %get-tuple-element.14), channel_id=1, source_target_pairs={{0,1},{1,2},{2,3},{3,4},{4,5},{5,6},{6,7},{7,8},{8,9},{9,10},{10,1... | collective-permute-start | bytes 49160 | tf_op jit(solution)/shard_map/ppermute | solution.py:22
  117.3 19.8 %collective-permute-start.7 = (bf16[32,256]{1,0:T(8,128)(2,1)}, bf16[32,256]{1,0:T(8,128)(2,1)}, u32[]{:S(2)}, u32[]{:S(2)}) collective-permute-start(bf16[32,256]{1,0:T(8,128)(2,1)} %get-tuple-element.15), channel_id=1, source_target_pairs={{1,0},{2,1},{3,2},{4,3},{5,4},{6,5},{7,6},{8,7},{9,8},{10,9},{11,1... | collective-permute-start | bytes 49160 | tf_op jit(solution)/shard_map/ppermute | solution.py:24
  118.8 8.8 %copy-start.15 = (s32[2048]{0:T(1024)}, s32[2048]{0:T(1024)S(1)}, u32[]{:S(2)}) copy-start(s32[2048]{0:T(1024)S(1)} %broadcast_select_fusion) | copy-start | bytes 24580
  127.6 24.0 %all-to-all-start = ((s32[16,1,256]{2,1,0:T(1,128)}), s32[16,1,256]{2,1,0:T(1,128)S(1)}, u32[]{:S(2)}, u32[]{:S(2)}) async-start(s32[16,1,256]{2,1,0:T(1,128)} %bitcast.4), calls=%async_computation | async-start | bytes 32768 | tf_op jit(solution)/shard_map/all_to_all | solution.py:142
  140.0 0.9 copy-start.13
  151.6 16.1 %all-to-all-start.1 = ((bf16[16,2,4096]{2,1,0:T(2,128)(2,1)}), bf16[16,2,4096]{2,1,0:T(2,128)(2,1)S(1)}, u32[]{:S(2)}, u32[]{:S(2)}) async-start(bf16[16,2,4096]{2,1,0:T(2,128)(2,1)} %reshape.246), calls=%async_computation.2 | async-start | bytes 524288 | tf_op jit(solution)/shard_map/all_to_all | solution.py:141
  157.7 106.6 %reduce-scatter.5.cloned.1.call-start = ((), (), s32[]{:S(2)}) async-start(), calls=%async_computation.5 | async-start | bytes 557056 | tf_op jit(solution)/shard_map/reduce_scatter | solution.py:59
  169.5 30.1 %copy-start.9 = (bf16[8,32,256]{2,1,0:T(8,128)(2,1)S(1)}, bf16[8,32,256]{2,1,0:T(8,128)(2,1)}, u32[]{:S(2)}) copy-start(bf16[8,32,256]{2,1,0:T(8,128)(2,1)} %param.39) | copy-start | bytes 393220
  198.7 3.0 %copy-start.18 = (pred[128]{0:T(512)(128)(4,1)S(1)}, pred[128]{0:T(512)(128)(4,1)}, u32[]{:S(2)}) copy-start(pred[128]{0:T(512)(128)(4,1)} %copy-done.17) | copy-start | bytes 388
  198.7 0.8 copy-start.3
  205.8 3.9 %copy-start.4 = (bf16[2048,32]{1,0:T(8,128)(2,1)S(1)}, bf16[2048,32]{1,0:T(8,128)(2,1)}, u32[]{:S(2)}) copy-start(bf16[2048,32]{1,0:T(8,128)(2,1)} %copy-done.3) | copy-start | bytes 393220
  205.8 3.9 %copy-start.5 = (bf16[8,256,256]{2,1,0:T(8,128)(2,1)S(1)}, bf16[8,256,256]{2,1,0:T(8,128)(2,1)}, u32[]{:S(2)}) copy-start(bf16[8,256,256]{2,1,0:T(8,128)(2,1)} %param.38) | copy-start | bytes 3145732
  205.8 59.4 %copy-start.10 = (bf16[8,32,256]{2,1,0:T(8,128)(2,1)S(1)}, bf16[8,32,256]{2,1,0:T(8,128)(2,1)}, u32[]{:S(2)}) copy-start(bf16[8,32,256]{2,1,0:T(8,128)(2,1)} %param.40) | copy-start | bytes 393220
Sparse Core Ops, SparseCore 0:
  26.8 60.3 reduce-scatter.2
  209.8 54.4 reduce-scatter.4
where the time goes:
time: 274 us; the launch traced here: 273 us
  waiting for transfers between devices  117 us (43%)
  other arithmetic  48.8 us (18%)
  local copies, waits for them, and re-layouts  45.1 us (16%)
  starting transfers between devices  30.8 us (11%)
  matrix products  16.9 us (6%)
  between operations  14.1 us (5%)
    reduce_scatter x2, waiting for transfers between devices, far_field(): summed = lax.psum_scatter(dense, 'surf', scatter_dimension=0, tiled=True)  103 us
    scatter-add x1, other arithmetic, shards(): gathered = jnp.zeros((NP_DEV, INC), jnp.float32).at[arrived_index.reshape...  27.2 us
    unnamed x58, local copies, waits for them, and re-layouts  20 us
    ppermute x4, starting transfers between devices, with_halo(): lax.ppermute(tail, axis, [(i, (i + 1) % count) for i in range(ends)])  13.2 us
    all_to_all x1, waiting for transfers between devices, shards(): lax.all_to_all(send_rows, 'surf', split_axis=0, concat_axis=0, tiled=True)  9.75 us
    all_to_all x1, starting transfers between devices, shards(): lax.all_to_all(send_index, 'surf', split_axis=0, concat_axis=0, tiled=True)  6.02 us
    all_to_all x1, starting transfers between devices, shards(): lax.all_to_all(send_rows, 'surf', split_axis=0, concat_axis=0, tiled=True)  6.01 us
  transfers between devices with their start and end apart: 12, of which 5 were waited for; matrix products, arithmetic and copies ran while one was open for 20% of the time, Pallas kernels for 0%

commit v1 on v0

v1 whole, which is shorter than its diff:
```python
import functools

import jax
import jax.numpy as jnp
from jax import lax
from jax.experimental import pallas as pl
from jax.experimental.pallas import tpu as pltpu
from jax.sharding import PartitionSpec as P

TILE = 256
INC = 32
RANK = 32
BLK = 8
NP_DEV = 2048
IDX_ROWS = 16
F32 = jnp.float32
BF16 = jnp.bfloat16
NT = (((1,), (1,)), ((), ()))
VMEM_LIMIT = 48 * 1024 * 1024


def dot(a, b):
    return jnp.dot(a, b, preferred_element_type=F32)


def dot_nt(a, b):
    return lax.dot_general(a, b, NT, preferred_element_type=F32)


def iota(shape, dim):
    return lax.broadcasted_iota(jnp.int32, shape, dim)


def block(array, i):
    return array[:, i * TILE : (i + 1) * TILE]


def call(body, outs, args, scratch=(), smem=(), flops=0, name=None):
    specs = [
        pl.BlockSpec(memory_space=pltpu.SMEM if k in smem else pltpu.VMEM) for k in range(len(args))
    ]
    outs = tuple(jax.ShapeDtypeStruct(s, d) for s, d in outs)
    size = sum(a.size * a.dtype.itemsize for a in args) + sum(
        o.size * o.dtype.itemsize for o in outs
    )
    return pl.pallas_call(
        body,
        out_shape=outs,
        in_specs=specs,
        out_specs=tuple(pl.BlockSpec(memory_space=pltpu.VMEM) for _ in outs),
        scratch_shapes=list(scratch),
        compiler_params=pltpu.CompilerParams(vmem_limit_bytes=VMEM_LIMIT),
        cost_estimate=pl.CostEstimate(flops=flops, bytes_accessed=size, transcendentals=0),
        name=name,
    )(*args)


def transpose_coupling(coupling_ref, turned):
    turned[...] = coupling_ref[...].astype(F32).T


def far_terms(value, compress_ref, turned, source_ref, owner_ref, block_ref, coef, spread, pick, terms, out_ref):
    for s in range(BLK):
        coef[:, s * RANK : (s + 1) * RANK] = dot_nt(block(value, s), compress_ref[s])
    width = BLK * RANK
    keep = (iota((RANK, width), 1) % RANK) == iota((RANK, width), 0)
    for i in range(INC):
        spread[i * RANK : (i + 1) * RANK, :] = jnp.where(keep, coef[i : i + 1, :], 0.0).astype(BF16)
    tiles = source_ref.shape[1]
    chosen = (iota((width, tiles), 0) // RANK) == source_ref[...]
    pick[...] = dot(spread[...], chosen.astype(F32).astype(BF16))

    def step(pair, carry):
        rows = pl.multiple_of(pair * (2 * RANK), 2 * RANK)
        got = pick[pl.ds(rows, 2 * RANK), :]
        first = jnp.zeros((RANK, tiles), F32)
        second = jnp.zeros((RANK, tiles), F32)
        for r in range(RANK):
            factor = turned[r * RANK : (r + 1) * RANK, :]
            first += got[r : r + 1, :] * factor
            second += got[RANK + r : RANK + r + 1, :] * factor
        terms[pl.ds(rows, 2 * RANK), :] = jnp.concatenate([first, second], axis=0).astype(BF16)
        return carry

    lax.fori_loop(0, INC // 2, step, 0)
    targets = out_ref.shape[0]
    place = owner_ref[...] * BLK + block_ref[...]
    select = (iota((targets, tiles), 0) == place).astype(F32).astype(BF16)
    out_ref[...] = dot_nt(select, terms[...]).astype(BF16)


def far_scratch(tiles):
    return [
        pltpu.VMEM((INC, BLK * RANK), F32),
        pltpu.VMEM((INC * RANK, BLK * RANK), BF16),
        pltpu.VMEM((INC * RANK, tiles), F32),
        pltpu.VMEM((INC * RANK, tiles), BF16),
    ]


def far_up_body(value_ref, compress_ref, coupling_ref, source_ref, owner_ref, block_ref, out_ref, turned, *scratch):
    transpose_coupling(coupling_ref, turned)
    far_terms(value_ref[...], compress_ref, turned, source_ref, owner_ref, block_ref, *scratch, out_ref)


def far_down(arrived_ref, spread, expand_ref):
    rows = arrived_ref.shape[0]
    total = jnp.sum(arrived_ref[...].astype(F32).reshape(rows // BLK, BLK, INC * RANK), axis=0)
    width = INC * RANK
    keep = (iota((INC, width), 1) // RANK) == iota((INC, width), 0)
    for b in range(BLK):
        spread[b * INC : (b + 1) * INC, :] = jnp.where(keep, total[b : b + 1, :], 0.0).astype(BF16)
    fold = ((iota((width, RANK), 0) % RANK) == iota((width, RANK), 1)).astype(F32).astype(BF16)
    sums = dot(spread[...], fold).astype(BF16)
    return [dot(sums[b * INC : (b + 1) * INC, :], expand_ref[b]) for b in range(BLK)]


def near_body(target_ref, source_ref, cells_ref, tiles_ref, out_ref, total):
    total[...] = jnp.zeros_like(total)
    start = lax.axis_index("surf") * BLK - 1

    def step(k, carry):
        rel = source_ref[k] - start
        cell = cells_ref[:, pl.ds(pl.multiple_of(rel * TILE, TILE), TILE)]
        total[target_ref[k]] += dot(cell, tiles_ref[k])
        return carry

    lax.fori_loop(0, tiles_ref.shape[0], step, 0, unroll=4)
    for b in range(BLK):
        out_ref[:, b * TILE : (b + 1) * TILE] = total[b]


def products_body(inverse_ref, lower_ref, upper_ref, lower_out, upper_out):
    for b in range(BLK):
        lower_out[b] = dot(lower_ref[b], inverse_ref[b]).astype(BF16)
        upper_out[b] = dot(upper_ref[b], inverse_ref[b]).astype(BF16)


def solve_body(
    arrived_ref, near_ref, expand_ref, inverse_ref, lower_ref, upper_ref,
    start_out, next_out, left_out, right_out, spread,
):
    far = far_down(arrived_ref, spread, expand_ref)
    start, low = [], []
    for b in range(BLK):
        field = (block(near_ref, b) + far[b]).astype(BF16)
        value = dot(field, inverse_ref[b])
        start.append(value)
        low.append(value.astype(BF16))
        start_out[:, b * TILE : (b + 1) * TILE] = value
    after = []
    for b in range(BLK):
        value = start[b]
        if b > 0:
            value = value - dot(low[b - 1], lower_ref[b])
        if b < BLK - 1:
            value = value - dot(low[b + 1], upper_ref[b])
        after.append(value)
        next_out[:, b * TILE : (b + 1) * TILE] = value
    last = BLK - 1
    left_out[0] = low[0]
    left_out[1] = after[0].astype(BF16)
    left_out[2] = (start[0] - dot(after[1].astype(BF16), upper_ref[0])).astype(BF16)
    right_out[0] = low[last]
    right_out[1] = after[last].astype(BF16)
    right_out[2] = (start[last] - dot(after[last - 1].astype(BF16), lower_ref[last])).astype(BF16)


def finish_body(
    start_ref, next_ref, from_left, from_right, upper_left, lower_right, lower_ref, upper_ref,
    weight_ref, index_rows, place_ref, bounds_ref, send_ref, lhs, ordered,
):
    last = BLK - 1
    start = [block(start_ref, b) for b in range(BLK)]
    low = [start[0].astype(BF16), start[last].astype(BF16)]
    now = [block(next_ref, b) for b in range(BLK)]
    beside_left = from_left[1].astype(F32) - dot(low[0], upper_left[...])
    beside_right = from_right[1].astype(F32) - dot(low[1], lower_right[...])
    now[0] = now[0] - dot(from_left[0], lower_ref[0])
    now[last] = now[last] - dot(from_right[0], upper_ref[last])

    def sweep(values, left, right):
        values = [v.astype(BF16) for v in values]
        chain = [left.astype(BF16)] + values + [right.astype(BF16)]
        return values, [
            start[b] - dot(chain[b], lower_ref[b]) - dot(chain[b + 2], upper_ref[b])
            for b in range(BLK)
        ]

    values, then = sweep(now, beside_left, beside_right)
    beside_left = from_left[2].astype(F32) - dot(values[0], upper_left[...])
    beside_right = from_right[2].astype(F32) - dot(values[last], lower_right[...])
    values, then = sweep(then, beside_left, beside_right)
    for b in range(BLK):
        solved = then[b].astype(BF16).astype(F32)
        lhs[0:INC, b * TILE : (b + 1) * TILE] = (solved * block(weight_ref, b)).astype(BF16)
    lhs[INC : INC + IDX_ROWS, :] = index_rows[...]
    lane = iota((TILE, TILE), 1)
    columns = [jnp.broadcast_to(place_ref[:, b : b + 1], (TILE, TILE)) for b in range(BLK)]
    for p in range(BLK):
        total = jnp.zeros((INC + IDX_ROWS, TILE), F32)
        for b in range(BLK):
            hot = (lane + p * TILE == columns[b]).astype(F32).astype(BF16)
            total += dot(lhs[:, b * TILE : (b + 1) * TILE], hot)
        ordered[:, p * TILE : (p + 1) * TILE] = total
    owners, rows, window = send_ref.shape
    ordered[:, NP_DEV:] = jnp.zeros((rows, ordered.shape[1] - NP_DEV), F32)
    row = iota((rows, window), 0)
    slot = iota((rows, window), 1)
    wide = window + 128
    for o in range(owners):
        begin = bounds_ref[o, 0]
        base = pl.multiple_of((begin // 128) * 128, 128)
        piece = ordered[:, pl.ds(base, wide)]
        piece = pltpu.roll(piece, wide - (begin - base), 1)[:, :window]
        empty = (row >= INC) & (slot >= bounds_ref[o, 1])
        send_ref[o] = jnp.where(empty, -16.0, piece).astype(BF16)


def order_body(owner_ref, index_ref, place_out, bounds_out, rows_out, ranks):
    owners = bounds_out.shape[0]
    before = (iota((TILE, TILE), 0) < iota((TILE, TILE), 1)).astype(F32).astype(BF16)
    number = iota((owners, TILE), 0)
    count = jnp.zeros((owners, 1), F32)
    begin = jnp.zeros((owners, 1), F32)
    hots, carries = [], []
    for c in range(BLK):
        names = owner_ref[:, c * TILE : (c + 1) * TILE]
        hot = (number == names).astype(F32)
        hots.append(hot)
        carries.append(count)
        count = count + jnp.sum(hot, axis=1, keepdims=True)
        begin = begin + jnp.sum((names < number).astype(F32), axis=1, keepdims=True)
    for c in range(BLK):
        rank = dot(hots[c].astype(BF16), before)
        ranks[c : c + 1, :] = jnp.sum(hots[c] * (rank + carries[c] + begin), axis=0, keepdims=True)
    place_out[...] = ranks[...].T.astype(jnp.int32)
    pair = iota((owners, 2), 1)
    bounds_out[...] = jnp.where(pair == 0, begin, count).astype(jnp.int32)
    row = iota((IDX_ROWS, NP_DEV), 0)
    index = index_ref[...]
    digits = jnp.where(row == 0, index // TILE, jnp.where(row == 1, index % TILE, 0))
    rows_out[...] = digits.astype(F32).astype(BF16)


def gather_body(
    arrived_ref, compress_ref, coupling_ref, source_ref, owner_ref, block_ref,
    field_out, out_ref, index, turned, *scratch,
):
    transpose_coupling(coupling_ref, turned)
    owners, rows, window = arrived_ref.shape
    for e in range(owners):
        digits = arrived_ref[e, INC:, :].astype(F32)
        index[e : e + 1, :] = digits[0:1] * TILE + digits[1:2]
    columns = index[...].T.astype(jnp.int32)
    lane = iota((window, TILE), 1)
    wide = [jnp.broadcast_to(columns[:, e : e + 1], (window, TILE)) for e in range(owners)]
    for b in range(BLK):
        total = jnp.zeros((INC, TILE), F32)
        for e in range(owners):
            hot = (lane + b * TILE == wide[e]).astype(F32).astype(BF16)
            total += dot(arrived_ref[e, 0:INC, :], hot)
        field_out[:, b * TILE : (b + 1) * TILE] = total.astype(BF16)
    far_terms(field_out[...], compress_ref, turned, source_ref, owner_ref, block_ref, *scratch, out_ref)


def self_body(field_ref, self_ref, out_ref):
    for b in range(BLK):
        out_ref[:, b * TILE : (b + 1) * TILE] = dot(block(field_ref, b), self_ref[b])


def answer_body(arrived_ref, near_ref, expand_ref, out_ref, spread):
    far = far_down(arrived_ref, spread, expand_ref)
    for b in range(BLK):
        out_ref[:, b * TILE : (b + 1) * TILE] = (block(near_ref, b) + far[b]).astype(BF16)


def exchange(array, surf_count):
    shape = array.shape
    array = array.reshape((surf_count, shape[0] // surf_count) + shape[1:])
    array = lax.all_to_all(array, "surf", split_axis=0, concat_axis=0, tiled=True)
    return array.reshape(shape)


def shards(
    currents, near_tiles, near_target, near_source, primal_compress, primal_expand, primal_coupling,
    far_source, far_owner, far_block, gram_inverse, gram_lower, gram_upper, refine_weight,
    dual_owner, dual_index, dual_self, dual_compress, dual_expand, dual_coupling,
):
    surf_count = lax.axis_size("surf")
    tiles = far_source.shape[0]
    targets = surf_count * BLK
    capacity = max(2, 2 * NP_DEV // surf_count)
    window = max(128, -(-capacity // 128) * 128)
    to_right = [(i, i + 1) for i in range(surf_count - 1)]
    to_left = [(i + 1, i) for i in range(surf_count - 1)]
    source = far_source.reshape(1, tiles)
    owner = far_owner.reshape(1, tiles)
    place = far_block.reshape(1, tiles)

    from_left = lax.ppermute(currents[:, NP_DEV - TILE :], "surf", to_right)
    from_right = lax.ppermute(currents[:, :TILE], "surf", to_left)
    turned = pltpu.VMEM((RANK * RANK, tiles), F32)

    (partial,) = call(
        far_up_body,
        [((targets, INC * RANK), BF16)],
        (currents, primal_compress, primal_coupling, source, owner, place),
        scratch=[turned] + far_scratch(tiles),
        name="far_up",
    )
    arrived = exchange(partial, surf_count)

    lower, upper = call(
        products_body,
        [((BLK, TILE, TILE), BF16)] * 2,
        (gram_inverse, gram_lower, gram_upper),
        name="products",
    )
    upper_left = lax.ppermute(upper[BLK - 1], "surf", to_right)
    lower_right = lax.ppermute(lower[0], "surf", to_left)
    cells = jnp.concatenate([from_left, currents, from_right], axis=1)
    (near_part,) = call(
        near_body,
        [((INC, NP_DEV), F32)],
        (near_target, near_source, cells, near_tiles),
        scratch=[pltpu.VMEM((BLK, INC, TILE), F32)],
        smem=(0, 1),
        name="near",
    )
    where_to, bounds, index_rows = call(
        order_body,
        [((TILE, BLK), jnp.int32), ((surf_count, 2), jnp.int32), ((IDX_ROWS, NP_DEV), BF16)],
        (dual_owner.reshape(1, NP_DEV), dual_index.reshape(1, NP_DEV)),
        scratch=[pltpu.VMEM((BLK, TILE), F32)],
        name="order",
    )

    start, after, left_note, right_note = call(
        solve_body,
        [((INC, NP_DEV), F32)] * 2 + [((3, INC, TILE), BF16)] * 2,
        (arrived, near_part, primal_expand, gram_inverse, lower, upper),
        scratch=[pltpu.VMEM((BLK * INC, INC * RANK), BF16)],
        name="solve",
    )
    note_left = lax.ppermute(right_note, "surf", to_right)
    note_right = lax.ppermute(left_note, "surf", to_left)
    (send,) = call(
        finish_body,
        [((surf_count, INC + IDX_ROWS, window), BF16)],
        (
            start, after, note_left, note_right, upper_left, lower_right, lower, upper,
            refine_weight.reshape(1, NP_DEV), index_rows, where_to, bounds,
        ),
        scratch=[
            pltpu.VMEM((INC + IDX_ROWS, NP_DEV), BF16),
            pltpu.VMEM((INC + IDX_ROWS, NP_DEV + window + 128), F32),
        ],
        smem=(11,),
        name="finish",
    )
    shares = lax.all_to_all(send, "surf", split_axis=0, concat_axis=0, tiled=True)
    field, partial = call(
        gather_body,
        [((INC, NP_DEV), BF16), ((targets, INC * RANK), BF16)],
        (shares, dual_compress, dual_coupling, source, owner, place),
        scratch=[pltpu.VMEM((surf_count, window), F32), turned] + far_scratch(tiles),
        name="gather",
    )
    arrived = exchange(partial, surf_count)
    (near_dual,) = call(self_body, [((INC, NP_DEV), F32)], (field, dual_self), name="self_part")
    (response,) = call(
        answer_body,
        [((INC, NP_DEV), BF16)],
        (arrived, near_dual, dual_expand),
        scratch=[pltpu.VMEM((BLK * INC, INC * RANK), BF16)],
        name="answer",
    )
    return response


def solution(mesh):
    both = ("groups", "surf")
    row, flat = P(None, both), P(both)
    cube, flat2 = P(both, None, None), P(both, None)
    return jax.shard_map(
        shards,
        mesh=mesh,
        in_specs=(
            row, cube, flat, flat, cube, cube, flat2, flat, flat2, flat, cube, cube, cube, flat,
            flat2, flat, cube, cube, cube, flat2,
        ),
        out_specs=row,
        check_vma=False,
    )
```

time: 274 us -> 95.4 us (0.35)
  waiting for transfers between devices: 117 us -> 11.7 us
  other arithmetic: 48.8 us -> 0.92 us
  local copies, waits for them, and re-layouts: 45.1 us -> 13.5 us
  Pallas kernels: 0 us -> 21.7 us
  blocking collectives: 0 us -> 20.8 us
  matrix products: 16.9 us -> 0 us
  between operations: 14.1 us -> 0.28 us
  starting transfers between devices: 30.8 us -> 25.6 us
    reduce_scatter x2 -> x0, waiting for transfers between devices: 103 us -> none  [far_field(): summed = lax.psum_scatter(dense, 'surf', scatter_dimension=0, tiled=True)]
    scatter-add x3 -> x0, other arithmetic: 32 us -> none  [the longest x1 27.2 us: shards(): gathered = jnp.zeros((NP_DEV, INC), jnp.float32).at[arrived_index.reshape...]
    pallas_call x0 -> x9, Pallas kernels: none -> 21.7 us  [call(): pl.pallas_call(body, out_shape=outs, in_specs=specs, out_specs=tuple((pl....]
    all_to_all x0 -> x1, blocking collectives: none -> 20.8 us  [shards(): lax.all_to_all(send, 'surf', split_axis=0, concat_axis=0, tiled=True)]
    dot_general x19 -> x0, matrix products: 16.9 us -> none  [the longest x1 5.18 us: shards(): jnp.einsum('ikt,kts->iks', picked, near_tiles, preferred_element_type=jnp...]
    reshape x13 -> x0, local copies, waits for them, and re-layouts: 10.6 us -> none  [the longest x2 4.63 us: far_field(): coupling.reshape(tile_count, rank_size, rank_size)]
    unnamed x58 -> x46, local copies, waits for them, and re-layouts: 20 us -> 11.4 us
    ppermute x8 -> x6, starting transfers between devices: 18.6 us -> 12.8 us  [the longest x1 4.3 us: shards(): note_left = lax.ppermute(right_note, 'surf', to_right)]
  transfers between devices with their start and end apart: 12 -> 8, of which waited for: 5 -> 2; matrix products, arithmetic and copies ran while one was open for 20% -> 2% of each run, Pallas kernels for 0% -> 12%
where the time goes in v1:
time: 95.4 us; the launch traced here: 94.6 us
  starting transfers between devices  25.6 us (27%)
  Pallas kernels  21.7 us (23%)
  blocking collectives  20.8 us (22%)
  local copies, waits for them, and re-layouts  13.5 us (14%)
  waiting for transfers between devices  11.7 us (12%)
    pallas_call x9, Pallas kernels, call(): pl.pallas_call(body, out_shape=outs, in_specs=specs, out_specs=tuple((pl....  21.7 us
    all_to_all x1, blocking collectives, shards(): lax.all_to_all(send, 'surf', split_axis=0, concat_axis=0, tiled=True)  20.8 us
    all_to_all x2, starting transfers between devices, exchange(): lax.all_to_all(array, 'surf', split_axis=0, concat_axis=0, tiled=True)  12.9 us
    unnamed x46, local copies, waits for them, and re-layouts  11.4 us
    all_to_all x2, waiting for transfers between devices, exchange(): lax.all_to_all(array, 'surf', split_axis=0, concat_axis=0, tiled=True)  9.74 us
    ppermute x1, starting transfers between devices, shards(): note_left = lax.ppermute(right_note, 'surf', to_right)  4.3 us
    ppermute x1, starting transfers between devices, shards(): from_left = lax.ppermute(currents[:, NP_DEV - TILE:], 'surf', to_right)  2.35 us
    ppermute x1, starting transfers between devices, shards(): upper_left = lax.ppermute(upper[BLK - 1], 'surf', to_right)  2.25 us
  transfers between devices with their start and end apart: 8, of which 2 were waited for; matrix products, arithmetic and copies ran while one was open for 2% of the time, Pallas kernels for 12%

profile of v1, /device:TPU:0, one launch (start us, length us, event | category | flops | bytes accessed | tf_op | source)
XLA Modules:
  0.0 94.6 jit_solution(1543973187191501964)
XLA Ops:
  0.0 0.8 fusion
  0.8 2.3 %collective-permute-start = (bf16[32,256]{1,0:T(8,128)(2,1)S(1)}, bf16[32,256]{1,0:T(8,128)(2,1)S(1)}, u32[]{:S(2)}, u32[]{:S(2)}) collective-permute-start(bf16[32,256]{1,0:T(8,128)(2,1)S(1)} %get-tuple-element.27), channel_id=1, source_target_pairs={{0,1},{1,2},{2,3},{3,4},{4,5},{5,6},{6,7},{7,8},{8,9},{9,10},{10,1... | collective-permute-start | bytes 49160 | tf_op jit(solution)/shard_map/ppermute | solution.py:301
  3.2 1.3 %collective-permute-start.1 = (bf16[32,256]{1,0:T(8,128)(2,1)S(1)}, bf16[32,256]{1,0:T(8,128)(2,1)S(1)}, u32[]{:S(2)}, u32[]{:S(2)}) collective-permute-start(bf16[32,256]{1,0:T(8,128)(2,1)S(1)} %get-tuple-element.28), channel_id=1, source_target_pairs={{1,0},{2,1},{3,2},{4,3},{5,4},{6,5},{7,6},{8,7},{9,8},{10,9},{11,1... | collective-permute-start | bytes 49160 | tf_op jit(solution)/shard_map/ppermute | solution.py:302
  4.5 0.0 copy-start.5
  4.5 0.9 copy-done.5
  5.4 0.9 %copy-done.6 = bf16[128,1024]{1,0:T(8,128)(2,1)S(1)} copy-done((bf16[128,1024]{1,0:T(8,128)(2,1)S(1)}, bf16[128,1024]{1,0:T(8,128)(2,1)}, u32[]{:S(2)}) %copy-start.6) | copy-done | bytes 262168
  6.3 0.9 copy-done.8
  7.2 0.7 copy-done.15
  7.9 0.7 copy-done.17
  8.6 0.7 copy-done.19
  9.2 2.8 %far_up.1 = bf16[128,1024]{1,0:T(8,128)(2,1)} custom-call(bf16[32,2048]{1,0:T(8,128)(2,1)S(1)} %copy-done.5, bf16[8,32,256]{2,1,0:T(8,128)(2,1)S(1)} %copy-done.8, bf16[128,1024]{1,0:T(8,128)(2,1)S(1)} %copy-done.6, s32[1,128]{1,0:T(1,128)S(1)} %bitcast.18, s32[1,128]{1,0:T(1,128)S(1)} %bitcast.20, s32[1,128]{1,0:T(1,128)S(1)} %bitcast.22), custom_call_target="tpu_custom_call" | custom-call | bytes 787968 | tf_op jit(solution)/shard_map/far_up/pallas_call | solution.py:46
  12.0 9.4 %all-to-all-start = ((bf16[16,8,1024]{2,1,0:T(8,128)(2,1)}), bf16[16,8,1024]{2,1,0:T(8,128)(2,1)}, u32[]{:S(2)}, u32[]{:S(2)}) async-start(bf16[16,8,1024]{2,1,0:T(8,128)(2,1)} %bitcast.3), calls=%async_computation | async-start | bytes 524288 | tf_op jit(solution)/shard_map/all_to_all | solution.py:281
  21.4 0.0 copy-start
  21.4 1.2 %copy-done = bf16[8,256,256]{2,1,0:T(8,128)(2,1)S(1)} copy-done((bf16[8,256,256]{2,1,0:T(8,128)(2,1)S(1)}, bf16[8,256,256]{2,1,0:T(8,128)(2,1)}, u32[]{:S(2)}) %copy-start) | copy-done | bytes 1048600
  22.6 1.2 %copy-done.2 = bf16[8,256,256]{2,1,0:T(8,128)(2,1)S(1)} copy-done((bf16[8,256,256]{2,1,0:T(8,128)(2,1)S(1)}, bf16[8,256,256]{2,1,0:T(8,128)(2,1)}, u32[]{:S(2)}) %copy-start.2) | copy-done | bytes 1048600
  23.9 1.2 %copy-done.3 = bf16[8,256,256]{2,1,0:T(8,128)(2,1)S(1)} copy-done((bf16[8,256,256]{2,1,0:T(8,128)(2,1)S(1)}, bf16[8,256,256]{2,1,0:T(8,128)(2,1)}, u32[]{:S(2)}) %copy-start.3) | copy-done | bytes 1048600
  25.1 0.7 products.1
  25.8 0.0 copy-start.13
  25.8 0.0 copy-start.12
  25.8 0.7 slice_bitcast_fusion.1
  26.5 2.3 %collective-permute-start.4 = (bf16[256,256]{1,0:T(8,128)(2,1)}, bf16[256,256]{1,0:T(8,128)(2,1)S(1)}, u32[]{:S(2)}, u32[]{:S(2)}) collective-permute-start(bf16[256,256]{1,0:T(8,128)(2,1)} %slice_bitcast_fusion.1), channel_id=1, source_target_pairs={{0,1},{1,2},{2,3},{3,4},{4,5},{5,6},{6,7},{7,8},{8,9},{9,10},{10,1... | collective-permute-start | bytes 393224 | tf_op jit(solution)/shard_map/ppermute | solution.py:320
  28.7 0.7 slice_bitcast_fusion
  29.4 1.3 %collective-permute-start.5 = (bf16[256,256]{1,0:T(8,128)(2,1)}, bf16[256,256]{1,0:T(8,128)(2,1)}, u32[]{:S(2)}, u32[]{:S(2)}) collective-permute-start(bf16[256,256]{1,0:T(8,128)(2,1)} %slice_bitcast_fusion), channel_id=1, source_target_pairs={{1,0},{2,1},{3,2},{4,3},{5,4},{6,5},{7,6},{8,7},{9,8},{10,9},{11,1... | collective-permute-start | bytes 393224 | tf_op jit(solution)/shard_map/ppermute | solution.py:321
  30.7 0.0 collective-permute-done
  30.7 0.0 collective-permute-done.1
  30.7 0.9 pad_maximum_fusion.cells_ref
  31.6 0.0 copy-start.21
  31.6 0.6 copy-done.21
  32.3 0.7 copy-done.22
  32.9 5.3 %near.1.near_ref = f32[32,2048]{1,0:T(8,128)S(1)} custom-call(s32[48]{0:T(128)S(1)} %copy-done.21, s32[48]{0:T(128)S(1)} %copy-done.22, bf16[32,2560]{1,0:T(8,128)(2,1)S(1)} %pad_maximum_fusion.cells_ref, bf16[48,256,256]{2,1,0:T(8,128)(2,1)} %tiles_ref.1), custom_call_target="tpu_custom_call" | custom-call | bytes 6717824 | tf_op jit(solution)/shard_map/near/pallas_call | solution.py:46
  38.2 0.0 copy-start.7
  38.2 0.0 copy-start.9
  38.3 0.0 copy-start.11
  38.3 0.9 copy-done.11
  39.2 2.0 %solve.1 = (f32[32,2048]{1,0:T(8,128)S(1)}, f32[32,2048]{1,0:T(8,128)S(1)}, bf16[3,32,256]{2,1,0:T(8,128)(2,1)S(1)}, bf16[3,32,256]{2,1,0:T(8,128)(2,1)S(1)}) custom-call(bf16[128,1024]{1,0:T(8,128)(2,1)} %bitcast.4.arrived_ref, f32[32,2048]{1,0:T(8,128)S(1)} %near.1.near_ref, bf16[8,32,256]{2,1,0:T(8,128)(2,1)S(1)} %copy-done.11, ...), custom_call_target="tpu_custom_call" | custom-call | bytes 4423680 | tf_op jit(solution)/shard_map/solve/pallas_call | solution.py:46
  41.2 4.3 %collective-permute-start.2 = (bf16[3,32,256]{2,1,0:T(8,128)(2,1)S(1)}, bf16[3,32,256]{2,1,0:T(8,128)(2,1)S(1)}, u32[]{:S(2)}, u32[]{:S(2)}) collective-permute-start(bf16[3,32,256]{2,1,0:T(8,128)(2,1)S(1)} %get-tuple-element.20), channel_id=1, source_target_pairs={{0,1},{1,2},{2,3},{3,4},{4,5},{5,6},{6,7},{7,8},{8,9},{9,10},{10,1... | collective-permute-start | bytes 147464 | tf_op jit(solution)/shard_map/ppermute | solution.py:346
  45.5 1.3 %collective-permute-start.3 = (bf16[3,32,256]{2,1,0:T(8,128)(2,1)S(1)}, bf16[3,32,256]{2,1,0:T(8,128)(2,1)S(1)}, u32[]{:S(2)}, u32[]{:S(2)}) collective-permute-start(bf16[3,32,256]{2,1,0:T(8,128)(2,1)S(1)} %get-tuple-element.21), channel_id=1, source_target_pairs={{1,0},{2,1},{3,2},{4,3},{5,4},{6,5},{7,6},{8,7},{9,8},{10,9},{11,1... | collective-permute-start | bytes 147464 | tf_op jit(solution)/shard_map/ppermute | solution.py:347
  46.8 0.0 copy-start.14
  46.8 0.7 copy-done.14
  47.5 0.4 order.1
  47.9 1.9 %collective-permute-done.3.from_right = bf16[3,32,256]{2,1,0:T(8,128)(2,1)S(1)} collective-permute-done((bf16[3,32,256]{2,1,0:T(8,128)(2,1)S(1)}, bf16[3,32,256]{2,1,0:T(8,128)(2,1)S(1)}, u32[]{:S(2)}, u32[]{:S(2)}) %collective-permute-start.3) | collective-permute-done | bytes 49184 | tf_op jit(solution)/shard_map/ppermute | solution.py:347
  49.9 3.2 %finish.1 = bf16[16,48,256]{2,1,0:T(8,128)(2,1)S(1)} custom-call(f32[32,2048]{1,0:T(8,128)S(1)} %get-tuple-element.18.start_ref, f32[32,2048]{1,0:T(8,128)S(1)} %get-tuple-element.19.next_ref, bf16[3,32,256]{2,1,0:T(8,128)(2,1)S(1)} %collective-permute-done.2.from_left, bf16[3,32,256]{2,1,0:T(8,128)(2,1)S(1)} %collective-permute-done.3.from_right, ...), custom_call_target="tpu_custom_call" | custom-call | bytes 3457152 | tf_op jit(solution)/shard_map/finish/pallas_call | solution.py:46
  53.1 20.8 %all_to_all.15.arrived_ref = bf16[16,48,256]{2,1,0:T(8,128)(2,1)S(1)} all-to-all(bf16[16,48,256]{2,1,0:T(8,128)(2,1)S(1)} %finish.1), channel_id=1, replica_groups=mesh['groups'=2,'surf'=16] {'surf'}, dimensions={0} | all-to-all | bytes 786432 | tf_op jit(solution)/shard_map/all_to_all | solution.py:362
  74.0 5.9 %gather.1 = (bf16[32,2048]{1,0:T(8,128)(2,1)S(1)}, bf16[128,1024]{1,0:T(8,128)(2,1)}) custom-call(bf16[16,48,256]{2,1,0:T(8,128)(2,1)S(1)} %all_to_all.15.arrived_ref, bf16[8,32,256]{2,1,0:T(8,128)(2,1)S(1)} %copy-done.9, bf16[128,1024]{1,0:T(8,128)(2,1)S(1)} %copy-done.7, s32[1,128]{1,0:T(1,128)S(1)} %bitcast.19, s32[1,128]{1,0:T(1,128)S(1)} %bitcast.21, ...), custom_call_target="tpu_custom_call" | custom-call | bytes 1181184 | tf_op jit(solution)/shard_map/gather/pallas_call | solution.py:46
  79.9 3.5 %all-to-all-start.2 = ((bf16[16,8,1024]{2,1,0:T(8,128)(2,1)}), bf16[16,8,1024]{2,1,0:T(8,128)(2,1)S(1)}, u32[]{:S(2)}, u32[]{:S(2)}) async-start(bf16[16,8,1024]{2,1,0:T(8,128)(2,1)} %bitcast.10), calls=%async_computation.2 | async-start | bytes 524288 | tf_op jit(solution)/shard_map/all_to_all | solution.py:281
  83.4 0.3 self_part.1.near_ref
  83.7 9.7 %all-to-all-done.2 = bf16[16,8,1024]{2,1,0:T(8,128)(2,1)S(1)} async-done(((bf16[16,8,1024]{2,1,0:T(8,128)(2,1)}), bf16[16,8,1024]{2,1,0:T(8,128)(2,1)S(1)}, u32[]{:S(2)}, u32[]{:S(2)}) %all-to-all-start.2) | async-done | bytes 262176 | tf_op jit(solution)/shard_map/all_to_all | solution.py:281
  93.4 1.1 %answer.1 = bf16[32,2048]{1,0:T(8,128)(2,1)} custom-call(bf16[128,1024]{1,0:T(8,128)(2,1)S(1)} %bitcast.14, f32[32,2048]{1,0:T(8,128)S(1)} %self_part.1.near_ref, bf16[8,32,256]{2,1,0:T(8,128)(2,1)S(1)} %copy-done.10), custom_call_target="tpu_custom_call" | custom-call | bytes 786432 | tf_op jit(solution)/shard_map/answer/pallas_call | solution.py:46
  (28 shorter events, 0.1 us)
Async XLA Ops:
  0.0 38.3 %copy-start.1 = (bf16[8,256,256]{2,1,0:T(8,128)(2,1)S(1)}, bf16[8,256,256]{2,1,0:T(8,128)(2,1)}, u32[]{:S(2)}) copy-start(bf16[8,256,256]{2,1,0:T(8,128)(2,1)} %inverse_ref.3) | copy-start | bytes 3145732
  0.8 29.9 %collective-permute-start = (bf16[32,256]{1,0:T(8,128)(2,1)S(1)}, bf16[32,256]{1,0:T(8,128)(2,1)S(1)}, u32[]{:S(2)}, u32[]{:S(2)}) collective-permute-start(bf16[32,256]{1,0:T(8,128)(2,1)S(1)} %get-tuple-element.27), channel_id=1, source_target_pairs={{0,1},{1,2},{2,3},{3,4},{4,5},{5,6},{6,7},{7,8},{8,9},{9,10},{10,1... | collective-permute-start | bytes 49160 | tf_op jit(solution)/shard_map/ppermute | solution.py:301
  3.2 27.5 %collective-permute-start.1 = (bf16[32,256]{1,0:T(8,128)(2,1)S(1)}, bf16[32,256]{1,0:T(8,128)(2,1)S(1)}, u32[]{:S(2)}, u32[]{:S(2)}) collective-permute-start(bf16[32,256]{1,0:T(8,128)(2,1)S(1)} %get-tuple-element.28), channel_id=1, source_target_pairs={{1,0},{2,1},{3,2},{4,3},{5,4},{6,5},{7,6},{8,7},{9,8},{10,9},{11,1... | collective-permute-start | bytes 49160 | tf_op jit(solution)/shard_map/ppermute | solution.py:302
  4.5 0.9 copy-start.5
  5.4 0.9 %copy-start.6 = (bf16[128,1024]{1,0:T(8,128)(2,1)S(1)}, bf16[128,1024]{1,0:T(8,128)(2,1)}, u32[]{:S(2)}) copy-start(bf16[128,1024]{1,0:T(8,128)(2,1)} %coupling_ref.2) | copy-start | bytes 786436
  6.3 0.9 copy-start.8
  7.2 0.7 copy-start.15
  7.9 0.7 copy-start.17
  8.6 0.7 copy-start.19
  12.0 26.2 %all-to-all-start = ((bf16[16,8,1024]{2,1,0:T(8,128)(2,1)}), bf16[16,8,1024]{2,1,0:T(8,128)(2,1)}, u32[]{:S(2)}, u32[]{:S(2)}) async-start(bf16[16,8,1024]{2,1,0:T(8,128)(2,1)} %bitcast.3), calls=%async_computation | async-start | bytes 524288 | tf_op jit(solution)/shard_map/all_to_all | solution.py:281
  21.4 1.2 %copy-start = (bf16[8,256,256]{2,1,0:T(8,128)(2,1)S(1)}, bf16[8,256,256]{2,1,0:T(8,128)(2,1)}, u32[]{:S(2)}) copy-start(bf16[8,256,256]{2,1,0:T(8,128)(2,1)} %inverse_ref.3) | copy-start | bytes 3145732
  22.6 1.2 %copy-start.2 = (bf16[8,256,256]{2,1,0:T(8,128)(2,1)S(1)}, bf16[8,256,256]{2,1,0:T(8,128)(2,1)}, u32[]{:S(2)}) copy-start(bf16[8,256,256]{2,1,0:T(8,128)(2,1)} %lower_ref.1) | copy-start | bytes 3145732
  23.9 1.2 %copy-start.3 = (bf16[8,256,256]{2,1,0:T(8,128)(2,1)S(1)}, bf16[8,256,256]{2,1,0:T(8,128)(2,1)}, u32[]{:S(2)}) copy-start(bf16[8,256,256]{2,1,0:T(8,128)(2,1)} %upper_ref.1) | copy-start | bytes 3145732
  25.8 21.0 %copy-start.13 = (s32[2048,1]{0,1:T(1,128)S(1)}, s32[2048,1]{0,1:T(1,128)}, u32[]{:S(2)}) copy-start(s32[2048,1]{0,1:T(1,128)} %param.34) | copy-start | bytes 24580
  25.8 24.1 %copy-start.12 = (f32[2048]{0:T(1024)S(1)}, f32[2048]{0:T(1024)}, u32[]{:S(2)}) copy-start(f32[2048]{0:T(1024)} %param.33) | copy-start | bytes 24580
  26.5 21.4 %collective-permute-start.4 = (bf16[256,256]{1,0:T(8,128)(2,1)}, bf16[256,256]{1,0:T(8,128)(2,1)S(1)}, u32[]{:S(2)}, u32[]{:S(2)}) collective-permute-start(bf16[256,256]{1,0:T(8,128)(2,1)} %slice_bitcast_fusion.1), channel_id=1, source_target_pairs={{0,1},{1,2},{2,3},{3,4},{4,5},{5,6},{6,7},{7,8},{8,9},{9,10},{10,1... | collective-permute-start | bytes 393224 | tf_op jit(solution)/shard_map/ppermute | solution.py:320
  29.4 18.5 %collective-permute-start.5 = (bf16[256,256]{1,0:T(8,128)(2,1)}, bf16[256,256]{1,0:T(8,128)(2,1)}, u32[]{:S(2)}, u32[]{:S(2)}) collective-permute-start(bf16[256,256]{1,0:T(8,128)(2,1)} %slice_bitcast_fusion), channel_id=1, source_target_pairs={{1,0},{2,1},{3,2},{4,3},{5,4},{6,5},{7,6},{8,7},{9,8},{10,9},{11,1... | collective-permute-start | bytes 393224 | tf_op jit(solution)/shard_map/ppermute | solution.py:321
  31.6 0.7 copy-start.21
  32.3 0.7 copy-start.22
  38.2 35.8 %copy-start.7 = (bf16[128,1024]{1,0:T(8,128)(2,1)S(1)}, bf16[128,1024]{1,0:T(8,128)(2,1)}, u32[]{:S(2)}) copy-start(bf16[128,1024]{1,0:T(8,128)(2,1)} %coupling_ref.3) | copy-start | bytes 786436
  38.2 35.7 %copy-start.9 = (bf16[8,32,256]{2,1,0:T(8,128)(2,1)S(1)}, bf16[8,32,256]{2,1,0:T(8,128)(2,1)}, u32[]{:S(2)}) copy-start(bf16[8,32,256]{2,1,0:T(8,128)(2,1)} %compress_ref.3) | copy-start | bytes 393220
  38.3 1.0 %copy-start.11 = (bf16[8,32,256]{2,1,0:T(8,128)(2,1)S(1)}, bf16[8,32,256]{2,1,0:T(8,128)(2,1)}, u32[]{:S(2)}) copy-start(bf16[8,32,256]{2,1,0:T(8,128)(2,1)} %expand_ref.2) | copy-start | bytes 393220
  39.2 34.8 %copy-start.16 = (s32[128]{0:T(128)S(1)}, s32[128]{0:T(128)}, u32[]{:S(2)}) copy-start(s32[128]{0:T(128)} %param.27) | copy-start | bytes 1540
  39.2 34.8 %copy-start.18 = (s32[128,1]{0,1:T(1,128)S(1)}, s32[128,1]{0,1:T(1,128)}, u32[]{:S(2)}) copy-start(s32[128,1]{0,1:T(1,128)} %param.28) | copy-start | bytes 1540
  39.2 34.8 %copy-start.20 = (s32[128]{0:T(128)S(1)}, s32[128]{0:T(128)}, u32[]{:S(2)}) copy-start(s32[128]{0:T(128)} %param.29) | copy-start | bytes 1540
  41.2 42.2 %copy-start.4 = (bf16[8,256,256]{2,1,0:T(8,128)(2,1)S(1)}, bf16[8,256,256]{2,1,0:T(8,128)(2,1)}, u32[]{:S(2)}) copy-start(bf16[8,256,256]{2,1,0:T(8,128)(2,1)} %self_ref.1) | copy-start | bytes 3145732
  41.2 52.2 %copy-start.10 = (bf16[8,32,256]{2,1,0:T(8,128)(2,1)S(1)}, bf16[8,32,256]{2,1,0:T(8,128)(2,1)}, u32[]{:S(2)}) copy-start(bf16[8,32,256]{2,1,0:T(8,128)(2,1)} %expand_ref.3) | copy-start | bytes 393220
  41.2 6.7 %collective-permute-start.2 = (bf16[3,32,256]{2,1,0:T(8,128)(2,1)S(1)}, bf16[3,32,256]{2,1,0:T(8,128)(2,1)S(1)}, u32[]{:S(2)}, u32[]{:S(2)}) collective-permute-start(bf16[3,32,256]{2,1,0:T(8,128)(2,1)S(1)} %get-tuple-element.20), channel_id=1, source_target_pairs={{0,1},{1,2},{2,3},{3,4},{4,5},{5,6},{6,7},{7,8},{8,9},{9,10},{10,1... | collective-permute-start | bytes 147464 | tf_op jit(solution)/shard_map/ppermute | solution.py:346
  45.5 4.4 %collective-permute-start.3 = (bf16[3,32,256]{2,1,0:T(8,128)(2,1)S(1)}, bf16[3,32,256]{2,1,0:T(8,128)(2,1)S(1)}, u32[]{:S(2)}, u32[]{:S(2)}) collective-permute-start(bf16[3,32,256]{2,1,0:T(8,128)(2,1)S(1)} %get-tuple-element.21), channel_id=1, source_target_pairs={{1,0},{2,1},{3,2},{4,3},{5,4},{6,5},{7,6},{8,7},{9,8},{10,9},{11,1... | collective-permute-start | bytes 147464 | tf_op jit(solution)/shard_map/ppermute | solution.py:347
  46.8 0.7 copy-start.14
  79.9 13.6 %all-to-all-start.2 = ((bf16[16,8,1024]{2,1,0:T(8,128)(2,1)}), bf16[16,8,1024]{2,1,0:T(8,128)(2,1)S(1)}, u32[]{:S(2)}, u32[]{:S(2)}) async-start(bf16[16,8,1024]{2,1,0:T(8,128)(2,1)} %bitcast.10), calls=%async_computation.2 | async-start | bytes 524288 | tf_op jit(solution)/shard_map/all_to_all | solution.py:281

commit v2 on v1

v2 whole, which is shorter than its diff:
```python
import jax
import jax.numpy as jnp
from jax import lax
from jax.experimental import pallas as pl
from jax.experimental.pallas import tpu as pltpu
from jax.sharding import PartitionSpec as P

TILE = 256
INC = 32
RANK = 32
BLK = 8
NP_DEV = 2048
LANES = 128
IDX_ROWS = 16
TAIL = 8
NEAR_CHUNK = 8
F32 = jnp.float32
BF16 = jnp.bfloat16
I32 = jnp.int32
NT = (((1,), (1,)), ((), ()))
VMEM_LIMIT = 24 * 1024 * 1024


def dot(a, b):
    return jnp.dot(a, b, preferred_element_type=F32)


def dot_nt(a, b):
    return lax.dot_general(a, b, NT, preferred_element_type=F32)


def iota(shape, dim):
    return lax.broadcasted_iota(I32, shape, dim)


def block(array, i):
    return array[:, i * TILE : (i + 1) * TILE]


def as_hot(mask):
    return mask.astype(F32).astype(BF16)


def call(body, outs, args, scratch=(), smem=(), held=(), far=(), small=(), name=None):
    spaces = [
        pltpu.SMEM if k in smem else pltpu.HBM if k in held or k in far else pltpu.VMEM
        for k in range(len(args))
    ]
    outs = tuple(jax.ShapeDtypeStruct(s, d) for s, d in outs)
    size = sum(a.size * a.dtype.itemsize for a in args) + sum(
        o.size * o.dtype.itemsize for o in outs
    )
    buffers = [
        (pltpu.SMEM if k in small else pltpu.VMEM)(args[k].shape, args[k].dtype) for k in held
    ]
    waits = [pltpu.SemaphoreType.DMA(()) for _ in held]

    def wrapped(*refs):
        ins = list(refs[: len(args)])
        rest = refs[len(args) : len(refs) - 2 * len(held)]
        extra = refs[len(refs) - 2 * len(held) :]
        for n, k in enumerate(held):
            ins[k] = pltpu.make_async_copy(ins[k], extra[n], extra[len(held) + n])
            ins[k].start()
            ins[k] = (ins[k], extra[n])
        body(*ins, *rest)

    return pl.pallas_call(
        wrapped,
        out_shape=outs,
        in_specs=[pl.BlockSpec(memory_space=m) for m in spaces],
        out_specs=tuple(pl.BlockSpec(memory_space=pltpu.VMEM) for _ in outs),
        scratch_shapes=list(scratch) + buffers + waits,
        compiler_params=pltpu.CompilerParams(vmem_limit_bytes=VMEM_LIMIT),
        cost_estimate=pl.CostEstimate(flops=0, bytes_accessed=size, transcendentals=0),
        name=name,
    )(*[pltpu.with_memory_space_constraint(a, m) if m is pltpu.HBM else a for a, m in zip(args, spaces)])


def ready(operand):
    operand[0].wait()
    return operand[1]


def far_terms(blocks, compress, coupling, source, owner, place, coef, turned, spread, pick, terms, out_ref):
    coupling = ready(coupling)
    turned[...] = coupling[...].astype(F32).T
    compress = ready(compress)
    for s in range(BLK):
        coef[:, s * RANK : (s + 1) * RANK] = dot_nt(blocks[s], compress[s])
    width = BLK * RANK
    keep = (iota((RANK, width), 1) % RANK) == iota((RANK, width), 0)
    for i in range(INC):
        spread[i * RANK : (i + 1) * RANK, :] = jnp.where(keep, coef[i : i + 1, :], 0.0).astype(BF16)
    source = ready(source)
    tiles = source.shape[1]
    pick[...] = dot(spread[...], as_hot((iota((width, tiles), 0) // RANK) == source[...]))

    def step(pair, carry):
        rows = pl.multiple_of(pair * (2 * RANK), 2 * RANK)
        got = pick[pl.ds(rows, 2 * RANK), :]
        first = jnp.zeros((RANK, tiles), F32)
        second = jnp.zeros((RANK, tiles), F32)
        for r in range(RANK):
            factor = turned[r * RANK : (r + 1) * RANK, :]
            first += got[r : r + 1, :] * factor
            second += got[RANK + r : RANK + r + 1, :] * factor
        terms[pl.ds(rows, 2 * RANK), :] = jnp.concatenate([first, second], axis=0).astype(BF16)
        return carry

    lax.fori_loop(0, INC // 2, step, 0)
    targets = out_ref.shape[0]
    owner, place = ready(owner), ready(place)
    select = as_hot(iota((targets, tiles), 0) == owner[...] * BLK + place[...])
    out_ref[...] = dot_nt(select, terms[...]).astype(BF16)


def far_scratch(tiles):
    return [
        pltpu.VMEM((INC, BLK * RANK), F32),
        pltpu.VMEM((RANK * RANK, tiles), F32),
        pltpu.VMEM((INC * RANK, BLK * RANK), BF16),
        pltpu.VMEM((INC * RANK, tiles), F32),
        pltpu.VMEM((INC * RANK, tiles), BF16),
    ]


def far_up_body(value, compress, coupling, source, owner, place, out_ref, first_out, last_out, *scratch):
    value = ready(value)
    first_out[...] = block(value, 0)
    last_out[...] = block(value, BLK - 1)
    blocks = [block(value, s) for s in range(BLK)]
    far_terms(blocks, compress, coupling, source, owner, place, *scratch, out_ref)


def far_down(arrived_ref, spread, expand):
    rows = arrived_ref.shape[0]
    total = jnp.sum(arrived_ref[...].astype(F32).reshape(rows // BLK, BLK, INC * RANK), axis=0)
    width = INC * RANK
    keep = (iota((INC, width), 1) // RANK) == iota((INC, width), 0)
    for b in range(BLK):
        spread[b * INC : (b + 1) * INC, :] = jnp.where(keep, total[b : b + 1, :], 0.0).astype(BF16)
    fold = as_hot((iota((width, RANK), 0) % RANK) == iota((width, RANK), 1))
    sums = dot(spread[...], fold).astype(BF16)
    expand = ready(expand)
    return [dot(sums[b * INC : (b + 1) * INC, :], expand[b]) for b in range(BLK)]


def order(owner, index, ranks, owners, window, high_out, low_out, bounds_out, rows_out):
    before = as_hot(iota((TILE, TILE), 0) < iota((TILE, TILE), 1))
    number = iota((owners, TILE), 0)
    count = jnp.zeros((owners, 1), F32)
    begin = jnp.zeros((owners, 1), F32)
    hots, carries = [], []
    for c in range(BLK):
        names = block(owner, c)
        hot = (number == names).astype(F32)
        hots.append(hot)
        carries.append(count)
        count = count + jnp.sum(hot, axis=1, keepdims=True)
        begin = begin + jnp.sum((names < number).astype(F32), axis=1, keepdims=True)
    for c in range(BLK):
        rank = dot(hots[c].astype(BF16), before)
        ranks[c : c + 1, :] = jnp.sum(hots[c] * (rank + carries[c] + begin), axis=0, keepdims=True)
    spots = ranks[...].astype(I32)
    high_out[...] = spots // TILE
    low = (spots % TILE).astype(F32).T.astype(I32)
    lane = iota((TILE, TILE), 1)
    for c in range(BLK):
        low_out[c * TILE : (c + 1) * TILE, :] = as_hot(lane == low[:, c : c + 1])
    pair = iota((owners, 2), 1)
    bounds_out[...] = jnp.where(pair == 0, begin, count).astype(I32)
    row = iota((IDX_ROWS, NP_DEV), 0)
    index = index[...]
    digits = jnp.where(row % 2 == 0, index // TILE, index % TILE)
    rows_out[...] = jnp.where(row < 2 * (window // LANES), digits, 0).astype(F32).astype(BF16)


def prepare_body(
    target, origin, own, from_left, from_right, inverse, lower, upper, owner, index, tiles_ref,
    near_out, lower_out, upper_out, lower_edge, upper_edge, high_out, low_out, bounds_out, rows_out,
    cells, total, ranks, tiles, arrivals,
):
    count = tiles_ref.shape[0]
    copies = []
    for c in range(count // NEAR_CHUNK):
        part = pl.ds(c * NEAR_CHUNK, NEAR_CHUNK)
        copy = pltpu.make_async_copy(tiles_ref.at[part], tiles.at[part], arrivals.at[c])
        copy.start()
        copies.append(copy)
    owner, index = ready(owner), ready(index)
    window = max(LANES, -(-(2 * NP_DEV // bounds_out.shape[0]) // LANES) * LANES)
    order(owner, index, ranks, bounds_out.shape[0], window, high_out, low_out, bounds_out, rows_out)
    inverse, lower, upper = ready(inverse), ready(lower), ready(upper)
    for b in range(BLK):
        lower_out[b] = dot(lower[b], inverse[b]).astype(BF16)
        upper_out[b] = dot(upper[b], inverse[b]).astype(BF16)
    lower_edge[...] = lower_out[0]
    upper_edge[...] = upper_out[BLK - 1]
    own = ready(own)
    cells[0] = from_left[...]
    cells[BLK + 1] = from_right[...]
    for b in range(BLK):
        cells[b + 1] = block(own, b)
    total[...] = jnp.zeros_like(total)
    target, origin = ready(target), ready(origin)
    start = lax.axis_index("surf") * BLK - 1
    for c, copy in enumerate(copies):
        copy.wait()
        for k in range(c * NEAR_CHUNK, (c + 1) * NEAR_CHUNK):
            total[target[k]] += dot(cells[origin[k] - start], tiles[k])
    for b in range(BLK):
        near_out[:, b * TILE : (b + 1) * TILE] = total[b]


def solve_body(
    arrived_ref, near_ref, expand, inverse, lower_ref, upper_ref,
    start_out, next_out, left_out, right_out, spread,
):
    far = far_down(arrived_ref, spread, expand)
    inverse = ready(inverse)
    start, low = [], []
    for b in range(BLK):
        field = (block(near_ref, b) + far[b]).astype(BF16)
        value = dot(field, inverse[b])
        start.append(value)
        low.append(value.astype(BF16))
        start_out[:, b * TILE : (b + 1) * TILE] = value
    after = []
    for b in range(BLK):
        value = start[b]
        if b > 0:
            value = value - dot(low[b - 1], lower_ref[b])
        if b < BLK - 1:
            value = value - dot(low[b + 1], upper_ref[b])
        after.append(value)
        next_out[:, b * TILE : (b + 1) * TILE] = value
    last = BLK - 1
    left_out[0] = low[0]
    left_out[1] = after[0].astype(BF16)
    left_out[2] = (start[0] - dot(after[1].astype(BF16), upper_ref[0])).astype(BF16)
    right_out[0] = low[last]
    right_out[1] = after[last].astype(BF16)
    right_out[2] = (start[last] - dot(after[last - 1].astype(BF16), lower_ref[last])).astype(BF16)


def finish_body(
    start_ref, next_ref, from_left, from_right, upper_left, lower_right, lower_ref, upper_ref,
    weight, index_rows, high_ref, low_ref, bounds_ref, send_ref, spread, ordered,
):
    last = BLK - 1
    position = lax.axis_index("surf")
    has_left = (position > 0).astype(F32)
    has_right = (position < lax.axis_size("surf") - 1).astype(F32)
    start = [block(start_ref, b) for b in range(BLK)]
    low = [start[0].astype(BF16), start[last].astype(BF16)]
    now = [block(next_ref, b) for b in range(BLK)]
    beside_left = (from_left[1].astype(F32) - dot(low[0], upper_left[...])) * has_left
    beside_right = (from_right[1].astype(F32) - dot(low[1], lower_right[...])) * has_right
    now[0] = now[0] - dot(from_left[0], lower_ref[0]) * has_left
    now[last] = now[last] - dot(from_right[0], upper_ref[last]) * has_right

    def sweep(values, left, right):
        values = [v.astype(BF16) for v in values]
        chain = [left.astype(BF16)] + values + [right.astype(BF16)]
        return values, [
            start[b] - dot(chain[b], lower_ref[b]) - dot(chain[b + 2], upper_ref[b])
            for b in range(BLK)
        ]

    values, then = sweep(now, beside_left, beside_right)
    beside_left = (from_left[2].astype(F32) - dot(values[0], upper_left[...])) * has_left
    beside_right = (from_right[2].astype(F32) - dot(values[last], lower_right[...])) * has_right
    values, then = sweep(then, beside_left, beside_right)
    weight = ready(weight)
    rows = INC + IDX_ROWS
    for b in range(BLK):
        solved = then[b].astype(BF16).astype(F32)
        shares = solved * block(weight, b)
        every = jnp.concatenate([shares, block(index_rows, b).astype(F32)], axis=0)
        high = high_ref[b : b + 1, :]
        for h in range(BLK):
            spread[h * rows : (h + 1) * rows, b * TILE : (b + 1) * TILE] = jnp.where(
                high == h, every, 0.0
            ).astype(BF16)
    sorted_rows = dot(spread[...], low_ref[...])
    for h in range(BLK):
        ordered[:, h * TILE : (h + 1) * TILE] = sorted_rows[h * rows : (h + 1) * rows]
    owners = send_ref.shape[0]
    pieces = (send_ref.shape[1] - TAIL) // INC
    wide = (pieces + 1) * LANES
    ordered[:, NP_DEV:] = jnp.zeros((rows, ordered.shape[1] - NP_DEV), F32)
    row = iota((TAIL, LANES), 0)
    slot = iota((TAIL, LANES), 1) + (row // 2) * LANES
    for o in range(owners):
        begin = bounds_ref[o, 0]
        base = pl.multiple_of((begin // LANES) * LANES, LANES)
        piece = pltpu.roll(ordered[:, pl.ds(base, wide)], wide - (begin - base), 1)
        parts = [piece[:INC, j * LANES : (j + 1) * LANES] for j in range(pieces)]
        tail = piece[INC : INC + TAIL, :LANES]
        for j in range(1, pieces):
            tail = jnp.where(row // 2 == j, piece[INC : INC + TAIL, j * LANES : (j + 1) * LANES], tail)
        tail = jnp.where(slot >= bounds_ref[o, 1], -16.0, tail)
        send_ref[o] = jnp.concatenate(parts + [tail], axis=0).astype(BF16)


def gather_body(
    arrived_ref, compress, coupling, source, owner, place,
    field_out, out_ref, index, spread, hot, *scratch,
):
    owners, rows, _ = arrived_ref.shape
    pieces = (rows - TAIL) // INC
    for e in range(owners):
        digits = arrived_ref[e].astype(F32)
        tail = digits[INC * pieces :]
        for j in range(pieces):
            k = e * pieces + j
            part = digits[j * INC : (j + 1) * INC]
            high = tail[2 * j : 2 * j + 1]
            index[k : k + 1, :] = tail[2 * j + 1 : 2 * j + 2]
            for h in range(BLK):
                spread[h * INC : (h + 1) * INC, k * LANES : (k + 1) * LANES] = jnp.where(
                    high == h, part, 0.0
                ).astype(BF16)
    columns = index[...].T.astype(I32)
    lane = iota((LANES, TILE), 1)
    for k in range(owners * pieces):
        hot[k * LANES : (k + 1) * LANES, :] = as_hot(lane == columns[:, k : k + 1])
    field = dot(spread[...], hot[...]).astype(BF16)
    blocks = [field[b * INC : (b + 1) * INC] for b in range(BLK)]
    for b in range(BLK):
        field_out[b] = blocks[b]
    far_terms(blocks, compress, coupling, source, owner, place, *scratch, out_ref)


def self_body(field_ref, tiles, out_ref):
    tiles = ready(tiles)
    for b in range(BLK):
        out_ref[:, b * TILE : (b + 1) * TILE] = dot(field_ref[b], tiles[b])


def answer_body(arrived_ref, near_ref, expand, out_ref, spread):
    far = far_down(arrived_ref, spread, expand)
    for b in range(BLK):
        out_ref[:, b * TILE : (b + 1) * TILE] = (block(near_ref, b) + far[b]).astype(BF16)


def exchange(array, surf_count):
    shape = array.shape
    array = array.reshape((surf_count, shape[0] // surf_count) + shape[1:])
    array = lax.all_to_all(array, "surf", split_axis=0, concat_axis=0, tiled=True)
    return array.reshape(shape)


def shards(
    currents, near_tiles, near_target, near_source, primal_compress, primal_expand, primal_coupling,
    far_source, far_owner, far_block, gram_inverse, gram_lower, gram_upper, refine_weight,
    dual_owner, dual_index, dual_self, dual_compress, dual_expand, dual_coupling,
):
    surf_count = lax.axis_size("surf")
    tiles = far_source.shape[0]
    near_count = near_tiles.shape[0]
    targets = surf_count * BLK
    capacity = max(2, 2 * NP_DEV // surf_count)
    pieces = -(-capacity // LANES)
    to_right = [(i, (i + 1) % surf_count) for i in range(surf_count)]
    to_left = [((i + 1) % surf_count, i) for i in range(surf_count)]
    lists = (far_source.reshape(1, tiles), far_owner.reshape(1, tiles), far_block.reshape(1, tiles))
    square = ((TILE, TILE), BF16)
    cube = ((BLK, TILE, TILE), BF16)

    partial, first, last = call(
        far_up_body,
        [((targets, INC * RANK), BF16), ((INC, TILE), BF16), ((INC, TILE), BF16)],
        (currents, primal_compress, primal_coupling) + lists,
        scratch=far_scratch(tiles),
        held=(2, 0, 1, 3, 4, 5),
        name="far_up",
    )
    from_left = lax.ppermute(last, "surf", to_right)
    from_right = lax.ppermute(first, "surf", to_left)
    arrived = exchange(partial, surf_count)

    near_part, lower, upper, lower_edge, upper_edge, high, low, bounds, index_rows = call(
        prepare_body,
        [
            ((INC, NP_DEV), F32), cube, cube, square, square, ((BLK, TILE), I32),
            ((NP_DEV, TILE), BF16), ((surf_count, 2), I32), ((IDX_ROWS, NP_DEV), BF16),
        ],
        (
            near_target, near_source, currents, from_left, from_right, gram_inverse, gram_lower,
            gram_upper, dual_owner.reshape(1, NP_DEV), dual_index.reshape(1, NP_DEV), near_tiles,
        ),
        scratch=[
            pltpu.VMEM((BLK + 2, INC, TILE), BF16),
            pltpu.VMEM((BLK, INC, TILE), F32),
            pltpu.VMEM((BLK, TILE), F32),
            pltpu.VMEM(near_tiles.shape, BF16),
            pltpu.SemaphoreType.DMA((near_count // NEAR_CHUNK,)),
        ],
        held=(8, 9, 5, 6, 7, 2, 0, 1),
        far=(10,),
        small=(0, 1),
        name="prepare",
    )
    upper_left = lax.ppermute(upper_edge, "surf", to_right)
    lower_right = lax.ppermute(lower_edge, "surf", to_left)

    start, after, left_note, right_note = call(
        solve_body,
        [((INC, NP_DEV), F32)] * 2 + [((3, INC, TILE), BF16)] * 2,
        (arrived, near_part, primal_expand, gram_inverse, lower, upper),
        scratch=[pltpu.VMEM((BLK * INC, INC * RANK), BF16)],
        held=(2, 3),
        name="solve",
    )
    note_left = lax.ppermute(right_note, "surf", to_right)
    note_right = lax.ppermute(left_note, "surf", to_left)
    rows = INC + IDX_ROWS
    (send,) = call(
        finish_body,
        [((surf_count, INC * pieces + TAIL, LANES), BF16)],
        (
            start, after, note_left, note_right, upper_left, lower_right, lower, upper,
            refine_weight.reshape(1, NP_DEV), index_rows, high, low, bounds,
        ),
        scratch=[
            pltpu.VMEM((BLK * rows, NP_DEV), BF16),
            pltpu.VMEM((rows, NP_DEV + (pieces + 1) * LANES), F32),
        ],
        smem=(12,),
        held=(8,),
        name="finish",
    )
    shares = lax.all_to_all(send, "surf", split_axis=0, concat_axis=0, tiled=True)
    slots = surf_count * pieces * LANES
    field, partial = call(
        gather_body,
        [((BLK, INC, TILE), BF16), ((targets, INC * RANK), BF16)],
        (shares, dual_compress, dual_coupling) + lists,
        scratch=[
            pltpu.VMEM((surf_count * pieces, LANES), F32),
            pltpu.VMEM((BLK * INC, slots), BF16),
            pltpu.VMEM((slots, TILE), BF16),
        ]
        + far_scratch(tiles),
        held=(2, 1, 3, 4, 5),
        name="gather",
    )
    arrived = exchange(partial, surf_count)
    (near_dual,) = call(
        self_body, [((INC, NP_DEV), F32)], (field, dual_self), held=(1,), name="self_part"
    )
    (response,) = call(
        answer_body,
        [((INC, NP_DEV), BF16)],
        (arrived, near_dual, dual_expand),
        scratch=[pltpu.VMEM((BLK * INC, INC * RANK), BF16)],
        held=(2,),
        name="answer",
    )
    return response


def solution(mesh):
    both = ("groups", "surf")
    row, flat = P(None, both), P(both)
    cube, flat2 = P(both, None, None), P(both, None)
    return jax.shard_map(
        shards,
        mesh=mesh,
        in_specs=(
            row, cube, flat, flat, cube, cube, flat2, flat, flat2, flat, cube, cube, cube, flat,
            flat2, flat, cube, cube, cube, flat2,
        ),
        out_specs=row,
        check_vma=False,
    )
```

time: 95.4 us -> 84 us (0.88)
  local copies, waits for them, and re-layouts: 13.5 us -> 3.1 us
  blocking collectives: 20.8 us -> 16.2 us
  waiting for transfers between devices: 11.7 us -> 15.7 us
  Pallas kernels: 21.7 us -> 24 us
  starting transfers between devices: 25.6 us -> 24.4 us
    unnamed x46 -> x8, local copies, waits for them, and re-layouts: 11.4 us -> 3.1 us
    ppermute x4, waiting for transfers between devices: 0.01 us -> 5.43 us  [the longest x1 5.42 us: shards(): from_left = lax.ppermute(last, 'surf', to_right)]
    all_to_all x1, blocking collectives: 20.8 us -> 16.2 us  [shards(): lax.all_to_all(send, 'surf', split_axis=0, concat_axis=0, tiled=True)]
    ppermute x1, starting transfers between devices: 4.3 us -> 0.06 us  [shards(): note_left = lax.ppermute(right_note, 'surf', to_right)]
    ppermute x1, starting transfers between devices: 1.29 us -> 4.43 us  [shards(): note_right = lax.ppermute(left_note, 'surf', to_left)]
    pallas_call x9 -> x7, Pallas kernels: 21.7 us -> 24 us  [call(): pl.pallas_call(wrapped, out_shape=outs, in_specs=[pl.BlockSpec(memory_spa...]
    all_to_all x2, starting transfers between devices: 12.9 us -> 10.9 us  [exchange(): lax.all_to_all(array, 'surf', split_axis=0, concat_axis=0, tiled=True)]
    ppermute x1, waiting for transfers between devices: 1.94 us -> 0.01 us  [shards(): note_right = lax.ppermute(left_note, 'surf', to_left)]
  transfers between devices with their start and end apart: 8 -> 8, of which waited for: 2 -> 3; matrix products, arithmetic and copies ran while one was open for 2% -> 0% of each run, Pallas kernels for 12% -> 12%
where the time goes in v2:
time: 84 us; the launch traced here: 83.4 us
  starting transfers between devices  24.4 us (29%)
  Pallas kernels  24 us (29%)
  blocking collectives  16.2 us (19%)
  waiting for transfers between devices  15.7 us (19%)
  local copies, waits for them, and re-layouts  3.1 us (4%)
    pallas_call x7, Pallas kernels, call(): pl.pallas_call(wrapped, out_shape=outs, in_specs=[pl.BlockSpec(memory_spa...  24 us
    all_to_all x1, blocking collectives, shards(): lax.all_to_all(send, 'surf', split_axis=0, concat_axis=0, tiled=True)  16.2 us
    all_to_all x2, starting transfers between devices, exchange(): lax.all_to_all(array, 'surf', split_axis=0, concat_axis=0, tiled=True)  10.9 us
    all_to_all x2, waiting for transfers between devices, exchange(): lax.all_to_all(array, 'surf', split_axis=0, concat_axis=0, tiled=True)  8.48 us
    ppermute x1, waiting for transfers between devices, shards(): from_left = lax.ppermute(last, 'surf', to_right)  5.42 us
    ppermute x1, starting transfers between devices, shards(): lower_right = lax.ppermute(lower_edge, 'surf', to_left)  4.44 us
    ppermute x1, starting transfers between devices, shards(): note_right = lax.ppermute(left_note, 'surf', to_left)  4.43 us
    ppermute x1, starting transfers between devices, shards(): from_right = lax.ppermute(first, 'surf', to_left)  4.08 us
  transfers between devices with their start and end apart: 8, of which 3 were waited for; matrix products, arithmetic and copies ran while one was open for 0% of the time, Pallas kernels for 12%

profile of v2, /device:TPU:0, one launch (start us, length us, event | category | flops | bytes accessed | tf_op | source)
XLA Modules:
  0.0 83.4 jit_solution(2229973877600146248)
XLA Ops:
  0.0 4.1 %far_up.1 = (bf16[128,1024]{1,0:T(8,128)(2,1)}, bf16[32,256]{1,0:T(8,128)(2,1)S(1)}, bf16[32,256]{1,0:T(8,128)(2,1)S(1)}) custom-call(bf16[32,2048]{1,0:T(8,128)(2,1)} %refs_2_.6, bf16[8,32,256]{2,1,0:T(8,128)(2,1)} %refs_1_.4, bf16[128,1024]{1,0:T(8,128)(2,1)} %refs_2_.5, s32[1,128]{1,0:T(1,128)} %bitcast.15, s32[1,128]{1,0:T(1,128)} %bitcast.17, ...), custom_call_target="tpu_custom_call" | custom-call | bytes 820736 | tf_op jit(solution)/shard_map/far_up/pallas_call | solution.py:68
  4.1 7.4 %all-to-all-start = ((bf16[16,8,1024]{2,1,0:T(8,128)(2,1)}), bf16[16,8,1024]{2,1,0:T(8,128)(2,1)S(1)}, u32[]{:S(2)}, u32[]{:S(2)}) async-start(bf16[16,8,1024]{2,1,0:T(8,128)(2,1)} %bitcast.3), calls=%async_computation | async-start | bytes 524288 | tf_op jit(solution)/shard_map/all_to_all | solution.py:351
  11.5 0.4 collective-permute-start
  11.9 4.1 %collective-permute-start.1 = (bf16[32,256]{1,0:T(8,128)(2,1)S(1)}, bf16[32,256]{1,0:T(8,128)(2,1)S(1)}, u32[]{:S(2)}, u32[]{:S(2)}) collective-permute-start(bf16[32,256]{1,0:T(8,128)(2,1)S(1)} %get-tuple-element.25), channel_id=1, source_target_pairs={{1,0},{2,1},{3,2},{4,3},{5,4},{6,5},{7,6},{8,7},{9,8},{10,9},{11,1... | collective-permute-start | bytes 49160 | tf_op jit(solution)/shard_map/ppermute | solution.py:381
  16.0 5.4 %collective-permute-done.refs_3_ = bf16[32,256]{1,0:T(8,128)(2,1)S(1)} collective-permute-done((bf16[32,256]{1,0:T(8,128)(2,1)S(1)}, bf16[32,256]{1,0:T(8,128)(2,1)S(1)}, u32[]{:S(2)}, u32[]{:S(2)}) %collective-permute-start) | collective-permute-done | bytes 16416 | tf_op jit(solution)/shard_map/ppermute | solution.py:380
  21.4 0.0 collective-permute-done.1.refs_4_
  21.4 6.6 %prepare.1 = (f32[32,2048]{1,0:T(8,128)S(1)}, bf16[8,256,256]{2,1,0:T(8,128)(2,1)S(1)}, bf16[8,256,256]{2,1,0:T(8,128)(2,1)S(1)}, bf16[256,256]{1,0:T(8,128)(2,1...) custom-call(s32[48]{0:T(128)} %refs_0_.3, ...), custom_call_target="tpu_custom_call" | custom-call | bytes 13361664 | tf_op jit(solution)/shard_map/prepare/pallas_call | solution.py:68
  28.0 0.0 copy-start
  28.0 0.7 copy-done
  28.7 0.0 copy-start.2
  28.7 0.6 copy-done.2
  29.3 0.0 collective-permute-start.4
  29.3 4.4 %collective-permute-start.5 = (bf16[256,256]{1,0:T(8,128)(2,1)}, bf16[256,256]{1,0:T(8,128)(2,1)}, u32[]{:S(2)}, u32[]{:S(2)}) collective-permute-start(bf16[256,256]{1,0:T(8,128)(2,1)} %get-tuple-element.34), channel_id=1, source_target_pairs={{1,0},{2,1},{3,2},{4,3},{5,4},{6,5},{7,6},{8,7},{9,8},{10,9},{11,1... | collective-permute-start | bytes 393224 | tf_op jit(solution)/shard_map/ppermute | solution.py:407
  33.7 0.0 all-to-all-done
  33.7 0.0 copy-start.1
  33.7 0.9 %copy-done.1 = f32[32,2048]{1,0:T(8,128)S(1)} copy-done((f32[32,2048]{1,0:T(8,128)S(1)}, f32[32,2048]{1,0:T(8,128)}, u32[]{:S(2)}) %copy-start.1) | copy-done | bytes 262168
  34.7 2.2 %solve.1 = (f32[32,2048]{1,0:T(8,128)S(1)}, f32[32,2048]{1,0:T(8,128)S(1)}, bf16[3,32,256]{2,1,0:T(8,128)(2,1)S(1)}, bf16[3,32,256]{2,1,0:T(8,128)(2,1)S(1)}) custom-call(bf16[128,1024]{1,0:T(8,128)(2,1)S(1)} %bitcast.11, f32[32,2048]{1,0:T(8,128)S(1)} %copy-done.1, bf16[8,32,256]{2,1,0:T(8,128)(2,1)} %refs_2_.7, bf16[8,256,256]{2,1,0:T(8,128)(2,1)} %refs_3_.1, ...), custom_call_target="tpu_custom_call" | custom-call | bytes 4423680 | tf_op jit(solution)/shard_map/solve/pallas_call | solution.py:68
  36.9 0.1 collective-permute-start.2
  36.9 4.4 %collective-permute-start.3 = (bf16[3,32,256]{2,1,0:T(8,128)(2,1)S(1)}, bf16[3,32,256]{2,1,0:T(8,128)(2,1)S(1)}, u32[]{:S(2)}, u32[]{:S(2)}) collective-permute-start(bf16[3,32,256]{2,1,0:T(8,128)(2,1)S(1)} %get-tuple-element.32), channel_id=1, source_target_pairs={{1,0},{2,1},{3,2},{4,3},{5,4},{6,5},{7,6},{8,7},{9,8},{10,9},{11,1... | collective-permute-start | bytes 147464 | tf_op jit(solution)/shard_map/ppermute | solution.py:418
  41.4 0.0 collective-permute-done.4.refs_4_
  41.4 0.0 collective-permute-done.5.refs_5_
  41.4 1.8 %collective-permute-done.2.refs_2_ = bf16[3,32,256]{2,1,0:T(8,128)(2,1)S(1)} collective-permute-done((bf16[3,32,256]{2,1,0:T(8,128)(2,1)S(1)}, bf16[3,32,256]{2,1,0:T(8,128)(2,1)S(1)}, u32[]{:S(2)}, u32[]{:S(2)}) %collective-permute-start.2) | collective-permute-done | bytes 49184 | tf_op jit(solution)/shard_map/ppermute | solution.py:417
  43.1 0.0 collective-permute-done.3.refs_3_
  43.1 0.0 copy-start.3
  43.1 0.8 %copy-done.3 = bf16[16,2048]{1,0:T(8,128)(2,1)S(1)} copy-done((bf16[16,2048]{1,0:T(8,128)(2,1)S(1)}, bf16[16,2048]{1,0:T(8,128)(2,1)}, u32[]{:S(2)}) %copy-start.3) | copy-done | bytes 65560
  44.0 2.7 %finish.1 = bf16[16,72,128]{2,1,0:T(8,128)(2,1)S(1)} custom-call(f32[32,2048]{1,0:T(8,128)S(1)} %get-tuple-element.29.refs_0_, f32[32,2048]{1,0:T(8,128)S(1)} %get-tuple-element.30.refs_1_, bf16[3,32,256]{2,1,0:T(8,128)(2,1)S(1)} %collective-permute-done.2.refs_2_, bf16[3,32,256]{2,1,0:T(8,128)(2,1)S(1)} %collective-permute-done.3.refs_3_, ...), custom_call_target="tpu_custom_call" | custom-call | bytes 4407424 | tf_op jit(solution)/shard_map/finish/pallas_call | solution.py:68
  46.7 16.2 %all_to_all.15.refs_0_ = bf16[16,72,128]{2,1,0:T(8,128)(2,1)S(1)} all-to-all(bf16[16,72,128]{2,1,0:T(8,128)(2,1)S(1)} %finish.1), channel_id=1, replica_groups=mesh['groups'=2,'surf'=16] {'surf'}, dimensions={0} | all-to-all | bytes 589824 | tf_op jit(solution)/shard_map/all_to_all | solution.py:435
  62.9 5.1 %gather.1 = (bf16[8,32,256]{2,1,0:T(8,128)(2,1)S(1)}, bf16[128,1024]{1,0:T(8,128)(2,1)}) custom-call(bf16[16,72,128]{2,1,0:T(8,128)(2,1)S(1)} %all_to_all.15.refs_0_, bf16[8,32,256]{2,1,0:T(8,128)(2,1)} %refs_1_.6, bf16[128,1024]{1,0:T(8,128)(2,1)} %refs_2_.8, s32[1,128]{1,0:T(1,128)} %bitcast.16, s32[1,128]{1,0:T(1,128)} %bitcast.18, s32[1,128]{1,0:T(1,128)} %bitcast.20), custom_call_target="tpu_custom_call" | custom-call | bytes 1082880 | tf_op jit(solution)/shard_map/gather/pallas_call | solution.py:68
  68.0 3.5 %all-to-all-start.2 = ((bf16[16,8,1024]{2,1,0:T(8,128)(2,1)}), bf16[16,8,1024]{2,1,0:T(8,128)(2,1)S(1)}, u32[]{:S(2)}, u32[]{:S(2)}) async-start(bf16[16,8,1024]{2,1,0:T(8,128)(2,1)} %bitcast.8), calls=%async_computation.2 | async-start | bytes 524288 | tf_op jit(solution)/shard_map/all_to_all | solution.py:351
  71.6 1.5 %self_part.1.refs_1_ = f32[32,2048]{1,0:T(8,128)S(1)} custom-call(bf16[8,32,256]{2,1,0:T(8,128)(2,1)S(1)} %get-tuple-element.40.refs_0_, bf16[8,256,256]{2,1,0:T(8,128)(2,1)} %refs_1_.7), custom_call_target="tpu_custom_call" | custom-call | bytes 1441792 | tf_op jit(solution)/shard_map/self_part/pallas_call | solution.py:68
  73.1 8.5 %all-to-all-done.2 = bf16[16,8,1024]{2,1,0:T(8,128)(2,1)S(1)} async-done(((bf16[16,8,1024]{2,1,0:T(8,128)(2,1)}), bf16[16,8,1024]{2,1,0:T(8,128)(2,1)S(1)}, u32[]{:S(2)}, u32[]{:S(2)}) %all-to-all-start.2) | async-done | bytes 262176 | tf_op jit(solution)/shard_map/all_to_all | solution.py:351
  81.6 1.9 %answer.1 = bf16[32,2048]{1,0:T(8,128)(2,1)} custom-call(bf16[128,1024]{1,0:T(8,128)(2,1)S(1)} %bitcast.10, f32[32,2048]{1,0:T(8,128)S(1)} %self_part.1.refs_1_, bf16[8,32,256]{2,1,0:T(8,128)(2,1)} %refs_2_.9), custom_call_target="tpu_custom_call" | custom-call | bytes 786432 | tf_op jit(solution)/shard_map/answer/pallas_call | solution.py:68
Async XLA Ops:
  4.1 29.7 %all-to-all-start = ((bf16[16,8,1024]{2,1,0:T(8,128)(2,1)}), bf16[16,8,1024]{2,1,0:T(8,128)(2,1)S(1)}, u32[]{:S(2)}, u32[]{:S(2)}) async-start(bf16[16,8,1024]{2,1,0:T(8,128)(2,1)} %bitcast.3), calls=%async_computation | async-start | bytes 524288 | tf_op jit(solution)/shard_map/all_to_all | solution.py:351
  11.5 9.9 %collective-permute-start = (bf16[32,256]{1,0:T(8,128)(2,1)S(1)}, bf16[32,256]{1,0:T(8,128)(2,1)S(1)}, u32[]{:S(2)}, u32[]{:S(2)}) collective-permute-start(bf16[32,256]{1,0:T(8,128)(2,1)S(1)} %get-tuple-element.24), channel_id=1, source_target_pairs={{0,1},{1,2},{2,3},{3,4},{4,5},{5,6},{6,7},{7,8},{8,9},{9,10},{10,1... | collective-permute-start | bytes 49160 | tf_op jit(solution)/shard_map/ppermute | solution.py:380
  11.9 9.5 %collective-permute-start.1 = (bf16[32,256]{1,0:T(8,128)(2,1)S(1)}, bf16[32,256]{1,0:T(8,128)(2,1)S(1)}, u32[]{:S(2)}, u32[]{:S(2)}) collective-permute-start(bf16[32,256]{1,0:T(8,128)(2,1)S(1)} %get-tuple-element.25), channel_id=1, source_target_pairs={{1,0},{2,1},{3,2},{4,3},{5,4},{6,5},{7,6},{8,7},{9,8},{10,9},{11,1... | collective-permute-start | bytes 49160 | tf_op jit(solution)/shard_map/ppermute | solution.py:381
  28.0 0.7 copy-start
  28.7 0.6 copy-start.2
  29.3 12.1 %collective-permute-start.4 = (bf16[256,256]{1,0:T(8,128)(2,1)}, bf16[256,256]{1,0:T(8,128)(2,1)S(1)}, u32[]{:S(2)}, u32[]{:S(2)}) collective-permute-start(bf16[256,256]{1,0:T(8,128)(2,1)} %get-tuple-element.33), channel_id=1, source_target_pairs={{0,1},{1,2},{2,3},{3,4},{4,5},{5,6},{6,7},{7,8},{8,9},{9,10},{10,1... | collective-permute-start | bytes 393224 | tf_op jit(solution)/shard_map/ppermute | solution.py:406
  29.3 12.1 %collective-permute-start.5 = (bf16[256,256]{1,0:T(8,128)(2,1)}, bf16[256,256]{1,0:T(8,128)(2,1)}, u32[]{:S(2)}, u32[]{:S(2)}) collective-permute-start(bf16[256,256]{1,0:T(8,128)(2,1)} %get-tuple-element.34), channel_id=1, source_target_pairs={{1,0},{2,1},{3,2},{4,3},{5,4},{6,5},{7,6},{8,7},{9,8},{10,9},{11,1... | collective-permute-start | bytes 393224 | tf_op jit(solution)/shard_map/ppermute | solution.py:407
  33.7 1.0 %copy-start.1 = (f32[32,2048]{1,0:T(8,128)S(1)}, f32[32,2048]{1,0:T(8,128)}, u32[]{:S(2)}) copy-start(f32[32,2048]{1,0:T(8,128)} %copy-done) | copy-start | bytes 786436
  36.9 6.3 %collective-permute-start.2 = (bf16[3,32,256]{2,1,0:T(8,128)(2,1)S(1)}, bf16[3,32,256]{2,1,0:T(8,128)(2,1)S(1)}, u32[]{:S(2)}, u32[]{:S(2)}) collective-permute-start(bf16[3,32,256]{2,1,0:T(8,128)(2,1)S(1)} %get-tuple-element.31), channel_id=1, source_target_pairs={{0,1},{1,2},{2,3},{3,4},{4,5},{5,6},{6,7},{7,8},{8,9},{9,10},{10,1... | collective-permute-start | bytes 147464 | tf_op jit(solution)/shard_map/ppermute | solution.py:417
  36.9 6.2 %collective-permute-start.3 = (bf16[3,32,256]{2,1,0:T(8,128)(2,1)S(1)}, bf16[3,32,256]{2,1,0:T(8,128)(2,1)S(1)}, u32[]{:S(2)}, u32[]{:S(2)}) collective-permute-start(bf16[3,32,256]{2,1,0:T(8,128)(2,1)S(1)} %get-tuple-element.32), channel_id=1, source_target_pairs={{1,0},{2,1},{3,2},{4,3},{5,4},{6,5},{7,6},{8,7},{9,8},{10,9},{11,1... | collective-permute-start | bytes 147464 | tf_op jit(solution)/shard_map/ppermute | solution.py:418
  43.1 0.8 %copy-start.3 = (bf16[16,2048]{1,0:T(8,128)(2,1)S(1)}, bf16[16,2048]{1,0:T(8,128)(2,1)}, u32[]{:S(2)}) copy-start(bf16[16,2048]{1,0:T(8,128)(2,1)} %copy-done.2) | copy-start | bytes 196612
  68.0 13.6 %all-to-all-start.2 = ((bf16[16,8,1024]{2,1,0:T(8,128)(2,1)}), bf16[16,8,1024]{2,1,0:T(8,128)(2,1)S(1)}, u32[]{:S(2)}, u32[]{:S(2)}) async-start(bf16[16,8,1024]{2,1,0:T(8,128)(2,1)} %bitcast.8), calls=%async_computation.2 | async-start | bytes 524288 | tf_op jit(solution)/shard_map/all_to_all | solution.py:351

commit v3 on v2

--- a/solution.py
+++ b/solution.py
@@ -41,14 +41,15 @@
     return mask.astype(F32).astype(BF16)
 
 
-def call(body, outs, args, scratch=(), smem=(), held=(), far=(), small=(), name=None):
+def call(body, outs, args, scratch=(), smem=(), held=(), far=(), small=(), pinned=(), kept=(), flops=0, name=None):
     spaces = [
         pltpu.SMEM if k in smem else pltpu.HBM if k in held or k in far else pltpu.VMEM
         for k in range(len(args))
     ]
-    outs = tuple(jax.ShapeDtypeStruct(s, d) for s, d in outs)
-    size = sum(a.size * a.dtype.itemsize for a in args) + sum(
-        o.size * o.dtype.itemsize for o in outs
+    size = sum(a.size * a.dtype.itemsize for a in args)
+    outs = tuple(
+        pltpu.VMEM(s, d) if k in kept else jax.ShapeDtypeStruct(s, d)
+        for k, (s, d) in enumerate(outs)
     )
     buffers = [
         (pltpu.SMEM if k in small else pltpu.VMEM)(args[k].shape, args[k].dtype) for k in held
@@ -72,14 +73,23 @@
         out_specs=tuple(pl.BlockSpec(memory_space=pltpu.VMEM) for _ in outs),
         scratch_shapes=list(scratch) + buffers + waits,
         compiler_params=pltpu.CompilerParams(vmem_limit_bytes=VMEM_LIMIT),
-        cost_estimate=pl.CostEstimate(flops=0, bytes_accessed=size, transcendentals=0),
+        cost_estimate=pl.CostEstimate(flops=flops, bytes_accessed=size, transcendentals=0),
         name=name,
-    )(*[pltpu.with_memory_space_constraint(a, m) if m is pltpu.HBM else a for a, m in zip(args, spaces)])
+    )(*[pltpu.with_memory_space_constraint(a, m) if m is pltpu.HBM or k in pinned else a for k, (a, m) in enumerate(zip(args, spaces))])
 
 
 def ready(operand):
     operand[0].wait()
     return operand[1]
+
+
+def fill_hot(hot, columns):
+    height, count = columns.shape
+    columns = columns.astype(BF16)
+    lane = iota((height, TILE), 1).astype(F32).astype(BF16)
+    one, zero = jnp.ones((height, TILE), BF16), jnp.zeros((height, TILE), BF16)
+    for k in range(count):
+        hot[k * height : (k + 1) * height, :] = jnp.where(lane == columns[:, k : k + 1], one, zero)
 
 
 def far_terms(blocks, compress, coupling, source, owner, place, coef, turned, spread, pick, terms, out_ref):
@@ -125,10 +135,8 @@
     ]
 
 
-def far_up_body(value, compress, coupling, source, owner, place, out_ref, first_out, last_out, *scratch):
+def far_up_body(value, compress, coupling, source, owner, place, out_ref, *scratch):
     value = ready(value)
-    first_out[...] = block(value, 0)
-    last_out[...] = block(value, BLK - 1)
     blocks = [block(value, s) for s in range(BLK)]
     far_terms(blocks, compress, coupling, source, owner, place, *scratch, out_ref)
 
@@ -164,10 +172,7 @@
         ranks[c : c + 1, :] = jnp.sum(hots[c] * (rank + carries[c] + begin), axis=0, keepdims=True)
     spots = ranks[...].astype(I32)
     high_out[...] = spots // TILE
-    low = (spots % TILE).astype(F32).T.astype(I32)
-    lane = iota((TILE, TILE), 1)
-    for c in range(BLK):
-        low_out[c * TILE : (c + 1) * TILE, :] = as_hot(lane == low[:, c : c + 1])
+    low_out[...] = (spots % TILE).astype(F32).T
     pair = iota((owners, 2), 1)
     bounds_out[...] = jnp.where(pair == 0, begin, count).astype(I32)
     row = iota((IDX_ROWS, NP_DEV), 0)
@@ -179,7 +184,7 @@
 def prepare_body(
     target, origin, own, from_left, from_right, inverse, lower, upper, owner, index, tiles_ref,
     near_out, lower_out, upper_out, lower_edge, upper_edge, high_out, low_out, bounds_out, rows_out,
-    cells, total, ranks, tiles, arrivals,
+    cells, total, products, ranks, tiles, arrivals,
 ):
     count = tiles_ref.shape[0]
     copies = []
@@ -198,8 +203,8 @@
     lower_edge[...] = lower_out[0]
     upper_edge[...] = upper_out[BLK - 1]
     own = ready(own)
-    cells[0] = from_left[...]
-    cells[BLK + 1] = from_right[...]
+    cells[0] = block(from_left, BLK - 1)
+    cells[BLK + 1] = block(from_right, 0)
     for b in range(BLK):
         cells[b + 1] = block(own, b)
     total[...] = jnp.zeros_like(total)
@@ -208,7 +213,9 @@
     for c, copy in enumerate(copies):
         copy.wait()
         for k in range(c * NEAR_CHUNK, (c + 1) * NEAR_CHUNK):
-            total[target[k]] += dot(cells[origin[k] - start], tiles[k])
+            products[k] = dot(cells[origin[k] - start], tiles[k])
+    for k in range(count):
+        total[target[k]] += products[k]
     for b in range(BLK):
         near_out[:, b * TILE : (b + 1) * TILE] = total[b]
 
@@ -246,8 +253,9 @@
 
 def finish_body(
     start_ref, next_ref, from_left, from_right, upper_left, lower_right, lower_ref, upper_ref,
-    weight, index_rows, high_ref, low_ref, bounds_ref, send_ref, spread, ordered,
+    weight, index_rows, high_ref, low_ref, bounds_ref, send_ref, spread, hot, ordered,
 ):
+    fill_hot(hot, low_ref[...])
     last = BLK - 1
     position = lax.axis_index("surf")
     has_left = (position > 0).astype(F32)
@@ -277,13 +285,13 @@
     for b in range(BLK):
         solved = then[b].astype(BF16).astype(F32)
         shares = solved * block(weight, b)
-        every = jnp.concatenate([shares, block(index_rows, b).astype(F32)], axis=0)
-        high = high_ref[b : b + 1, :]
+        every = jnp.concatenate([shares.astype(BF16), block(index_rows, b)], axis=0)
+        high = high_ref[b : b + 1, :].astype(F32).astype(BF16)
         for h in range(BLK):
             spread[h * rows : (h + 1) * rows, b * TILE : (b + 1) * TILE] = jnp.where(
-                high == h, every, 0.0
-            ).astype(BF16)
-    sorted_rows = dot(spread[...], low_ref[...])
+                high == h, every, jnp.zeros_like(every)
+            )
+    sorted_rows = dot(spread[...], hot[...])
     for h in range(BLK):
         ordered[:, h * TILE : (h + 1) * TILE] = sorted_rows[h * rows : (h + 1) * rows]
     owners = send_ref.shape[0]
@@ -311,21 +319,18 @@
     owners, rows, _ = arrived_ref.shape
     pieces = (rows - TAIL) // INC
     for e in range(owners):
-        digits = arrived_ref[e].astype(F32)
-        tail = digits[INC * pieces :]
+        tail = arrived_ref[e].astype(F32)[INC * pieces :]
+        marks = tail.astype(BF16)
         for j in range(pieces):
             k = e * pieces + j
-            part = digits[j * INC : (j + 1) * INC]
-            high = tail[2 * j : 2 * j + 1]
+            part = arrived_ref[e, j * INC : (j + 1) * INC, :]
+            high = marks[2 * j : 2 * j + 1]
             index[k : k + 1, :] = tail[2 * j + 1 : 2 * j + 2]
             for h in range(BLK):
                 spread[h * INC : (h + 1) * INC, k * LANES : (k + 1) * LANES] = jnp.where(
-                    high == h, part, 0.0
-                ).astype(BF16)
-    columns = index[...].T.astype(I32)
-    lane = iota((LANES, TILE), 1)
-    for k in range(owners * pieces):
-        hot[k * LANES : (k + 1) * LANES, :] = as_hot(lane == columns[:, k : k + 1])
+                    high == h, part, jnp.zeros_like(part)
+                )
+    fill_hot(hot, index[...].T)
     field = dot(spread[...], hot[...]).astype(BF16)
     blocks = [field[b * INC : (b + 1) * INC] for b in range(BLK)]
     for b in range(BLK):
@@ -369,23 +374,24 @@
     square = ((TILE, TILE), BF16)
     cube = ((BLK, TILE, TILE), BF16)
 
-    partial, first, last = call(
+    from_left = lax.ppermute(currents, "surf", to_right)
+    from_right = lax.ppermute(currents, "surf", to_left)
+    (partial,) = call(
         far_up_body,
-        [((targets, INC * RANK), BF16), ((INC, TILE), BF16), ((INC, TILE), BF16)],
+        [((targets, INC * RANK), BF16)],
         (currents, primal_compress, primal_coupling) + lists,
         scratch=far_scratch(tiles),
         held=(2, 0, 1, 3, 4, 5),
+        flops=10**11,
         name="far_up",
     )
-    from_left = lax.ppermute(last, "surf", to_right)
-    from_right = lax.ppermute(first, "surf", to_left)
     arrived = exchange(partial, surf_count)
 
     near_part, lower, upper, lower_edge, upper_edge, high, low, bounds, index_rows = call(
         prepare_body,
         [
             ((INC, NP_DEV), F32), cube, cube, square, square, ((BLK, TILE), I32),
-            ((NP_DEV, TILE), BF16), ((surf_count, 2), I32), ((IDX_ROWS, NP_DEV), BF16),
+            ((TILE, BLK), F32), ((surf_count, 2), I32), ((IDX_ROWS, NP_DEV), BF16),
         ],
         (
             near_target, near_source, currents, from_left, from_right, gram_inverse, gram_lower,
@@ -394,6 +400,7 @@
         scratch=[
             pltpu.VMEM((BLK + 2, INC, TILE), BF16),
             pltpu.VMEM((BLK, INC, TILE), F32),
+            pltpu.VMEM((near_count, INC, TILE), F32),
             pltpu.VMEM((BLK, TILE), F32),
             pltpu.VMEM(near_tiles.shape, BF16),
             pltpu.SemaphoreType.DMA((near_count // NEAR_CHUNK,)),
@@ -401,6 +408,8 @@
         held=(8, 9, 5, 6, 7, 2, 0, 1),
         far=(10,),
         small=(0, 1),
+        kept=(0, 8),
+        flops=10**11,
         name="prepare",
     )
     upper_left = lax.ppermute(upper_edge, "surf", to_right)
@@ -412,6 +421,7 @@
         (arrived, near_part, primal_expand, gram_inverse, lower, upper),
         scratch=[pltpu.VMEM((BLK * INC, INC * RANK), BF16)],
         held=(2, 3),
+        pinned=(1,),
         name="solve",
     )
     note_left = lax.ppermute(right_note, "surf", to_right)
@@ -426,10 +436,12 @@
         ),
         scratch=[
             pltpu.VMEM((BLK * rows, NP_DEV), BF16),
+            pltpu.VMEM((NP_DEV, TILE), BF16),
             pltpu.VMEM((rows, NP_DEV + (pieces + 1) * LANES), F32),
         ],
         smem=(12,),
         held=(8,),
+        pinned=(9,),
         name="finish",
     )
     shares = lax.all_to_all(send, "surf", split_axis=0, concat_axis=0, tiled=True)

time: 84 us -> 71.8 us (0.85)
  waiting for transfers between devices: 15.7 us -> 10.3 us
  local copies, waits for them, and re-layouts: 3.1 us -> 0 us
  starting transfers between devices: 24.4 us -> 21.7 us
  Pallas kernels: 24 us -> 23.1 us
    ppermute x2, waiting for transfers between devices: 5.43 us -> 0.01 us  [the longest x1 0.01 us: shards(): from_left = lax.ppermute(currents, 'surf', to_right)]
    all_to_all x2, starting transfers between devices: 10.9 us -> 7.24 us  [exchange(): lax.all_to_all(array, 'surf', split_axis=0, concat_axis=0, tiled=True)]
    unnamed x8 -> x0, local copies, waits for them, and re-layouts: 3.1 us -> none
    ppermute x2, starting transfers between devices: 4.49 us -> 5.45 us  [the longest x1 4.99 us: shards(): from_right = lax.ppermute(currents, 'surf', to_left)]
    pallas_call x7, Pallas kernels: 24 us -> 23.1 us  [call(): pl.pallas_call(wrapped, out_shape=outs, in_specs=[pl.BlockSpec(memory_spa...]
  transfers between devices with their start and end apart: 8 -> 8, of which waited for: 3 -> 2; matrix products, arithmetic and copies ran while one was open for 0% -> 0% of each run, Pallas kernels for 12% -> 19%
where the time goes in v3:
time: 71.8 us; the launch traced here: 71.3 us
  Pallas kernels  23.1 us (32%)
  starting transfers between devices  21.7 us (30%)
  blocking collectives  16.2 us (23%)
  waiting for transfers between devices  10.3 us (14%)
    pallas_call x7, Pallas kernels, call(): pl.pallas_call(wrapped, out_shape=outs, in_specs=[pl.BlockSpec(memory_spa...  23.1 us
    all_to_all x1, blocking collectives, shards(): lax.all_to_all(send, 'surf', split_axis=0, concat_axis=0, tiled=True)  16.2 us
    all_to_all x2, waiting for transfers between devices, exchange(): lax.all_to_all(array, 'surf', split_axis=0, concat_axis=0, tiled=True)  8.48 us
    all_to_all x2, starting transfers between devices, exchange(): lax.all_to_all(array, 'surf', split_axis=0, concat_axis=0, tiled=True)  7.24 us
    ppermute x1, starting transfers between devices, shards(): from_right = lax.ppermute(currents, 'surf', to_left)  4.99 us
    ppermute x1, starting transfers between devices, shards(): note_right = lax.ppermute(left_note, 'surf', to_left)  4.43 us
    ppermute x1, starting transfers between devices, shards(): lower_right = lax.ppermute(lower_edge, 'surf', to_left)  4.05 us
    ppermute x1, waiting for transfers between devices, shards(): note_left = lax.ppermute(right_note, 'surf', to_right)  1.76 us
  transfers between devices with their start and end apart: 8, of which 2 were waited for; matrix products, arithmetic and copies ran while one was open for 0% of the time, Pallas kernels for 19%

profile of v3, /device:TPU:0, one launch (start us, length us, event | category | flops | bytes accessed | tf_op | source)
XLA Modules:
  0.0 71.3 jit_solution(6663557984706873627)
XLA Ops:
  0.0 0.5 collective-permute-start
  0.5 5.0 %collective-permute-start.1 = (bf16[32,2048]{1,0:T(8,128)(2,1)}, bf16[32,2048]{1,0:T(8,128)(2,1)S(1)}, u32[]{:S(2)}, u32[]{:S(2)}) collective-permute-start(bf16[32,2048]{1,0:T(8,128)(2,1)} %refs_2_.6), channel_id=1, source_target_pairs={{1,0},{2,1},{3,2},{4,3},{5,4},{6,5},{7,6},{8,7},{9,8},{10,9},{11,1... | collective-permute-start | bytes 393224 | tf_op jit(solution)/shard_map/ppermute | solution.py:378
  5.4 4.1 %far_up.1 = bf16[128,1024]{1,0:T(8,128)(2,1)} custom-call(bf16[32,2048]{1,0:T(8,128)(2,1)} %refs_2_.6, bf16[8,32,256]{2,1,0:T(8,128)(2,1)} %refs_1_.4, bf16[128,1024]{1,0:T(8,128)(2,1)} %refs_2_.5, s32[1,128]{1,0:T(1,128)} %bitcast.13, s32[1,128]{1,0:T(1,128)} %bitcast.15, s32[1,128]{1,0:T(1,128)} %bitcast.17), custom_call_target="tpu_custom_call" | custom-call | flops 99999997952 | bytes 525824 | tf_op jit(solution)/shard_map/far_up/pallas_call | solution.py:69
  9.5 3.7 %all-to-all-start = ((bf16[16,8,1024]{2,1,0:T(8,128)(2,1)}), bf16[16,8,1024]{2,1,0:T(8,128)(2,1)S(1)}, u32[]{:S(2)}, u32[]{:S(2)}) async-start(bf16[16,8,1024]{2,1,0:T(8,128)(2,1)} %bitcast.3), calls=%async_computation | async-start | bytes 524288 | tf_op jit(solution)/shard_map/all_to_all | solution.py:356
  13.2 0.0 collective-permute-done.refs_3_
  13.2 0.0 collective-permute-done.1.refs_4_
  13.3 6.1 %prepare.1 = (f32[32,2048]{1,0:T(8,128)S(1)}, bf16[8,256,256]{2,1,0:T(8,128)(2,1)S(1)}, bf16[8,256,256]{2,1,0:T(8,128)(2,1)S(1)}, bf16[256,256]{1,0:T(8,128)(2,1...) custom-call(s32[48]{0:T(128)} %refs_0_.3, ...), custom_call_target="tpu_custom_call" | custom-call | flops 99999997952 | bytes 9847168 | tf_op jit(solution)/shard_map/prepare/pallas_call | solution.py:69
  19.3 0.5 collective-permute-start.4
  19.8 4.0 %collective-permute-start.5 = (bf16[256,256]{1,0:T(8,128)(2,1)S(1)}, bf16[256,256]{1,0:T(8,128)(2,1)S(1)}, u32[]{:S(2)}, u32[]{:S(2)}) collective-permute-start(bf16[256,256]{1,0:T(8,128)(2,1)S(1)} %get-tuple-element.28), channel_id=1, source_target_pairs={{1,0},{2,1},{3,2},{4,3},{5,4},{6,5},{7,6},{8,7},{9,8},{10,9},{11,1... | collective-permute-start | bytes 393224 | tf_op jit(solution)/shard_map/ppermute | solution.py:416
  23.9 0.0 all-to-all-done
  23.9 2.1 %solve.1 = (f32[32,2048]{1,0:T(8,128)S(1)}, f32[32,2048]{1,0:T(8,128)S(1)}, bf16[3,32,256]{2,1,0:T(8,128)(2,1)S(1)}, bf16[3,32,256]{2,1,0:T(8,128)(2,1)S(1)}) custom-call(bf16[128,1024]{1,0:T(8,128)(2,1)S(1)} %bitcast.11, f32[32,2048]{1,0:T(8,128)S(1)} %get-tuple-element.20.refs_1_, bf16[8,32,256]{2,1,0:T(8,128)(2,1)} %refs_2_.7, ...), custom_call_target="tpu_custom_call" | custom-call | bytes 3801088 | tf_op jit(solution)/shard_map/solve/pallas_call | solution.py:69
  26.0 0.1 collective-permute-start.2
  26.1 4.4 %collective-permute-start.3 = (bf16[3,32,256]{2,1,0:T(8,128)(2,1)S(1)}, bf16[3,32,256]{2,1,0:T(8,128)(2,1)S(1)}, u32[]{:S(2)}, u32[]{:S(2)}) collective-permute-start(bf16[3,32,256]{2,1,0:T(8,128)(2,1)S(1)} %get-tuple-element.26), channel_id=1, source_target_pairs={{1,0},{2,1},{3,2},{4,3},{5,4},{6,5},{7,6},{8,7},{9,8},{10,9},{11,1... | collective-permute-start | bytes 147464 | tf_op jit(solution)/shard_map/ppermute | solution.py:428
  30.5 0.0 collective-permute-done.4.refs_4_
  30.5 0.0 collective-permute-done.5.refs_5_
  30.5 1.8 %collective-permute-done.2.refs_2_ = bf16[3,32,256]{2,1,0:T(8,128)(2,1)S(1)} collective-permute-done((bf16[3,32,256]{2,1,0:T(8,128)(2,1)S(1)}, bf16[3,32,256]{2,1,0:T(8,128)(2,1)S(1)}, u32[]{:S(2)}, u32[]{:S(2)}) %collective-permute-start.2) | collective-permute-done | bytes 49184 | tf_op jit(solution)/shard_map/ppermute | solution.py:427
  32.3 0.0 collective-permute-done.3.refs_3_
  32.3 2.5 %finish.1 = bf16[16,72,128]{2,1,0:T(8,128)(2,1)S(1)} custom-call(f32[32,2048]{1,0:T(8,128)S(1)} %get-tuple-element.23.refs_0_, f32[32,2048]{1,0:T(8,128)S(1)} %get-tuple-element.24.refs_1_, bf16[3,32,256]{2,1,0:T(8,128)(2,1)S(1)} %collective-permute-done.2.refs_2_, bf16[3,32,256]{2,1,0:T(8,128)(2,1)S(1)} %collective-permute-done.3.refs_3_, ...), custom_call_target="tpu_custom_call" | custom-call | bytes 3072128 | tf_op jit(solution)/shard_map/finish/pallas_call | solution.py:69
  34.7 16.2 %all_to_all.15.refs_0_ = bf16[16,72,128]{2,1,0:T(8,128)(2,1)S(1)} all-to-all(bf16[16,72,128]{2,1,0:T(8,128)(2,1)S(1)} %finish.1), channel_id=1, replica_groups=mesh['groups'=2,'surf'=16] {'surf'}, dimensions={0} | all-to-all | bytes 589824 | tf_op jit(solution)/shard_map/all_to_all | solution.py:447
  50.9 5.0 %gather.1 = (bf16[8,32,256]{2,1,0:T(8,128)(2,1)S(1)}, bf16[128,1024]{1,0:T(8,128)(2,1)}) custom-call(bf16[16,72,128]{2,1,0:T(8,128)(2,1)S(1)} %all_to_all.15.refs_0_, bf16[8,32,256]{2,1,0:T(8,128)(2,1)} %refs_1_.6, bf16[128,1024]{1,0:T(8,128)(2,1)} %refs_2_.8, s32[1,128]{1,0:T(1,128)} %bitcast.14, s32[1,128]{1,0:T(1,128)} %bitcast.16, s32[1,128]{1,0:T(1,128)} %bitcast.18), custom_call_target="tpu_custom_call" | custom-call | bytes 689664 | tf_op jit(solution)/shard_map/gather/pallas_call | solution.py:69
  55.9 3.5 %all-to-all-start.2 = ((bf16[16,8,1024]{2,1,0:T(8,128)(2,1)}), bf16[16,8,1024]{2,1,0:T(8,128)(2,1)S(1)}, u32[]{:S(2)}, u32[]{:S(2)}) async-start(bf16[16,8,1024]{2,1,0:T(8,128)(2,1)} %bitcast.8), calls=%async_computation.2 | async-start | bytes 524288 | tf_op jit(solution)/shard_map/all_to_all | solution.py:356
  59.5 1.5 %self_part.1.refs_1_ = f32[32,2048]{1,0:T(8,128)S(1)} custom-call(bf16[8,32,256]{2,1,0:T(8,128)(2,1)S(1)} %get-tuple-element.34.refs_0_, bf16[8,256,256]{2,1,0:T(8,128)(2,1)} %refs_1_.7), custom_call_target="tpu_custom_call" | custom-call | bytes 1179648 | tf_op jit(solution)/shard_map/self_part/pallas_call | solution.py:69
  61.0 8.5 %all-to-all-done.2 = bf16[16,8,1024]{2,1,0:T(8,128)(2,1)S(1)} async-done(((bf16[16,8,1024]{2,1,0:T(8,128)(2,1)}), bf16[16,8,1024]{2,1,0:T(8,128)(2,1)S(1)}, u32[]{:S(2)}, u32[]{:S(2)}) %all-to-all-start.2) | async-done | bytes 262176 | tf_op jit(solution)/shard_map/all_to_all | solution.py:356
  69.5 1.9 %answer.1 = bf16[32,2048]{1,0:T(8,128)(2,1)} custom-call(bf16[128,1024]{1,0:T(8,128)(2,1)S(1)} %bitcast.10, f32[32,2048]{1,0:T(8,128)S(1)} %self_part.1.refs_1_, bf16[8,32,256]{2,1,0:T(8,128)(2,1)} %refs_2_.9), custom_call_target="tpu_custom_call" | custom-call | bytes 655360 | tf_op jit(solution)/shard_map/answer/pallas_call | solution.py:69
Async XLA Ops:
  0.0 13.2 %collective-permute-start = (bf16[32,2048]{1,0:T(8,128)(2,1)}, bf16[32,2048]{1,0:T(8,128)(2,1)S(1)}, u32[]{:S(2)}, u32[]{:S(2)}) collective-permute-start(bf16[32,2048]{1,0:T(8,128)(2,1)} %refs_2_.6), channel_id=1, source_target_pairs={{0,1},{1,2},{2,3},{3,4},{4,5},{5,6},{6,7},{7,8},{8,9},{9,10},{10,1... | collective-permute-start | bytes 393224 | tf_op jit(solution)/shard_map/ppermute | solution.py:377
  0.5 12.8 %collective-permute-start.1 = (bf16[32,2048]{1,0:T(8,128)(2,1)}, bf16[32,2048]{1,0:T(8,128)(2,1)S(1)}, u32[]{:S(2)}, u32[]{:S(2)}) collective-permute-start(bf16[32,2048]{1,0:T(8,128)(2,1)} %refs_2_.6), channel_id=1, source_target_pairs={{1,0},{2,1},{3,2},{4,3},{5,4},{6,5},{7,6},{8,7},{9,8},{10,9},{11,1... | collective-permute-start | bytes 393224 | tf_op jit(solution)/shard_map/ppermute | solution.py:378
  9.5 14.3 %all-to-all-start = ((bf16[16,8,1024]{2,1,0:T(8,128)(2,1)}), bf16[16,8,1024]{2,1,0:T(8,128)(2,1)S(1)}, u32[]{:S(2)}, u32[]{:S(2)}) async-start(bf16[16,8,1024]{2,1,0:T(8,128)(2,1)} %bitcast.3), calls=%async_computation | async-start | bytes 524288 | tf_op jit(solution)/shard_map/all_to_all | solution.py:356
  19.3 11.2 %collective-permute-start.4 = (bf16[256,256]{1,0:T(8,128)(2,1)S(1)}, bf16[256,256]{1,0:T(8,128)(2,1)S(1)}, u32[]{:S(2)}, u32[]{:S(2)}) collective-permute-start(bf16[256,256]{1,0:T(8,128)(2,1)S(1)} %get-tuple-element.27), channel_id=1, source_target_pairs={{0,1},{1,2},{2,3},{3,4},{4,5},{5,6},{6,7},{7,8},{8,9},{9,10},{10,1... | collective-permute-start | bytes 393224 | tf_op jit(solution)/shard_map/ppermute | solution.py:415
  19.8 10.7 %collective-permute-start.5 = (bf16[256,256]{1,0:T(8,128)(2,1)S(1)}, bf16[256,256]{1,0:T(8,128)(2,1)S(1)}, u32[]{:S(2)}, u32[]{:S(2)}) collective-permute-start(bf16[256,256]{1,0:T(8,128)(2,1)S(1)} %get-tuple-element.28), channel_id=1, source_target_pairs={{1,0},{2,1},{3,2},{4,3},{5,4},{6,5},{7,6},{8,7},{9,8},{10,9},{11,1... | collective-permute-start | bytes 393224 | tf_op jit(solution)/shard_map/ppermute | solution.py:416
  26.0 6.3 %collective-permute-start.2 = (bf16[3,32,256]{2,1,0:T(8,128)(2,1)S(1)}, bf16[3,32,256]{2,1,0:T(8,128)(2,1)S(1)}, u32[]{:S(2)}, u32[]{:S(2)}) collective-permute-start(bf16[3,32,256]{2,1,0:T(8,128)(2,1)S(1)} %get-tuple-element.25), channel_id=1, source_target_pairs={{0,1},{1,2},{2,3},{3,4},{4,5},{5,6},{6,7},{7,8},{8,9},{9,10},{10,1... | collective-permute-start | bytes 147464 | tf_op jit(solution)/shard_map/ppermute | solution.py:427
  26.1 6.2 %collective-permute-start.3 = (bf16[3,32,256]{2,1,0:T(8,128)(2,1)S(1)}, bf16[3,32,256]{2,1,0:T(8,128)(2,1)S(1)}, u32[]{:S(2)}, u32[]{:S(2)}) collective-permute-start(bf16[3,32,256]{2,1,0:T(8,128)(2,1)S(1)} %get-tuple-element.26), channel_id=1, source_target_pairs={{1,0},{2,1},{3,2},{4,3},{5,4},{6,5},{7,6},{8,7},{9,8},{10,9},{11,1... | collective-permute-start | bytes 147464 | tf_op jit(solution)/shard_map/ppermute | solution.py:428
  55.9 13.6 %all-to-all-start.2 = ((bf16[16,8,1024]{2,1,0:T(8,128)(2,1)}), bf16[16,8,1024]{2,1,0:T(8,128)(2,1)S(1)}, u32[]{:S(2)}, u32[]{:S(2)}) async-start(bf16[16,8,1024]{2,1,0:T(8,128)(2,1)} %bitcast.8), calls=%async_computation.2 | async-start | bytes 524288 | tf_op jit(solution)/shard_map/all_to_all | solution.py:356

commit v4 on v3

--- a/solution.py
+++ b/solution.py
@@ -182,8 +182,8 @@
 
 
 def prepare_body(
-    target, origin, own, from_left, from_right, inverse, lower, upper, owner, index, tiles_ref,
-    near_out, lower_out, upper_out, lower_edge, upper_edge, high_out, low_out, bounds_out, rows_out,
+    target, origin, own, inner, outer, inverse, lower, upper, owner, index, tiles_ref,
+    near_out, lower_out, upper_out, inner_edge, outer_edge, high_out, low_out, bounds_out, rows_out,
     cells, total, products, ranks, tiles, arrivals,
 ):
     count = tiles_ref.shape[0]
@@ -200,16 +200,29 @@
     for b in range(BLK):
         lower_out[b] = dot(lower[b], inverse[b]).astype(BF16)
         upper_out[b] = dot(upper[b], inverse[b]).astype(BF16)
-    lower_edge[...] = lower_out[0]
-    upper_edge[...] = upper_out[BLK - 1]
+    position = lax.axis_index("surf")
+    even = position % 2 == 0
+
+    @pl.when(even)
+    def _():
+        inner_edge[...] = upper_out[BLK - 1]
+        outer_edge[...] = lower_out[0]
+        cells[0] = block(outer, BLK - 1)
+        cells[BLK + 1] = block(inner, 0)
+
+    @pl.when(jnp.logical_not(even))
+    def _():
+        inner_edge[...] = lower_out[0]
+        outer_edge[...] = upper_out[BLK - 1]
+        cells[0] = block(inner, BLK - 1)
+        cells[BLK + 1] = block(outer, 0)
+
     own = ready(own)
-    cells[0] = block(from_left, BLK - 1)
-    cells[BLK + 1] = block(from_right, 0)
     for b in range(BLK):
         cells[b + 1] = block(own, b)
     total[...] = jnp.zeros_like(total)
     target, origin = ready(target), ready(origin)
-    start = lax.axis_index("surf") * BLK - 1
+    start = position * BLK - 1
     for c, copy in enumerate(copies):
         copy.wait()
         for k in range(c * NEAR_CHUNK, (c + 1) * NEAR_CHUNK):
@@ -222,7 +235,7 @@
 
 def solve_body(
     arrived_ref, near_ref, expand, inverse, lower_ref, upper_ref,
-    start_out, next_out, left_out, right_out, spread,
+    start_out, next_out, inner_out, outer_out, notes, spread,
 ):
     far = far_down(arrived_ref, spread, expand)
     inverse = ready(inverse)
@@ -243,21 +256,32 @@
         after.append(value)
         next_out[:, b * TILE : (b + 1) * TILE] = value
     last = BLK - 1
-    left_out[0] = low[0]
-    left_out[1] = after[0].astype(BF16)
-    left_out[2] = (start[0] - dot(after[1].astype(BF16), upper_ref[0])).astype(BF16)
-    right_out[0] = low[last]
-    right_out[1] = after[last].astype(BF16)
-    right_out[2] = (start[last] - dot(after[last - 1].astype(BF16), lower_ref[last])).astype(BF16)
+    odd = lax.axis_index("surf") % 2
+    notes[0, 0] = low[last]
+    notes[0, 1] = after[last].astype(BF16)
+    notes[0, 2] = (start[last] - dot(after[last - 1].astype(BF16), lower_ref[last])).astype(BF16)
+    notes[1, 0] = low[0]
+    notes[1, 1] = after[0].astype(BF16)
+    notes[1, 2] = (start[0] - dot(after[1].astype(BF16), upper_ref[0])).astype(BF16)
+    inner_out[...] = notes[odd]
+    outer_out[...] = notes[1 - odd]
 
 
 def finish_body(
-    start_ref, next_ref, from_left, from_right, upper_left, lower_right, lower_ref, upper_ref,
-    weight, index_rows, high_ref, low_ref, bounds_ref, send_ref, spread, hot, ordered,
+    start_ref, next_ref, inner_note, outer_note, inner_edge, outer_edge, lower_ref, upper_ref,
+    weight, index_rows, high_ref, low_ref, bounds_ref, send_ref,
+    notes, edges, spread, hot, ordered,
 ):
     fill_hot(hot, low_ref[...])
     last = BLK - 1
     position = lax.axis_index("surf")
+    odd = position % 2
+    notes[0] = inner_note[...]
+    notes[1] = outer_note[...]
+    edges[0] = inner_edge[...]
+    edges[1] = outer_edge[...]
+    from_left, from_right = notes.at[1 - odd], notes.at[odd]
+    upper_left, lower_right = edges.at[1 - odd], edges.at[odd]
     has_left = (position > 0).astype(F32)
     has_right = (position < lax.axis_size("surf") - 1).astype(F32)
     start = [block(start_ref, b) for b in range(BLK)]
@@ -350,6 +374,14 @@
         out_ref[:, b * TILE : (b + 1) * TILE] = (block(near_ref, b) + far[b]).astype(BF16)
 
 
+def swap(inner, outer, surf_count):
+    pairs = [(i, i ^ 1) for i in range(surf_count)]
+    others = [(0, 0), (surf_count - 1, surf_count - 1)]
+    for i in range(1, surf_count - 1, 2):
+        others += [(i, i + 1), (i + 1, i)]
+    return lax.ppermute(inner, "surf", pairs), lax.ppermute(outer, "surf", others)
+
+
 def exchange(array, surf_count):
     shape = array.shape
     array = array.reshape((surf_count, shape[0] // surf_count) + shape[1:])
@@ -368,14 +400,11 @@
     targets = surf_count * BLK
     capacity = max(2, 2 * NP_DEV // surf_count)
     pieces = -(-capacity // LANES)
-    to_right = [(i, (i + 1) % surf_count) for i in range(surf_count)]
-    to_left = [((i + 1) % surf_count, i) for i in range(surf_count)]
     lists = (far_source.reshape(1, tiles), far_owner.reshape(1, tiles), far_block.reshape(1, tiles))
     square = ((TILE, TILE), BF16)
     cube = ((BLK, TILE, TILE), BF16)
 
-    from_left = lax.ppermute(currents, "surf", to_right)
-    from_right = lax.ppermute(currents, "surf", to_left)
+    inner, outer = swap(currents, currents, surf_count)
     (partial,) = call(
         far_up_body,
         [((targets, INC * RANK), BF16)],
@@ -387,14 +416,14 @@
     )
     arrived = exchange(partial, surf_count)
 
-    near_part, lower, upper, lower_edge, upper_edge, high, low, bounds, index_rows = call(
+    near_part, lower, upper, inner_edge, outer_edge, high, low, bounds, index_rows = call(
         prepare_body,
         [
             ((INC, NP_DEV), F32), cube, cube, square, square, ((BLK, TILE), I32),
             ((TILE, BLK), F32), ((surf_count, 2), I32), ((IDX_ROWS, NP_DEV), BF16),
         ],
         (
-            near_target, near_source, currents, from_left, from_right, gram_inverse, gram_lower,
+            near_target, near_source, currents, inner, outer, gram_inverse, gram_lower,
             gram_upper, dual_owner.reshape(1, NP_DEV), dual_index.reshape(1, NP_DEV), near_tiles,
         ),
         scratch=[
@@ -412,29 +441,32 @@
         flops=10**11,
         name="prepare",
     )
-    upper_left = lax.ppermute(upper_edge, "surf", to_right)
-    lower_right = lax.ppermute(lower_edge, "surf", to_left)
-
-    start, after, left_note, right_note = call(
+    inner_edge, outer_edge = swap(inner_edge, outer_edge, surf_count)
+
+    start, after, inner_note, outer_note = call(
         solve_body,
         [((INC, NP_DEV), F32)] * 2 + [((3, INC, TILE), BF16)] * 2,
         (arrived, near_part, primal_expand, gram_inverse, lower, upper),
-        scratch=[pltpu.VMEM((BLK * INC, INC * RANK), BF16)],
+        scratch=[
+            pltpu.VMEM((2, 3, INC, TILE), BF16),
+            pltpu.VMEM((BLK * INC, INC * RANK), BF16),
+        ],
         held=(2, 3),
         pinned=(1,),
         name="solve",
     )
-    note_left = lax.ppermute(right_note, "surf", to_right)
-    note_right = lax.ppermute(left_note, "surf", to_left)
+    inner_note, outer_note = swap(inner_note, outer_note, surf_count)
     rows = INC + IDX_ROWS
     (send,) = call(
         finish_body,
         [((surf_count, INC * pieces + TAIL, LANES), BF16)],
         (
-            start, after, note_left, note_right, upper_left, lower_right, lower, upper,
+            start, after, inner_note, outer_note, inner_edge, outer_edge, lower, upper,
             refine_weight.reshape(1, NP_DEV), index_rows, high, low, bounds,
         ),
         scratch=[
+            pltpu.VMEM((2, 3, INC, TILE), BF16),
+            pltpu.VMEM((2, TILE, TILE), BF16),
             pltpu.VMEM((BLK * rows, NP_DEV), BF16),
             pltpu.VMEM((NP_DEV, TILE), BF16),
             pltpu.VMEM((rows, NP_DEV + (pieces + 1) * LANES), F32),

time: 71.8 us -> 71.6 us (level)
  starting transfers between devices: 21.7 us -> 15.6 us
  blocking collectives: 16.2 us -> 20.4 us
  waiting for transfers between devices: 10.3 us -> 11.6 us
    ppermute x6, starting transfers between devices: 14.4 us -> 4.12 us  [the longest x3 2.86 us: swap(): lax.ppermute(outer, 'surf', others)]
    all_to_all x1, blocking collectives: 16.2 us -> 20.4 us  [shards(): lax.all_to_all(send, 'surf', split_axis=0, concat_axis=0, tiled=True)]
    all_to_all x2, starting transfers between devices: 7.24 us -> 11.5 us  [exchange(): lax.all_to_all(array, 'surf', split_axis=0, concat_axis=0, tiled=True)]
    all_to_all x2, waiting for transfers between devices: 8.48 us -> 11.3 us  [exchange(): lax.all_to_all(array, 'surf', split_axis=0, concat_axis=0, tiled=True)]
    ppermute x6, waiting for transfers between devices: 1.78 us -> 0.31 us  [the longest x3 0.31 us: swap(): lax.ppermute(inner, 'surf', pairs)]
  transfers between devices with their start and end apart: 8 -> 8, of which waited for: 2 -> 3; matrix products, arithmetic and copies ran while one was open for 0% -> 0% of each run, Pallas kernels for 19% -> 19%
where the time goes in v4:
time: 71.6 us; the launch traced here: 71 us
  Pallas kernels  23.3 us (33%)
  blocking collectives  20.4 us (28%)
  starting transfers between devices  15.6 us (22%)
  waiting for transfers between devices  11.6 us (16%)
    pallas_call x7, Pallas kernels, call(): pl.pallas_call(wrapped, out_shape=outs, in_specs=[pl.BlockSpec(memory_spa...  23.3 us
    all_to_all x1, blocking collectives, shards(): lax.all_to_all(send, 'surf', split_axis=0, concat_axis=0, tiled=True)  20.4 us
    all_to_all x2, starting transfers between devices, exchange(): lax.all_to_all(array, 'surf', split_axis=0, concat_axis=0, tiled=True)  11.5 us
    all_to_all x2, waiting for transfers between devices, exchange(): lax.all_to_all(array, 'surf', split_axis=0, concat_axis=0, tiled=True)  11.3 us
    ppermute x3, starting transfers between devices, swap(): lax.ppermute(outer, 'surf', others)  2.86 us
  transfers between devices with their start and end apart: 8, of which 3 were waited for; matrix products, arithmetic and copies ran while one was open for 0% of the time, Pallas kernels for 19%

profile of v4, /device:TPU:0, one launch (start us, length us, event | category | flops | bytes accessed | tf_op | source)
XLA Modules:
  0.0 71.0 jit_solution(9324935149558228618)
XLA Ops:
  0.0 0.5 collective-permute-start
  0.5 1.6 %collective-permute-start.1 = (bf16[32,2048]{1,0:T(8,128)(2,1)}, bf16[32,2048]{1,0:T(8,128)(2,1)S(1)}, u32[]{:S(2)}, u32[]{:S(2)}) collective-permute-start(bf16[32,2048]{1,0:T(8,128)(2,1)} %refs_2_.6), channel_id=1, source_target_pairs={{0,0},{15,15},{1,2},{2,1},{3,4},{4,3},{5,6},{6,5},{7,8},{8,7},{9,1... | collective-permute-start | bytes 393224 | tf_op jit(solution)/shard_map/ppermute | solution.py:382
  2.0 4.1 %far_up.1 = bf16[128,1024]{1,0:T(8,128)(2,1)} custom-call(bf16[32,2048]{1,0:T(8,128)(2,1)} %refs_2_.6, bf16[8,32,256]{2,1,0:T(8,128)(2,1)} %refs_1_.4, bf16[128,1024]{1,0:T(8,128)(2,1)} %refs_2_.5, s32[1,128]{1,0:T(1,128)} %bitcast.13, s32[1,128]{1,0:T(1,128)} %bitcast.15, s32[1,128]{1,0:T(1,128)} %bitcast.17), custom_call_target="tpu_custom_call" | custom-call | flops 99999997952 | bytes 525824 | tf_op jit(solution)/shard_map/far_up/pallas_call | solution.py:69
  6.1 7.9 %all-to-all-start = ((bf16[16,8,1024]{2,1,0:T(8,128)(2,1)}), bf16[16,8,1024]{2,1,0:T(8,128)(2,1)S(1)}, u32[]{:S(2)}, u32[]{:S(2)}) async-start(bf16[16,8,1024]{2,1,0:T(8,128)(2,1)} %bitcast.3), calls=%async_computation | async-start | bytes 524288 | tf_op jit(solution)/shard_map/all_to_all | solution.py:388
  14.0 0.0 collective-permute-done.refs_3_
  14.0 0.0 collective-permute-done.1.refs_4_
  14.0 6.1 %prepare.1 = (f32[32,2048]{1,0:T(8,128)S(1)}, bf16[8,256,256]{2,1,0:T(8,128)(2,1)S(1)}, bf16[8,256,256]{2,1,0:T(8,128)(2,1)S(1)}, bf16[256,256]{1,0:T(8,128)(2,1...) custom-call(s32[48]{0:T(128)} %refs_0_.3, ...), custom_call_target="tpu_custom_call" | custom-call | flops 99999997952 | bytes 9847168 | tf_op jit(solution)/shard_map/prepare/pallas_call | solution.py:69
  20.1 0.5 collective-permute-start.4
  20.6 0.7 collective-permute-start.5
  21.3 2.8 %all-to-all-done = bf16[16,8,1024]{2,1,0:T(8,128)(2,1)S(1)} async-done(((bf16[16,8,1024]{2,1,0:T(8,128)(2,1)}), bf16[16,8,1024]{2,1,0:T(8,128)(2,1)S(1)}, u32[]{:S(2)}, u32[]{:S(2)}) %all-to-all-start) | async-done | bytes 262176 | tf_op jit(solution)/shard_map/all_to_all | solution.py:388
  24.1 2.1 %solve.1 = (f32[32,2048]{1,0:T(8,128)S(1)}, f32[32,2048]{1,0:T(8,128)S(1)}, bf16[3,32,256]{2,1,0:T(8,128)(2,1)S(1)}, bf16[3,32,256]{2,1,0:T(8,128)(2,1)S(1)}) custom-call(bf16[128,1024]{1,0:T(8,128)(2,1)S(1)} %bitcast.11, f32[32,2048]{1,0:T(8,128)S(1)} %get-tuple-element.20.refs_1_, bf16[8,32,256]{2,1,0:T(8,128)(2,1)} %refs_2_.7, ...), custom_call_target="tpu_custom_call" | custom-call | bytes 3801088 | tf_op jit(solution)/shard_map/solve/pallas_call | solution.py:69
  26.2 0.3 collective-permute-start.2
  26.5 0.7 collective-permute-start.3
  27.2 0.0 collective-permute-done.4.refs_4_
  27.2 0.0 collective-permute-done.5.refs_5_
  27.2 0.3 collective-permute-done.2.refs_2_
  27.5 0.0 collective-permute-done.3.refs_3_
  27.5 2.7 %finish.1 = bf16[16,72,128]{2,1,0:T(8,128)(2,1)S(1)} custom-call(f32[32,2048]{1,0:T(8,128)S(1)} %get-tuple-element.23.refs_0_, f32[32,2048]{1,0:T(8,128)S(1)} %get-tuple-element.24.refs_1_, bf16[3,32,256]{2,1,0:T(8,128)(2,1)S(1)} %collective-permute-done.2.refs_2_, bf16[3,32,256]{2,1,0:T(8,128)(2,1)S(1)} %collective-permute-done.3.refs_3_, ...), custom_call_target="tpu_custom_call" | custom-call | bytes 3072128 | tf_op jit(solution)/shard_map/finish/pallas_call | solution.py:69
  30.2 20.4 %all_to_all.15.refs_0_ = bf16[16,72,128]{2,1,0:T(8,128)(2,1)S(1)} all-to-all(bf16[16,72,128]{2,1,0:T(8,128)(2,1)S(1)} %finish.1), channel_id=1, replica_groups=mesh['groups'=2,'surf'=16] {'surf'}, dimensions={0} | all-to-all | bytes 589824 | tf_op jit(solution)/shard_map/all_to_all | solution.py:479
  50.6 5.0 %gather.1 = (bf16[8,32,256]{2,1,0:T(8,128)(2,1)S(1)}, bf16[128,1024]{1,0:T(8,128)(2,1)}) custom-call(bf16[16,72,128]{2,1,0:T(8,128)(2,1)S(1)} %all_to_all.15.refs_0_, bf16[8,32,256]{2,1,0:T(8,128)(2,1)} %refs_1_.6, bf16[128,1024]{1,0:T(8,128)(2,1)} %refs_2_.8, s32[1,128]{1,0:T(1,128)} %bitcast.14, s32[1,128]{1,0:T(1,128)} %bitcast.16, s32[1,128]{1,0:T(1,128)} %bitcast.18), custom_call_target="tpu_custom_call" | custom-call | bytes 689664 | tf_op jit(solution)/shard_map/gather/pallas_call | solution.py:69
  55.6 3.5 %all-to-all-start.2 = ((bf16[16,8,1024]{2,1,0:T(8,128)(2,1)}), bf16[16,8,1024]{2,1,0:T(8,128)(2,1)S(1)}, u32[]{:S(2)}, u32[]{:S(2)}) async-start(bf16[16,8,1024]{2,1,0:T(8,128)(2,1)} %bitcast.8), calls=%async_computation.2 | async-start | bytes 524288 | tf_op jit(solution)/shard_map/all_to_all | solution.py:388
  59.2 1.5 %self_part.1.refs_1_ = f32[32,2048]{1,0:T(8,128)S(1)} custom-call(bf16[8,32,256]{2,1,0:T(8,128)(2,1)S(1)} %get-tuple-element.34.refs_0_, bf16[8,256,256]{2,1,0:T(8,128)(2,1)} %refs_1_.7), custom_call_target="tpu_custom_call" | custom-call | bytes 1179648 | tf_op jit(solution)/shard_map/self_part/pallas_call | solution.py:69
  60.7 8.5 %all-to-all-done.2 = bf16[16,8,1024]{2,1,0:T(8,128)(2,1)S(1)} async-done(((bf16[16,8,1024]{2,1,0:T(8,128)(2,1)}), bf16[16,8,1024]{2,1,0:T(8,128)(2,1)S(1)}, u32[]{:S(2)}, u32[]{:S(2)}) %all-to-all-start.2) | async-done | bytes 262176 | tf_op jit(solution)/shard_map/all_to_all | solution.py:388
  69.2 1.9 %answer.1 = bf16[32,2048]{1,0:T(8,128)(2,1)} custom-call(bf16[128,1024]{1,0:T(8,128)(2,1)S(1)} %bitcast.10, f32[32,2048]{1,0:T(8,128)S(1)} %self_part.1.refs_1_, bf16[8,32,256]{2,1,0:T(8,128)(2,1)} %refs_2_.9), custom_call_target="tpu_custom_call" | custom-call | bytes 655360 | tf_op jit(solution)/shard_map/answer/pallas_call | solution.py:69
Async XLA Ops:
  0.0 14.0 %collective-permute-start = (bf16[32,2048]{1,0:T(8,128)(2,1)}, bf16[32,2048]{1,0:T(8,128)(2,1)S(1)}, u32[]{:S(2)}, u32[]{:S(2)}) collective-permute-start(bf16[32,2048]{1,0:T(8,128)(2,1)} %refs_2_.6), channel_id=1, source_target_pairs={{0,1},{1,0},{2,3},{3,2},{4,5},{5,4},{6,7},{7,6},{8,9},{9,8},{10,11... | collective-permute-start | bytes 393224 | tf_op jit(solution)/shard_map/ppermute | solution.py:382
  0.5 13.6 %collective-permute-start.1 = (bf16[32,2048]{1,0:T(8,128)(2,1)}, bf16[32,2048]{1,0:T(8,128)(2,1)S(1)}, u32[]{:S(2)}, u32[]{:S(2)}) collective-permute-start(bf16[32,2048]{1,0:T(8,128)(2,1)} %refs_2_.6), channel_id=1, source_target_pairs={{0,0},{15,15},{1,2},{2,1},{3,4},{4,3},{5,6},{6,5},{7,8},{8,7},{9,1... | collective-permute-start | bytes 393224 | tf_op jit(solution)/shard_map/ppermute | solution.py:382
  6.1 18.0 %all-to-all-start = ((bf16[16,8,1024]{2,1,0:T(8,128)(2,1)}), bf16[16,8,1024]{2,1,0:T(8,128)(2,1)S(1)}, u32[]{:S(2)}, u32[]{:S(2)}) async-start(bf16[16,8,1024]{2,1,0:T(8,128)(2,1)} %bitcast.3), calls=%async_computation | async-start | bytes 524288 | tf_op jit(solution)/shard_map/all_to_all | solution.py:388
  20.1 7.1 %collective-permute-start.4 = (bf16[256,256]{1,0:T(8,128)(2,1)S(1)}, bf16[256,256]{1,0:T(8,128)(2,1)S(1)}, u32[]{:S(2)}, u32[]{:S(2)}) collective-permute-start(bf16[256,256]{1,0:T(8,128)(2,1)S(1)} %get-tuple-element.27), channel_id=1, source_target_pairs={{0,1},{1,0},{2,3},{3,2},{4,5},{5,4},{6,7},{7,6},{8,9},{9,8},{10,11... | collective-permute-start | bytes 393224 | tf_op jit(solution)/shard_map/ppermute | solution.py:382
  20.6 6.6 %collective-permute-start.5 = (bf16[256,256]{1,0:T(8,128)(2,1)S(1)}, bf16[256,256]{1,0:T(8,128)(2,1)S(1)}, u32[]{:S(2)}, u32[]{:S(2)}) collective-permute-start(bf16[256,256]{1,0:T(8,128)(2,1)S(1)} %get-tuple-element.28), channel_id=1, source_target_pairs={{0,0},{15,15},{1,2},{2,1},{3,4},{4,3},{5,6},{6,5},{7,8},{8,7},{9,1... | collective-permute-start | bytes 393224 | tf_op jit(solution)/shard_map/ppermute | solution.py:382
  26.2 1.3 %collective-permute-start.2 = (bf16[3,32,256]{2,1,0:T(8,128)(2,1)S(1)}, bf16[3,32,256]{2,1,0:T(8,128)(2,1)S(1)}, u32[]{:S(2)}, u32[]{:S(2)}) collective-permute-start(bf16[3,32,256]{2,1,0:T(8,128)(2,1)S(1)} %get-tuple-element.25), channel_id=1, source_target_pairs={{0,1},{1,0},{2,3},{3,2},{4,5},{5,4},{6,7},{7,6},{8,9},{9,8},{10,11... | collective-permute-start | bytes 147464 | tf_op jit(solution)/shard_map/ppermute | solution.py:382
  26.5 1.0 %collective-permute-start.3 = (bf16[3,32,256]{2,1,0:T(8,128)(2,1)S(1)}, bf16[3,32,256]{2,1,0:T(8,128)(2,1)S(1)}, u32[]{:S(2)}, u32[]{:S(2)}) collective-permute-start(bf16[3,32,256]{2,1,0:T(8,128)(2,1)S(1)} %get-tuple-element.26), channel_id=1, source_target_pairs={{0,0},{15,15},{1,2},{2,1},{3,4},{4,3},{5,6},{6,5},{7,8},{8,7},{9,1... | collective-permute-start | bytes 147464 | tf_op jit(solution)/shard_map/ppermute | solution.py:382
  55.6 13.6 %all-to-all-start.2 = ((bf16[16,8,1024]{2,1,0:T(8,128)(2,1)}), bf16[16,8,1024]{2,1,0:T(8,128)(2,1)S(1)}, u32[]{:S(2)}, u32[]{:S(2)}) async-start(bf16[16,8,1024]{2,1,0:T(8,128)(2,1)} %bitcast.8), calls=%async_computation.2 | async-start | bytes 524288 | tf_op jit(solution)/shard_map/all_to_all | solution.py:388

commit v5 on v4

--- a/solution.py
+++ b/solution.py
@@ -18,7 +18,7 @@
 BF16 = jnp.bfloat16
 I32 = jnp.int32
 NT = (((1,), (1,)), ((), ()))
-VMEM_LIMIT = 24 * 1024 * 1024
+VMEM_LIMIT = 36 * 1024 * 1024
 
 
 def dot(a, b):
@@ -92,12 +92,23 @@
         hot[k * height : (k + 1) * height, :] = jnp.where(lane == columns[:, k : k + 1], one, zero)
 
 
-def far_terms(blocks, compress, coupling, source, owner, place, coef, turned, spread, pick, terms, out_ref):
+def coefficients(blocks, compress):
+    width = BLK * RANK
+    every = dot_nt(blocks, compress[...].reshape(width, TILE))
+    owner = iota((INC, width), 1) // RANK
+    coef = jnp.zeros((INC, width), F32)
+    for s in range(BLK):
+        coef = jnp.where(owner == s, every[s * INC : (s + 1) * INC], coef)
+    return coef
+
+
+def far_up_body(value, compress, coupling, source, owner, place, out_ref, blocks, turned, spread, pick, terms):
     coupling = ready(coupling)
     turned[...] = coupling[...].astype(F32).T
-    compress = ready(compress)
+    value, compress = ready(value), ready(compress)
     for s in range(BLK):
-        coef[:, s * RANK : (s + 1) * RANK] = dot_nt(blocks[s], compress[s])
+        blocks[s * INC : (s + 1) * INC, :] = block(value, s)
+    coef = coefficients(blocks[...], compress)
     width = BLK * RANK
     keep = (iota((RANK, width), 1) % RANK) == iota((RANK, width), 0)
     for i in range(INC):
@@ -127,18 +138,12 @@
 
 def far_scratch(tiles):
     return [
-        pltpu.VMEM((INC, BLK * RANK), F32),
+        pltpu.VMEM((BLK * INC, TILE), BF16),
         pltpu.VMEM((RANK * RANK, tiles), F32),
         pltpu.VMEM((INC * RANK, BLK * RANK), BF16),
         pltpu.VMEM((INC * RANK, tiles), F32),
         pltpu.VMEM((INC * RANK, tiles), BF16),
     ]
-
-
-def far_up_body(value, compress, coupling, source, owner, place, out_ref, *scratch):
-    value = ready(value)
-    blocks = [block(value, s) for s in range(BLK)]
-    far_terms(blocks, compress, coupling, source, owner, place, *scratch, out_ref)
 
 
 def far_down(arrived_ref, spread, expand):
@@ -337,8 +342,7 @@
 
 
 def gather_body(
-    arrived_ref, compress, coupling, source, owner, place,
-    field_out, out_ref, index, spread, hot, *scratch,
+    arrived_ref, compress, couple_ref, field_out, out_ref, index, spread, hot,
 ):
     owners, rows, _ = arrived_ref.shape
     pieces = (rows - TAIL) // INC
@@ -356,10 +360,40 @@
                 )
     fill_hot(hot, index[...].T)
     field = dot(spread[...], hot[...]).astype(BF16)
-    blocks = [field[b * INC : (b + 1) * INC] for b in range(BLK)]
-    for b in range(BLK):
-        field_out[b] = blocks[b]
-    far_terms(blocks, compress, coupling, source, owner, place, *scratch, out_ref)
+    for b in range(BLK):
+        field_out[b] = field[b * INC : (b + 1) * INC]
+    coef = coefficients(field, ready(compress)).astype(BF16)
+    for o in range(out_ref.shape[0]):
+        out_ref[o] = dot(coef, block(couple_ref, o)).astype(BF16)
+
+
+def couple_body(coupling, source, owner, place, out_ref, total, lanes):
+    tiles, width = lanes.shape[0], BLK * RANK
+    flat = RANK * RANK
+    total[...] = jnp.zeros_like(total)
+    coupling = ready(coupling)
+    lanes[...] = coupling[...].astype(F32)
+    keep = (iota((RANK, flat), 1) % RANK) == iota((RANK, flat), 0)
+    fold = as_hot((iota((flat, width), 0) // RANK) == (iota((flat, width), 1) % RANK))
+    number = iota((RANK, width), 1) // RANK
+    source, owner, place = ready(source), ready(owner), ready(place)
+    group = 8
+
+    def step(c, carry):
+        begin = pl.multiple_of(c * group, group)
+        rows = lanes[pl.ds(begin, group), :]
+        tall = [jnp.where(keep, rows[k : k + 1], 0.0).astype(BF16) for k in range(group)]
+        turned = dot(jnp.concatenate(tall, axis=0), fold)
+        for k in range(group):
+            f = begin + k
+            tile = jnp.where(number == source[0, f], turned[k * RANK : (k + 1) * RANK], 0.0)
+            total[owner[0, f] * BLK + place[0, f]] += tile
+        return carry
+
+    lax.fori_loop(0, tiles // group, step, 0)
+    for o in range(out_ref.shape[1] // TILE):
+        part = total[o * BLK : (o + 1) * BLK].reshape(TILE, width)
+        out_ref[:, o * TILE : (o + 1) * TILE] = part.T.astype(BF16)
 
 
 def self_body(field_ref, tiles, out_ref):
@@ -369,9 +403,15 @@
 
 
 def answer_body(arrived_ref, near_ref, expand, out_ref, spread):
-    far = far_down(arrived_ref, spread, expand)
-    for b in range(BLK):
-        out_ref[:, b * TILE : (b + 1) * TILE] = (block(near_ref, b) + far[b]).astype(BF16)
+    total = jnp.sum(arrived_ref[...].astype(F32), axis=0)
+    number = iota(total.shape, 1) // RANK
+    for b in range(BLK):
+        spread[b * INC : (b + 1) * INC, :] = jnp.where(number == b, total, 0.0).astype(BF16)
+    far = dot(spread[...], ready(expand)[...].reshape(BLK * RANK, TILE))
+    for b in range(BLK):
+        out_ref[:, b * TILE : (b + 1) * TILE] = (
+            block(near_ref, b) + far[b * INC : (b + 1) * INC]
+        ).astype(BF16)
 
 
 def swap(inner, outer, surf_count):
@@ -478,20 +518,29 @@
     )
     shares = lax.all_to_all(send, "surf", split_axis=0, concat_axis=0, tiled=True)
     slots = surf_count * pieces * LANES
+    (couple,) = call(
+        couple_body,
+        [((BLK * RANK, targets * RANK), BF16)],
+        (dual_coupling,) + lists,
+        scratch=[pltpu.VMEM((targets, RANK, BLK * RANK), F32), pltpu.VMEM((tiles, INC * RANK), F32)],
+        held=(0, 1, 2, 3),
+        small=(1, 2, 3),
+        flops=10**10,
+        name="couple",
+    )
     field, partial = call(
         gather_body,
-        [((BLK, INC, TILE), BF16), ((targets, INC * RANK), BF16)],
-        (shares, dual_compress, dual_coupling) + lists,
+        [((BLK, INC, TILE), BF16), ((surf_count, INC, BLK * RANK), BF16)],
+        (shares, dual_compress, couple),
         scratch=[
             pltpu.VMEM((surf_count * pieces, LANES), F32),
             pltpu.VMEM((BLK * INC, slots), BF16),
             pltpu.VMEM((slots, TILE), BF16),
-        ]
-        + far_scratch(tiles),
-        held=(2, 1, 3, 4, 5),
+        ],
+        held=(1,),
         name="gather",
     )
-    arrived = exchange(partial, surf_count)
+    arrived = lax.all_to_all(partial, "surf", split_axis=0, concat_axis=0, tiled=True)
     (near_dual,) = call(
         self_body, [((INC, NP_DEV), F32)], (field, dual_self), held=(1,), name="self_part"
     )
@@ -499,7 +548,7 @@
         answer_body,
         [((INC, NP_DEV), BF16)],
         (arrived, near_dual, dual_expand),
-        scratch=[pltpu.VMEM((BLK * INC, INC * RANK), BF16)],
+        scratch=[pltpu.VMEM((BLK * INC, BLK * RANK), BF16)],
         held=(2,),
         name="answer",
     )

time: 71.6 us -> 70.9 us (level)
  blocking collectives: 20.4 us -> 0 us
  starting transfers between devices: 15.6 us -> 25.6 us
  Pallas kernels: 23.3 us -> 29.1 us
  waiting for transfers between devices: 11.6 us -> 15.4 us
    all_to_all x1 -> x0, blocking collectives: 20.4 us -> none  [shards(): lax.all_to_all(send, 'surf', split_axis=0, concat_axis=0, tiled=True)]
    all_to_all x0 -> x2, starting transfers between devices: none -> 13.6 us  [the longest x1 10.1 us: shards(): lax.all_to_all(send, 'surf', split_axis=0, concat_axis=0, tiled=True)]
    all_to_all x0 -> x2, waiting for transfers between devices: none -> 12.3 us  [the longest x1 8.47 us: shards(): lax.all_to_all(partial, 'surf', split_axis=0, concat_axis=0, tiled=True)]
    all_to_all x2 -> x1, waiting for transfers between devices: 11.3 us -> 2.79 us  [exchange(): lax.all_to_all(array, 'surf', split_axis=0, concat_axis=0, tiled=True)]
    pallas_call x7 -> x8, Pallas kernels: 23.3 us -> 29.1 us  [call(): pl.pallas_call(wrapped, out_shape=outs, in_specs=[pl.BlockSpec(memory_spa...]
    all_to_all x2 -> x1, starting transfers between devices: 11.5 us -> 7.92 us  [exchange(): lax.all_to_all(array, 'surf', split_axis=0, concat_axis=0, tiled=True)]
  transfers between devices with their start and end apart: 8 -> 9, of which waited for: 3 -> 4; matrix products, arithmetic and copies ran while one was open for 0% -> 0% of each run, Pallas kernels for 19% -> 29%
where the time goes in v5:
time: 70.9 us; the launch traced here: 70.3 us
  Pallas kernels  29.1 us (41%)
  starting transfers between devices  25.6 us (36%)
  waiting for transfers between devices  15.4 us (22%)
    pallas_call x8, Pallas kernels, call(): pl.pallas_call(wrapped, out_shape=outs, in_specs=[pl.BlockSpec(memory_spa...  29.1 us
    all_to_all x1, starting transfers between devices, shards(): lax.all_to_all(send, 'surf', split_axis=0, concat_axis=0, tiled=True)  10.1 us
    all_to_all x1, waiting for transfers between devices, shards(): lax.all_to_all(partial, 'surf', split_axis=0, concat_axis=0, tiled=True)  8.47 us
    all_to_all x1, starting transfers between devices, exchange(): lax.all_to_all(array, 'surf', split_axis=0, concat_axis=0, tiled=True)  7.92 us
    all_to_all x1, waiting for transfers between devices, shards(): lax.all_to_all(send, 'surf', split_axis=0, concat_axis=0, tiled=True)  3.87 us
    all_to_all x1, starting transfers between devices, shards(): lax.all_to_all(partial, 'surf', split_axis=0, concat_axis=0, tiled=True)  3.54 us
    ppermute x3, starting transfers between devices, swap(): lax.ppermute(outer, 'surf', others)  2.86 us
    all_to_all x1, waiting for transfers between devices, exchange(): lax.all_to_all(array, 'surf', split_axis=0, concat_axis=0, tiled=True)  2.79 us
  transfers between devices with their start and end apart: 9, of which 4 were waited for; matrix products, arithmetic and copies ran while one was open for 0% of the time, Pallas kernels for 29%

profile of v5, /device:TPU:0, one launch (start us, length us, event | category | flops | bytes accessed | tf_op | source)
XLA Modules:
  0.0 70.3 jit_solution(11274812547053431817)
XLA Ops:
  0.0 0.5 collective-permute-start
  0.5 1.6 %collective-permute-start.1 = (bf16[32,2048]{1,0:T(8,128)(2,1)}, bf16[32,2048]{1,0:T(8,128)(2,1)S(1)}, u32[]{:S(2)}, u32[]{:S(2)}) collective-permute-start(bf16[32,2048]{1,0:T(8,128)(2,1)} %refs_2_.5), channel_id=1, source_target_pairs={{0,0},{15,15},{1,2},{2,1},{3,4},{4,3},{5,6},{6,5},{7,8},{8,7},{9,1... | collective-permute-start | bytes 393224 | tf_op jit(solution)/shard_map/ppermute | solution.py:422
  2.0 4.1 %far_up.1 = bf16[128,1024]{1,0:T(8,128)(2,1)} custom-call(bf16[32,2048]{1,0:T(8,128)(2,1)} %refs_2_.5, bf16[8,32,256]{2,1,0:T(8,128)(2,1)} %refs_1_.4, bf16[128,1024]{1,0:T(8,128)(2,1)} %refs_2_.4, s32[1,128]{1,0:T(1,128)} %bitcast.12, s32[1,128]{1,0:T(1,128)} %bitcast.14, s32[1,128]{1,0:T(1,128)} %bitcast.16), custom_call_target="tpu_custom_call" | custom-call | flops 99999997952 | bytes 525824 | tf_op jit(solution)/shard_map/far_up/pallas_call | solution.py:69
  6.1 7.9 %all-to-all-start = ((bf16[16,8,1024]{2,1,0:T(8,128)(2,1)}), bf16[16,8,1024]{2,1,0:T(8,128)(2,1)S(1)}, u32[]{:S(2)}, u32[]{:S(2)}) async-start(bf16[16,8,1024]{2,1,0:T(8,128)(2,1)} %bitcast.3), calls=%async_computation | async-start | bytes 524288 | tf_op jit(solution)/shard_map/all_to_all | solution.py:428
  14.0 0.0 collective-permute-done.refs_3_
  14.0 0.0 collective-permute-done.1.refs_4_
  14.0 6.1 %prepare.1 = (f32[32,2048]{1,0:T(8,128)S(1)}, bf16[8,256,256]{2,1,0:T(8,128)(2,1)S(1)}, bf16[8,256,256]{2,1,0:T(8,128)(2,1)S(1)}, bf16[256,256]{1,0:T(8,128)(2,1...) custom-call(s32[48]{0:T(128)} %refs_0_.4, ...), custom_call_target="tpu_custom_call" | custom-call | flops 99999997952 | bytes 9847168 | tf_op jit(solution)/shard_map/prepare/pallas_call | solution.py:69
  20.1 0.5 collective-permute-start.4
  20.6 0.7 collective-permute-start.5
  21.3 2.8 %all-to-all-done = bf16[16,8,1024]{2,1,0:T(8,128)(2,1)S(1)} async-done(((bf16[16,8,1024]{2,1,0:T(8,128)(2,1)}), bf16[16,8,1024]{2,1,0:T(8,128)(2,1)S(1)}, u32[]{:S(2)}, u32[]{:S(2)}) %all-to-all-start) | async-done | bytes 262176 | tf_op jit(solution)/shard_map/all_to_all | solution.py:428
  24.1 2.1 %solve.1 = (f32[32,2048]{1,0:T(8,128)S(1)}, f32[32,2048]{1,0:T(8,128)S(1)}, bf16[3,32,256]{2,1,0:T(8,128)(2,1)S(1)}, bf16[3,32,256]{2,1,0:T(8,128)(2,1)S(1)}) custom-call(bf16[128,1024]{1,0:T(8,128)(2,1)S(1)} %bitcast.8, f32[32,2048]{1,0:T(8,128)S(1)} %get-tuple-element.20.refs_1_, bf16[8,32,256]{2,1,0:T(8,128)(2,1)} %refs_2_.6, ...), custom_call_target="tpu_custom_call" | custom-call | bytes 3801088 | tf_op jit(solution)/shard_map/solve/pallas_call | solution.py:69
  26.2 0.3 collective-permute-start.2
  26.5 0.7 collective-permute-start.3
  27.2 0.0 collective-permute-done.4.refs_4_
  27.2 0.0 collective-permute-done.5.refs_5_
  27.2 0.3 collective-permute-done.2.refs_2_
  27.5 0.0 collective-permute-done.3.refs_3_
  27.5 3.4 %finish.1 = bf16[16,72,128]{2,1,0:T(8,128)(2,1)} custom-call(f32[32,2048]{1,0:T(8,128)S(1)} %get-tuple-element.23.refs_0_, f32[32,2048]{1,0:T(8,128)S(1)} %get-tuple-element.24.refs_1_, bf16[3,32,256]{2,1,0:T(8,128)(2,1)S(1)} %collective-permute-done.2.refs_2_, bf16[3,32,256]{2,1,0:T(8,128)(2,1)S(1)} %collective-permute-done.3.refs_3_, ...), custom_call_target="tpu_custom_call" | custom-call | bytes 3072128 | tf_op jit(solution)/shard_map/finish/pallas_call | solution.py:69
  30.9 10.1 %all-to-all-start.1 = ((bf16[16,72,128]{2,1,0:T(8,128)(2,1)}), bf16[16,72,128]{2,1,0:T(8,128)(2,1)S(1)}, u32[]{:S(2)}, u32[]{:S(2)}) async-start(bf16[16,72,128]{2,1,0:T(8,128)(2,1)} %finish.1), calls=%async_computation.1 | async-start | bytes 589824 | tf_op jit(solution)/shard_map/all_to_all | solution.py:519
  41.0 6.7 %couple.1.refs_2_ = bf16[256,4096]{1,0:T(8,128)(2,1)S(1)} custom-call(bf16[128,1024]{1,0:T(8,128)(2,1)} %refs_0_.5, s32[1,128]{1,0:T(1,128)} %bitcast.13, s32[1,128]{1,0:T(1,128)} %bitcast.15, s32[1,128]{1,0:T(1,128)} %bitcast.17), custom_call_target="tpu_custom_call" | custom-call | flops 10000000000 | bytes 263680 | tf_op jit(solution)/shard_map/couple/pallas_call | solution.py:69
  47.7 3.9 %all-to-all-done.1.refs_0_ = bf16[16,72,128]{2,1,0:T(8,128)(2,1)S(1)} async-done(((bf16[16,72,128]{2,1,0:T(8,128)(2,1)}), bf16[16,72,128]{2,1,0:T(8,128)(2,1)S(1)}, u32[]{:S(2)}, u32[]{:S(2)}) %all-to-all-start.1) | async-done | bytes 294944 | tf_op jit(solution)/shard_map/all_to_all | solution.py:519
  51.5 3.4 %gather.1 = (bf16[8,32,256]{2,1,0:T(8,128)(2,1)S(1)}, bf16[16,32,256]{2,1,0:T(8,128)(2,1)}) custom-call(bf16[16,72,128]{2,1,0:T(8,128)(2,1)S(1)} %all-to-all-done.1.refs_0_, bf16[8,32,256]{2,1,0:T(8,128)(2,1)} %refs_1_.6, bf16[256,4096]{1,0:T(8,128)(2,1)S(1)} %couple.1.refs_2_), custom_call_target="tpu_custom_call" | custom-call | bytes 2523136 | tf_op jit(solution)/shard_map/gather/pallas_call | solution.py:69
  55.0 3.5 %all-to-all-start.2 = ((bf16[16,32,256]{2,1,0:T(8,128)(2,1)}), bf16[16,32,256]{2,1,0:T(8,128)(2,1)S(1)}, u32[]{:S(2)}, u32[]{:S(2)}) async-start(bf16[16,32,256]{2,1,0:T(8,128)(2,1)} %get-tuple-element.33), calls=%async_computation.2 | async-start | bytes 524288 | tf_op jit(solution)/shard_map/all_to_all | solution.py:543
  58.5 1.5 %self_part.1.refs_1_ = f32[32,2048]{1,0:T(8,128)S(1)} custom-call(bf16[8,32,256]{2,1,0:T(8,128)(2,1)S(1)} %get-tuple-element.34.refs_0_, bf16[8,256,256]{2,1,0:T(8,128)(2,1)} %refs_1_.7), custom_call_target="tpu_custom_call" | custom-call | bytes 1179648 | tf_op jit(solution)/shard_map/self_part/pallas_call | solution.py:69
  60.1 8.5 %all-to-all-done.2.refs_0_ = bf16[16,32,256]{2,1,0:T(8,128)(2,1)S(1)} async-done(((bf16[16,32,256]{2,1,0:T(8,128)(2,1)}), bf16[16,32,256]{2,1,0:T(8,128)(2,1)S(1)}, u32[]{:S(2)}, u32[]{:S(2)}) %all-to-all-start.2) | async-done | bytes 262176 | tf_op jit(solution)/shard_map/all_to_all | solution.py:543
  68.5 1.8 %answer.1 = bf16[32,2048]{1,0:T(8,128)(2,1)} custom-call(bf16[16,32,256]{2,1,0:T(8,128)(2,1)S(1)} %all-to-all-done.2.refs_0_, f32[32,2048]{1,0:T(8,128)S(1)} %self_part.1.refs_1_, bf16[8,32,256]{2,1,0:T(8,128)(2,1)} %refs_2_.7), custom_call_target="tpu_custom_call" | custom-call | bytes 655360 | tf_op jit(solution)/shard_map/answer/pallas_call | solution.py:69
Async XLA Ops:
  0.0 14.0 %collective-permute-start = (bf16[32,2048]{1,0:T(8,128)(2,1)}, bf16[32,2048]{1,0:T(8,128)(2,1)S(1)}, u32[]{:S(2)}, u32[]{:S(2)}) collective-permute-start(bf16[32,2048]{1,0:T(8,128)(2,1)} %refs_2_.5), channel_id=1, source_target_pairs={{0,1},{1,0},{2,3},{3,2},{4,5},{5,4},{6,7},{7,6},{8,9},{9,8},{10,11... | collective-permute-start | bytes 393224 | tf_op jit(solution)/shard_map/ppermute | solution.py:422
  0.5 13.6 %collective-permute-start.1 = (bf16[32,2048]{1,0:T(8,128)(2,1)}, bf16[32,2048]{1,0:T(8,128)(2,1)S(1)}, u32[]{:S(2)}, u32[]{:S(2)}) collective-permute-start(bf16[32,2048]{1,0:T(8,128)(2,1)} %refs_2_.5), channel_id=1, source_target_pairs={{0,0},{15,15},{1,2},{2,1},{3,4},{4,3},{5,6},{6,5},{7,8},{8,7},{9,1... | collective-permute-start | bytes 393224 | tf_op jit(solution)/shard_map/ppermute | solution.py:422
  6.1 18.0 %all-to-all-start = ((bf16[16,8,1024]{2,1,0:T(8,128)(2,1)}), bf16[16,8,1024]{2,1,0:T(8,128)(2,1)S(1)}, u32[]{:S(2)}, u32[]{:S(2)}) async-start(bf16[16,8,1024]{2,1,0:T(8,128)(2,1)} %bitcast.3), calls=%async_computation | async-start | bytes 524288 | tf_op jit(solution)/shard_map/all_to_all | solution.py:428
  20.1 7.1 %collective-permute-start.4 = (bf16[256,256]{1,0:T(8,128)(2,1)S(1)}, bf16[256,256]{1,0:T(8,128)(2,1)S(1)}, u32[]{:S(2)}, u32[]{:S(2)}) collective-permute-start(bf16[256,256]{1,0:T(8,128)(2,1)S(1)} %get-tuple-element.27), channel_id=1, source_target_pairs={{0,1},{1,0},{2,3},{3,2},{4,5},{5,4},{6,7},{7,6},{8,9},{9,8},{10,11... | collective-permute-start | bytes 393224 | tf_op jit(solution)/shard_map/ppermute | solution.py:422
  20.6 6.6 %collective-permute-start.5 = (bf16[256,256]{1,0:T(8,128)(2,1)S(1)}, bf16[256,256]{1,0:T(8,128)(2,1)S(1)}, u32[]{:S(2)}, u32[]{:S(2)}) collective-permute-start(bf16[256,256]{1,0:T(8,128)(2,1)S(1)} %get-tuple-element.28), channel_id=1, source_target_pairs={{0,0},{15,15},{1,2},{2,1},{3,4},{4,3},{5,6},{6,5},{7,8},{8,7},{9,1... | collective-permute-start | bytes 393224 | tf_op jit(solution)/shard_map/ppermute | solution.py:422
  26.2 1.3 %collective-permute-start.2 = (bf16[3,32,256]{2,1,0:T(8,128)(2,1)S(1)}, bf16[3,32,256]{2,1,0:T(8,128)(2,1)S(1)}, u32[]{:S(2)}, u32[]{:S(2)}) collective-permute-start(bf16[3,32,256]{2,1,0:T(8,128)(2,1)S(1)} %get-tuple-element.25), channel_id=1, source_target_pairs={{0,1},{1,0},{2,3},{3,2},{4,5},{5,4},{6,7},{7,6},{8,9},{9,8},{10,11... | collective-permute-start | bytes 147464 | tf_op jit(solution)/shard_map/ppermute | solution.py:422
  26.5 1.0 %collective-permute-start.3 = (bf16[3,32,256]{2,1,0:T(8,128)(2,1)S(1)}, bf16[3,32,256]{2,1,0:T(8,128)(2,1)S(1)}, u32[]{:S(2)}, u32[]{:S(2)}) collective-permute-start(bf16[3,32,256]{2,1,0:T(8,128)(2,1)S(1)} %get-tuple-element.26), channel_id=1, source_target_pairs={{0,0},{15,15},{1,2},{2,1},{3,4},{4,3},{5,6},{6,5},{7,8},{8,7},{9,1... | collective-permute-start | bytes 147464 | tf_op jit(solution)/shard_map/ppermute | solution.py:422
  30.9 20.7 %all-to-all-start.1 = ((bf16[16,72,128]{2,1,0:T(8,128)(2,1)}), bf16[16,72,128]{2,1,0:T(8,128)(2,1)S(1)}, u32[]{:S(2)}, u32[]{:S(2)}) async-start(bf16[16,72,128]{2,1,0:T(8,128)(2,1)} %finish.1), calls=%async_computation.1 | async-start | bytes 589824 | tf_op jit(solution)/shard_map/all_to_all | solution.py:519
  55.0 13.6 %all-to-all-start.2 = ((bf16[16,32,256]{2,1,0:T(8,128)(2,1)}), bf16[16,32,256]{2,1,0:T(8,128)(2,1)S(1)}, u32[]{:S(2)}, u32[]{:S(2)}) async-start(bf16[16,32,256]{2,1,0:T(8,128)(2,1)} %get-tuple-element.33), calls=%async_computation.2 | async-start | bytes 524288 | tf_op jit(solution)/shard_map/all_to_all | solution.py:543

commit v6 on v5

--- a/solution.py
+++ b/solution.py
@@ -19,6 +19,8 @@
 I32 = jnp.int32
 NT = (((1,), (1,)), ((), ()))
 VMEM_LIMIT = 36 * 1024 * 1024
+PRODUCT_COST = 10**9
+NEAR_COST = 10**9
 
 
 def dot(a, b):
@@ -102,12 +104,48 @@
     return coef
 
 
-def far_up_body(value, compress, coupling, source, owner, place, out_ref, blocks, turned, spread, pick, terms):
+def far_up_body(
+    value, compress, coupling, source, owner, place, inverse_ref, lower_ref, upper_ref,
+    out_ref, inner_out, outer_out, blocks, turned, spread, pick, terms, waits,
+):
+    even = lax.axis_index("surf") % 2 == 0
+    last = BLK - 1
+
+    def message(to_right, out, first):
+        edge, beside = (last, upper_ref) if to_right else (0, lower_ref)
+        return [
+            pltpu.make_async_copy(beside.at[edge], out.at[pl.ds(INC, TILE)], waits.at[first]),
+            pltpu.make_async_copy(
+                inverse_ref.at[edge], out.at[pl.ds(INC + TILE, TILE)], waits.at[first + 1]
+            ),
+        ]
+
+    @pl.when(even)
+    def _():
+        for copy in message(True, inner_out, 0) + message(False, outer_out, 2):
+            copy.start()
+
+    @pl.when(jnp.logical_not(even))
+    def _():
+        for copy in message(False, inner_out, 0) + message(True, outer_out, 2):
+            copy.start()
+
     coupling = ready(coupling)
     turned[...] = coupling[...].astype(F32).T
     value, compress = ready(value), ready(compress)
     for s in range(BLK):
         blocks[s * INC : (s + 1) * INC, :] = block(value, s)
+
+    @pl.when(even)
+    def _():
+        inner_out[0:INC, :] = block(value, last)
+        outer_out[0:INC, :] = block(value, 0)
+
+    @pl.when(jnp.logical_not(even))
+    def _():
+        inner_out[0:INC, :] = block(value, 0)
+        outer_out[0:INC, :] = block(value, last)
+
     coef = coefficients(blocks[...], compress)
     width = BLK * RANK
     keep = (iota((RANK, width), 1) % RANK) == iota((RANK, width), 0)
@@ -135,6 +173,16 @@
     select = as_hot(iota((targets, tiles), 0) == owner[...] * BLK + place[...])
     out_ref[...] = dot_nt(select, terms[...]).astype(BF16)
 
+    @pl.when(even)
+    def _():
+        for copy in message(True, inner_out, 0) + message(False, outer_out, 2):
+            copy.wait()
+
+    @pl.when(jnp.logical_not(even))
+    def _():
+        for copy in message(False, inner_out, 0) + message(True, outer_out, 2):
+            copy.wait()
+
 
 def far_scratch(tiles):
     return [
@@ -146,7 +194,7 @@
     ]
 
 
-def far_down(arrived_ref, spread, expand):
+def far_sums(arrived_ref, spread):
     rows = arrived_ref.shape[0]
     total = jnp.sum(arrived_ref[...].astype(F32).reshape(rows // BLK, BLK, INC * RANK), axis=0)
     width = INC * RANK
@@ -154,9 +202,7 @@
     for b in range(BLK):
         spread[b * INC : (b + 1) * INC, :] = jnp.where(keep, total[b : b + 1, :], 0.0).astype(BF16)
     fold = as_hot((iota((width, RANK), 0) % RANK) == iota((width, RANK), 1))
-    sums = dot(spread[...], fold).astype(BF16)
-    expand = ready(expand)
-    return [dot(sums[b * INC : (b + 1) * INC, :], expand[b]) for b in range(BLK)]
+    return dot(spread[...], fold).astype(BF16)
 
 
 def order(owner, index, ranks, owners, window, high_out, low_out, bounds_out, rows_out):
@@ -186,10 +232,23 @@
     rows_out[...] = jnp.where(row < 2 * (window // LANES), digits, 0).astype(F32).astype(BF16)
 
 
-def prepare_body(
-    target, origin, own, inner, outer, inverse, lower, upper, owner, index, tiles_ref,
-    near_out, lower_out, upper_out, inner_edge, outer_edge, high_out, low_out, bounds_out, rows_out,
-    cells, total, products, ranks, tiles, arrivals,
+def products_body(
+    inverse, lower, upper, expand, owner, index,
+    lower_out, upper_out, expand_out, high_out, low_out, bounds_out, rows_out, ranks,
+):
+    owner, index = ready(owner), ready(index)
+    window = max(LANES, -(-(2 * NP_DEV // bounds_out.shape[0]) // LANES) * LANES)
+    order(owner, index, ranks, bounds_out.shape[0], window, high_out, low_out, bounds_out, rows_out)
+    inverse, lower, upper, expand = ready(inverse), ready(lower), ready(upper), ready(expand)
+    for b in range(BLK):
+        lower_out[b] = dot(lower[b], inverse[b]).astype(BF16)
+        upper_out[b] = dot(upper[b], inverse[b]).astype(BF16)
+        expand_out[b] = dot(expand[b], inverse[b]).astype(BF16)
+
+
+def near_body(
+    target, origin, own, inner_ref, outer_ref, inverse, tiles_ref,
+    near_out, edges_out, cells, total, products, pair, tiles, arrivals,
 ):
     count = tiles_ref.shape[0]
     copies = []
@@ -198,35 +257,19 @@
         copy = pltpu.make_async_copy(tiles_ref.at[part], tiles.at[part], arrivals.at[c])
         copy.start()
         copies.append(copy)
-    owner, index = ready(owner), ready(index)
-    window = max(LANES, -(-(2 * NP_DEV // bounds_out.shape[0]) // LANES) * LANES)
-    order(owner, index, ranks, bounds_out.shape[0], window, high_out, low_out, bounds_out, rows_out)
-    inverse, lower, upper = ready(inverse), ready(lower), ready(upper)
-    for b in range(BLK):
-        lower_out[b] = dot(lower[b], inverse[b]).astype(BF16)
-        upper_out[b] = dot(upper[b], inverse[b]).astype(BF16)
     position = lax.axis_index("surf")
-    even = position % 2 == 0
-
-    @pl.when(even)
-    def _():
-        inner_edge[...] = upper_out[BLK - 1]
-        outer_edge[...] = lower_out[0]
-        cells[0] = block(outer, BLK - 1)
-        cells[BLK + 1] = block(inner, 0)
-
-    @pl.when(jnp.logical_not(even))
-    def _():
-        inner_edge[...] = lower_out[0]
-        outer_edge[...] = upper_out[BLK - 1]
-        cells[0] = block(inner, BLK - 1)
-        cells[BLK + 1] = block(outer, 0)
-
-    own = ready(own)
+    odd = position % 2
+    pair[0] = inner_ref[...]
+    pair[1] = outer_ref[...]
+    from_left, from_right = pair.at[1 - odd], pair.at[odd]
+    cells[0] = from_left[0:INC, :]
+    cells[BLK + 1] = from_right[0:INC, :]
+    for n, message in enumerate((from_left, from_right)):
+        edges_out[n] = dot(message[INC : INC + TILE, :], message[INC + TILE :, :]).astype(BF16)
+    own, target, origin = ready(own), ready(target), ready(origin)
     for b in range(BLK):
         cells[b + 1] = block(own, b)
     total[...] = jnp.zeros_like(total)
-    target, origin = ready(target), ready(origin)
     start = position * BLK - 1
     for c, copy in enumerate(copies):
         copy.wait()
@@ -234,20 +277,19 @@
             products[k] = dot(cells[origin[k] - start], tiles[k])
     for k in range(count):
         total[target[k]] += products[k]
-    for b in range(BLK):
-        near_out[:, b * TILE : (b + 1) * TILE] = total[b]
+    inverse = ready(inverse)
+    for b in range(BLK):
+        near_out[:, b * TILE : (b + 1) * TILE] = dot(total[b].astype(BF16), inverse[b])
 
 
 def solve_body(
-    arrived_ref, near_ref, expand, inverse, lower_ref, upper_ref,
+    arrived_ref, near_ref, expand_ref, lower_ref, upper_ref,
     start_out, next_out, inner_out, outer_out, notes, spread,
 ):
-    far = far_down(arrived_ref, spread, expand)
-    inverse = ready(inverse)
+    sums = far_sums(arrived_ref, spread)
     start, low = [], []
     for b in range(BLK):
-        field = (block(near_ref, b) + far[b]).astype(BF16)
-        value = dot(field, inverse[b])
+        value = block(near_ref, b) + dot(sums[b * INC : (b + 1) * INC, :], expand_ref[b])
         start.append(value)
         low.append(value.astype(BF16))
         start_out[:, b * TILE : (b + 1) * TILE] = value
@@ -273,9 +315,9 @@
 
 
 def finish_body(
-    start_ref, next_ref, inner_note, outer_note, inner_edge, outer_edge, lower_ref, upper_ref,
+    start_ref, next_ref, inner_note, outer_note, edges, lower_ref, upper_ref,
     weight, index_rows, high_ref, low_ref, bounds_ref, send_ref,
-    notes, edges, spread, hot, ordered,
+    notes, spread, hot, ordered,
 ):
     fill_hot(hot, low_ref[...])
     last = BLK - 1
@@ -283,10 +325,8 @@
     odd = position % 2
     notes[0] = inner_note[...]
     notes[1] = outer_note[...]
-    edges[0] = inner_edge[...]
-    edges[1] = outer_edge[...]
     from_left, from_right = notes.at[1 - odd], notes.at[odd]
-    upper_left, lower_right = edges.at[1 - odd], edges.at[odd]
+    upper_left, lower_right = edges.at[0], edges.at[1]
     has_left = (position > 0).astype(F32)
     has_right = (position < lax.axis_size("surf") - 1).astype(F32)
     start = [block(start_ref, b) for b in range(BLK)]
@@ -362,12 +402,12 @@
     field = dot(spread[...], hot[...]).astype(BF16)
     for b in range(BLK):
         field_out[b] = field[b * INC : (b + 1) * INC]
-    coef = coefficients(field, ready(compress)).astype(BF16)
+    coef = coefficients(field, compress).astype(BF16)
     for o in range(out_ref.shape[0]):
         out_ref[o] = dot(coef, block(couple_ref, o)).astype(BF16)
 
 
-def couple_body(coupling, source, owner, place, out_ref, total, lanes):
+def couple_body(coupling, source, owner, place, basis, out_ref, basis_out, total, lanes):
     tiles, width = lanes.shape[0], BLK * RANK
     flat = RANK * RANK
     total[...] = jnp.zeros_like(total)
@@ -394,9 +434,11 @@
     for o in range(out_ref.shape[1] // TILE):
         part = total[o * BLK : (o + 1) * BLK].reshape(TILE, width)
         out_ref[:, o * TILE : (o + 1) * TILE] = part.T.astype(BF16)
-
-
-def self_body(field_ref, tiles, out_ref):
+    basis_out[...] = ready(basis)[...]
+
+
+def self_body(field_ref, tiles, basis, out_ref, basis_out):
+    basis_out[...] = ready(basis)[...]
     tiles = ready(tiles)
     for b in range(BLK):
         out_ref[:, b * TILE : (b + 1) * TILE] = dot(field_ref[b], tiles[b])
@@ -407,7 +449,7 @@
     number = iota(total.shape, 1) // RANK
     for b in range(BLK):
         spread[b * INC : (b + 1) * INC, :] = jnp.where(number == b, total, 0.0).astype(BF16)
-    far = dot(spread[...], ready(expand)[...].reshape(BLK * RANK, TILE))
+    far = dot(spread[...], expand[...].reshape(BLK * RANK, TILE))
     for b in range(BLK):
         out_ref[:, b * TILE : (b + 1) * TILE] = (
             block(near_ref, b) + far[b * INC : (b + 1) * INC]
@@ -441,58 +483,61 @@
     capacity = max(2, 2 * NP_DEV // surf_count)
     pieces = -(-capacity // LANES)
     lists = (far_source.reshape(1, tiles), far_owner.reshape(1, tiles), far_block.reshape(1, tiles))
-    square = ((TILE, TILE), BF16)
     cube = ((BLK, TILE, TILE), BF16)
 
-    inner, outer = swap(currents, currents, surf_count)
-    (partial,) = call(
+    message = ((INC + 2 * TILE, TILE), BF16)
+    partial, inner, outer = call(
         far_up_body,
-        [((targets, INC * RANK), BF16)],
-        (currents, primal_compress, primal_coupling) + lists,
-        scratch=far_scratch(tiles),
+        [((targets, INC * RANK), BF16), message, message],
+        (currents, primal_compress, primal_coupling) + lists + (gram_inverse, gram_lower, gram_upper),
+        scratch=far_scratch(tiles) + [pltpu.SemaphoreType.DMA((4,))],
         held=(2, 0, 1, 3, 4, 5),
-        flops=10**11,
+        far=(6, 7, 8),
         name="far_up",
     )
     arrived = exchange(partial, surf_count)
-
-    near_part, lower, upper, inner_edge, outer_edge, high, low, bounds, index_rows = call(
-        prepare_body,
+    inner, outer = swap(inner, outer, surf_count)
+    lower, upper, expanded, high, low, bounds, index_rows = call(
+        products_body,
         [
-            ((INC, NP_DEV), F32), cube, cube, square, square, ((BLK, TILE), I32),
-            ((TILE, BLK), F32), ((surf_count, 2), I32), ((IDX_ROWS, NP_DEV), BF16),
+            cube, cube, ((BLK, RANK, TILE), BF16), ((BLK, TILE), I32), ((TILE, BLK), F32),
+            ((surf_count, 2), I32), ((IDX_ROWS, NP_DEV), BF16),
         ],
         (
-            near_target, near_source, currents, inner, outer, gram_inverse, gram_lower,
-            gram_upper, dual_owner.reshape(1, NP_DEV), dual_index.reshape(1, NP_DEV), near_tiles,
+            gram_inverse, gram_lower, gram_upper, primal_expand,
+            dual_owner.reshape(1, NP_DEV), dual_index.reshape(1, NP_DEV),
         ),
+        scratch=[pltpu.VMEM((BLK, TILE), F32)],
+        held=(4, 5, 0, 1, 2, 3),
+        flops=PRODUCT_COST,
+        name="products",
+    )
+    near_part, edges = call(
+        near_body,
+        [((INC, NP_DEV), F32), ((2, TILE, TILE), BF16)],
+        (near_target, near_source, currents, inner, outer, gram_inverse, near_tiles),
         scratch=[
             pltpu.VMEM((BLK + 2, INC, TILE), BF16),
             pltpu.VMEM((BLK, INC, TILE), F32),
             pltpu.VMEM((near_count, INC, TILE), F32),
-            pltpu.VMEM((BLK, TILE), F32),
+            pltpu.VMEM((2,) + message[0], BF16),
             pltpu.VMEM(near_tiles.shape, BF16),
             pltpu.SemaphoreType.DMA((near_count // NEAR_CHUNK,)),
         ],
-        held=(8, 9, 5, 6, 7, 2, 0, 1),
-        far=(10,),
+        held=(2, 0, 1, 5),
+        far=(6,),
         small=(0, 1),
-        kept=(0, 8),
-        flops=10**11,
-        name="prepare",
-    )
-    inner_edge, outer_edge = swap(inner_edge, outer_edge, surf_count)
-
+        flops=NEAR_COST,
+        name="near",
+    )
     start, after, inner_note, outer_note = call(
         solve_body,
         [((INC, NP_DEV), F32)] * 2 + [((3, INC, TILE), BF16)] * 2,
-        (arrived, near_part, primal_expand, gram_inverse, lower, upper),
+        (arrived, near_part, expanded, lower, upper),
         scratch=[
             pltpu.VMEM((2, 3, INC, TILE), BF16),
             pltpu.VMEM((BLK * INC, INC * RANK), BF16),
         ],
-        held=(2, 3),
-        pinned=(1,),
         name="solve",
     )
     inner_note, outer_note = swap(inner_note, outer_note, surf_count)
@@ -501,29 +546,27 @@
         finish_body,
         [((surf_count, INC * pieces + TAIL, LANES), BF16)],
         (
-            start, after, inner_note, outer_note, inner_edge, outer_edge, lower, upper,
+            start, after, inner_note, outer_note, edges, lower, upper,
             refine_weight.reshape(1, NP_DEV), index_rows, high, low, bounds,
         ),
         scratch=[
             pltpu.VMEM((2, 3, INC, TILE), BF16),
-            pltpu.VMEM((2, TILE, TILE), BF16),
             pltpu.VMEM((BLK * rows, NP_DEV), BF16),
             pltpu.VMEM((NP_DEV, TILE), BF16),
             pltpu.VMEM((rows, NP_DEV + (pieces + 1) * LANES), F32),
         ],
-        smem=(12,),
-        held=(8,),
-        pinned=(9,),
+        smem=(11,),
+        held=(7,),
         name="finish",
     )
     shares = lax.all_to_all(send, "surf", split_axis=0, concat_axis=0, tiled=True)
     slots = surf_count * pieces * LANES
-    (couple,) = call(
+    couple, compress = call(
         couple_body,
-        [((BLK * RANK, targets * RANK), BF16)],
-        (dual_coupling,) + lists,
+        [((BLK * RANK, targets * RANK), BF16), (dual_compress.shape, BF16)],
+        (dual_coupling,) + lists + (dual_compress,),
         scratch=[pltpu.VMEM((targets, RANK, BLK * RANK), F32), pltpu.VMEM((tiles, INC * RANK), F32)],
-        held=(0, 1, 2, 3),
+        held=(0, 1, 2, 3, 4),
         small=(1, 2, 3),
         flops=10**10,
         name="couple",
@@ -531,25 +574,27 @@
     field, partial = call(
         gather_body,
         [((BLK, INC, TILE), BF16), ((surf_count, INC, BLK * RANK), BF16)],
-        (shares, dual_compress, couple),
+        (shares, compress, couple),
         scratch=[
             pltpu.VMEM((surf_count * pieces, LANES), F32),
             pltpu.VMEM((BLK * INC, slots), BF16),
             pltpu.VMEM((slots, TILE), BF16),
         ],
-        held=(1,),
         name="gather",
     )
     arrived = lax.all_to_all(partial, "surf", split_axis=0, concat_axis=0, tiled=True)
-    (near_dual,) = call(
-        self_body, [((INC, NP_DEV), F32)], (field, dual_self), held=(1,), name="self_part"
+    near_dual, expand = call(
+        self_body,
+        [((INC, NP_DEV), F32), (dual_expand.shape, BF16)],
+        (field, dual_self, dual_expand),
+        held=(2, 1),
+        name="self_part",
     )
     (response,) = call(
         answer_body,
         [((INC, NP_DEV), BF16)],
-        (arrived, near_dual, dual_expand),
+        (arrived, near_dual, expand),
         scratch=[pltpu.VMEM((BLK * INC, BLK * RANK), BF16)],
-        held=(2,),
         name="answer",
     )
     return response

time: 70.9 us -> 71.5 us (level)
  starting transfers between devices: 25.6 us -> 29.2 us
  Pallas kernels: 29.1 us -> 27 us
    ppermute x3 -> x2, starting transfers between devices: 1.25 us -> 5.88 us  [swap(): lax.ppermute(inner, 'surf', pairs)]
    pallas_call x8 -> x9, Pallas kernels: 29.1 us -> 27 us  [call(): pl.pallas_call(wrapped, out_shape=outs, in_specs=[pl.BlockSpec(memory_spa...]
    ppermute x3 -> x2, starting transfers between devices: 2.86 us -> 1.32 us  [swap(): lax.ppermute(outer, 'surf', others)]
    all_to_all x1, starting transfers between devices: 10.1 us -> 11 us  [shards(): lax.all_to_all(send, 'surf', split_axis=0, concat_axis=0, tiled=True)]
  transfers between devices with their start and end apart: 9 -> 7, of which waited for: 4 -> 4; matrix products, arithmetic and copies ran while one was open for 0% -> 0% of each run, Pallas kernels for 29% -> 21%
where the time goes in v6:
time: 71.5 us; the launch traced here: 70.9 us
  starting transfers between devices  29.2 us (41%)
  Pallas kernels  27 us (38%)
  waiting for transfers between devices  14.7 us (21%)
    pallas_call x9, Pallas kernels, call(): pl.pallas_call(wrapped, out_shape=outs, in_specs=[pl.BlockSpec(memory_spa...  27 us
    all_to_all x1, starting transfers between devices, shards(): lax.all_to_all(send, 'surf', split_axis=0, concat_axis=0, tiled=True)  11 us
    all_to_all x1, waiting for transfers between devices, shards(): lax.all_to_all(partial, 'surf', split_axis=0, concat_axis=0, tiled=True)  8.39 us
    all_to_all x1, starting transfers between devices, exchange(): lax.all_to_all(array, 'surf', split_axis=0, concat_axis=0, tiled=True)  7.4 us
    ppermute x2, starting transfers between devices, swap(): lax.ppermute(inner, 'surf', pairs)  5.88 us
    all_to_all x1, waiting for transfers between devices, shards(): lax.all_to_all(send, 'surf', split_axis=0, concat_axis=0, tiled=True)  3.81 us
    all_to_all x1, starting transfers between devices, shards(): lax.all_to_all(partial, 'surf', split_axis=0, concat_axis=0, tiled=True)  3.53 us
    all_to_all x1, waiting for transfers between devices, exchange(): lax.all_to_all(array, 'surf', split_axis=0, concat_axis=0, tiled=True)  2.24 us
  transfers between devices with their start and end apart: 7, of which 4 were waited for; matrix products, arithmetic and copies ran while one was open for 0% of the time, Pallas kernels for 21%

profile of v6, /device:TPU:0, one launch (start us, length us, event | category | flops | bytes accessed | tf_op | source)
XLA Modules:
  0.0 70.9 jit_solution(16117300544542412538)
XLA Ops:
  0.0 4.3 %far_up.1 = (bf16[128,1024]{1,0:T(8,128)(2,1)}, bf16[544,256]{1,0:T(8,128)(2,1)S(1)}, bf16[544,256]{1,0:T(8,128)(2,1)S(1)}) custom-call(bf16[32,2048]{1,0:T(8,128)(2,1)} %refs_2_.5, bf16[8,32,256]{2,1,0:T(8,128)(2,1)} %refs_1_.4, bf16[128,1024]{1,0:T(8,128)(2,1)} %refs_2_.4, s32[1,128]{1,0:T(1,128)} %bitcast.10, s32[1,128]{1,0:T(1,128)} %bitcast.12, ...), custom_call_target="tpu_custom_call" | custom-call | bytes 3671552 | tf_op jit(solution)/shard_map/far_up/pallas_call | solution.py:71
  4.3 7.4 %all-to-all-start = ((bf16[16,8,1024]{2,1,0:T(8,128)(2,1)}), bf16[16,8,1024]{2,1,0:T(8,128)(2,1)S(1)}, u32[]{:S(2)}, u32[]{:S(2)}) async-start(bf16[16,8,1024]{2,1,0:T(8,128)(2,1)} %bitcast.3), calls=%async_computation | async-start | bytes 524288 | tf_op jit(solution)/shard_map/all_to_all | solution.py:470
  11.7 0.4 collective-permute-start
  12.1 0.7 collective-permute-start.1
  12.8 2.8 %products.1 = (bf16[8,256,256]{2,1,0:T(8,128)(2,1)S(1)}, bf16[8,256,256]{2,1,0:T(8,128)(2,1)S(1)}, bf16[8,32,256]{2,1,0:T(8,128)(2,1)S(1)}, s32[8,256]{1,0:T(8,1...) custom-call(bf16[8,256,256]{2,1,0:T(8,128)(2,1)} %refs_0_.6, ...), custom_call_target="tpu_custom_call" | custom-call | flops 1000000000 | bytes 3293184 | tf_op jit(solution)/shard_map/products/pallas_call | solution.py:71
  15.6 0.0 collective-permute-done.refs_3_
  15.6 0.0 collective-permute-done.1.refs_4_
  15.6 3.9 %near.1 = (f32[32,2048]{1,0:T(8,128)S(1)}, bf16[2,256,256]{2,1,0:T(8,128)(2,1)S(1)}) custom-call(s32[48]{0:T(128)} %refs_0_.5, s32[48]{0:T(128)} %refs_1_.5, bf16[32,2048]{1,0:T(8,128)(2,1)} %refs_2_.5, bf16[544,256]{1,0:T(8,128)(2,1)S(1)} %collective-permute-done.refs_3_, bf16[544,256]{1,0:T(8,128)(2,1)S(1)} %collective-permute-done.1.refs_4_, ...), custom_call_target="tpu_custom_call" | custom-call | flops 1000000000 | bytes 8028544 | tf_op jit(solution)/shard_map/near/pallas_call | solution.py:71
  19.5 2.2 %all-to-all-done = bf16[16,8,1024]{2,1,0:T(8,128)(2,1)S(1)} async-done(((bf16[16,8,1024]{2,1,0:T(8,128)(2,1)}), bf16[16,8,1024]{2,1,0:T(8,128)(2,1)S(1)}, u32[]{:S(2)}, u32[]{:S(2)}) %all-to-all-start) | async-done | bytes 262176 | tf_op jit(solution)/shard_map/all_to_all | solution.py:470
  21.7 0.9 %solve.1 = (f32[32,2048]{1,0:T(8,128)S(1)}, f32[32,2048]{1,0:T(8,128)S(1)}, bf16[3,32,256]{2,1,0:T(8,128)(2,1)S(1)}, bf16[3,32,256]{2,1,0:T(8,128)(2,1)S(1)}) custom-call(bf16[128,1024]{1,0:T(8,128)(2,1)S(1)} %bitcast.8, f32[32,2048]{1,0:T(8,128)S(1)} %get-tuple-element.30.refs_1_, bf16[8,32,256]{2,1,0:T(8,128)(2,1)S(1)} %get-tuple-element.31.refs_2_, ...), custom_call_target="tpu_custom_call" | custom-call | bytes 2752512 | tf_op jit(solution)/shard_map/solve/pallas_call | solution.py:71
  22.6 5.5 %collective-permute-start.2 = (bf16[3,32,256]{2,1,0:T(8,128)(2,1)S(1)}, bf16[3,32,256]{2,1,0:T(8,128)(2,1)S(1)}, u32[]{:S(2)}, u32[]{:S(2)}) collective-permute-start(bf16[3,32,256]{2,1,0:T(8,128)(2,1)S(1)} %get-tuple-element.36), channel_id=1, source_target_pairs={{0,1},{1,0},{2,3},{3,2},{4,5},{5,4},{6,7},{7,6},{8,9},{9,8},{10,11... | collective-permute-start | bytes 147464 | tf_op jit(solution)/shard_map/ppermute | solution.py:464
  28.1 0.7 collective-permute-start.3
  28.7 0.2 collective-permute-done.2.refs_2_
  28.9 0.0 collective-permute-done.3.refs_3_
  28.9 3.3 %finish.1 = bf16[16,72,128]{2,1,0:T(8,128)(2,1)} custom-call(f32[32,2048]{1,0:T(8,128)S(1)} %get-tuple-element.34.refs_0_, f32[32,2048]{1,0:T(8,128)S(1)} %get-tuple-element.35.refs_1_, bf16[3,32,256]{2,1,0:T(8,128)(2,1)S(1)} %collective-permute-done.2.refs_2_, bf16[3,32,256]{2,1,0:T(8,128)(2,1)S(1)} %collective-permute-done.3.refs_3_, ...), custom_call_target="tpu_custom_call" | custom-call | bytes 3072128 | tf_op jit(solution)/shard_map/finish/pallas_call | solution.py:71
  32.3 11.0 %all-to-all-start.1 = ((bf16[16,72,128]{2,1,0:T(8,128)(2,1)}), bf16[16,72,128]{2,1,0:T(8,128)(2,1)S(1)}, u32[]{:S(2)}, u32[]{:S(2)}) async-start(bf16[16,72,128]{2,1,0:T(8,128)(2,1)} %finish.1), calls=%async_computation.1 | async-start | bytes 589824 | tf_op jit(solution)/shard_map/all_to_all | solution.py:562
  43.3 6.8 %couple.1 = (bf16[256,4096]{1,0:T(8,128)(2,1)S(1)}, bf16[8,32,256]{2,1,0:T(8,128)(2,1)S(1)}) custom-call(bf16[128,1024]{1,0:T(8,128)(2,1)} %refs_0_.7, s32[1,128]{1,0:T(1,128)} %bitcast.11, s32[1,128]{1,0:T(1,128)} %bitcast.13, s32[1,128]{1,0:T(1,128)} %bitcast.15, bf16[8,32,256]{2,1,0:T(8,128)(2,1)} %refs_4_.1), custom_call_target="tpu_custom_call" | custom-call | flops 10000000000 | bytes 394752 | tf_op jit(solution)/shard_map/couple/pallas_call | solution.py:71
  50.1 3.8 %all-to-all-done.1.refs_0_ = bf16[16,72,128]{2,1,0:T(8,128)(2,1)S(1)} async-done(((bf16[16,72,128]{2,1,0:T(8,128)(2,1)}), bf16[16,72,128]{2,1,0:T(8,128)(2,1)S(1)}, u32[]{:S(2)}, u32[]{:S(2)}) %all-to-all-start.1) | async-done | bytes 294944 | tf_op jit(solution)/shard_map/all_to_all | solution.py:562
  53.9 2.6 %gather.1 = (bf16[8,32,256]{2,1,0:T(8,128)(2,1)S(1)}, bf16[16,32,256]{2,1,0:T(8,128)(2,1)}) custom-call(bf16[16,72,128]{2,1,0:T(8,128)(2,1)S(1)} %all-to-all-done.1.refs_0_, bf16[8,32,256]{2,1,0:T(8,128)(2,1)S(1)} %get-tuple-element.43.refs_1_, bf16[256,4096]{1,0:T(8,128)(2,1)S(1)} %get-tuple-element.44.refs_2_), custom_call_target="tpu_custom_call" | custom-call | bytes 2523136 | tf_op jit(solution)/shard_map/gather/pallas_call | solution.py:71
  56.5 3.5 %all-to-all-start.2 = ((bf16[16,32,256]{2,1,0:T(8,128)(2,1)}), bf16[16,32,256]{2,1,0:T(8,128)(2,1)S(1)}, u32[]{:S(2)}, u32[]{:S(2)}) async-start(bf16[16,32,256]{2,1,0:T(8,128)(2,1)} %get-tuple-element.45), calls=%async_computation.2 | async-start | bytes 524288 | tf_op jit(solution)/shard_map/all_to_all | solution.py:585
  60.1 1.6 %self_part.1 = (f32[32,2048]{1,0:T(8,128)S(1)}, bf16[8,32,256]{2,1,0:T(8,128)(2,1)S(1)}) custom-call(bf16[8,32,256]{2,1,0:T(8,128)(2,1)S(1)} %get-tuple-element.46.refs_0_, bf16[8,256,256]{2,1,0:T(8,128)(2,1)} %refs_1_.7, bf16[8,32,256]{2,1,0:T(8,128)(2,1)} %refs_2_.7), custom_call_target="tpu_custom_call" | custom-call | bytes 1310720 | tf_op jit(solution)/shard_map/self_part/pallas_call | solution.py:71
  61.7 8.4 %all-to-all-done.2.refs_0_ = bf16[16,32,256]{2,1,0:T(8,128)(2,1)S(1)} async-done(((bf16[16,32,256]{2,1,0:T(8,128)(2,1)}), bf16[16,32,256]{2,1,0:T(8,128)(2,1)S(1)}, u32[]{:S(2)}, u32[]{:S(2)}) %all-to-all-start.2) | async-done | bytes 262176 | tf_op jit(solution)/shard_map/all_to_all | solution.py:585
  70.1 0.9 %answer.1 = bf16[32,2048]{1,0:T(8,128)(2,1)} custom-call(bf16[16,32,256]{2,1,0:T(8,128)(2,1)S(1)} %all-to-all-done.2.refs_0_, f32[32,2048]{1,0:T(8,128)S(1)} %get-tuple-element.47.refs_1_, bf16[8,32,256]{2,1,0:T(8,128)(2,1)S(1)} %get-tuple-element.48.refs_2_), custom_call_target="tpu_custom_call" | custom-call | bytes 655360 | tf_op jit(solution)/shard_map/answer/pallas_call | solution.py:71
Async XLA Ops:
  4.3 17.5 %all-to-all-start = ((bf16[16,8,1024]{2,1,0:T(8,128)(2,1)}), bf16[16,8,1024]{2,1,0:T(8,128)(2,1)S(1)}, u32[]{:S(2)}, u32[]{:S(2)}) async-start(bf16[16,8,1024]{2,1,0:T(8,128)(2,1)} %bitcast.3), calls=%async_computation | async-start | bytes 524288 | tf_op jit(solution)/shard_map/all_to_all | solution.py:470
  11.7 3.9 %collective-permute-start = (bf16[544,256]{1,0:T(8,128)(2,1)S(1)}, bf16[544,256]{1,0:T(8,128)(2,1)S(1)}, u32[]{:S(2)}, u32[]{:S(2)}) collective-permute-start(bf16[544,256]{1,0:T(8,128)(2,1)S(1)} %get-tuple-element.28), channel_id=1, source_target_pairs={{0,1},{1,0},{2,3},{3,2},{4,5},{5,4},{6,7},{7,6},{8,9},{9,8},{10,11... | collective-permute-start | bytes 835592 | tf_op jit(solution)/shard_map/ppermute | solution.py:464
  12.1 3.5 %collective-permute-start.1 = (bf16[544,256]{1,0:T(8,128)(2,1)S(1)}, bf16[544,256]{1,0:T(8,128)(2,1)S(1)}, u32[]{:S(2)}, u32[]{:S(2)}) collective-permute-start(bf16[544,256]{1,0:T(8,128)(2,1)S(1)} %get-tuple-element.29), channel_id=1, source_target_pairs={{0,0},{15,15},{1,2},{2,1},{3,4},{4,3},{5,6},{6,5},{7,8},{8,7},{9,1... | collective-permute-start | bytes 835592 | tf_op jit(solution)/shard_map/ppermute | solution.py:464
  22.6 6.4 %collective-permute-start.2 = (bf16[3,32,256]{2,1,0:T(8,128)(2,1)S(1)}, bf16[3,32,256]{2,1,0:T(8,128)(2,1)S(1)}, u32[]{:S(2)}, u32[]{:S(2)}) collective-permute-start(bf16[3,32,256]{2,1,0:T(8,128)(2,1)S(1)} %get-tuple-element.36), channel_id=1, source_target_pairs={{0,1},{1,0},{2,3},{3,2},{4,5},{5,4},{6,7},{7,6},{8,9},{9,8},{10,11... | collective-permute-start | bytes 147464 | tf_op jit(solution)/shard_map/ppermute | solution.py:464
  28.1 0.9 %collective-permute-start.3 = (bf16[3,32,256]{2,1,0:T(8,128)(2,1)S(1)}, bf16[3,32,256]{2,1,0:T(8,128)(2,1)S(1)}, u32[]{:S(2)}, u32[]{:S(2)}) collective-permute-start(bf16[3,32,256]{2,1,0:T(8,128)(2,1)S(1)} %get-tuple-element.37), channel_id=1, source_target_pairs={{0,0},{15,15},{1,2},{2,1},{3,4},{4,3},{5,6},{6,5},{7,8},{8,7},{9,1... | collective-permute-start | bytes 147464 | tf_op jit(solution)/shard_map/ppermute | solution.py:464
  32.3 21.6 %all-to-all-start.1 = ((bf16[16,72,128]{2,1,0:T(8,128)(2,1)}), bf16[16,72,128]{2,1,0:T(8,128)(2,1)S(1)}, u32[]{:S(2)}, u32[]{:S(2)}) async-start(bf16[16,72,128]{2,1,0:T(8,128)(2,1)} %finish.1), calls=%async_computation.1 | async-start | bytes 589824 | tf_op jit(solution)/shard_map/all_to_all | solution.py:562
  56.5 13.5 %all-to-all-start.2 = ((bf16[16,32,256]{2,1,0:T(8,128)(2,1)}), bf16[16,32,256]{2,1,0:T(8,128)(2,1)S(1)}, u32[]{:S(2)}, u32[]{:S(2)}) async-start(bf16[16,32,256]{2,1,0:T(8,128)(2,1)} %get-tuple-element.45), calls=%async_computation.2 | async-start | bytes 524288 | tf_op jit(solution)/shard_map/all_to_all | solution.py:585

commit v7 on v6

--- a/solution.py
+++ b/solution.py
@@ -105,46 +105,18 @@
 
 
 def far_up_body(
-    value, compress, coupling, source, owner, place, inverse_ref, lower_ref, upper_ref,
-    out_ref, inner_out, outer_out, blocks, turned, spread, pick, terms, waits,
+    value, compress, coupling, source, owner, place,
+    out_ref, inner_out, outer_out, blocks, turned, spread, pick, terms,
 ):
-    even = lax.axis_index("surf") % 2 == 0
-    last = BLK - 1
-
-    def message(to_right, out, first):
-        edge, beside = (last, upper_ref) if to_right else (0, lower_ref)
-        return [
-            pltpu.make_async_copy(beside.at[edge], out.at[pl.ds(INC, TILE)], waits.at[first]),
-            pltpu.make_async_copy(
-                inverse_ref.at[edge], out.at[pl.ds(INC + TILE, TILE)], waits.at[first + 1]
-            ),
-        ]
-
-    @pl.when(even)
-    def _():
-        for copy in message(True, inner_out, 0) + message(False, outer_out, 2):
-            copy.start()
-
-    @pl.when(jnp.logical_not(even))
-    def _():
-        for copy in message(False, inner_out, 0) + message(True, outer_out, 2):
-            copy.start()
-
     coupling = ready(coupling)
     turned[...] = coupling[...].astype(F32).T
     value, compress = ready(value), ready(compress)
     for s in range(BLK):
         blocks[s * INC : (s + 1) * INC, :] = block(value, s)
 
-    @pl.when(even)
-    def _():
-        inner_out[0:INC, :] = block(value, last)
-        outer_out[0:INC, :] = block(value, 0)
-
-    @pl.when(jnp.logical_not(even))
-    def _():
-        inner_out[0:INC, :] = block(value, 0)
-        outer_out[0:INC, :] = block(value, last)
+    odd = lax.axis_index("surf") % 2
+    inner_out[...] = blocks[pl.ds(pl.multiple_of((1 - odd) * ((BLK - 1) * INC), INC), INC), :]
+    outer_out[...] = blocks[pl.ds(pl.multiple_of(odd * ((BLK - 1) * INC), INC), INC), :]
 
     coef = coefficients(blocks[...], compress)
     width = BLK * RANK
@@ -173,16 +145,6 @@
     select = as_hot(iota((targets, tiles), 0) == owner[...] * BLK + place[...])
     out_ref[...] = dot_nt(select, terms[...]).astype(BF16)
 
-    @pl.when(even)
-    def _():
-        for copy in message(True, inner_out, 0) + message(False, outer_out, 2):
-            copy.wait()
-
-    @pl.when(jnp.logical_not(even))
-    def _():
-        for copy in message(False, inner_out, 0) + message(True, outer_out, 2):
-            copy.wait()
-
 
 def far_scratch(tiles):
     return [
@@ -205,7 +167,10 @@
     return dot(spread[...], fold).astype(BF16)
 
 
-def order(owner, index, ranks, owners, window, high_out, low_out, bounds_out, rows_out):
+def order_body(owner, index, high_out, hot_out, bounds_out, rows_out, ranks):
+    owner, index = ready(owner), ready(index)
+    owners = bounds_out.shape[0]
+    pieces = -(-max(2, 2 * NP_DEV // owners) // LANES)
     before = as_hot(iota((TILE, TILE), 0) < iota((TILE, TILE), 1))
     number = iota((owners, TILE), 0)
     count = jnp.zeros((owners, 1), F32)
@@ -223,22 +188,18 @@
         ranks[c : c + 1, :] = jnp.sum(hots[c] * (rank + carries[c] + begin), axis=0, keepdims=True)
     spots = ranks[...].astype(I32)
     high_out[...] = spots // TILE
-    low_out[...] = (spots % TILE).astype(F32).T
+    fill_hot(hot_out, (spots % TILE).astype(F32).T)
     pair = iota((owners, 2), 1)
     bounds_out[...] = jnp.where(pair == 0, begin, count).astype(I32)
     row = iota((IDX_ROWS, NP_DEV), 0)
     index = index[...]
     digits = jnp.where(row % 2 == 0, index // TILE, index % TILE)
-    rows_out[...] = jnp.where(row < 2 * (window // LANES), digits, 0).astype(F32).astype(BF16)
+    rows_out[...] = jnp.where(row < 2 * pieces, digits, 0).astype(F32).astype(BF16)
 
 
 def products_body(
-    inverse, lower, upper, expand, owner, index,
-    lower_out, upper_out, expand_out, high_out, low_out, bounds_out, rows_out, ranks,
+    inverse, lower, upper, expand, lower_out, upper_out, expand_out,
 ):
-    owner, index = ready(owner), ready(index)
-    window = max(LANES, -(-(2 * NP_DEV // bounds_out.shape[0]) // LANES) * LANES)
-    order(owner, index, ranks, bounds_out.shape[0], window, high_out, low_out, bounds_out, rows_out)
     inverse, lower, upper, expand = ready(inverse), ready(lower), ready(upper), ready(expand)
     for b in range(BLK):
         lower_out[b] = dot(lower[b], inverse[b]).astype(BF16)
@@ -248,7 +209,7 @@
 
 def near_body(
     target, origin, own, inner_ref, outer_ref, inverse, tiles_ref,
-    near_out, edges_out, cells, total, products, pair, tiles, arrivals,
+    near_out, cells, total, products, pair, tiles, arrivals,
 ):
     count = tiles_ref.shape[0]
     copies = []
@@ -261,11 +222,8 @@
     odd = position % 2
     pair[0] = inner_ref[...]
     pair[1] = outer_ref[...]
-    from_left, from_right = pair.at[1 - odd], pair.at[odd]
-    cells[0] = from_left[0:INC, :]
-    cells[BLK + 1] = from_right[0:INC, :]
-    for n, message in enumerate((from_left, from_right)):
-        edges_out[n] = dot(message[INC : INC + TILE, :], message[INC + TILE :, :]).astype(BF16)
+    cells[0] = pair[1 - odd]
+    cells[BLK + 1] = pair[odd]
     own, target, origin = ready(own), ready(target), ready(origin)
     for b in range(BLK):
         cells[b + 1] = block(own, b)
@@ -304,51 +262,69 @@
         next_out[:, b * TILE : (b + 1) * TILE] = value
     last = BLK - 1
     odd = lax.axis_index("surf") % 2
-    notes[0, 0] = low[last]
-    notes[0, 1] = after[last].astype(BF16)
-    notes[0, 2] = (start[last] - dot(after[last - 1].astype(BF16), lower_ref[last])).astype(BF16)
-    notes[1, 0] = low[0]
-    notes[1, 1] = after[0].astype(BF16)
-    notes[1, 2] = (start[0] - dot(after[1].astype(BF16), upper_ref[0])).astype(BF16)
+    for n, (edge, inside, away, back) in enumerate(
+        ((last, last - 1, lower_ref, upper_ref), (0, 1, upper_ref, lower_ref))
+    ):
+        feedless = start[edge] - dot(after[inside].astype(BF16), away[edge])
+        notes[n, 0:INC, :] = low[edge]
+        notes[n, INC : 2 * INC, :] = after[edge].astype(BF16)
+        notes[n, 2 * INC : 3 * INC, :] = feedless.astype(BF16)
+        notes[n, 3 * INC :, :] = back[edge]
     inner_out[...] = notes[odd]
     outer_out[...] = notes[1 - odd]
 
 
+def middle_body(start_ref, next_ref, lower_ref, upper_ref, second_out, third_out):
+    last = BLK - 1
+    now = [block(next_ref, b).astype(BF16) for b in range(BLK)]
+    second = []
+    for b in range(BLK):
+        value = block(start_ref, b)
+        if b > 1:
+            value = value - dot(now[b - 1], lower_ref[b])
+        if b < last - 1:
+            value = value - dot(now[b + 1], upper_ref[b])
+        second.append(value.astype(BF16))
+        second_out[:, b * TILE : (b + 1) * TILE] = value
+    for b in range(BLK):
+        value = block(start_ref, b)
+        if 2 < b < last:
+            value = value - dot(second[b - 1], lower_ref[b])
+        if 0 < b < last - 2:
+            value = value - dot(second[b + 1], upper_ref[b])
+        third_out[:, b * TILE : (b + 1) * TILE] = value
+
+
 def finish_body(
-    start_ref, next_ref, inner_note, outer_note, edges, lower_ref, upper_ref,
-    weight, index_rows, high_ref, low_ref, bounds_ref, send_ref,
-    notes, spread, hot, ordered,
+    start_ref, next_ref, second_ref, third_ref, inner_note, outer_note, lower_ref, upper_ref,
+    weight, index_rows, high_ref, hot_ref, bounds_ref, send_ref,
+    notes, spread, ordered,
 ):
-    fill_hot(hot, low_ref[...])
-    last = BLK - 1
     position = lax.axis_index("surf")
     odd = position % 2
     notes[0] = inner_note[...]
     notes[1] = outer_note[...]
-    from_left, from_right = notes.at[1 - odd], notes.at[odd]
-    upper_left, lower_right = edges.at[0], edges.at[1]
-    has_left = (position > 0).astype(F32)
-    has_right = (position < lax.axis_size("surf") - 1).astype(F32)
-    start = [block(start_ref, b) for b in range(BLK)]
-    low = [start[0].astype(BF16), start[last].astype(BF16)]
-    now = [block(next_ref, b) for b in range(BLK)]
-    beside_left = (from_left[1].astype(F32) - dot(low[0], upper_left[...])) * has_left
-    beside_right = (from_right[1].astype(F32) - dot(low[1], lower_right[...])) * has_right
-    now[0] = now[0] - dot(from_left[0], lower_ref[0]) * has_left
-    now[last] = now[last] - dot(from_right[0], upper_ref[last]) * has_right
-
-    def sweep(values, left, right):
-        values = [v.astype(BF16) for v in values]
-        chain = [left.astype(BF16)] + values + [right.astype(BF16)]
-        return values, [
-            start[b] - dot(chain[b], lower_ref[b]) - dot(chain[b + 2], upper_ref[b])
-            for b in range(BLK)
-        ]
-
-    values, then = sweep(now, beside_left, beside_right)
-    beside_left = (from_left[2].astype(F32) - dot(values[0], upper_left[...])) * has_left
-    beside_right = (from_right[2].astype(F32) - dot(values[last], lower_right[...])) * has_right
-    values, then = sweep(then, beside_left, beside_right)
+    then = [block(third_ref, b) for b in range(BLK)]
+    for left in (True, False):
+        n = 1 - odd if left else odd
+        exists = (position > 0) if left else (position < lax.axis_size("surf") - 1)
+        exists = exists.astype(F32)
+        edge, step = (0, 1) if left else (BLK - 1, -1)
+        toward, away = (lower_ref, upper_ref) if left else (upper_ref, lower_ref)
+        one, two = edge + step, edge + 2 * step
+        first = block(start_ref, edge).astype(BF16)
+        beyond = notes[n, 3 * INC :, :]
+        beside = notes[n, INC : 2 * INC, :].astype(F32) - dot(first, beyond)
+        beside = (beside * exists).astype(BF16)
+        now = block(next_ref, edge) - dot(notes[n, 0:INC, :], toward[edge]) * exists
+        now = now.astype(BF16)
+        beside_next = notes[n, 2 * INC : 3 * INC, :].astype(F32) - dot(now, beyond)
+        beside_next = (beside_next * exists).astype(BF16)
+        second = (block(second_ref, edge) - dot(beside, toward[edge])).astype(BF16)
+        second_one = (block(second_ref, one) - dot(now, toward[one])).astype(BF16)
+        then[edge] = then[edge] - dot(beside_next, toward[edge]) - dot(second_one, away[edge])
+        then[one] = then[one] - dot(second, toward[one])
+        then[two] = then[two] - dot(second_one, toward[two])
     weight = ready(weight)
     rows = INC + IDX_ROWS
     for b in range(BLK):
@@ -360,7 +336,7 @@
             spread[h * rows : (h + 1) * rows, b * TILE : (b + 1) * TILE] = jnp.where(
                 high == h, every, jnp.zeros_like(every)
             )
-    sorted_rows = dot(spread[...], hot[...])
+    sorted_rows = dot(spread[...], hot_ref[...])
     for h in range(BLK):
         ordered[:, h * TILE : (h + 1) * TILE] = sorted_rows[h * rows : (h + 1) * rows]
     owners = send_ref.shape[0]
@@ -485,36 +461,29 @@
     lists = (far_source.reshape(1, tiles), far_owner.reshape(1, tiles), far_block.reshape(1, tiles))
     cube = ((BLK, TILE, TILE), BF16)
 
-    message = ((INC + 2 * TILE, TILE), BF16)
+    message = ((INC, TILE), BF16)
+    note = ((3 * INC + TILE, TILE), BF16)
     partial, inner, outer = call(
         far_up_body,
         [((targets, INC * RANK), BF16), message, message],
-        (currents, primal_compress, primal_coupling) + lists + (gram_inverse, gram_lower, gram_upper),
-        scratch=far_scratch(tiles) + [pltpu.SemaphoreType.DMA((4,))],
+        (currents, primal_compress, primal_coupling) + lists,
+        scratch=far_scratch(tiles),
         held=(2, 0, 1, 3, 4, 5),
-        far=(6, 7, 8),
         name="far_up",
     )
     arrived = exchange(partial, surf_count)
     inner, outer = swap(inner, outer, surf_count)
-    lower, upper, expanded, high, low, bounds, index_rows = call(
+    lower, upper, expanded = call(
         products_body,
-        [
-            cube, cube, ((BLK, RANK, TILE), BF16), ((BLK, TILE), I32), ((TILE, BLK), F32),
-            ((surf_count, 2), I32), ((IDX_ROWS, NP_DEV), BF16),
-        ],
-        (
-            gram_inverse, gram_lower, gram_upper, primal_expand,
-            dual_owner.reshape(1, NP_DEV), dual_index.reshape(1, NP_DEV),
-        ),
-        scratch=[pltpu.VMEM((BLK, TILE), F32)],
-        held=(4, 5, 0, 1, 2, 3),
+        [cube, cube, ((BLK, RANK, TILE), BF16)],
+        (gram_inverse, gram_lower, gram_upper, primal_expand),
+        held=(0, 1, 2, 3),
         flops=PRODUCT_COST,
         name="products",
     )
-    near_part, edges = call(
+    (near_part,) = call(
         near_body,
-        [((INC, NP_DEV), F32), ((2, TILE, TILE), BF16)],
+        [((INC, NP_DEV), F32)],
         (near_target, near_source, currents, inner, outer, gram_inverse, near_tiles),
         scratch=[
             pltpu.VMEM((BLK + 2, INC, TILE), BF16),
@@ -532,31 +501,49 @@
     )
     start, after, inner_note, outer_note = call(
         solve_body,
-        [((INC, NP_DEV), F32)] * 2 + [((3, INC, TILE), BF16)] * 2,
+        [((INC, NP_DEV), F32)] * 2 + [note] * 2,
         (arrived, near_part, expanded, lower, upper),
         scratch=[
-            pltpu.VMEM((2, 3, INC, TILE), BF16),
+            pltpu.VMEM((2,) + note[0], BF16),
             pltpu.VMEM((BLK * INC, INC * RANK), BF16),
         ],
         name="solve",
     )
     inner_note, outer_note = swap(inner_note, outer_note, surf_count)
     rows = INC + IDX_ROWS
+    high, hot, bounds, index_rows = call(
+        order_body,
+        [
+            ((BLK, TILE), I32), ((NP_DEV, TILE), BF16), ((surf_count, 2), I32),
+            ((IDX_ROWS, NP_DEV), BF16),
+        ],
+        (dual_owner.reshape(1, NP_DEV), dual_index.reshape(1, NP_DEV)),
+        scratch=[pltpu.VMEM((BLK, TILE), F32)],
+        held=(0, 1),
+        flops=10**9,
+        name="order",
+    )
+    second, third = call(
+        middle_body,
+        [((INC, NP_DEV), F32)] * 2,
+        (start, after, lower, upper),
+        flops=10**9,
+        name="middle",
+    )
     (send,) = call(
         finish_body,
         [((surf_count, INC * pieces + TAIL, LANES), BF16)],
         (
-            start, after, inner_note, outer_note, edges, lower, upper,
-            refine_weight.reshape(1, NP_DEV), index_rows, high, low, bounds,
+            start, after, second, third, inner_note, outer_note, lower, upper,
+            refine_weight.reshape(1, NP_DEV), index_rows, high, hot, bounds,
         ),
         scratch=[
-            pltpu.VMEM((2, 3, INC, TILE), BF16),
+            pltpu.VMEM((2,) + note[0], BF16),
             pltpu.VMEM((BLK * rows, NP_DEV), BF16),
-            pltpu.VMEM((NP_DEV, TILE), BF16),
             pltpu.VMEM((rows, NP_DEV + (pieces + 1) * LANES), F32),
         ],
-        smem=(11,),
-        held=(7,),
+        smem=(12,),
+        held=(8,),
         name="finish",
     )
     shares = lax.all_to_all(send, "surf", split_axis=0, concat_axis=0, tiled=True)

time: 71.5 us -> 69.7 us (0.975)
  starting transfers between devices: 29.2 us -> 26.1 us
  Pallas kernels: 27 us -> 29.2 us
  waiting for transfers between devices: 14.7 us -> 13.8 us
    ppermute x2, starting transfers between devices: 5.88 us -> 1.96 us  [swap(): lax.ppermute(inner, 'surf', pairs)]
    pallas_call x9 -> x11, Pallas kernels: 27 us -> 29.2 us  [call(): pl.pallas_call(wrapped, out_shape=outs, in_specs=[pl.BlockSpec(memory_spa...]
    all_to_all x1, starting transfers between devices: 11 us -> 11.9 us  [shards(): lax.all_to_all(send, 'surf', split_axis=0, concat_axis=0, tiled=True)]
  transfers between devices with their start and end apart: 7 -> 7, of which waited for: 4 -> 3; matrix products, arithmetic and copies ran while one was open for 0% -> 0% of each run, Pallas kernels for 21% -> 26%
where the time goes in v7:
time: 69.7 us; the launch traced here: 69.2 us
  Pallas kernels  29.2 us (42%)
  starting transfers between devices  26.1 us (37%)
  waiting for transfers between devices  13.8 us (20%)
    pallas_call x11, Pallas kernels, call(): pl.pallas_call(wrapped, out_shape=outs, in_specs=[pl.BlockSpec(memory_spa...  29.2 us
    all_to_all x1, starting transfers between devices, shards(): lax.all_to_all(send, 'surf', split_axis=0, concat_axis=0, tiled=True)  11.9 us
    all_to_all x1, waiting for transfers between devices, shards(): lax.all_to_all(partial, 'surf', split_axis=0, concat_axis=0, tiled=True)  8.39 us
    all_to_all x1, starting transfers between devices, exchange(): lax.all_to_all(array, 'surf', split_axis=0, concat_axis=0, tiled=True)  7.4 us
    all_to_all x1, waiting for transfers between devices, shards(): lax.all_to_all(send, 'surf', split_axis=0, concat_axis=0, tiled=True)  3.81 us
    all_to_all x1, starting transfers between devices, shards(): lax.all_to_all(partial, 'surf', split_axis=0, concat_axis=0, tiled=True)  3.53 us
    ppermute x2, starting transfers between devices, swap(): lax.ppermute(inner, 'surf', pairs)  1.96 us
    all_to_all x1, waiting for transfers between devices, exchange(): lax.all_to_all(array, 'surf', split_axis=0, concat_axis=0, tiled=True)  1.55 us
  transfers between devices with their start and end apart: 7, of which 3 were waited for; matrix products, arithmetic and copies ran while one was open for 0% of the time, Pallas kernels for 26%

profile of v7, /device:TPU:0, one launch (start us, length us, event | category | flops | bytes accessed | tf_op | source)
XLA Modules:
  0.0 69.2 jit_solution(10358417597407922988)
XLA Ops:
  0.0 4.1 %far_up.1 = (bf16[128,1024]{1,0:T(8,128)(2,1)}, bf16[32,256]{1,0:T(8,128)(2,1)S(1)}, bf16[32,256]{1,0:T(8,128)(2,1)S(1)}) custom-call(bf16[32,2048]{1,0:T(8,128)(2,1)} %refs_2_.5, bf16[8,32,256]{2,1,0:T(8,128)(2,1)} %refs_1_.4, bf16[128,1024]{1,0:T(8,128)(2,1)} %refs_2_.4, s32[1,128]{1,0:T(1,128)} %bitcast.10, s32[1,128]{1,0:T(1,128)} %bitcast.12, ...), custom_call_target="tpu_custom_call" | custom-call | bytes 525824 | tf_op jit(solution)/shard_map/far_up/pallas_call | solution.py:71
  4.1 7.4 %all-to-all-start = ((bf16[16,8,1024]{2,1,0:T(8,128)(2,1)}), bf16[16,8,1024]{2,1,0:T(8,128)(2,1)S(1)}, u32[]{:S(2)}, u32[]{:S(2)}) async-start(bf16[16,8,1024]{2,1,0:T(8,128)(2,1)} %bitcast.3), calls=%async_computation | async-start | bytes 524288 | tf_op jit(solution)/shard_map/all_to_all | solution.py:446
  11.5 0.4 collective-permute-start
  11.9 0.7 collective-permute-start.1
  12.6 2.8 %products.1 = (bf16[8,256,256]{2,1,0:T(8,128)(2,1)S(1)}, bf16[8,256,256]{2,1,0:T(8,128)(2,1)S(1)}, bf16[8,32,256]{2,1,0:T(8,128)(2,1)S(1)}) custom-call(bf16[8,256,256]{2,1,0:T(8,128)(2,1)} %refs_0_.6, bf16[8,256,256]{2,1,0:T(8,128)(2,1)} %refs_1_.6, bf16[8,256,256]{2,1,0:T(8,128)(2,1)} %refs_2_.6, bf16[8,32,256]{2,1,0:T(8,128)(2,1)} %refs_3_.1), custom_call_target="tpu_custom_call" | custom-call | flops 1000000000 | bytes 3276800 | tf_op jit(solution)/shard_map/products/pallas_call | solution.py:71
  15.3 0.0 collective-permute-done.refs_3_
  15.3 0.0 collective-permute-done.1.refs_4_
  15.3 4.6 %near.1.refs_1_ = f32[32,2048]{1,0:T(8,128)S(1)} custom-call(s32[48]{0:T(128)} %refs_0_.5, s32[48]{0:T(128)} %refs_1_.5, bf16[32,2048]{1,0:T(8,128)(2,1)} %refs_2_.5, bf16[32,256]{1,0:T(8,128)(2,1)S(1)} %collective-permute-done.refs_3_, bf16[32,256]{1,0:T(8,128)(2,1)S(1)} %collective-permute-done.1.refs_4_, bf16[8,256,256]{2,1,0:T(8,128)(2,1)} %refs_0_.6, ...), custom_call_target="tpu_custom_call" | custom-call | flops 1000000000 | bytes 7504256 | tf_op jit(solution)/shard_map/near/pallas_call | solution.py:71
  20.0 1.5 %all-to-all-done = bf16[16,8,1024]{2,1,0:T(8,128)(2,1)S(1)} async-done(((bf16[16,8,1024]{2,1,0:T(8,128)(2,1)}), bf16[16,8,1024]{2,1,0:T(8,128)(2,1)S(1)}, u32[]{:S(2)}, u32[]{:S(2)}) %all-to-all-start) | async-done | bytes 262176 | tf_op jit(solution)/shard_map/all_to_all | solution.py:446
  21.5 0.9 %solve.1 = (f32[32,2048]{1,0:T(8,128)S(1)}, f32[32,2048]{1,0:T(8,128)S(1)}, bf16[352,256]{1,0:T(8,128)(2,1)S(1)}, bf16[352,256]{1,0:T(8,128)(2,1)S(1)}) custom-call(bf16[128,1024]{1,0:T(8,128)(2,1)S(1)} %bitcast.8, f32[32,2048]{1,0:T(8,128)S(1)} %near.1.refs_1_, bf16[8,32,256]{2,1,0:T(8,128)(2,1)S(1)} %get-tuple-element.30.refs_2_, ...), custom_call_target="tpu_custom_call" | custom-call | bytes 2752512 | tf_op jit(solution)/shard_map/solve/pallas_call | solution.py:71
  22.4 1.5 %collective-permute-start.2 = (bf16[352,256]{1,0:T(8,128)(2,1)S(1)}, bf16[352,256]{1,0:T(8,128)(2,1)S(1)}, u32[]{:S(2)}, u32[]{:S(2)}) collective-permute-start(bf16[352,256]{1,0:T(8,128)(2,1)S(1)} %get-tuple-element.37), channel_id=1, source_target_pairs={{0,1},{1,0},{2,3},{3,2},{4,5},{5,4},{6,7},{7,6},{8,9},{9,8},{10,11... | collective-permute-start | bytes 540680 | tf_op jit(solution)/shard_map/ppermute | solution.py:440
  24.0 0.7 collective-permute-start.3
  24.6 1.4 %order.1 = (s32[8,256]{1,0:T(8,128)S(1)}, bf16[2048,256]{1,0:T(8,128)(2,1)S(1)}, s32[16,2]{1,0:T(8,128)S(1)}, bf16[16,2048]{1,0:T(8,128)(2,1)S(1)}) custom-call(s32[1,2048]{1,0:T(1,128)} %bitcast.16, s32[1,2048]{1,0:T(1,128)} %bitcast.17), custom_call_target="tpu_custom_call" | custom-call | flops 1000000000 | bytes 16384 | tf_op jit(solution)/shard_map/order/pallas_call | solution.py:71
  26.0 0.6 middle.1
  26.6 0.0 collective-permute-done.2.refs_4_
  26.6 0.0 collective-permute-done.3.refs_5_
  26.6 3.1 %finish.1 = bf16[16,72,128]{2,1,0:T(8,128)(2,1)} custom-call(f32[32,2048]{1,0:T(8,128)S(1)} %get-tuple-element.33.refs_0_, f32[32,2048]{1,0:T(8,128)S(1)} %get-tuple-element.34.refs_1_, f32[32,2048]{1,0:T(8,128)S(1)} %get-tuple-element.35.refs_2_, f32[32,2048]{1,0:T(8,128)S(1)} %get-tuple-element.36.refs_3_, ...), custom_call_target="tpu_custom_call" | custom-call | bytes 4636800 | tf_op jit(solution)/shard_map/finish/pallas_call | solution.py:71
  29.6 11.9 %all-to-all-start.1 = ((bf16[16,72,128]{2,1,0:T(8,128)(2,1)}), bf16[16,72,128]{2,1,0:T(8,128)(2,1)S(1)}, u32[]{:S(2)}, u32[]{:S(2)}) async-start(bf16[16,72,128]{2,1,0:T(8,128)(2,1)} %finish.1), calls=%async_computation.1 | async-start | bytes 589824 | tf_op jit(solution)/shard_map/all_to_all | solution.py:549
  41.6 6.8 %couple.1 = (bf16[256,4096]{1,0:T(8,128)(2,1)S(1)}, bf16[8,32,256]{2,1,0:T(8,128)(2,1)S(1)}) custom-call(bf16[128,1024]{1,0:T(8,128)(2,1)} %refs_0_.7, s32[1,128]{1,0:T(1,128)} %bitcast.11, s32[1,128]{1,0:T(1,128)} %bitcast.13, s32[1,128]{1,0:T(1,128)} %bitcast.15, bf16[8,32,256]{2,1,0:T(8,128)(2,1)} %refs_4_.1), custom_call_target="tpu_custom_call" | custom-call | flops 10000000000 | bytes 394752 | tf_op jit(solution)/shard_map/couple/pallas_call | solution.py:71
  48.3 3.8 %all-to-all-done.1.refs_0_ = bf16[16,72,128]{2,1,0:T(8,128)(2,1)S(1)} async-done(((bf16[16,72,128]{2,1,0:T(8,128)(2,1)}), bf16[16,72,128]{2,1,0:T(8,128)(2,1)S(1)}, u32[]{:S(2)}, u32[]{:S(2)}) %all-to-all-start.1) | async-done | bytes 294944 | tf_op jit(solution)/shard_map/all_to_all | solution.py:549
  52.1 2.6 %gather.1 = (bf16[8,32,256]{2,1,0:T(8,128)(2,1)S(1)}, bf16[16,32,256]{2,1,0:T(8,128)(2,1)}) custom-call(bf16[16,72,128]{2,1,0:T(8,128)(2,1)S(1)} %all-to-all-done.1.refs_0_, bf16[8,32,256]{2,1,0:T(8,128)(2,1)S(1)} %get-tuple-element.43.refs_1_, bf16[256,4096]{1,0:T(8,128)(2,1)S(1)} %get-tuple-element.44.refs_2_), custom_call_target="tpu_custom_call" | custom-call | bytes 2523136 | tf_op jit(solution)/shard_map/gather/pallas_call | solution.py:71
  54.7 3.5 %all-to-all-start.2 = ((bf16[16,32,256]{2,1,0:T(8,128)(2,1)}), bf16[16,32,256]{2,1,0:T(8,128)(2,1)S(1)}, u32[]{:S(2)}, u32[]{:S(2)}) async-start(bf16[16,32,256]{2,1,0:T(8,128)(2,1)} %get-tuple-element.45), calls=%async_computation.2 | async-start | bytes 524288 | tf_op jit(solution)/shard_map/all_to_all | solution.py:572
  58.3 1.6 %self_part.1 = (f32[32,2048]{1,0:T(8,128)S(1)}, bf16[8,32,256]{2,1,0:T(8,128)(2,1)S(1)}) custom-call(bf16[8,32,256]{2,1,0:T(8,128)(2,1)S(1)} %get-tuple-element.46.refs_0_, bf16[8,256,256]{2,1,0:T(8,128)(2,1)} %refs_1_.7, bf16[8,32,256]{2,1,0:T(8,128)(2,1)} %refs_2_.7), custom_call_target="tpu_custom_call" | custom-call | bytes 1310720 | tf_op jit(solution)/shard_map/self_part/pallas_call | solution.py:71
  59.9 8.4 %all-to-all-done.2.refs_0_ = bf16[16,32,256]{2,1,0:T(8,128)(2,1)S(1)} async-done(((bf16[16,32,256]{2,1,0:T(8,128)(2,1)}), bf16[16,32,256]{2,1,0:T(8,128)(2,1)S(1)}, u32[]{:S(2)}, u32[]{:S(2)}) %all-to-all-start.2) | async-done | bytes 262176 | tf_op jit(solution)/shard_map/all_to_all | solution.py:572
  68.3 0.9 %answer.1 = bf16[32,2048]{1,0:T(8,128)(2,1)} custom-call(bf16[16,32,256]{2,1,0:T(8,128)(2,1)S(1)} %all-to-all-done.2.refs_0_, f32[32,2048]{1,0:T(8,128)S(1)} %get-tuple-element.47.refs_1_, bf16[8,32,256]{2,1,0:T(8,128)(2,1)S(1)} %get-tuple-element.48.refs_2_), custom_call_target="tpu_custom_call" | custom-call | bytes 655360 | tf_op jit(solution)/shard_map/answer/pallas_call | solution.py:71
Async XLA Ops:
  4.1 17.5 %all-to-all-start = ((bf16[16,8,1024]{2,1,0:T(8,128)(2,1)}), bf16[16,8,1024]{2,1,0:T(8,128)(2,1)S(1)}, u32[]{:S(2)}, u32[]{:S(2)}) async-start(bf16[16,8,1024]{2,1,0:T(8,128)(2,1)} %bitcast.3), calls=%async_computation | async-start | bytes 524288 | tf_op jit(solution)/shard_map/all_to_all | solution.py:446
  11.5 3.8 %collective-permute-start = (bf16[32,256]{1,0:T(8,128)(2,1)S(1)}, bf16[32,256]{1,0:T(8,128)(2,1)S(1)}, u32[]{:S(2)}, u32[]{:S(2)}) collective-permute-start(bf16[32,256]{1,0:T(8,128)(2,1)S(1)} %get-tuple-element.28), channel_id=1, source_target_pairs={{0,1},{1,0},{2,3},{3,2},{4,5},{5,4},{6,7},{7,6},{8,9},{9,8},{10,11... | collective-permute-start | bytes 49160 | tf_op jit(solution)/shard_map/ppermute | solution.py:440
  11.9 3.4 %collective-permute-start.1 = (bf16[32,256]{1,0:T(8,128)(2,1)S(1)}, bf16[32,256]{1,0:T(8,128)(2,1)S(1)}, u32[]{:S(2)}, u32[]{:S(2)}) collective-permute-start(bf16[32,256]{1,0:T(8,128)(2,1)S(1)} %get-tuple-element.29), channel_id=1, source_target_pairs={{0,0},{15,15},{1,2},{2,1},{3,4},{4,3},{5,6},{6,5},{7,8},{8,7},{9,1... | collective-permute-start | bytes 49160 | tf_op jit(solution)/shard_map/ppermute | solution.py:440
  22.4 4.2 %collective-permute-start.2 = (bf16[352,256]{1,0:T(8,128)(2,1)S(1)}, bf16[352,256]{1,0:T(8,128)(2,1)S(1)}, u32[]{:S(2)}, u32[]{:S(2)}) collective-permute-start(bf16[352,256]{1,0:T(8,128)(2,1)S(1)} %get-tuple-element.37), channel_id=1, source_target_pairs={{0,1},{1,0},{2,3},{3,2},{4,5},{5,4},{6,7},{7,6},{8,9},{9,8},{10,11... | collective-permute-start | bytes 540680 | tf_op jit(solution)/shard_map/ppermute | solution.py:440
  24.0 2.6 %collective-permute-start.3 = (bf16[352,256]{1,0:T(8,128)(2,1)S(1)}, bf16[352,256]{1,0:T(8,128)(2,1)S(1)}, u32[]{:S(2)}, u32[]{:S(2)}) collective-permute-start(bf16[352,256]{1,0:T(8,128)(2,1)S(1)} %get-tuple-element.38), channel_id=1, source_target_pairs={{0,0},{15,15},{1,2},{2,1},{3,4},{4,3},{5,6},{6,5},{7,8},{8,7},{9,1... | collective-permute-start | bytes 540680 | tf_op jit(solution)/shard_map/ppermute | solution.py:440
  29.6 22.5 %all-to-all-start.1 = ((bf16[16,72,128]{2,1,0:T(8,128)(2,1)}), bf16[16,72,128]{2,1,0:T(8,128)(2,1)S(1)}, u32[]{:S(2)}, u32[]{:S(2)}) async-start(bf16[16,72,128]{2,1,0:T(8,128)(2,1)} %finish.1), calls=%async_computation.1 | async-start | bytes 589824 | tf_op jit(solution)/shard_map/all_to_all | solution.py:549
  54.7 13.5 %all-to-all-start.2 = ((bf16[16,32,256]{2,1,0:T(8,128)(2,1)}), bf16[16,32,256]{2,1,0:T(8,128)(2,1)S(1)}, u32[]{:S(2)}, u32[]{:S(2)}) async-start(bf16[16,32,256]{2,1,0:T(8,128)(2,1)} %get-tuple-element.45), calls=%async_computation.2 | async-start | bytes 524288 | tf_op jit(solution)/shard_map/all_to_all | solution.py:572

commit v8 on v7

--- a/solution.py
+++ b/solution.py
@@ -19,8 +19,6 @@
 I32 = jnp.int32
 NT = (((1,), (1,)), ((), ()))
 VMEM_LIMIT = 36 * 1024 * 1024
-PRODUCT_COST = 10**9
-NEAR_COST = 10**9
 
 
 def dot(a, b):
@@ -43,15 +41,14 @@
     return mask.astype(F32).astype(BF16)
 
 
-def call(body, outs, args, scratch=(), smem=(), held=(), far=(), small=(), pinned=(), kept=(), flops=0, name=None):
+def call(body, outs, args, scratch=(), smem=(), held=(), far=(), small=(), streamed=(), flops=0, name=None):
     spaces = [
         pltpu.SMEM if k in smem else pltpu.HBM if k in held or k in far else pltpu.VMEM
         for k in range(len(args))
     ]
     size = sum(a.size * a.dtype.itemsize for a in args)
     outs = tuple(
-        pltpu.VMEM(s, d) if k in kept else jax.ShapeDtypeStruct(s, d)
-        for k, (s, d) in enumerate(outs)
+        jax.ShapeDtypeStruct(s, d) for s, d in outs
     )
     buffers = [
         (pltpu.SMEM if k in small else pltpu.VMEM)(args[k].shape, args[k].dtype) for k in held
@@ -72,12 +69,15 @@
         wrapped,
         out_shape=outs,
         in_specs=[pl.BlockSpec(memory_space=m) for m in spaces],
-        out_specs=tuple(pl.BlockSpec(memory_space=pltpu.VMEM) for _ in outs),
+        out_specs=tuple(
+            pl.BlockSpec(memory_space=pl.ANY if k in streamed else pltpu.VMEM)
+            for k in range(len(outs))
+        ),
         scratch_shapes=list(scratch) + buffers + waits,
         compiler_params=pltpu.CompilerParams(vmem_limit_bytes=VMEM_LIMIT),
         cost_estimate=pl.CostEstimate(flops=flops, bytes_accessed=size, transcendentals=0),
         name=name,
-    )(*[pltpu.with_memory_space_constraint(a, m) if m is pltpu.HBM or k in pinned else a for k, (a, m) in enumerate(zip(args, spaces))])
+    )(*[pltpu.with_memory_space_constraint(a, m) if m is pltpu.HBM else a for a, m in zip(args, spaces)])
 
 
 def ready(operand):
@@ -106,18 +106,13 @@
 
 def far_up_body(
     value, compress, coupling, source, owner, place,
-    out_ref, inner_out, outer_out, blocks, turned, spread, pick, terms,
+    out_ref, blocks, turned, spread, pick, terms,
 ):
     coupling = ready(coupling)
     turned[...] = coupling[...].astype(F32).T
     value, compress = ready(value), ready(compress)
     for s in range(BLK):
         blocks[s * INC : (s + 1) * INC, :] = block(value, s)
-
-    odd = lax.axis_index("surf") % 2
-    inner_out[...] = blocks[pl.ds(pl.multiple_of((1 - odd) * ((BLK - 1) * INC), INC), INC), :]
-    outer_out[...] = blocks[pl.ds(pl.multiple_of(odd * ((BLK - 1) * INC), INC), INC), :]
-
     coef = coefficients(blocks[...], compress)
     width = BLK * RANK
     keep = (iota((RANK, width), 1) % RANK) == iota((RANK, width), 0)
@@ -197,19 +192,9 @@
     rows_out[...] = jnp.where(row < 2 * pieces, digits, 0).astype(F32).astype(BF16)
 
 
-def products_body(
-    inverse, lower, upper, expand, lower_out, upper_out, expand_out,
-):
-    inverse, lower, upper, expand = ready(inverse), ready(lower), ready(upper), ready(expand)
-    for b in range(BLK):
-        lower_out[b] = dot(lower[b], inverse[b]).astype(BF16)
-        upper_out[b] = dot(upper[b], inverse[b]).astype(BF16)
-        expand_out[b] = dot(expand[b], inverse[b]).astype(BF16)
-
-
-def near_body(
-    target, origin, own, inner_ref, outer_ref, inverse, tiles_ref,
-    near_out, cells, total, products, pair, tiles, arrivals,
+def prepare_body(
+    target, origin, own, inner_ref, outer_ref, inverse, lower, upper, expand, tiles_ref,
+    near_out, lower_out, upper_out, expand_out, cells, total, products, pair, tiles, arrivals,
 ):
     count = tiles_ref.shape[0]
     copies = []
@@ -222,8 +207,13 @@
     odd = position % 2
     pair[0] = inner_ref[...]
     pair[1] = outer_ref[...]
-    cells[0] = pair[1 - odd]
-    cells[BLK + 1] = pair[odd]
+    cells[0] = pair[1 - odd, :, NP_DEV - TILE :]
+    cells[BLK + 1] = pair[odd, :, :TILE]
+    inverse, lower, upper, expand = ready(inverse), ready(lower), ready(upper), ready(expand)
+    for b in range(BLK):
+        lower_out[b] = dot(lower[b], inverse[b]).astype(BF16)
+        upper_out[b] = dot(upper[b], inverse[b]).astype(BF16)
+        expand_out[b] = dot(expand[b], inverse[b]).astype(BF16)
     own, target, origin = ready(own), ready(target), ready(origin)
     for b in range(BLK):
         cells[b + 1] = block(own, b)
@@ -235,7 +225,6 @@
             products[k] = dot(cells[origin[k] - start], tiles[k])
     for k in range(count):
         total[target[k]] += products[k]
-    inverse = ready(inverse)
     for b in range(BLK):
         near_out[:, b * TILE : (b + 1) * TILE] = dot(total[b].astype(BF16), inverse[b])
 
@@ -298,7 +287,7 @@
 def finish_body(
     start_ref, next_ref, second_ref, third_ref, inner_note, outer_note, lower_ref, upper_ref,
     weight, index_rows, high_ref, hot_ref, bounds_ref, send_ref,
-    notes, spread, ordered,
+    notes, spread, ordered, stage, sent,
 ):
     position = lax.axis_index("surf")
     odd = position % 2
@@ -354,11 +343,14 @@
         for j in range(1, pieces):
             tail = jnp.where(row // 2 == j, piece[INC : INC + TAIL, j * LANES : (j + 1) * LANES], tail)
         tail = jnp.where(slot >= bounds_ref[o, 1], -16.0, tail)
-        send_ref[o] = jnp.concatenate(parts + [tail], axis=0).astype(BF16)
+        stage[o] = jnp.concatenate(parts + [tail], axis=0).astype(BF16)
+        pltpu.make_async_copy(stage.at[o], send_ref.at[o], sent.at[o]).start()
+    for o in range(owners):
+        pltpu.make_async_copy(stage.at[o], send_ref.at[o], sent.at[o]).wait()
 
 
 def gather_body(
-    arrived_ref, compress, couple_ref, field_out, out_ref, index, spread, hot,
+    arrived_ref, compress, couple_ref, field_out, out_ref, index, spread, hot, stage, sent,
 ):
     owners, rows, _ = arrived_ref.shape
     pieces = (rows - TAIL) // INC
@@ -380,7 +372,10 @@
         field_out[b] = field[b * INC : (b + 1) * INC]
     coef = coefficients(field, compress).astype(BF16)
     for o in range(out_ref.shape[0]):
-        out_ref[o] = dot(coef, block(couple_ref, o)).astype(BF16)
+        stage[o] = dot(coef, block(couple_ref, o)).astype(BF16)
+        pltpu.make_async_copy(stage.at[o], out_ref.at[o], sent.at[o]).start()
+    for o in range(out_ref.shape[0]):
+        pltpu.make_async_copy(stage.at[o], out_ref.at[o], sent.at[o]).wait()
 
 
 def couple_body(coupling, source, owner, place, basis, out_ref, basis_out, total, lanes):
@@ -461,43 +456,38 @@
     lists = (far_source.reshape(1, tiles), far_owner.reshape(1, tiles), far_block.reshape(1, tiles))
     cube = ((BLK, TILE, TILE), BF16)
 
-    message = ((INC, TILE), BF16)
     note = ((3 * INC + TILE, TILE), BF16)
-    partial, inner, outer = call(
+    inner, outer = swap(currents, currents, surf_count)
+    (partial,) = call(
         far_up_body,
-        [((targets, INC * RANK), BF16), message, message],
+        [((targets, INC * RANK), BF16)],
         (currents, primal_compress, primal_coupling) + lists,
         scratch=far_scratch(tiles),
         held=(2, 0, 1, 3, 4, 5),
+        flops=10**11,
         name="far_up",
     )
     arrived = exchange(partial, surf_count)
-    inner, outer = swap(inner, outer, surf_count)
-    lower, upper, expanded = call(
-        products_body,
-        [cube, cube, ((BLK, RANK, TILE), BF16)],
-        (gram_inverse, gram_lower, gram_upper, primal_expand),
-        held=(0, 1, 2, 3),
-        flops=PRODUCT_COST,
-        name="products",
-    )
-    (near_part,) = call(
-        near_body,
-        [((INC, NP_DEV), F32)],
-        (near_target, near_source, currents, inner, outer, gram_inverse, near_tiles),
+    near_part, lower, upper, expanded = call(
+        prepare_body,
+        [((INC, NP_DEV), F32), cube, cube, ((BLK, RANK, TILE), BF16)],
+        (
+            near_target, near_source, currents, inner, outer, gram_inverse, gram_lower, gram_upper,
+            primal_expand, near_tiles,
+        ),
         scratch=[
             pltpu.VMEM((BLK + 2, INC, TILE), BF16),
             pltpu.VMEM((BLK, INC, TILE), F32),
             pltpu.VMEM((near_count, INC, TILE), F32),
-            pltpu.VMEM((2,) + message[0], BF16),
+            pltpu.VMEM((2,) + currents.shape, BF16),
             pltpu.VMEM(near_tiles.shape, BF16),
             pltpu.SemaphoreType.DMA((near_count // NEAR_CHUNK,)),
         ],
-        held=(2, 0, 1, 5),
-        far=(6,),
+        held=(5, 6, 7, 8, 2, 0, 1),
+        far=(9,),
         small=(0, 1),
-        flops=NEAR_COST,
-        name="near",
+        flops=10**11,
+        name="prepare",
     )
     start, after, inner_note, outer_note = call(
         solve_body,
@@ -541,7 +531,10 @@
             pltpu.VMEM((2,) + note[0], BF16),
             pltpu.VMEM((BLK * rows, NP_DEV), BF16),
             pltpu.VMEM((rows, NP_DEV + (pieces + 1) * LANES), F32),
+            pltpu.VMEM((surf_count, INC * pieces + TAIL, LANES), BF16),
+            pltpu.SemaphoreType.DMA((surf_count,)),
         ],
+        streamed=(0,),
         smem=(12,),
         held=(8,),
         name="finish",
@@ -566,7 +559,10 @@
             pltpu.VMEM((surf_count * pieces, LANES), F32),
             pltpu.VMEM((BLK * INC, slots), BF16),
             pltpu.VMEM((slots, TILE), BF16),
+            pltpu.VMEM((surf_count, INC, BLK * RANK), BF16),
+            pltpu.SemaphoreType.DMA((surf_count,)),
         ],
+        streamed=(1,),
         name="gather",
     )
     arrived = lax.all_to_all(partial, "surf", split_axis=0, concat_axis=0, tiled=True)

time: 69.7 us -> 67.7 us (0.971)
  starting transfers between devices: 26.1 us -> 22.9 us
  waiting for transfers between devices: 13.8 us -> 15.7 us
  Pallas kernels: 29.2 us -> 28.3 us
    all_to_all x1, starting transfers between devices: 11.9 us -> 8.65 us  [shards(): lax.all_to_all(send, 'surf', split_axis=0, concat_axis=0, tiled=True)]
    all_to_all x1, waiting for transfers between devices: 1.55 us -> 3.5 us  [exchange(): lax.all_to_all(array, 'surf', split_axis=0, concat_axis=0, tiled=True)]
    ppermute x2, starting transfers between devices: 1.96 us -> 0.52 us  [swap(): lax.ppermute(inner, 'surf', pairs)]
    ppermute x2, starting transfers between devices: 1.31 us -> 2.22 us  [swap(): lax.ppermute(outer, 'surf', others)]
    pallas_call x11 -> x10, Pallas kernels: 29.2 us -> 28.3 us  [call(): pl.pallas_call(wrapped, out_shape=outs, in_specs=[pl.BlockSpec(memory_spa...]
  transfers between devices with their start and end apart: 7 -> 7, of which waited for: 3 -> 3; matrix products, arithmetic and copies ran while one was open for 0% -> 0% of each run, Pallas kernels for 26% -> 31%
where the time goes in v8:
time: 67.7 us; the launch traced here: 67.1 us
  Pallas kernels  28.3 us (42%)
  starting transfers between devices  22.9 us (34%)
  waiting for transfers between devices  15.7 us (23%)
    pallas_call x10, Pallas kernels, call(): pl.pallas_call(wrapped, out_shape=outs, in_specs=[pl.BlockSpec(memory_spa...  28.3 us
    all_to_all x1, starting transfers between devices, shards(): lax.all_to_all(send, 'surf', split_axis=0, concat_axis=0, tiled=True)  8.65 us
    all_to_all x1, waiting for transfers between devices, shards(): lax.all_to_all(partial, 'surf', split_axis=0, concat_axis=0, tiled=True)  8.39 us
    all_to_all x1, starting transfers between devices, exchange(): lax.all_to_all(array, 'surf', split_axis=0, concat_axis=0, tiled=True)  7.92 us
    all_to_all x1, waiting for transfers between devices, shards(): lax.all_to_all(send, 'surf', split_axis=0, concat_axis=0, tiled=True)  3.85 us
    all_to_all x1, starting transfers between devices, shards(): lax.all_to_all(partial, 'surf', split_axis=0, concat_axis=0, tiled=True)  3.54 us
    all_to_all x1, waiting for transfers between devices, exchange(): lax.all_to_all(array, 'surf', split_axis=0, concat_axis=0, tiled=True)  3.5 us
    ppermute x2, starting transfers between devices, swap(): lax.ppermute(outer, 'surf', others)  2.22 us
  transfers between devices with their start and end apart: 7, of which 3 were waited for; matrix products, arithmetic and copies ran while one was open for 0% of the time, Pallas kernels for 31%

profile of v8, /device:TPU:0, one launch (start us, length us, event | category | flops | bytes accessed | tf_op | source)
XLA Modules:
  0.0 67.1 jit_solution(288389516352521736)
XLA Ops:
  0.0 0.5 collective-permute-start
  0.5 1.6 %collective-permute-start.1 = (bf16[32,2048]{1,0:T(8,128)(2,1)}, bf16[32,2048]{1,0:T(8,128)(2,1)S(1)}, u32[]{:S(2)}, u32[]{:S(2)}) collective-permute-start(bf16[32,2048]{1,0:T(8,128)(2,1)} %refs_2_.4), channel_id=1, source_target_pairs={{0,0},{15,15},{1,2},{2,1},{3,4},{4,3},{5,6},{6,5},{7,8},{8,7},{9,1... | collective-permute-start | bytes 393224 | tf_op jit(solution)/shard_map/ppermute | solution.py:435
  2.0 4.1 %far_up.1 = bf16[128,1024]{1,0:T(8,128)(2,1)} custom-call(bf16[32,2048]{1,0:T(8,128)(2,1)} %refs_2_.4, bf16[8,32,256]{2,1,0:T(8,128)(2,1)} %refs_1_.3, bf16[128,1024]{1,0:T(8,128)(2,1)} %refs_2_.3, s32[1,128]{1,0:T(1,128)} %bitcast.12, s32[1,128]{1,0:T(1,128)} %bitcast.14, s32[1,128]{1,0:T(1,128)} %bitcast.16), custom_call_target="tpu_custom_call" | custom-call | flops 99999997952 | bytes 525824 | tf_op jit(solution)/shard_map/far_up/pallas_call | solution.py:68
  6.1 7.9 %all-to-all-start = ((bf16[16,8,1024]{2,1,0:T(8,128)(2,1)}), bf16[16,8,1024]{2,1,0:T(8,128)(2,1)S(1)}, u32[]{:S(2)}, u32[]{:S(2)}) async-start(bf16[16,8,1024]{2,1,0:T(8,128)(2,1)} %bitcast.3), calls=%async_computation | async-start | bytes 524288 | tf_op jit(solution)/shard_map/all_to_all | solution.py:441
  14.0 0.0 collective-permute-done.refs_3_
  14.0 0.0 collective-permute-done.1.refs_4_
  14.0 6.5 %prepare.1 = (f32[32,2048]{1,0:T(8,128)S(1)}, bf16[8,256,256]{2,1,0:T(8,128)(2,1)S(1)}, bf16[8,256,256]{2,1,0:T(8,128)(2,1)S(1)}, bf16[8,32,256]{2,1,0:T(8,128)(2,1)S(1)}) custom-call(s32[48]{0:T(128)} %refs_0_.4, s32[48]{0:T(128)} %refs_1_.4, bf16[32,2048]{1,0:T(8,128)(2,1)} %refs_2_.4, bf16[32,2048]{1,0:T(8,128)(2,1)S(1)} %collective-permute-done.refs_3_, ...), custom_call_target="tpu_custom_call" | custom-call | flops 99999997952 | bytes 9961856 | tf_op jit(solution)/shard_map/prepare/pallas_call | solution.py:68
  20.6 3.5 %all-to-all-done = bf16[16,8,1024]{2,1,0:T(8,128)(2,1)S(1)} async-done(((bf16[16,8,1024]{2,1,0:T(8,128)(2,1)}), bf16[16,8,1024]{2,1,0:T(8,128)(2,1)S(1)}, u32[]{:S(2)}, u32[]{:S(2)}) %all-to-all-start) | async-done | bytes 262176 | tf_op jit(solution)/shard_map/all_to_all | solution.py:441
  24.1 0.9 %solve.1 = (f32[32,2048]{1,0:T(8,128)S(1)}, f32[32,2048]{1,0:T(8,128)S(1)}, bf16[352,256]{1,0:T(8,128)(2,1)S(1)}, bf16[352,256]{1,0:T(8,128)(2,1)S(1)}) custom-call(bf16[128,1024]{1,0:T(8,128)(2,1)S(1)} %bitcast.8, f32[32,2048]{1,0:T(8,128)S(1)} %get-tuple-element.25.refs_1_, bf16[8,32,256]{2,1,0:T(8,128)(2,1)S(1)} %get-tuple-element.26.refs_2_, ...), custom_call_target="tpu_custom_call" | custom-call | bytes 2752512 | tf_op jit(solution)/shard_map/solve/pallas_call | solution.py:68
  24.9 0.1 collective-permute-start.2
  25.0 0.7 %collective-permute-start.3 = (bf16[352,256]{1,0:T(8,128)(2,1)S(1)}, bf16[352,256]{1,0:T(8,128)(2,1)S(1)}, u32[]{:S(2)}, u32[]{:S(2)}) collective-permute-start(bf16[352,256]{1,0:T(8,128)(2,1)S(1)} %get-tuple-element.34), channel_id=1, source_target_pairs={{0,0},{15,15},{1,2},{2,1},{3,4},{4,3},{5,6},{6,5},{7,8},{8,7},{9,1... | collective-permute-start | bytes 540680 | tf_op jit(solution)/shard_map/ppermute | solution.py:435
  25.7 1.4 %order.1 = (s32[8,256]{1,0:T(8,128)S(1)}, bf16[2048,256]{1,0:T(8,128)(2,1)S(1)}, s32[16,2]{1,0:T(8,128)S(1)}, bf16[16,2048]{1,0:T(8,128)(2,1)S(1)}) custom-call(s32[1,2048]{1,0:T(1,128)} %bitcast.10, s32[1,2048]{1,0:T(1,128)} %bitcast.11), custom_call_target="tpu_custom_call" | custom-call | flops 1000000000 | bytes 16384 | tf_op jit(solution)/shard_map/order/pallas_call | solution.py:68
  27.1 0.6 middle.1
  27.6 0.0 collective-permute-done.2.refs_4_
  27.6 0.0 collective-permute-done.3.refs_5_
  27.7 3.1 %finish.1 = bf16[16,72,128]{2,1,0:T(8,128)(2,1)} custom-call(f32[32,2048]{1,0:T(8,128)S(1)} %get-tuple-element.29.refs_0_, f32[32,2048]{1,0:T(8,128)S(1)} %get-tuple-element.30.refs_1_, f32[32,2048]{1,0:T(8,128)S(1)} %get-tuple-element.31.refs_2_, f32[32,2048]{1,0:T(8,128)S(1)} %get-tuple-element.32.refs_3_, ...), custom_call_target="tpu_custom_call" | custom-call | bytes 4636800 | tf_op jit(solution)/shard_map/finish/pallas_call | solution.py:68
  30.8 8.7 %all-to-all-start.1 = ((bf16[16,72,128]{2,1,0:T(8,128)(2,1)}), bf16[16,72,128]{2,1,0:T(8,128)(2,1)S(1)}, u32[]{:S(2)}, u32[]{:S(2)}) async-start(bf16[16,72,128]{2,1,0:T(8,128)(2,1)} %finish.1), calls=%async_computation.1 | async-start | bytes 589824 | tf_op jit(solution)/shard_map/all_to_all | solution.py:542
  39.4 6.7 %couple.1 = (bf16[256,4096]{1,0:T(8,128)(2,1)S(1)}, bf16[8,32,256]{2,1,0:T(8,128)(2,1)S(1)}) custom-call(bf16[128,1024]{1,0:T(8,128)(2,1)} %refs_0_.5, s32[1,128]{1,0:T(1,128)} %bitcast.13, s32[1,128]{1,0:T(1,128)} %bitcast.15, s32[1,128]{1,0:T(1,128)} %bitcast.17, bf16[8,32,256]{2,1,0:T(8,128)(2,1)} %refs_4_.1), custom_call_target="tpu_custom_call" | custom-call | flops 10000000000 | bytes 394752 | tf_op jit(solution)/shard_map/couple/pallas_call | solution.py:68
  46.1 3.8 %all-to-all-done.1.refs_0_ = bf16[16,72,128]{2,1,0:T(8,128)(2,1)S(1)} async-done(((bf16[16,72,128]{2,1,0:T(8,128)(2,1)}), bf16[16,72,128]{2,1,0:T(8,128)(2,1)S(1)}, u32[]{:S(2)}, u32[]{:S(2)}) %all-to-all-start.1) | async-done | bytes 294944 | tf_op jit(solution)/shard_map/all_to_all | solution.py:542
  50.0 2.7 %gather.1 = (bf16[8,32,256]{2,1,0:T(8,128)(2,1)S(1)}, bf16[16,32,256]{2,1,0:T(8,128)(2,1)}) custom-call(bf16[16,72,128]{2,1,0:T(8,128)(2,1)S(1)} %all-to-all-done.1.refs_0_, bf16[8,32,256]{2,1,0:T(8,128)(2,1)S(1)} %get-tuple-element.39.refs_1_, bf16[256,4096]{1,0:T(8,128)(2,1)S(1)} %get-tuple-element.40.refs_2_), custom_call_target="tpu_custom_call" | custom-call | bytes 2523136 | tf_op jit(solution)/shard_map/gather/pallas_call | solution.py:68
  52.7 3.5 %all-to-all-start.2 = ((bf16[16,32,256]{2,1,0:T(8,128)(2,1)}), bf16[16,32,256]{2,1,0:T(8,128)(2,1)S(1)}, u32[]{:S(2)}, u32[]{:S(2)}) async-start(bf16[16,32,256]{2,1,0:T(8,128)(2,1)} %get-tuple-element.41), calls=%async_computation.2 | async-start | bytes 524288 | tf_op jit(solution)/shard_map/all_to_all | solution.py:568
  56.2 1.6 %self_part.1 = (f32[32,2048]{1,0:T(8,128)S(1)}, bf16[8,32,256]{2,1,0:T(8,128)(2,1)S(1)}) custom-call(bf16[8,32,256]{2,1,0:T(8,128)(2,1)S(1)} %get-tuple-element.42.refs_0_, bf16[8,256,256]{2,1,0:T(8,128)(2,1)} %refs_1_.5, bf16[8,32,256]{2,1,0:T(8,128)(2,1)} %refs_2_.5), custom_call_target="tpu_custom_call" | custom-call | bytes 1310720 | tf_op jit(solution)/shard_map/self_part/pallas_call | solution.py:68
  57.8 8.4 %all-to-all-done.2.refs_0_ = bf16[16,32,256]{2,1,0:T(8,128)(2,1)S(1)} async-done(((bf16[16,32,256]{2,1,0:T(8,128)(2,1)}), bf16[16,32,256]{2,1,0:T(8,128)(2,1)S(1)}, u32[]{:S(2)}, u32[]{:S(2)}) %all-to-all-start.2) | async-done | bytes 262176 | tf_op jit(solution)/shard_map/all_to_all | solution.py:568
  66.2 0.9 %answer.1 = bf16[32,2048]{1,0:T(8,128)(2,1)} custom-call(bf16[16,32,256]{2,1,0:T(8,128)(2,1)S(1)} %all-to-all-done.2.refs_0_, f32[32,2048]{1,0:T(8,128)S(1)} %get-tuple-element.43.refs_1_, bf16[8,32,256]{2,1,0:T(8,128)(2,1)S(1)} %get-tuple-element.44.refs_2_), custom_call_target="tpu_custom_call" | custom-call | bytes 655360 | tf_op jit(solution)/shard_map/answer/pallas_call | solution.py:68
Async XLA Ops:
  0.0 14.0 %collective-permute-start = (bf16[32,2048]{1,0:T(8,128)(2,1)}, bf16[32,2048]{1,0:T(8,128)(2,1)S(1)}, u32[]{:S(2)}, u32[]{:S(2)}) collective-permute-start(bf16[32,2048]{1,0:T(8,128)(2,1)} %refs_2_.4), channel_id=1, source_target_pairs={{0,1},{1,0},{2,3},{3,2},{4,5},{5,4},{6,7},{7,6},{8,9},{9,8},{10,11... | collective-permute-start | bytes 393224 | tf_op jit(solution)/shard_map/ppermute | solution.py:435
  0.5 13.6 %collective-permute-start.1 = (bf16[32,2048]{1,0:T(8,128)(2,1)}, bf16[32,2048]{1,0:T(8,128)(2,1)S(1)}, u32[]{:S(2)}, u32[]{:S(2)}) collective-permute-start(bf16[32,2048]{1,0:T(8,128)(2,1)} %refs_2_.4), channel_id=1, source_target_pairs={{0,0},{15,15},{1,2},{2,1},{3,4},{4,3},{5,6},{6,5},{7,8},{8,7},{9,1... | collective-permute-start | bytes 393224 | tf_op jit(solution)/shard_map/ppermute | solution.py:435
  6.1 18.0 %all-to-all-start = ((bf16[16,8,1024]{2,1,0:T(8,128)(2,1)}), bf16[16,8,1024]{2,1,0:T(8,128)(2,1)S(1)}, u32[]{:S(2)}, u32[]{:S(2)}) async-start(bf16[16,8,1024]{2,1,0:T(8,128)(2,1)} %bitcast.3), calls=%async_computation | async-start | bytes 524288 | tf_op jit(solution)/shard_map/all_to_all | solution.py:441
  24.9 2.7 %collective-permute-start.2 = (bf16[352,256]{1,0:T(8,128)(2,1)S(1)}, bf16[352,256]{1,0:T(8,128)(2,1)S(1)}, u32[]{:S(2)}, u32[]{:S(2)}) collective-permute-start(bf16[352,256]{1,0:T(8,128)(2,1)S(1)} %get-tuple-element.33), channel_id=1, source_target_pairs={{0,1},{1,0},{2,3},{3,2},{4,5},{5,4},{6,7},{7,6},{8,9},{9,8},{10,11... | collective-permute-start | bytes 540680 | tf_op jit(solution)/shard_map/ppermute | solution.py:435
  25.0 2.6 %collective-permute-start.3 = (bf16[352,256]{1,0:T(8,128)(2,1)S(1)}, bf16[352,256]{1,0:T(8,128)(2,1)S(1)}, u32[]{:S(2)}, u32[]{:S(2)}) collective-permute-start(bf16[352,256]{1,0:T(8,128)(2,1)S(1)} %get-tuple-element.34), channel_id=1, source_target_pairs={{0,0},{15,15},{1,2},{2,1},{3,4},{4,3},{5,6},{6,5},{7,8},{8,7},{9,1... | collective-permute-start | bytes 540680 | tf_op jit(solution)/shard_map/ppermute | solution.py:435
  30.8 19.2 %all-to-all-start.1 = ((bf16[16,72,128]{2,1,0:T(8,128)(2,1)}), bf16[16,72,128]{2,1,0:T(8,128)(2,1)S(1)}, u32[]{:S(2)}, u32[]{:S(2)}) async-start(bf16[16,72,128]{2,1,0:T(8,128)(2,1)} %finish.1), calls=%async_computation.1 | async-start | bytes 589824 | tf_op jit(solution)/shard_map/all_to_all | solution.py:542
  52.7 13.6 %all-to-all-start.2 = ((bf16[16,32,256]{2,1,0:T(8,128)(2,1)}), bf16[16,32,256]{2,1,0:T(8,128)(2,1)S(1)}, u32[]{:S(2)}, u32[]{:S(2)}) async-start(bf16[16,32,256]{2,1,0:T(8,128)(2,1)} %get-tuple-element.41), calls=%async_computation.2 | async-start | bytes 524288 | tf_op jit(solution)/shard_map/all_to_all | solution.py:568

commit v9 on v8

--- a/solution.py
+++ b/solution.py
@@ -162,7 +162,7 @@
     return dot(spread[...], fold).astype(BF16)
 
 
-def order_body(owner, index, high_out, hot_out, bounds_out, rows_out, ranks):
+def order_body(owner, index, weight, high_out, hot_out, bounds_out, rows_out, weight_out, ranks):
     owner, index = ready(owner), ready(index)
     owners = bounds_out.shape[0]
     pieces = -(-max(2, 2 * NP_DEV // owners) // LANES)
@@ -190,6 +190,7 @@
     index = index[...]
     digits = jnp.where(row % 2 == 0, index // TILE, index % TILE)
     rows_out[...] = jnp.where(row < 2 * pieces, digits, 0).astype(F32).astype(BF16)
+    weight_out[...] = ready(weight)[...]
 
 
 def prepare_body(
@@ -314,7 +315,6 @@
         then[edge] = then[edge] - dot(beside_next, toward[edge]) - dot(second_one, away[edge])
         then[one] = then[one] - dot(second, toward[one])
         then[two] = then[two] - dot(second_one, toward[two])
-    weight = ready(weight)
     rows = INC + IDX_ROWS
     for b in range(BLK):
         solved = then[b].astype(BF16).astype(F32)
@@ -350,7 +350,7 @@
 
 
 def gather_body(
-    arrived_ref, compress, couple_ref, field_out, out_ref, index, spread, hot, stage, sent,
+    arrived_ref, compress, couple_ref, field_out, coef_out, give_out, index, spread, hot,
 ):
     owners, rows, _ = arrived_ref.shape
     pieces = (rows - TAIL) // INC
@@ -371,11 +371,24 @@
     for b in range(BLK):
         field_out[b] = field[b * INC : (b + 1) * INC]
     coef = coefficients(field, compress).astype(BF16)
-    for o in range(out_ref.shape[0]):
-        stage[o] = dot(coef, block(couple_ref, o)).astype(BF16)
-        pltpu.make_async_copy(stage.at[o], out_ref.at[o], sent.at[o]).start()
-    for o in range(out_ref.shape[0]):
-        pltpu.make_async_copy(stage.at[o], out_ref.at[o], sent.at[o]).wait()
+    coef_out[...] = coef
+    other = 1 - lax.axis_index("surf") % 2
+    for c in range(give_out.shape[0]):
+        give_out[c] = dot(coef, owner_columns(couple_ref, c, other)).astype(BF16)
+
+
+def owner_columns(couple_ref, chip, core):
+    return couple_ref[:, pl.ds(pl.multiple_of((2 * chip + core) * TILE, TILE), TILE)]
+
+
+def own_body(coef_ref, couple_ref, out_ref):
+    core = lax.axis_index("surf") % 2
+    for c in range(out_ref.shape[0]):
+        out_ref[c] = dot(coef_ref[...], owner_columns(couple_ref, c, core))
+
+
+def merge_body(own_ref, got_ref, out_ref):
+    out_ref[...] = (own_ref[...] + got_ref[...].astype(F32)).astype(BF16)
 
 
 def couple_body(coupling, source, owner, place, basis, out_ref, basis_out, total, lanes):
@@ -501,15 +514,18 @@
     )
     inner_note, outer_note = swap(inner_note, outer_note, surf_count)
     rows = INC + IDX_ROWS
-    high, hot, bounds, index_rows = call(
+    high, hot, bounds, index_rows, weight = call(
         order_body,
         [
             ((BLK, TILE), I32), ((NP_DEV, TILE), BF16), ((surf_count, 2), I32),
-            ((IDX_ROWS, NP_DEV), BF16),
+            ((IDX_ROWS, NP_DEV), BF16), ((1, NP_DEV), F32),
         ],
-        (dual_owner.reshape(1, NP_DEV), dual_index.reshape(1, NP_DEV)),
+        (
+            dual_owner.reshape(1, NP_DEV), dual_index.reshape(1, NP_DEV),
+            refine_weight.reshape(1, NP_DEV),
+        ),
         scratch=[pltpu.VMEM((BLK, TILE), F32)],
-        held=(0, 1),
+        held=(0, 1, 2),
         flops=10**9,
         name="order",
     )
@@ -525,7 +541,7 @@
         [((surf_count, INC * pieces + TAIL, LANES), BF16)],
         (
             start, after, second, third, inner_note, outer_note, lower, upper,
-            refine_weight.reshape(1, NP_DEV), index_rows, high, hot, bounds,
+            weight, index_rows, high, hot, bounds,
         ),
         scratch=[
             pltpu.VMEM((2,) + note[0], BF16),
@@ -536,7 +552,6 @@
         ],
         streamed=(0,),
         smem=(12,),
-        held=(8,),
         name="finish",
     )
     shares = lax.all_to_all(send, "surf", split_axis=0, concat_axis=0, tiled=True)
@@ -551,21 +566,29 @@
         flops=10**10,
         name="couple",
     )
-    field, partial = call(
+    half = (surf_count // 2, INC, BLK * RANK)
+    field, coef, give = call(
         gather_body,
-        [((BLK, INC, TILE), BF16), ((surf_count, INC, BLK * RANK), BF16)],
+        [((BLK, INC, TILE), BF16), ((INC, BLK * RANK), BF16), (half, BF16)],
         (shares, compress, couple),
         scratch=[
             pltpu.VMEM((surf_count * pieces, LANES), F32),
             pltpu.VMEM((BLK * INC, slots), BF16),
             pltpu.VMEM((slots, TILE), BF16),
-            pltpu.VMEM((surf_count, INC, BLK * RANK), BF16),
-            pltpu.SemaphoreType.DMA((surf_count,)),
         ],
-        streamed=(1,),
         name="gather",
     )
-    arrived = lax.all_to_all(partial, "surf", split_axis=0, concat_axis=0, tiled=True)
+    got = lax.ppermute(give, "surf", [(i, i ^ 1) for i in range(surf_count)])
+    (own,) = call(own_body, [(half, F32)], (coef, couple), flops=10**9, name="own")
+    (merged,) = call(merge_body, [(half, BF16)], (own, got), name="merge")
+    arrived = lax.all_to_all(
+        merged,
+        "surf",
+        split_axis=0,
+        concat_axis=0,
+        tiled=True,
+        axis_index_groups=[list(range(core, surf_count, 2)) for core in range(2)],
+    )
     near_dual, expand = call(
         self_body,
         [((INC, NP_DEV), F32), (dual_expand.shape, BF16)],

time: 67.7 us -> 65.7 us (0.970)
  waiting for transfers between devices: 15.7 us -> 14.3 us
    all_to_all x1, waiting for transfers between devices: 8.39 us -> 5.89 us  [shards(): lax.all_to_all(merged, 'surf', split_axis=0, concat_axis=0, tiled=True, a...]
    ppermute x0 -> x1, waiting for transfers between devices: none -> 1.04 us  [shards(): got = lax.ppermute(give, 'surf', [(i, i ^ 1) for i in range(surf_count)])]
    pallas_call x10 -> x12, Pallas kernels: 28.3 us -> 27.9 us  [call(): pl.pallas_call(wrapped, out_shape=outs, in_specs=[pl.BlockSpec(memory_spa...]
  transfers between devices with their start and end apart: 7 -> 8, of which waited for: 3 -> 4; matrix products, arithmetic and copies ran while one was open for 0% -> 0% of each run, Pallas kernels for 31% -> 32%
where the time goes in v9:
time: 65.7 us; the launch traced here: 65.1 us
  Pallas kernels  27.9 us (42%)
  starting transfers between devices  22.7 us (35%)
  waiting for transfers between devices  14.3 us (22%)
    pallas_call x12, Pallas kernels, call(): pl.pallas_call(wrapped, out_shape=outs, in_specs=[pl.BlockSpec(memory_spa...  27.9 us
    all_to_all x1, starting transfers between devices, shards(): lax.all_to_all(send, 'surf', split_axis=0, concat_axis=0, tiled=True)  8.63 us
    all_to_all x1, starting transfers between devices, exchange(): lax.all_to_all(array, 'surf', split_axis=0, concat_axis=0, tiled=True)  7.92 us
    all_to_all x1, waiting for transfers between devices, shards(): lax.all_to_all(merged, 'surf', split_axis=0, concat_axis=0, tiled=True, a...  5.89 us
    all_to_all x1, waiting for transfers between devices, shards(): lax.all_to_all(send, 'surf', split_axis=0, concat_axis=0, tiled=True)  3.86 us
    all_to_all x1, waiting for transfers between devices, exchange(): lax.all_to_all(array, 'surf', split_axis=0, concat_axis=0, tiled=True)  3.51 us
    all_to_all x1, starting transfers between devices, shards(): lax.all_to_all(merged, 'surf', split_axis=0, concat_axis=0, tiled=True, a...  3.37 us
    ppermute x2, starting transfers between devices, swap(): lax.ppermute(outer, 'surf', others)  2.22 us
  transfers between devices with their start and end apart: 8, of which 4 were waited for; matrix products, arithmetic and copies ran while one was open for 0% of the time, Pallas kernels for 32%

profile of v9, /device:TPU:0, one launch (start us, length us, event | category | flops | bytes accessed | tf_op | source)
XLA Modules:
  0.0 65.1 jit_solution(1683991811000323256)
XLA Ops:
  0.0 0.5 collective-permute-start
  0.5 1.6 %collective-permute-start.1 = (bf16[32,2048]{1,0:T(8,128)(2,1)}, bf16[32,2048]{1,0:T(8,128)(2,1)S(1)}, u32[]{:S(2)}, u32[]{:S(2)}) collective-permute-start(bf16[32,2048]{1,0:T(8,128)(2,1)} %refs_2_.4), channel_id=1, source_target_pairs={{0,0},{15,15},{1,2},{2,1},{3,4},{4,3},{5,6},{6,5},{7,8},{8,7},{9,1... | collective-permute-start | bytes 393224 | tf_op jit(solution)/shard_map/ppermute | solution.py:448
  2.0 4.1 %far_up.1 = bf16[128,1024]{1,0:T(8,128)(2,1)} custom-call(bf16[32,2048]{1,0:T(8,128)(2,1)} %refs_2_.4, bf16[8,32,256]{2,1,0:T(8,128)(2,1)} %refs_1_.3, bf16[128,1024]{1,0:T(8,128)(2,1)} %refs_2_.3, s32[1,128]{1,0:T(1,128)} %bitcast.12, s32[1,128]{1,0:T(1,128)} %bitcast.14, s32[1,128]{1,0:T(1,128)} %bitcast.16), custom_call_target="tpu_custom_call" | custom-call | flops 99999997952 | bytes 525824 | tf_op jit(solution)/shard_map/far_up/pallas_call | solution.py:68
  6.1 7.9 %all-to-all-start = ((bf16[16,8,1024]{2,1,0:T(8,128)(2,1)}), bf16[16,8,1024]{2,1,0:T(8,128)(2,1)S(1)}, u32[]{:S(2)}, u32[]{:S(2)}) async-start(bf16[16,8,1024]{2,1,0:T(8,128)(2,1)} %bitcast.3), calls=%async_computation | async-start | bytes 524288 | tf_op jit(solution)/shard_map/all_to_all | solution.py:454
  14.0 0.0 collective-permute-done.refs_3_
  14.0 0.0 collective-permute-done.1.refs_4_
  14.0 6.5 %prepare.1 = (f32[32,2048]{1,0:T(8,128)S(1)}, bf16[8,256,256]{2,1,0:T(8,128)(2,1)S(1)}, bf16[8,256,256]{2,1,0:T(8,128)(2,1)S(1)}, bf16[8,32,256]{2,1,0:T(8,128)(2,1)S(1)}) custom-call(s32[48]{0:T(128)} %refs_0_.4, s32[48]{0:T(128)} %refs_1_.4, bf16[32,2048]{1,0:T(8,128)(2,1)} %refs_2_.4, bf16[32,2048]{1,0:T(8,128)(2,1)S(1)} %collective-permute-done.refs_3_, ...), custom_call_target="tpu_custom_call" | custom-call | flops 99999997952 | bytes 9961856 | tf_op jit(solution)/shard_map/prepare/pallas_call | solution.py:68
  20.6 3.5 %all-to-all-done = bf16[16,8,1024]{2,1,0:T(8,128)(2,1)S(1)} async-done(((bf16[16,8,1024]{2,1,0:T(8,128)(2,1)}), bf16[16,8,1024]{2,1,0:T(8,128)(2,1)S(1)}, u32[]{:S(2)}, u32[]{:S(2)}) %all-to-all-start) | async-done | bytes 262176 | tf_op jit(solution)/shard_map/all_to_all | solution.py:454
  24.1 0.9 %solve.1 = (f32[32,2048]{1,0:T(8,128)S(1)}, f32[32,2048]{1,0:T(8,128)S(1)}, bf16[352,256]{1,0:T(8,128)(2,1)S(1)}, bf16[352,256]{1,0:T(8,128)(2,1)S(1)}) custom-call(bf16[128,1024]{1,0:T(8,128)(2,1)S(1)} %bitcast.8, f32[32,2048]{1,0:T(8,128)S(1)} %get-tuple-element.27.refs_1_, bf16[8,32,256]{2,1,0:T(8,128)(2,1)S(1)} %get-tuple-element.28.refs_2_, ...), custom_call_target="tpu_custom_call" | custom-call | bytes 2752512 | tf_op jit(solution)/shard_map/solve/pallas_call | solution.py:68
  24.9 0.1 collective-permute-start.2
  25.0 0.7 %collective-permute-start.3 = (bf16[352,256]{1,0:T(8,128)(2,1)S(1)}, bf16[352,256]{1,0:T(8,128)(2,1)S(1)}, u32[]{:S(2)}, u32[]{:S(2)}) collective-permute-start(bf16[352,256]{1,0:T(8,128)(2,1)S(1)} %get-tuple-element.36), channel_id=1, source_target_pairs={{0,0},{15,15},{1,2},{2,1},{3,4},{4,3},{5,6},{6,5},{7,8},{8,7},{9,1... | collective-permute-start | bytes 540680 | tf_op jit(solution)/shard_map/ppermute | solution.py:448
  25.7 1.4 %order.1 = (s32[8,256]{1,0:T(8,128)S(1)}, bf16[2048,256]{1,0:T(8,128)(2,1)S(1)}, s32[16,2]{1,0:T(8,128)S(1)}, bf16[16,2048]{1,0:T(8,128)(2,1)S(1)}, f32[1,2048]{1,0:T(1,128)S(1)}) custom-call(s32[1,2048]{1,0:T(1,128)} %bitcast.9, s32[1,2048]{1,0:T(1,128)} %bitcast.10, f32[1,2048]{1,0:T(1,128)} %bitcast.11), custom_call_target="tpu_custom_call" | custom-call | flops 1000000000 | bytes 24576 | tf_op jit(solution)/shard_map/order/pallas_call | solution.py:68
  27.1 0.6 middle.1
  27.6 0.0 collective-permute-done.2.refs_4_
  27.7 0.0 collective-permute-done.3.refs_5_
  27.7 2.9 %finish.1 = bf16[16,72,128]{2,1,0:T(8,128)(2,1)} custom-call(f32[32,2048]{1,0:T(8,128)S(1)} %get-tuple-element.31.refs_0_, f32[32,2048]{1,0:T(8,128)S(1)} %get-tuple-element.32.refs_1_, f32[32,2048]{1,0:T(8,128)S(1)} %get-tuple-element.33.refs_2_, f32[32,2048]{1,0:T(8,128)S(1)} %get-tuple-element.34.refs_3_, ...), custom_call_target="tpu_custom_call" | custom-call | bytes 4636800 | tf_op jit(solution)/shard_map/finish/pallas_call | solution.py:68
  30.6 8.6 %all-to-all-start.1 = ((bf16[16,72,128]{2,1,0:T(8,128)(2,1)}), bf16[16,72,128]{2,1,0:T(8,128)(2,1)S(1)}, u32[]{:S(2)}, u32[]{:S(2)}) async-start(bf16[16,72,128]{2,1,0:T(8,128)(2,1)} %finish.1), calls=%async_computation.1 | async-start | bytes 589824 | tf_op jit(solution)/shard_map/all_to_all | solution.py:557
  39.2 6.7 %couple.1 = (bf16[256,4096]{1,0:T(8,128)(2,1)S(1)}, bf16[8,32,256]{2,1,0:T(8,128)(2,1)S(1)}) custom-call(bf16[128,1024]{1,0:T(8,128)(2,1)} %refs_0_.5, s32[1,128]{1,0:T(1,128)} %bitcast.13, s32[1,128]{1,0:T(1,128)} %bitcast.15, s32[1,128]{1,0:T(1,128)} %bitcast.17, bf16[8,32,256]{2,1,0:T(8,128)(2,1)} %refs_4_.1), custom_call_target="tpu_custom_call" | custom-call | flops 10000000000 | bytes 394752 | tf_op jit(solution)/shard_map/couple/pallas_call | solution.py:68
  46.0 3.9 %all-to-all-done.1.refs_0_ = bf16[16,72,128]{2,1,0:T(8,128)(2,1)S(1)} async-done(((bf16[16,72,128]{2,1,0:T(8,128)(2,1)}), bf16[16,72,128]{2,1,0:T(8,128)(2,1)S(1)}, u32[]{:S(2)}, u32[]{:S(2)}) %all-to-all-start.1) | async-done | bytes 294944 | tf_op jit(solution)/shard_map/all_to_all | solution.py:557
  49.8 1.5 %gather.1 = (bf16[8,32,256]{2,1,0:T(8,128)(2,1)S(1)}, bf16[32,256]{1,0:T(8,128)(2,1)S(1)}, bf16[8,32,256]{2,1,0:T(8,128)(2,1)S(1)}) custom-call(bf16[16,72,128]{2,1,0:T(8,128)(2,1)S(1)} %all-to-all-done.1.refs_0_, bf16[8,32,256]{2,1,0:T(8,128)(2,1)S(1)} %get-tuple-element.42.refs_1_, bf16[256,4096]{1,0:T(8,128)(2,1)S(1)} %get-tuple-element.43.refs_2_.refs_1_), custom_call_target="tpu_custom_call" | custom-call | bytes 2523136 | tf_op jit(solution)/shard_map/gather/pallas_call | solution.py:68
  51.3 0.1 collective-permute-start.4
  51.4 0.3 own.1.refs_0_
  51.7 1.0 %collective-permute-done.4.refs_1_ = bf16[8,32,256]{2,1,0:T(8,128)(2,1)S(1)} collective-permute-done((bf16[8,32,256]{2,1,0:T(8,128)(2,1)S(1)}, bf16[8,32,256]{2,1,0:T(8,128)(2,1)S(1)}, u32[]{:S(2)}, u32[]{:S(2)}) %collective-permute-start.4) | collective-permute-done | bytes 131104 | tf_op jit(solution)/shard_map/ppermute | solution.py:581
  52.7 0.7 %merge.1 = bf16[8,32,256]{2,1,0:T(8,128)(2,1)} custom-call(f32[8,32,256]{2,1,0:T(8,128)S(1)} %own.1.refs_0_, bf16[8,32,256]{2,1,0:T(8,128)(2,1)S(1)} %collective-permute-done.4.refs_1_), custom_call_target="tpu_custom_call" | custom-call | bytes 393216 | tf_op jit(solution)/shard_map/merge/pallas_call | solution.py:68
  53.4 3.4 %all-to-all-start.2 = ((bf16[8,32,256]{2,1,0:T(8,128)(2,1)}), bf16[8,32,256]{2,1,0:T(8,128)(2,1)S(1)}, u32[]{:S(2)}, u32[]{:S(2)}) async-start(bf16[8,32,256]{2,1,0:T(8,128)(2,1)} %merge.1), calls=%async_computation.2 | async-start | bytes 262144 | tf_op jit(solution)/shard_map/all_to_all | solution.py:584
  56.8 1.6 %self_part.1 = (f32[32,2048]{1,0:T(8,128)S(1)}, bf16[8,32,256]{2,1,0:T(8,128)(2,1)S(1)}) custom-call(bf16[8,32,256]{2,1,0:T(8,128)(2,1)S(1)} %get-tuple-element.46.refs_0_, bf16[8,256,256]{2,1,0:T(8,128)(2,1)} %refs_1_.5, bf16[8,32,256]{2,1,0:T(8,128)(2,1)} %refs_2_.5), custom_call_target="tpu_custom_call" | custom-call | bytes 1310720 | tf_op jit(solution)/shard_map/self_part/pallas_call | solution.py:68
  58.4 5.9 %all-to-all-done.2.refs_0_ = bf16[8,32,256]{2,1,0:T(8,128)(2,1)S(1)} async-done(((bf16[8,32,256]{2,1,0:T(8,128)(2,1)}), bf16[8,32,256]{2,1,0:T(8,128)(2,1)S(1)}, u32[]{:S(2)}, u32[]{:S(2)}) %all-to-all-start.2) | async-done | bytes 131104 | tf_op jit(solution)/shard_map/all_to_all | solution.py:584
  64.3 0.8 %answer.1 = bf16[32,2048]{1,0:T(8,128)(2,1)} custom-call(bf16[8,32,256]{2,1,0:T(8,128)(2,1)S(1)} %all-to-all-done.2.refs_0_, f32[32,2048]{1,0:T(8,128)S(1)} %get-tuple-element.47.refs_1_, bf16[8,32,256]{2,1,0:T(8,128)(2,1)S(1)} %get-tuple-element.48.refs_2_), custom_call_target="tpu_custom_call" | custom-call | bytes 524288 | tf_op jit(solution)/shard_map/answer/pallas_call | solution.py:68
Async XLA Ops:
  0.0 14.0 %collective-permute-start = (bf16[32,2048]{1,0:T(8,128)(2,1)}, bf16[32,2048]{1,0:T(8,128)(2,1)S(1)}, u32[]{:S(2)}, u32[]{:S(2)}) collective-permute-start(bf16[32,2048]{1,0:T(8,128)(2,1)} %refs_2_.4), channel_id=1, source_target_pairs={{0,1},{1,0},{2,3},{3,2},{4,5},{5,4},{6,7},{7,6},{8,9},{9,8},{10,11... | collective-permute-start | bytes 393224 | tf_op jit(solution)/shard_map/ppermute | solution.py:448
  0.5 13.6 %collective-permute-start.1 = (bf16[32,2048]{1,0:T(8,128)(2,1)}, bf16[32,2048]{1,0:T(8,128)(2,1)S(1)}, u32[]{:S(2)}, u32[]{:S(2)}) collective-permute-start(bf16[32,2048]{1,0:T(8,128)(2,1)} %refs_2_.4), channel_id=1, source_target_pairs={{0,0},{15,15},{1,2},{2,1},{3,4},{4,3},{5,6},{6,5},{7,8},{8,7},{9,1... | collective-permute-start | bytes 393224 | tf_op jit(solution)/shard_map/ppermute | solution.py:448
  6.1 18.0 %all-to-all-start = ((bf16[16,8,1024]{2,1,0:T(8,128)(2,1)}), bf16[16,8,1024]{2,1,0:T(8,128)(2,1)S(1)}, u32[]{:S(2)}, u32[]{:S(2)}) async-start(bf16[16,8,1024]{2,1,0:T(8,128)(2,1)} %bitcast.3), calls=%async_computation | async-start | bytes 524288 | tf_op jit(solution)/shard_map/all_to_all | solution.py:454
  24.9 2.7 %collective-permute-start.2 = (bf16[352,256]{1,0:T(8,128)(2,1)S(1)}, bf16[352,256]{1,0:T(8,128)(2,1)S(1)}, u32[]{:S(2)}, u32[]{:S(2)}) collective-permute-start(bf16[352,256]{1,0:T(8,128)(2,1)S(1)} %get-tuple-element.35), channel_id=1, source_target_pairs={{0,1},{1,0},{2,3},{3,2},{4,5},{5,4},{6,7},{7,6},{8,9},{9,8},{10,11... | collective-permute-start | bytes 540680 | tf_op jit(solution)/shard_map/ppermute | solution.py:448
  25.0 2.6 %collective-permute-start.3 = (bf16[352,256]{1,0:T(8,128)(2,1)S(1)}, bf16[352,256]{1,0:T(8,128)(2,1)S(1)}, u32[]{:S(2)}, u32[]{:S(2)}) collective-permute-start(bf16[352,256]{1,0:T(8,128)(2,1)S(1)} %get-tuple-element.36), channel_id=1, source_target_pairs={{0,0},{15,15},{1,2},{2,1},{3,4},{4,3},{5,6},{6,5},{7,8},{8,7},{9,1... | collective-permute-start | bytes 540680 | tf_op jit(solution)/shard_map/ppermute | solution.py:448
  30.6 19.2 %all-to-all-start.1 = ((bf16[16,72,128]{2,1,0:T(8,128)(2,1)}), bf16[16,72,128]{2,1,0:T(8,128)(2,1)S(1)}, u32[]{:S(2)}, u32[]{:S(2)}) async-start(bf16[16,72,128]{2,1,0:T(8,128)(2,1)} %finish.1), calls=%async_computation.1 | async-start | bytes 589824 | tf_op jit(solution)/shard_map/all_to_all | solution.py:557
  51.3 1.4 %collective-permute-start.4 = (bf16[8,32,256]{2,1,0:T(8,128)(2,1)S(1)}, bf16[8,32,256]{2,1,0:T(8,128)(2,1)S(1)}, u32[]{:S(2)}, u32[]{:S(2)}) collective-permute-start(bf16[8,32,256]{2,1,0:T(8,128)(2,1)S(1)} %get-tuple-element.45), channel_id=1, source_target_pairs={{0,1},{1,0},{2,3},{3,2},{4,5},{5,4},{6,7},{7,6},{8,9},{9,8},{10,11... | collective-permute-start | bytes 393224 | tf_op jit(solution)/shard_map/ppermute | solution.py:581
  53.4 10.9 %all-to-all-start.2 = ((bf16[8,32,256]{2,1,0:T(8,128)(2,1)}), bf16[8,32,256]{2,1,0:T(8,128)(2,1)S(1)}, u32[]{:S(2)}, u32[]{:S(2)}) async-start(bf16[8,32,256]{2,1,0:T(8,128)(2,1)} %merge.1), calls=%async_computation.2 | async-start | bytes 262144 | tf_op jit(solution)/shard_map/all_to_all | solution.py:584

commit v10 on v9

--- a/solution.py
+++ b/solution.py
@@ -162,7 +162,7 @@
     return dot(spread[...], fold).astype(BF16)
 
 
-def order_body(owner, index, weight, high_out, hot_out, bounds_out, rows_out, weight_out, ranks):
+def order_body(owner, index, weight, _, high_out, hot_out, bounds_out, rows_out, weight_out, ranks):
     owner, index = ready(owner), ready(index)
     owners = bounds_out.shape[0]
     pieces = -(-max(2, 2 * NP_DEV // owners) // LANES)
@@ -287,7 +287,7 @@
 
 def finish_body(
     start_ref, next_ref, second_ref, third_ref, inner_note, outer_note, lower_ref, upper_ref,
-    weight, index_rows, high_ref, hot_ref, bounds_ref, send_ref,
+    weight, tails_ref, high_ref, hot_ref, bounds_ref, send_ref,
     notes, spread, ordered, stage, sent,
 ):
     position = lax.axis_index("surf")
@@ -315,38 +315,58 @@
         then[edge] = then[edge] - dot(beside_next, toward[edge]) - dot(second_one, away[edge])
         then[one] = then[one] - dot(second, toward[one])
         then[two] = then[two] - dot(second_one, toward[two])
-    rows = INC + IDX_ROWS
     for b in range(BLK):
         solved = then[b].astype(BF16).astype(F32)
-        shares = solved * block(weight, b)
-        every = jnp.concatenate([shares.astype(BF16), block(index_rows, b)], axis=0)
-        high = high_ref[b : b + 1, :].astype(F32).astype(BF16)
-        for h in range(BLK):
-            spread[h * rows : (h + 1) * rows, b * TILE : (b + 1) * TILE] = jnp.where(
-                high == h, every, jnp.zeros_like(every)
-            )
+        shares = (solved * block(weight, b)).astype(BF16)
+        by_high_digit(spread, shares, high_ref, b)
+    put_in_order(ordered, spread, hot_ref)
+    owners = send_ref.shape[0]
+    pieces = (send_ref.shape[1] - TAIL) // INC
+    for o in range(owners):
+        piece = owner_window(ordered, bounds_ref[o, 0], pieces)
+        parts = [piece[:, j * LANES : (j + 1) * LANES] for j in range(pieces)]
+        stage[o] = jnp.concatenate(parts + [tails_ref[o]], axis=0).astype(BF16)
+        pltpu.make_async_copy(stage.at[o], send_ref.at[o], sent.at[o]).start()
+    for o in range(owners):
+        pltpu.make_async_copy(stage.at[o], send_ref.at[o], sent.at[o]).wait()
+
+
+def by_high_digit(spread, values, high_ref, b):
+    rows = values.shape[0]
+    high = high_ref[b : b + 1, :].astype(F32).astype(BF16)
+    for h in range(BLK):
+        spread[h * rows : (h + 1) * rows, b * TILE : (b + 1) * TILE] = jnp.where(
+            high == h, values, jnp.zeros_like(values)
+        )
+
+
+def put_in_order(ordered, spread, hot_ref):
+    rows = ordered.shape[0]
     sorted_rows = dot(spread[...], hot_ref[...])
     for h in range(BLK):
         ordered[:, h * TILE : (h + 1) * TILE] = sorted_rows[h * rows : (h + 1) * rows]
-    owners = send_ref.shape[0]
-    pieces = (send_ref.shape[1] - TAIL) // INC
+    ordered[:, NP_DEV:] = jnp.zeros((rows, ordered.shape[1] - NP_DEV), F32)
+
+
+def owner_window(ordered, begin, pieces):
     wide = (pieces + 1) * LANES
-    ordered[:, NP_DEV:] = jnp.zeros((rows, ordered.shape[1] - NP_DEV), F32)
+    base = pl.multiple_of((begin // LANES) * LANES, LANES)
+    return pltpu.roll(ordered[:, pl.ds(base, wide)], wide - (begin - base), 1)
+
+
+def tails_body(index_rows, high_ref, hot_ref, bounds_ref, out_ref, spread, ordered):
+    for b in range(BLK):
+        by_high_digit(spread, block(index_rows, b), high_ref, b)
+    put_in_order(ordered, spread, hot_ref)
+    pieces = ordered.shape[1] // LANES - NP_DEV // LANES - 1
     row = iota((TAIL, LANES), 0)
     slot = iota((TAIL, LANES), 1) + (row // 2) * LANES
-    for o in range(owners):
-        begin = bounds_ref[o, 0]
-        base = pl.multiple_of((begin // LANES) * LANES, LANES)
-        piece = pltpu.roll(ordered[:, pl.ds(base, wide)], wide - (begin - base), 1)
-        parts = [piece[:INC, j * LANES : (j + 1) * LANES] for j in range(pieces)]
-        tail = piece[INC : INC + TAIL, :LANES]
+    for o in range(out_ref.shape[0]):
+        piece = owner_window(ordered, bounds_ref[o, 0], pieces)
+        tail = piece[:TAIL, :LANES]
         for j in range(1, pieces):
-            tail = jnp.where(row // 2 == j, piece[INC : INC + TAIL, j * LANES : (j + 1) * LANES], tail)
-        tail = jnp.where(slot >= bounds_ref[o, 1], -16.0, tail)
-        stage[o] = jnp.concatenate(parts + [tail], axis=0).astype(BF16)
-        pltpu.make_async_copy(stage.at[o], send_ref.at[o], sent.at[o]).start()
-    for o in range(owners):
-        pltpu.make_async_copy(stage.at[o], send_ref.at[o], sent.at[o]).wait()
+            tail = jnp.where(row // 2 == j, piece[:TAIL, j * LANES : (j + 1) * LANES], tail)
+        out_ref[o] = jnp.where(slot >= bounds_ref[o, 1], -16.0, tail)
 
 
 def gather_body(
@@ -445,7 +465,9 @@
     others = [(0, 0), (surf_count - 1, surf_count - 1)]
     for i in range(1, surf_count - 1, 2):
         others += [(i, i + 1), (i + 1, i)]
-    return lax.ppermute(inner, "surf", pairs), lax.ppermute(outer, "surf", others)
+    outer = lax.ppermute(outer, "surf", others)
+    inner = lax.ppermute(inner, "surf", pairs)
+    return inner, outer
 
 
 def exchange(array, surf_count):
@@ -513,7 +535,6 @@
         name="solve",
     )
     inner_note, outer_note = swap(inner_note, outer_note, surf_count)
-    rows = INC + IDX_ROWS
     high, hot, bounds, index_rows, weight = call(
         order_body,
         [
@@ -522,12 +543,24 @@
         ],
         (
             dual_owner.reshape(1, NP_DEV), dual_index.reshape(1, NP_DEV),
-            refine_weight.reshape(1, NP_DEV),
+            refine_weight.reshape(1, NP_DEV), start,
         ),
         scratch=[pltpu.VMEM((BLK, TILE), F32)],
         held=(0, 1, 2),
         flops=10**9,
         name="order",
+    )
+    (tails,) = call(
+        tails_body,
+        [((surf_count, TAIL, LANES), F32)],
+        (index_rows, high, hot, bounds),
+        scratch=[
+            pltpu.VMEM((BLK * IDX_ROWS, NP_DEV), BF16),
+            pltpu.VMEM((IDX_ROWS, NP_DEV + (pieces + 1) * LANES), F32),
+        ],
+        smem=(3,),
+        flops=10**9,
+        name="tails",
     )
     second, third = call(
         middle_body,
@@ -541,12 +574,12 @@
         [((surf_count, INC * pieces + TAIL, LANES), BF16)],
         (
             start, after, second, third, inner_note, outer_note, lower, upper,
-            weight, index_rows, high, hot, bounds,
+            weight, tails, high, hot, bounds,
         ),
         scratch=[
             pltpu.VMEM((2,) + note[0], BF16),
-            pltpu.VMEM((BLK * rows, NP_DEV), BF16),
-            pltpu.VMEM((rows, NP_DEV + (pieces + 1) * LANES), F32),
+            pltpu.VMEM((BLK * INC, NP_DEV), BF16),
+            pltpu.VMEM((INC, NP_DEV + (pieces + 1) * LANES), F32),
             pltpu.VMEM((surf_count, INC * pieces + TAIL, LANES), BF16),
             pltpu.SemaphoreType.DMA((surf_count,)),
         ],

time: 65.7 us -> 65.5 us (level)
  Pallas kernels: 27.9 us -> 29 us
  starting transfers between devices: 22.7 us -> 21.6 us
    all_to_all x1, starting transfers between devices: 8.63 us -> 7.49 us  [shards(): lax.all_to_all(send, 'surf', split_axis=0, concat_axis=0, tiled=True)]
    pallas_call x12 -> x13, Pallas kernels: 27.9 us -> 29 us  [call(): pl.pallas_call(wrapped, out_shape=outs, in_specs=[pl.BlockSpec(memory_spa...]
  transfers between devices with their start and end apart: 8 -> 8, of which waited for: 4 -> 4; matrix products, arithmetic and copies ran while one was open for 0% -> 0% of each run, Pallas kernels for 32% -> 34%
where the time goes in v10:
time: 65.5 us; the launch traced here: 65 us
  Pallas kernels  29 us (44%)
  starting transfers between devices  21.6 us (33%)
  waiting for transfers between devices  14.3 us (22%)
    pallas_call x13, Pallas kernels, call(): pl.pallas_call(wrapped, out_shape=outs, in_specs=[pl.BlockSpec(memory_spa...  29 us
    all_to_all x1, starting transfers between devices, exchange(): lax.all_to_all(array, 'surf', split_axis=0, concat_axis=0, tiled=True)  7.92 us
    all_to_all x1, starting transfers between devices, shards(): lax.all_to_all(send, 'surf', split_axis=0, concat_axis=0, tiled=True)  7.49 us
    all_to_all x1, waiting for transfers between devices, shards(): lax.all_to_all(merged, 'surf', split_axis=0, concat_axis=0, tiled=True, a...  5.89 us
    all_to_all x1, waiting for transfers between devices, shards(): lax.all_to_all(send, 'surf', split_axis=0, concat_axis=0, tiled=True)  3.81 us
    all_to_all x1, waiting for transfers between devices, exchange(): lax.all_to_all(array, 'surf', split_axis=0, concat_axis=0, tiled=True)  3.5 us
    all_to_all x1, starting transfers between devices, shards(): lax.all_to_all(merged, 'surf', split_axis=0, concat_axis=0, tiled=True, a...  3.37 us
    ppermute x2, starting transfers between devices, swap(): outer = lax.ppermute(outer, 'surf', others)  2.22 us
  transfers between devices with their start and end apart: 8, of which 4 were waited for; matrix products, arithmetic and copies ran while one was open for 0% of the time, Pallas kernels for 34%

profile of v10, /device:TPU:0, one launch (start us, length us, event | category | flops | bytes accessed | tf_op | source)
XLA Modules:
  0.0 65.0 jit_solution(18153346831716287732)
XLA Ops:
  0.0 0.5 collective-permute-start
  0.5 1.6 %collective-permute-start.1 = (bf16[32,2048]{1,0:T(8,128)(2,1)}, bf16[32,2048]{1,0:T(8,128)(2,1)S(1)}, u32[]{:S(2)}, u32[]{:S(2)}) collective-permute-start(bf16[32,2048]{1,0:T(8,128)(2,1)} %refs_2_.4), channel_id=1, source_target_pairs={{0,0},{15,15},{1,2},{2,1},{3,4},{4,3},{5,6},{6,5},{7,8},{8,7},{9,1... | collective-permute-start | bytes 393224 | tf_op jit(solution)/shard_map/ppermute | solution.py:468
  2.0 4.1 %far_up.1 = bf16[128,1024]{1,0:T(8,128)(2,1)} custom-call(bf16[32,2048]{1,0:T(8,128)(2,1)} %refs_2_.4, bf16[8,32,256]{2,1,0:T(8,128)(2,1)} %refs_1_.3, bf16[128,1024]{1,0:T(8,128)(2,1)} %refs_2_.3, s32[1,128]{1,0:T(1,128)} %bitcast.12, s32[1,128]{1,0:T(1,128)} %bitcast.14, s32[1,128]{1,0:T(1,128)} %bitcast.16), custom_call_target="tpu_custom_call" | custom-call | flops 99999997952 | bytes 525824 | tf_op jit(solution)/shard_map/far_up/pallas_call | solution.py:68
  6.1 7.9 %all-to-all-start = ((bf16[16,8,1024]{2,1,0:T(8,128)(2,1)}), bf16[16,8,1024]{2,1,0:T(8,128)(2,1)S(1)}, u32[]{:S(2)}, u32[]{:S(2)}) async-start(bf16[16,8,1024]{2,1,0:T(8,128)(2,1)} %bitcast.3), calls=%async_computation | async-start | bytes 524288 | tf_op jit(solution)/shard_map/all_to_all | solution.py:476
  14.0 0.0 collective-permute-done.refs_3_
  14.0 0.0 collective-permute-done.1.refs_4_
  14.0 6.5 %prepare.1 = (f32[32,2048]{1,0:T(8,128)S(1)}, bf16[8,256,256]{2,1,0:T(8,128)(2,1)S(1)}, bf16[8,256,256]{2,1,0:T(8,128)(2,1)S(1)}, bf16[8,32,256]{2,1,0:T(8,128)(2,1)S(1)}) custom-call(s32[48]{0:T(128)} %refs_0_.4, s32[48]{0:T(128)} %refs_1_.4, bf16[32,2048]{1,0:T(8,128)(2,1)} %refs_2_.4, bf16[32,2048]{1,0:T(8,128)(2,1)S(1)} %collective-permute-done.refs_3_, ...), custom_call_target="tpu_custom_call" | custom-call | flops 99999997952 | bytes 9961856 | tf_op jit(solution)/shard_map/prepare/pallas_call | solution.py:68
  20.6 3.5 %all-to-all-done = bf16[16,8,1024]{2,1,0:T(8,128)(2,1)S(1)} async-done(((bf16[16,8,1024]{2,1,0:T(8,128)(2,1)}), bf16[16,8,1024]{2,1,0:T(8,128)(2,1)S(1)}, u32[]{:S(2)}, u32[]{:S(2)}) %all-to-all-start) | async-done | bytes 262176 | tf_op jit(solution)/shard_map/all_to_all | solution.py:476
  24.1 0.9 %solve.1 = (f32[32,2048]{1,0:T(8,128)S(1)}, f32[32,2048]{1,0:T(8,128)S(1)}, bf16[352,256]{1,0:T(8,128)(2,1)S(1)}, bf16[352,256]{1,0:T(8,128)(2,1)S(1)}) custom-call(bf16[128,1024]{1,0:T(8,128)(2,1)S(1)} %bitcast.8, f32[32,2048]{1,0:T(8,128)S(1)} %get-tuple-element.27.refs_1_, bf16[8,32,256]{2,1,0:T(8,128)(2,1)S(1)} %get-tuple-element.28.refs_2_, ...), custom_call_target="tpu_custom_call" | custom-call | bytes 2752512 | tf_op jit(solution)/shard_map/solve/pallas_call | solution.py:68
  24.9 0.1 collective-permute-start.2
  25.0 0.7 %collective-permute-start.3 = (bf16[352,256]{1,0:T(8,128)(2,1)S(1)}, bf16[352,256]{1,0:T(8,128)(2,1)S(1)}, u32[]{:S(2)}, u32[]{:S(2)}) collective-permute-start(bf16[352,256]{1,0:T(8,128)(2,1)S(1)} %get-tuple-element.36), channel_id=1, source_target_pairs={{0,0},{15,15},{1,2},{2,1},{3,4},{4,3},{5,6},{6,5},{7,8},{8,7},{9,1... | collective-permute-start | bytes 540680 | tf_op jit(solution)/shard_map/ppermute | solution.py:468
  25.7 0.6 middle.1
  26.3 1.4 %order.1 = (s32[8,256]{1,0:T(8,128)S(1)}, bf16[2048,256]{1,0:T(8,128)(2,1)S(1)}, s32[16,2]{1,0:T(8,128)S(1)}, bf16[16,2048]{1,0:T(8,128)(2,1)S(1)}, f32[1,2048]{1,0:T(1,128)S(1)}) custom-call(s32[1,2048]{1,0:T(1,128)} %bitcast.9, s32[1,2048]{1,0:T(1,128)} %bitcast.10, f32[1,2048]{1,0:T(1,128)} %bitcast.11, f32[32,2048]{1,0:T(8,128)S(1)} %get-tuple-element.31.refs_0_.refs_3_), custom_call_target="tpu_custom_call" | custom-call | flops 1000000000 | bytes 286720 | tf_op jit(solution)/shard_map/order/pallas_call | solution.py:68
  27.6 1.1 %tails.1.refs_9_ = f32[16,8,128]{2,1,0:T(8,128)S(1)} custom-call(bf16[16,2048]{1,0:T(8,128)(2,1)S(1)} %get-tuple-element.38.refs_0_, s32[8,256]{1,0:T(8,128)S(1)} %get-tuple-element.39.refs_1_.refs_10_, bf16[2048,256]{1,0:T(8,128)(2,1)S(1)} %get-tuple-element.40.refs_2_.refs_11_, s32[16,2]{1,0:T(8,128)S(1)} %get-tuple-element.41.refs_3_.refs_12_), custom_call_target="tpu_custom_call" | custom-call | flops 1000000000 | bytes 1122432 | tf_op jit(solution)/shard_map/tails/pallas_call | solution.py:68
  28.8 0.0 collective-permute-done.2.refs_4_
  28.8 0.0 collective-permute-done.3.refs_5_
  28.8 2.8 %finish.1 = bf16[16,72,128]{2,1,0:T(8,128)(2,1)} custom-call(f32[32,2048]{1,0:T(8,128)S(1)} %get-tuple-element.31.refs_0_.refs_3_, f32[32,2048]{1,0:T(8,128)S(1)} %get-tuple-element.32.refs_1_, f32[32,2048]{1,0:T(8,128)S(1)} %get-tuple-element.33.refs_2_, f32[32,2048]{1,0:T(8,128)S(1)} %get-tuple-element.34.refs_3_, ...), custom_call_target="tpu_custom_call" | custom-call | bytes 4636800 | tf_op jit(solution)/shard_map/finish/pallas_call | solution.py:68
  31.6 7.5 %all-to-all-start.1 = ((bf16[16,72,128]{2,1,0:T(8,128)(2,1)}), bf16[16,72,128]{2,1,0:T(8,128)(2,1)S(1)}, u32[]{:S(2)}, u32[]{:S(2)}) async-start(bf16[16,72,128]{2,1,0:T(8,128)(2,1)} %finish.1), calls=%async_computation.1 | async-start | bytes 589824 | tf_op jit(solution)/shard_map/all_to_all | solution.py:590
  39.1 6.8 %couple.1 = (bf16[256,4096]{1,0:T(8,128)(2,1)S(1)}, bf16[8,32,256]{2,1,0:T(8,128)(2,1)S(1)}) custom-call(bf16[128,1024]{1,0:T(8,128)(2,1)} %refs_0_.5, s32[1,128]{1,0:T(1,128)} %bitcast.13, s32[1,128]{1,0:T(1,128)} %bitcast.15, s32[1,128]{1,0:T(1,128)} %bitcast.17, bf16[8,32,256]{2,1,0:T(8,128)(2,1)} %refs_4_.1), custom_call_target="tpu_custom_call" | custom-call | flops 10000000000 | bytes 394752 | tf_op jit(solution)/shard_map/couple/pallas_call | solution.py:68
  45.9 3.8 %all-to-all-done.1.refs_0_ = bf16[16,72,128]{2,1,0:T(8,128)(2,1)S(1)} async-done(((bf16[16,72,128]{2,1,0:T(8,128)(2,1)}), bf16[16,72,128]{2,1,0:T(8,128)(2,1)S(1)}, u32[]{:S(2)}, u32[]{:S(2)}) %all-to-all-start.1) | async-done | bytes 294944 | tf_op jit(solution)/shard_map/all_to_all | solution.py:590
  49.7 1.5 %gather.1 = (bf16[8,32,256]{2,1,0:T(8,128)(2,1)S(1)}, bf16[32,256]{1,0:T(8,128)(2,1)S(1)}, bf16[8,32,256]{2,1,0:T(8,128)(2,1)S(1)}) custom-call(bf16[16,72,128]{2,1,0:T(8,128)(2,1)S(1)} %all-to-all-done.1.refs_0_, bf16[8,32,256]{2,1,0:T(8,128)(2,1)S(1)} %get-tuple-element.42.refs_1_, bf16[256,4096]{1,0:T(8,128)(2,1)S(1)} %get-tuple-element.43.refs_2_.refs_1_), custom_call_target="tpu_custom_call" | custom-call | bytes 2523136 | tf_op jit(solution)/shard_map/gather/pallas_call | solution.py:68
  51.1 0.1 collective-permute-start.4
  51.2 0.3 own.1.refs_0_
  51.5 1.0 %collective-permute-done.4.refs_1_ = bf16[8,32,256]{2,1,0:T(8,128)(2,1)S(1)} collective-permute-done((bf16[8,32,256]{2,1,0:T(8,128)(2,1)S(1)}, bf16[8,32,256]{2,1,0:T(8,128)(2,1)S(1)}, u32[]{:S(2)}, u32[]{:S(2)}) %collective-permute-start.4) | collective-permute-done | bytes 131104 | tf_op jit(solution)/shard_map/ppermute | solution.py:614
  52.6 0.7 %merge.1 = bf16[8,32,256]{2,1,0:T(8,128)(2,1)} custom-call(f32[8,32,256]{2,1,0:T(8,128)S(1)} %own.1.refs_0_, bf16[8,32,256]{2,1,0:T(8,128)(2,1)S(1)} %collective-permute-done.4.refs_1_), custom_call_target="tpu_custom_call" | custom-call | bytes 393216 | tf_op jit(solution)/shard_map/merge/pallas_call | solution.py:68
  53.2 3.4 %all-to-all-start.2 = ((bf16[8,32,256]{2,1,0:T(8,128)(2,1)}), bf16[8,32,256]{2,1,0:T(8,128)(2,1)S(1)}, u32[]{:S(2)}, u32[]{:S(2)}) async-start(bf16[8,32,256]{2,1,0:T(8,128)(2,1)} %merge.1), calls=%async_computation.2 | async-start | bytes 262144 | tf_op jit(solution)/shard_map/all_to_all | solution.py:617
  56.6 1.6 %self_part.1 = (f32[32,2048]{1,0:T(8,128)S(1)}, bf16[8,32,256]{2,1,0:T(8,128)(2,1)S(1)}) custom-call(bf16[8,32,256]{2,1,0:T(8,128)(2,1)S(1)} %get-tuple-element.46.refs_0_, bf16[8,256,256]{2,1,0:T(8,128)(2,1)} %refs_1_.5, bf16[8,32,256]{2,1,0:T(8,128)(2,1)} %refs_2_.5), custom_call_target="tpu_custom_call" | custom-call | bytes 1310720 | tf_op jit(solution)/shard_map/self_part/pallas_call | solution.py:68
  58.2 5.9 %all-to-all-done.2.refs_0_ = bf16[8,32,256]{2,1,0:T(8,128)(2,1)S(1)} async-done(((bf16[8,32,256]{2,1,0:T(8,128)(2,1)}), bf16[8,32,256]{2,1,0:T(8,128)(2,1)S(1)}, u32[]{:S(2)}, u32[]{:S(2)}) %all-to-all-start.2) | async-done | bytes 131104 | tf_op jit(solution)/shard_map/all_to_all | solution.py:617
  64.1 0.8 %answer.1 = bf16[32,2048]{1,0:T(8,128)(2,1)} custom-call(bf16[8,32,256]{2,1,0:T(8,128)(2,1)S(1)} %all-to-all-done.2.refs_0_, f32[32,2048]{1,0:T(8,128)S(1)} %get-tuple-element.47.refs_1_, bf16[8,32,256]{2,1,0:T(8,128)(2,1)S(1)} %get-tuple-element.48.refs_2_), custom_call_target="tpu_custom_call" | custom-call | bytes 524288 | tf_op jit(solution)/shard_map/answer/pallas_call | solution.py:68
Async XLA Ops:
  0.0 14.0 %collective-permute-start = (bf16[32,2048]{1,0:T(8,128)(2,1)}, bf16[32,2048]{1,0:T(8,128)(2,1)S(1)}, u32[]{:S(2)}, u32[]{:S(2)}) collective-permute-start(bf16[32,2048]{1,0:T(8,128)(2,1)} %refs_2_.4), channel_id=1, source_target_pairs={{0,1},{1,0},{2,3},{3,2},{4,5},{5,4},{6,7},{7,6},{8,9},{9,8},{10,11... | collective-permute-start | bytes 393224 | tf_op jit(solution)/shard_map/ppermute | solution.py:469
  0.5 13.6 %collective-permute-start.1 = (bf16[32,2048]{1,0:T(8,128)(2,1)}, bf16[32,2048]{1,0:T(8,128)(2,1)S(1)}, u32[]{:S(2)}, u32[]{:S(2)}) collective-permute-start(bf16[32,2048]{1,0:T(8,128)(2,1)} %refs_2_.4), channel_id=1, source_target_pairs={{0,0},{15,15},{1,2},{2,1},{3,4},{4,3},{5,6},{6,5},{7,8},{8,7},{9,1... | collective-permute-start | bytes 393224 | tf_op jit(solution)/shard_map/ppermute | solution.py:468
  6.1 18.0 %all-to-all-start = ((bf16[16,8,1024]{2,1,0:T(8,128)(2,1)}), bf16[16,8,1024]{2,1,0:T(8,128)(2,1)S(1)}, u32[]{:S(2)}, u32[]{:S(2)}) async-start(bf16[16,8,1024]{2,1,0:T(8,128)(2,1)} %bitcast.3), calls=%async_computation | async-start | bytes 524288 | tf_op jit(solution)/shard_map/all_to_all | solution.py:476
  24.9 3.8 %collective-permute-start.2 = (bf16[352,256]{1,0:T(8,128)(2,1)S(1)}, bf16[352,256]{1,0:T(8,128)(2,1)S(1)}, u32[]{:S(2)}, u32[]{:S(2)}) collective-permute-start(bf16[352,256]{1,0:T(8,128)(2,1)S(1)} %get-tuple-element.35), channel_id=1, source_target_pairs={{0,1},{1,0},{2,3},{3,2},{4,5},{5,4},{6,7},{7,6},{8,9},{9,8},{10,11... | collective-permute-start | bytes 540680 | tf_op jit(solution)/shard_map/ppermute | solution.py:469
  25.0 3.8 %collective-permute-start.3 = (bf16[352,256]{1,0:T(8,128)(2,1)S(1)}, bf16[352,256]{1,0:T(8,128)(2,1)S(1)}, u32[]{:S(2)}, u32[]{:S(2)}) collective-permute-start(bf16[352,256]{1,0:T(8,128)(2,1)S(1)} %get-tuple-element.36), channel_id=1, source_target_pairs={{0,0},{15,15},{1,2},{2,1},{3,4},{4,3},{5,6},{6,5},{7,8},{8,7},{9,1... | collective-permute-start | bytes 540680 | tf_op jit(solution)/shard_map/ppermute | solution.py:468
  31.6 18.1 %all-to-all-start.1 = ((bf16[16,72,128]{2,1,0:T(8,128)(2,1)}), bf16[16,72,128]{2,1,0:T(8,128)(2,1)S(1)}, u32[]{:S(2)}, u32[]{:S(2)}) async-start(bf16[16,72,128]{2,1,0:T(8,128)(2,1)} %finish.1), calls=%async_computation.1 | async-start | bytes 589824 | tf_op jit(solution)/shard_map/all_to_all | solution.py:590
  51.1 1.4 %collective-permute-start.4 = (bf16[8,32,256]{2,1,0:T(8,128)(2,1)S(1)}, bf16[8,32,256]{2,1,0:T(8,128)(2,1)S(1)}, u32[]{:S(2)}, u32[]{:S(2)}) collective-permute-start(bf16[8,32,256]{2,1,0:T(8,128)(2,1)S(1)} %get-tuple-element.45), channel_id=1, source_target_pairs={{0,1},{1,0},{2,3},{3,2},{4,5},{5,4},{6,7},{7,6},{8,9},{9,8},{10,11... | collective-permute-start | bytes 393224 | tf_op jit(solution)/shard_map/ppermute | solution.py:614
  53.2 10.9 %all-to-all-start.2 = ((bf16[8,32,256]{2,1,0:T(8,128)(2,1)}), bf16[8,32,256]{2,1,0:T(8,128)(2,1)S(1)}, u32[]{:S(2)}, u32[]{:S(2)}) async-start(bf16[8,32,256]{2,1,0:T(8,128)(2,1)} %merge.1), calls=%async_computation.2 | async-start | bytes 262144 | tf_op jit(solution)/shard_map/all_to_all | solution.py:617

commit v11 on v10

--- a/solution.py
+++ b/solution.py
@@ -106,11 +106,12 @@
 
 def far_up_body(
     value, compress, coupling, source, owner, place,
-    out_ref, blocks, turned, spread, pick, terms,
+    out_ref, copy_out, blocks, turned, spread, pick, terms, stage, sent,
 ):
     coupling = ready(coupling)
     turned[...] = coupling[...].astype(F32).T
     value, compress = ready(value), ready(compress)
+    copy_out[...] = value[...]
     for s in range(BLK):
         blocks[s * INC : (s + 1) * INC, :] = block(value, s)
     coef = coefficients(blocks[...], compress)
@@ -134,11 +135,22 @@
         terms[pl.ds(rows, 2 * RANK), :] = jnp.concatenate([first, second], axis=0).astype(BF16)
         return carry
 
-    lax.fori_loop(0, INC // 2, step, 0)
     targets = out_ref.shape[0]
     owner, place = ready(owner), ready(place)
     select = as_hot(iota((targets, tiles), 0) == owner[...] * BLK + place[...])
-    out_ref[...] = dot_nt(select, terms[...]).astype(BF16)
+    chunks = 4
+    width = INC * RANK // chunks
+    copies = []
+    for c in range(chunks):
+        lax.fori_loop(c * (INC // 2 // chunks), (c + 1) * (INC // 2 // chunks), step, 0)
+        part = slice(c * width, (c + 1) * width)
+        stage[:, part] = dot_nt(select, terms[part, :]).astype(BF16)
+        columns = pl.ds(c * width, width)
+        copy = pltpu.make_async_copy(stage.at[:, columns], out_ref.at[:, columns], sent.at[c])
+        copy.start()
+        copies.append(copy)
+    for copy in copies:
+        copy.wait()
 
 
 def far_scratch(tiles):
@@ -264,7 +276,10 @@
     outer_out[...] = notes[1 - odd]
 
 
-def middle_body(start_ref, next_ref, lower_ref, upper_ref, second_out, third_out):
+def middle_body(
+    start_ref, next_ref, lower_ref, upper_ref, note_ref, second_out, third_out, note_out
+):
+    note_out[...] = note_ref[...]
     last = BLK - 1
     now = [block(next_ref, b).astype(BF16) for b in range(BLK)]
     second = []
@@ -460,14 +475,15 @@
         ).astype(BF16)
 
 
-def swap(inner, outer, surf_count):
-    pairs = [(i, i ^ 1) for i in range(surf_count)]
-    others = [(0, 0), (surf_count - 1, surf_count - 1)]
+def swap_inner(array, surf_count):
+    return lax.ppermute(array, "surf", [(i, i ^ 1) for i in range(surf_count)])
+
+
+def swap_outer(array, surf_count):
+    pairs = [(0, 0), (surf_count - 1, surf_count - 1)]
     for i in range(1, surf_count - 1, 2):
-        others += [(i, i + 1), (i + 1, i)]
-    outer = lax.ppermute(outer, "surf", others)
-    inner = lax.ppermute(inner, "surf", pairs)
-    return inner, outer
+        pairs += [(i, i + 1), (i + 1, i)]
+    return lax.ppermute(array, "surf", pairs)
 
 
 def exchange(array, surf_count):
@@ -492,17 +508,20 @@
     cube = ((BLK, TILE, TILE), BF16)
 
     note = ((3 * INC + TILE, TILE), BF16)
-    inner, outer = swap(currents, currents, surf_count)
-    (partial,) = call(
+    outer = swap_outer(currents, surf_count)
+    partial, inner = call(
         far_up_body,
-        [((targets, INC * RANK), BF16)],
+        [((targets, INC * RANK), BF16), ((INC, NP_DEV), BF16)],
         (currents, primal_compress, primal_coupling) + lists,
-        scratch=far_scratch(tiles),
+        scratch=far_scratch(tiles)
+        + [pltpu.VMEM((targets, INC * RANK), BF16), pltpu.SemaphoreType.DMA((4,))],
+        streamed=(0,),
         held=(2, 0, 1, 3, 4, 5),
         flops=10**11,
         name="far_up",
     )
     arrived = exchange(partial, surf_count)
+    inner = swap_inner(inner, surf_count)
     near_part, lower, upper, expanded = call(
         prepare_body,
         [((INC, NP_DEV), F32), cube, cube, ((BLK, RANK, TILE), BF16)],
@@ -534,7 +553,7 @@
         ],
         name="solve",
     )
-    inner_note, outer_note = swap(inner_note, outer_note, surf_count)
+    outer_note = swap_outer(outer_note, surf_count)
     high, hot, bounds, index_rows, weight = call(
         order_body,
         [
@@ -562,13 +581,14 @@
         flops=10**9,
         name="tails",
     )
-    second, third = call(
+    second, third, inner_note = call(
         middle_body,
-        [((INC, NP_DEV), F32)] * 2,
-        (start, after, lower, upper),
+        [((INC, NP_DEV), F32)] * 2 + [note],
+        (start, after, lower, upper, inner_note),
         flops=10**9,
         name="middle",
     )
+    inner_note = swap_inner(inner_note, surf_count)
     (send,) = call(
         finish_body,
         [((surf_count, INC * pieces + TAIL, LANES), BF16)],

time: 65.5 us -> 65.8 us (level)
    ppermute x4, starting transfers between devices: 2.75 us -> 6.87 us  [the longest x2 4.64 us: swap_inner(): return lax.ppermute(array, 'surf', [(i, i ^ 1) for i in range(surf_count)])]
    all_to_all x1, starting transfers between devices: 7.92 us -> 4.99 us  [exchange(): lax.all_to_all(array, 'surf', split_axis=0, concat_axis=0, tiled=True)]
    all_to_all x1, starting transfers between devices: 7.49 us -> 6.16 us  [shards(): lax.all_to_all(send, 'surf', split_axis=0, concat_axis=0, tiled=True)]
  transfers between devices with their start and end apart: 8 -> 8, of which waited for: 4 -> 4; matrix products, arithmetic and copies ran while one was open for 0% -> 0% of each run, Pallas kernels for 34% -> 35%
where the time goes in v11:
time: 65.8 us; the launch traced here: 65.2 us
  Pallas kernels  29.3 us (45%)
  starting transfers between devices  21.5 us (33%)
  waiting for transfers between devices  14.3 us (22%)
    pallas_call x13, Pallas kernels, call(): pl.pallas_call(wrapped, out_shape=outs, in_specs=[pl.BlockSpec(memory_spa...  29.3 us
    all_to_all x1, starting transfers between devices, shards(): lax.all_to_all(send, 'surf', split_axis=0, concat_axis=0, tiled=True)  6.16 us
    all_to_all x1, waiting for transfers between devices, shards(): lax.all_to_all(merged, 'surf', split_axis=0, concat_axis=0, tiled=True, a...  5.89 us
    all_to_all x1, starting transfers between devices, exchange(): lax.all_to_all(array, 'surf', split_axis=0, concat_axis=0, tiled=True)  4.99 us
    ppermute x2, starting transfers between devices, swap_inner(): return lax.ppermute(array, 'surf', [(i, i ^ 1) for i in range(surf_count)])  4.64 us
    all_to_all x1, waiting for transfers between devices, shards(): lax.all_to_all(send, 'surf', split_axis=0, concat_axis=0, tiled=True)  3.86 us
    all_to_all x1, waiting for transfers between devices, exchange(): lax.all_to_all(array, 'surf', split_axis=0, concat_axis=0, tiled=True)  3.51 us
    all_to_all x1, starting transfers between devices, shards(): lax.all_to_all(merged, 'surf', split_axis=0, concat_axis=0, tiled=True, a...  3.37 us
  transfers between devices with their start and end apart: 8, of which 4 were waited for; matrix products, arithmetic and copies ran while one was open for 0% of the time, Pallas kernels for 35%

profile of v11, /device:TPU:0, one launch (start us, length us, event | category | flops | bytes accessed | tf_op | source)
XLA Modules:
  0.0 65.2 jit_solution(17812676072509655346)
XLA Ops:
  0.0 1.6 %collective-permute-start.1 = (bf16[32,2048]{1,0:T(8,128)(2,1)}, bf16[32,2048]{1,0:T(8,128)(2,1)S(1)}, u32[]{:S(2)}, u32[]{:S(2)}) collective-permute-start(bf16[32,2048]{1,0:T(8,128)(2,1)} %refs_2_.4), channel_id=1, source_target_pairs={{0,0},{15,15},{1,2},{2,1},{3,4},{4,3},{5,6},{6,5},{7,8},{8,7},{9,1... | collective-permute-start | bytes 393224 | tf_op jit(solution)/shard_map/ppermute | solution.py:486
  1.6 4.5 %far_up.1 = (bf16[128,1024]{1,0:T(8,128)(2,1)}, bf16[32,2048]{1,0:T(8,128)(2,1)S(1)}) custom-call(bf16[32,2048]{1,0:T(8,128)(2,1)} %refs_2_.4, bf16[8,32,256]{2,1,0:T(8,128)(2,1)} %refs_1_.3, bf16[128,1024]{1,0:T(8,128)(2,1)} %refs_2_.3, s32[1,128]{1,0:T(1,128)} %bitcast.12, s32[1,128]{1,0:T(1,128)} %bitcast.14, s32[1,128]{1,0:T(1,128)} %bitcast.16), custom_call_target="tpu_custom_call" | custom-call | flops 99999997952 | bytes 525824 | tf_op jit(solution)/shard_map/far_up/pallas_call | solution.py:68
  6.0 3.5 %collective-permute-start = (bf16[32,2048]{1,0:T(8,128)(2,1)S(1)}, bf16[32,2048]{1,0:T(8,128)(2,1)S(1)}, u32[]{:S(2)}, u32[]{:S(2)}) collective-permute-start(bf16[32,2048]{1,0:T(8,128)(2,1)S(1)} %get-tuple-element.31), channel_id=1, source_target_pairs={{0,1},{1,0},{2,3},{3,2},{4,5},{5,4},{6,7},{7,6},{8,9},{9,8},{10,11... | collective-permute-start | bytes 393224 | tf_op jit(solution)/shard_map/ppermute | solution.py:479
  9.6 5.0 %all-to-all-start = ((bf16[16,8,1024]{2,1,0:T(8,128)(2,1)}), bf16[16,8,1024]{2,1,0:T(8,128)(2,1)S(1)}, u32[]{:S(2)}, u32[]{:S(2)}) async-start(bf16[16,8,1024]{2,1,0:T(8,128)(2,1)} %bitcast.3), calls=%async_computation | async-start | bytes 524288 | tf_op jit(solution)/shard_map/all_to_all | solution.py:492
  14.5 0.0 collective-permute-done.1.refs_4_
  14.6 0.0 collective-permute-done.refs_3_
  14.6 6.5 %prepare.1 = (f32[32,2048]{1,0:T(8,128)S(1)}, bf16[8,256,256]{2,1,0:T(8,128)(2,1)S(1)}, bf16[8,256,256]{2,1,0:T(8,128)(2,1)S(1)}, bf16[8,32,256]{2,1,0:T(8,128)(2,1)S(1)}) custom-call(s32[48]{0:T(128)} %refs_0_.4, s32[48]{0:T(128)} %refs_1_.4, bf16[32,2048]{1,0:T(8,128)(2,1)} %refs_2_.4, bf16[32,2048]{1,0:T(8,128)(2,1)S(1)} %collective-permute-done.refs_3_, ...), custom_call_target="tpu_custom_call" | custom-call | flops 99999997952 | bytes 9961856 | tf_op jit(solution)/shard_map/prepare/pallas_call | solution.py:68
  21.1 3.5 %all-to-all-done = bf16[16,8,1024]{2,1,0:T(8,128)(2,1)S(1)} async-done(((bf16[16,8,1024]{2,1,0:T(8,128)(2,1)}), bf16[16,8,1024]{2,1,0:T(8,128)(2,1)S(1)}, u32[]{:S(2)}, u32[]{:S(2)}) %all-to-all-start) | async-done | bytes 262176 | tf_op jit(solution)/shard_map/all_to_all | solution.py:492
  24.6 0.9 %solve.1 = (f32[32,2048]{1,0:T(8,128)S(1)}, f32[32,2048]{1,0:T(8,128)S(1)}, bf16[352,256]{1,0:T(8,128)(2,1)S(1)}, bf16[352,256]{1,0:T(8,128)(2,1)S(1)}) custom-call(bf16[128,1024]{1,0:T(8,128)(2,1)S(1)} %bitcast.8, f32[32,2048]{1,0:T(8,128)S(1)} %get-tuple-element.32.refs_1_, bf16[8,32,256]{2,1,0:T(8,128)(2,1)S(1)} %get-tuple-element.33.refs_2_, ...), custom_call_target="tpu_custom_call" | custom-call | bytes 2752512 | tf_op jit(solution)/shard_map/solve/pallas_call | solution.py:68
  25.5 0.7 %collective-permute-start.3 = (bf16[352,256]{1,0:T(8,128)(2,1)S(1)}, bf16[352,256]{1,0:T(8,128)(2,1)S(1)}, u32[]{:S(2)}, u32[]{:S(2)}) collective-permute-start(bf16[352,256]{1,0:T(8,128)(2,1)S(1)} %get-tuple-element.42), channel_id=1, source_target_pairs={{0,0},{15,15},{1,2},{2,1},{3,4},{4,3},{5,6},{6,5},{7,8},{8,7},{9,1... | collective-permute-start | bytes 540680 | tf_op jit(solution)/shard_map/ppermute | solution.py:486
  26.1 0.6 middle.1
  26.7 1.1 %collective-permute-start.2 = (bf16[352,256]{1,0:T(8,128)(2,1)S(1)}, bf16[352,256]{1,0:T(8,128)(2,1)S(1)}, u32[]{:S(2)}, u32[]{:S(2)}) collective-permute-start(bf16[352,256]{1,0:T(8,128)(2,1)S(1)} %get-tuple-element.41), channel_id=1, source_target_pairs={{0,1},{1,0},{2,3},{3,2},{4,5},{5,4},{6,7},{7,6},{8,9},{9,8},{10,11... | collective-permute-start | bytes 540680 | tf_op jit(solution)/shard_map/ppermute | solution.py:479
  27.9 1.4 %order.1 = (s32[8,256]{1,0:T(8,128)S(1)}, bf16[2048,256]{1,0:T(8,128)(2,1)S(1)}, s32[16,2]{1,0:T(8,128)S(1)}, bf16[16,2048]{1,0:T(8,128)(2,1)S(1)}, f32[1,2048]{1,0:T(1,128)S(1)}) custom-call(s32[1,2048]{1,0:T(1,128)} %bitcast.9, s32[1,2048]{1,0:T(1,128)} %bitcast.10, f32[1,2048]{1,0:T(1,128)} %bitcast.11, f32[32,2048]{1,0:T(8,128)S(1)} %get-tuple-element.36.refs_0_.refs_3_), custom_call_target="tpu_custom_call" | custom-call | flops 1000000000 | bytes 286720 | tf_op jit(solution)/shard_map/order/pallas_call | solution.py:68
  29.2 1.1 %tails.1.refs_9_ = f32[16,8,128]{2,1,0:T(8,128)S(1)} custom-call(bf16[16,2048]{1,0:T(8,128)(2,1)S(1)} %get-tuple-element.44.refs_0_, s32[8,256]{1,0:T(8,128)S(1)} %get-tuple-element.45.refs_1_.refs_10_, bf16[2048,256]{1,0:T(8,128)(2,1)S(1)} %get-tuple-element.46.refs_2_.refs_11_, s32[16,2]{1,0:T(8,128)S(1)} %get-tuple-element.47.refs_3_.refs_12_), custom_call_target="tpu_custom_call" | custom-call | flops 1000000000 | bytes 1122432 | tf_op jit(solution)/shard_map/tails/pallas_call | solution.py:68
  30.4 0.0 collective-permute-done.3.refs_5_
  30.4 0.0 collective-permute-done.2.refs_4_
  30.4 2.8 %finish.1 = bf16[16,72,128]{2,1,0:T(8,128)(2,1)} custom-call(f32[32,2048]{1,0:T(8,128)S(1)} %get-tuple-element.36.refs_0_.refs_3_, f32[32,2048]{1,0:T(8,128)S(1)} %get-tuple-element.37.refs_1_, f32[32,2048]{1,0:T(8,128)S(1)} %get-tuple-element.39.refs_2_, f32[32,2048]{1,0:T(8,128)S(1)} %get-tuple-element.40.refs_3_, ...), custom_call_target="tpu_custom_call" | custom-call | bytes 4636800 | tf_op jit(solution)/shard_map/finish/pallas_call | solution.py:68
  33.2 6.2 %all-to-all-start.1 = ((bf16[16,72,128]{2,1,0:T(8,128)(2,1)}), bf16[16,72,128]{2,1,0:T(8,128)(2,1)S(1)}, u32[]{:S(2)}, u32[]{:S(2)}) async-start(bf16[16,72,128]{2,1,0:T(8,128)(2,1)} %finish.1), calls=%async_computation.1 | async-start | bytes 589824 | tf_op jit(solution)/shard_map/all_to_all | solution.py:610
  39.4 6.7 %couple.1 = (bf16[256,4096]{1,0:T(8,128)(2,1)S(1)}, bf16[8,32,256]{2,1,0:T(8,128)(2,1)S(1)}) custom-call(bf16[128,1024]{1,0:T(8,128)(2,1)} %refs_0_.5, s32[1,128]{1,0:T(1,128)} %bitcast.13, s32[1,128]{1,0:T(1,128)} %bitcast.15, s32[1,128]{1,0:T(1,128)} %bitcast.17, bf16[8,32,256]{2,1,0:T(8,128)(2,1)} %refs_4_.1), custom_call_target="tpu_custom_call" | custom-call | flops 10000000000 | bytes 394752 | tf_op jit(solution)/shard_map/couple/pallas_call | solution.py:68
  46.1 3.9 %all-to-all-done.1.refs_0_ = bf16[16,72,128]{2,1,0:T(8,128)(2,1)S(1)} async-done(((bf16[16,72,128]{2,1,0:T(8,128)(2,1)}), bf16[16,72,128]{2,1,0:T(8,128)(2,1)S(1)}, u32[]{:S(2)}, u32[]{:S(2)}) %all-to-all-start.1) | async-done | bytes 294944 | tf_op jit(solution)/shard_map/all_to_all | solution.py:610
  49.9 1.5 %gather.1 = (bf16[8,32,256]{2,1,0:T(8,128)(2,1)S(1)}, bf16[32,256]{1,0:T(8,128)(2,1)S(1)}, bf16[8,32,256]{2,1,0:T(8,128)(2,1)S(1)}) custom-call(bf16[16,72,128]{2,1,0:T(8,128)(2,1)S(1)} %all-to-all-done.1.refs_0_, bf16[8,32,256]{2,1,0:T(8,128)(2,1)S(1)} %get-tuple-element.48.refs_1_, bf16[256,4096]{1,0:T(8,128)(2,1)S(1)} %get-tuple-element.49.refs_2_.refs_1_), custom_call_target="tpu_custom_call" | custom-call | bytes 2523136 | tf_op jit(solution)/shard_map/gather/pallas_call | solution.py:68
  51.4 0.1 collective-permute-start.4
  51.5 0.3 own.1.refs_0_
  51.8 1.0 %collective-permute-done.4.refs_1_ = bf16[8,32,256]{2,1,0:T(8,128)(2,1)S(1)} collective-permute-done((bf16[8,32,256]{2,1,0:T(8,128)(2,1)S(1)}, bf16[8,32,256]{2,1,0:T(8,128)(2,1)S(1)}, u32[]{:S(2)}, u32[]{:S(2)}) %collective-permute-start.4) | collective-permute-done | bytes 131104 | tf_op jit(solution)/shard_map/ppermute | solution.py:634
  52.8 0.7 %merge.1 = bf16[8,32,256]{2,1,0:T(8,128)(2,1)} custom-call(f32[8,32,256]{2,1,0:T(8,128)S(1)} %own.1.refs_0_, bf16[8,32,256]{2,1,0:T(8,128)(2,1)S(1)} %collective-permute-done.4.refs_1_), custom_call_target="tpu_custom_call" | custom-call | bytes 393216 | tf_op jit(solution)/shard_map/merge/pallas_call | solution.py:68
  53.5 3.4 %all-to-all-start.2 = ((bf16[8,32,256]{2,1,0:T(8,128)(2,1)}), bf16[8,32,256]{2,1,0:T(8,128)(2,1)S(1)}, u32[]{:S(2)}, u32[]{:S(2)}) async-start(bf16[8,32,256]{2,1,0:T(8,128)(2,1)} %merge.1), calls=%async_computation.2 | async-start | bytes 262144 | tf_op jit(solution)/shard_map/all_to_all | solution.py:637
  56.9 1.6 %self_part.1 = (f32[32,2048]{1,0:T(8,128)S(1)}, bf16[8,32,256]{2,1,0:T(8,128)(2,1)S(1)}) custom-call(bf16[8,32,256]{2,1,0:T(8,128)(2,1)S(1)} %get-tuple-element.52.refs_0_, bf16[8,256,256]{2,1,0:T(8,128)(2,1)} %refs_1_.5, bf16[8,32,256]{2,1,0:T(8,128)(2,1)} %refs_2_.5), custom_call_target="tpu_custom_call" | custom-call | bytes 1310720 | tf_op jit(solution)/shard_map/self_part/pallas_call | solution.py:68
  58.5 5.9 %all-to-all-done.2.refs_0_ = bf16[8,32,256]{2,1,0:T(8,128)(2,1)S(1)} async-done(((bf16[8,32,256]{2,1,0:T(8,128)(2,1)}), bf16[8,32,256]{2,1,0:T(8,128)(2,1)S(1)}, u32[]{:S(2)}, u32[]{:S(2)}) %all-to-all-start.2) | async-done | bytes 131104 | tf_op jit(solution)/shard_map/all_to_all | solution.py:637
  64.4 0.8 %answer.1 = bf16[32,2048]{1,0:T(8,128)(2,1)} custom-call(bf16[8,32,256]{2,1,0:T(8,128)(2,1)S(1)} %all-to-all-done.2.refs_0_, f32[32,2048]{1,0:T(8,128)S(1)} %get-tuple-element.53.refs_1_, bf16[8,32,256]{2,1,0:T(8,128)(2,1)S(1)} %get-tuple-element.54.refs_2_), custom_call_target="tpu_custom_call" | custom-call | bytes 524288 | tf_op jit(solution)/shard_map/answer/pallas_call | solution.py:68
Async XLA Ops:
  0.0 14.5 %collective-permute-start.1 = (bf16[32,2048]{1,0:T(8,128)(2,1)}, bf16[32,2048]{1,0:T(8,128)(2,1)S(1)}, u32[]{:S(2)}, u32[]{:S(2)}) collective-permute-start(bf16[32,2048]{1,0:T(8,128)(2,1)} %refs_2_.4), channel_id=1, source_target_pairs={{0,0},{15,15},{1,2},{2,1},{3,4},{4,3},{5,6},{6,5},{7,8},{8,7},{9,1... | collective-permute-start | bytes 393224 | tf_op jit(solution)/shard_map/ppermute | solution.py:486
  6.0 8.5 %collective-permute-start = (bf16[32,2048]{1,0:T(8,128)(2,1)S(1)}, bf16[32,2048]{1,0:T(8,128)(2,1)S(1)}, u32[]{:S(2)}, u32[]{:S(2)}) collective-permute-start(bf16[32,2048]{1,0:T(8,128)(2,1)S(1)} %get-tuple-element.31), channel_id=1, source_target_pairs={{0,1},{1,0},{2,3},{3,2},{4,5},{5,4},{6,7},{7,6},{8,9},{9,8},{10,11... | collective-permute-start | bytes 393224 | tf_op jit(solution)/shard_map/ppermute | solution.py:479
  9.6 15.0 %all-to-all-start = ((bf16[16,8,1024]{2,1,0:T(8,128)(2,1)}), bf16[16,8,1024]{2,1,0:T(8,128)(2,1)S(1)}, u32[]{:S(2)}, u32[]{:S(2)}) async-start(bf16[16,8,1024]{2,1,0:T(8,128)(2,1)} %bitcast.3), calls=%async_computation | async-start | bytes 524288 | tf_op jit(solution)/shard_map/all_to_all | solution.py:492
  25.5 4.9 %collective-permute-start.3 = (bf16[352,256]{1,0:T(8,128)(2,1)S(1)}, bf16[352,256]{1,0:T(8,128)(2,1)S(1)}, u32[]{:S(2)}, u32[]{:S(2)}) collective-permute-start(bf16[352,256]{1,0:T(8,128)(2,1)S(1)} %get-tuple-element.42), channel_id=1, source_target_pairs={{0,0},{15,15},{1,2},{2,1},{3,4},{4,3},{5,6},{6,5},{7,8},{8,7},{9,1... | collective-permute-start | bytes 540680 | tf_op jit(solution)/shard_map/ppermute | solution.py:486
  26.7 3.7 %collective-permute-start.2 = (bf16[352,256]{1,0:T(8,128)(2,1)S(1)}, bf16[352,256]{1,0:T(8,128)(2,1)S(1)}, u32[]{:S(2)}, u32[]{:S(2)}) collective-permute-start(bf16[352,256]{1,0:T(8,128)(2,1)S(1)} %get-tuple-element.41), channel_id=1, source_target_pairs={{0,1},{1,0},{2,3},{3,2},{4,5},{5,4},{6,7},{7,6},{8,9},{9,8},{10,11... | collective-permute-start | bytes 540680 | tf_op jit(solution)/shard_map/ppermute | solution.py:479
  33.2 16.7 %all-to-all-start.1 = ((bf16[16,72,128]{2,1,0:T(8,128)(2,1)}), bf16[16,72,128]{2,1,0:T(8,128)(2,1)S(1)}, u32[]{:S(2)}, u32[]{:S(2)}) async-start(bf16[16,72,128]{2,1,0:T(8,128)(2,1)} %finish.1), calls=%async_computation.1 | async-start | bytes 589824 | tf_op jit(solution)/shard_map/all_to_all | solution.py:610
  51.4 1.4 %collective-permute-start.4 = (bf16[8,32,256]{2,1,0:T(8,128)(2,1)S(1)}, bf16[8,32,256]{2,1,0:T(8,128)(2,1)S(1)}, u32[]{:S(2)}, u32[]{:S(2)}) collective-permute-start(bf16[8,32,256]{2,1,0:T(8,128)(2,1)S(1)} %get-tuple-element.51), channel_id=1, source_target_pairs={{0,1},{1,0},{2,3},{3,2},{4,5},{5,4},{6,7},{7,6},{8,9},{9,8},{10,11... | collective-permute-start | bytes 393224 | tf_op jit(solution)/shard_map/ppermute | solution.py:634
  53.5 10.9 %all-to-all-start.2 = ((bf16[8,32,256]{2,1,0:T(8,128)(2,1)}), bf16[8,32,256]{2,1,0:T(8,128)(2,1)S(1)}, u32[]{:S(2)}, u32[]{:S(2)}) async-start(bf16[8,32,256]{2,1,0:T(8,128)(2,1)} %merge.1), calls=%async_computation.2 | async-start | bytes 262144 | tf_op jit(solution)/shard_map/all_to_all | solution.py:637

commit v12 on v11

--- a/solution.py
+++ b/solution.py
@@ -106,12 +106,11 @@
 
 def far_up_body(
     value, compress, coupling, source, owner, place,
-    out_ref, copy_out, blocks, turned, spread, pick, terms, stage, sent,
+    out_ref, blocks, turned, spread, pick, terms,
 ):
     coupling = ready(coupling)
     turned[...] = coupling[...].astype(F32).T
     value, compress = ready(value), ready(compress)
-    copy_out[...] = value[...]
     for s in range(BLK):
         blocks[s * INC : (s + 1) * INC, :] = block(value, s)
     coef = coefficients(blocks[...], compress)
@@ -135,22 +134,11 @@
         terms[pl.ds(rows, 2 * RANK), :] = jnp.concatenate([first, second], axis=0).astype(BF16)
         return carry
 
+    lax.fori_loop(0, INC // 2, step, 0)
     targets = out_ref.shape[0]
     owner, place = ready(owner), ready(place)
     select = as_hot(iota((targets, tiles), 0) == owner[...] * BLK + place[...])
-    chunks = 4
-    width = INC * RANK // chunks
-    copies = []
-    for c in range(chunks):
-        lax.fori_loop(c * (INC // 2 // chunks), (c + 1) * (INC // 2 // chunks), step, 0)
-        part = slice(c * width, (c + 1) * width)
-        stage[:, part] = dot_nt(select, terms[part, :]).astype(BF16)
-        columns = pl.ds(c * width, width)
-        copy = pltpu.make_async_copy(stage.at[:, columns], out_ref.at[:, columns], sent.at[c])
-        copy.start()
-        copies.append(copy)
-    for copy in copies:
-        copy.wait()
+    out_ref[...] = dot_nt(select, terms[...]).astype(BF16)
 
 
 def far_scratch(tiles):
@@ -508,20 +496,17 @@
     cube = ((BLK, TILE, TILE), BF16)
 
     note = ((3 * INC + TILE, TILE), BF16)
-    outer = swap_outer(currents, surf_count)
-    partial, inner = call(
+    inner, outer = swap_inner(currents, surf_count), swap_outer(currents, surf_count)
+    (partial,) = call(
         far_up_body,
-        [((targets, INC * RANK), BF16), ((INC, NP_DEV), BF16)],
+        [((targets, INC * RANK), BF16)],
         (currents, primal_compress, primal_coupling) + lists,
-        scratch=far_scratch(tiles)
-        + [pltpu.VMEM((targets, INC * RANK), BF16), pltpu.SemaphoreType.DMA((4,))],
-        streamed=(0,),
+        scratch=far_scratch(tiles),
         held=(2, 0, 1, 3, 4, 5),
         flops=10**11,
         name="far_up",
     )
     arrived = exchange(partial, surf_count)
-    inner = swap_inner(inner, surf_count)
     near_part, lower, upper, expanded = call(
         prepare_body,
         [((INC, NP_DEV), F32), cube, cube, ((BLK, RANK, TILE), BF16)],

time: 65.8 us -> 65.2 us (level)
    ppermute x2, starting transfers between devices: 4.64 us -> 1.59 us  [swap_inner(): return lax.ppermute(array, 'surf', [(i, i ^ 1) for i in range(surf_count)])]
    all_to_all x1, starting transfers between devices: 4.99 us -> 7.92 us  [exchange(): lax.all_to_all(array, 'surf', split_axis=0, concat_axis=0, tiled=True)]
  transfers between devices with their start and end apart: 8 -> 8, of which waited for: 4 -> 4; matrix products, arithmetic and copies ran while one was open for 0% -> 0% of each run, Pallas kernels for 35% -> 34%
where the time goes in v12:
time: 65.2 us; the launch traced here: 64.7 us
  Pallas kernels  29 us (44%)
  starting transfers between devices  21.3 us (33%)
  waiting for transfers between devices  14.3 us (22%)
    pallas_call x13, Pallas kernels, call(): pl.pallas_call(wrapped, out_shape=outs, in_specs=[pl.BlockSpec(memory_spa...  29 us
    all_to_all x1, starting transfers between devices, exchange(): lax.all_to_all(array, 'surf', split_axis=0, concat_axis=0, tiled=True)  7.92 us
    all_to_all x1, starting transfers between devices, shards(): lax.all_to_all(send, 'surf', split_axis=0, concat_axis=0, tiled=True)  6.16 us
    all_to_all x1, waiting for transfers between devices, shards(): lax.all_to_all(merged, 'surf', split_axis=0, concat_axis=0, tiled=True, a...  5.89 us
    all_to_all x1, waiting for transfers between devices, shards(): lax.all_to_all(send, 'surf', split_axis=0, concat_axis=0, tiled=True)  3.81 us
    all_to_all x1, waiting for transfers between devices, exchange(): lax.all_to_all(array, 'surf', split_axis=0, concat_axis=0, tiled=True)  3.51 us
    all_to_all x1, starting transfers between devices, shards(): lax.all_to_all(merged, 'surf', split_axis=0, concat_axis=0, tiled=True, a...  3.37 us
    ppermute x2, starting transfers between devices, swap_outer(): return lax.ppermute(array, 'surf', pairs)  2.22 us
  transfers between devices with their start and end apart: 8, of which 4 were waited for; matrix products, arithmetic and copies ran while one was open for 0% of the time, Pallas kernels for 34%

profile of v12, /device:TPU:0, one launch (start us, length us, event | category | flops | bytes accessed | tf_op | source)
XLA Modules:
  0.0 64.7 jit_solution(5455360458700084565)
XLA Ops:
  0.0 0.5 collective-permute-start
  0.5 1.6 %collective-permute-start.1 = (bf16[32,2048]{1,0:T(8,128)(2,1)}, bf16[32,2048]{1,0:T(8,128)(2,1)S(1)}, u32[]{:S(2)}, u32[]{:S(2)}) collective-permute-start(bf16[32,2048]{1,0:T(8,128)(2,1)} %refs_2_.4), channel_id=1, source_target_pairs={{0,0},{15,15},{1,2},{2,1},{3,4},{4,3},{5,6},{6,5},{7,8},{8,7},{9,1... | collective-permute-start | bytes 393224 | tf_op jit(solution)/shard_map/ppermute | solution.py:474
  2.0 4.1 %far_up.1 = bf16[128,1024]{1,0:T(8,128)(2,1)} custom-call(bf16[32,2048]{1,0:T(8,128)(2,1)} %refs_2_.4, bf16[8,32,256]{2,1,0:T(8,128)(2,1)} %refs_1_.3, bf16[128,1024]{1,0:T(8,128)(2,1)} %refs_2_.3, s32[1,128]{1,0:T(1,128)} %bitcast.12, s32[1,128]{1,0:T(1,128)} %bitcast.14, s32[1,128]{1,0:T(1,128)} %bitcast.16), custom_call_target="tpu_custom_call" | custom-call | flops 99999997952 | bytes 525824 | tf_op jit(solution)/shard_map/far_up/pallas_call | solution.py:68
  6.1 7.9 %all-to-all-start = ((bf16[16,8,1024]{2,1,0:T(8,128)(2,1)}), bf16[16,8,1024]{2,1,0:T(8,128)(2,1)S(1)}, u32[]{:S(2)}, u32[]{:S(2)}) async-start(bf16[16,8,1024]{2,1,0:T(8,128)(2,1)} %bitcast.3), calls=%async_computation | async-start | bytes 524288 | tf_op jit(solution)/shard_map/all_to_all | solution.py:480
  14.0 0.0 collective-permute-done.refs_3_
  14.0 0.0 collective-permute-done.1.refs_4_
  14.0 6.5 %prepare.1 = (f32[32,2048]{1,0:T(8,128)S(1)}, bf16[8,256,256]{2,1,0:T(8,128)(2,1)S(1)}, bf16[8,256,256]{2,1,0:T(8,128)(2,1)S(1)}, bf16[8,32,256]{2,1,0:T(8,128)(2,1)S(1)}) custom-call(s32[48]{0:T(128)} %refs_0_.4, s32[48]{0:T(128)} %refs_1_.4, bf16[32,2048]{1,0:T(8,128)(2,1)} %refs_2_.4, bf16[32,2048]{1,0:T(8,128)(2,1)S(1)} %collective-permute-done.refs_3_, ...), custom_call_target="tpu_custom_call" | custom-call | flops 99999997952 | bytes 9961856 | tf_op jit(solution)/shard_map/prepare/pallas_call | solution.py:68
  20.6 3.5 %all-to-all-done = bf16[16,8,1024]{2,1,0:T(8,128)(2,1)S(1)} async-done(((bf16[16,8,1024]{2,1,0:T(8,128)(2,1)}), bf16[16,8,1024]{2,1,0:T(8,128)(2,1)S(1)}, u32[]{:S(2)}, u32[]{:S(2)}) %all-to-all-start) | async-done | bytes 262176 | tf_op jit(solution)/shard_map/all_to_all | solution.py:480
  24.1 0.9 %solve.1 = (f32[32,2048]{1,0:T(8,128)S(1)}, f32[32,2048]{1,0:T(8,128)S(1)}, bf16[352,256]{1,0:T(8,128)(2,1)S(1)}, bf16[352,256]{1,0:T(8,128)(2,1)S(1)}) custom-call(bf16[128,1024]{1,0:T(8,128)(2,1)S(1)} %bitcast.8, f32[32,2048]{1,0:T(8,128)S(1)} %get-tuple-element.28.refs_1_, bf16[8,32,256]{2,1,0:T(8,128)(2,1)S(1)} %get-tuple-element.29.refs_2_, ...), custom_call_target="tpu_custom_call" | custom-call | bytes 2752512 | tf_op jit(solution)/shard_map/solve/pallas_call | solution.py:68
  24.9 0.7 %collective-permute-start.3 = (bf16[352,256]{1,0:T(8,128)(2,1)S(1)}, bf16[352,256]{1,0:T(8,128)(2,1)S(1)}, u32[]{:S(2)}, u32[]{:S(2)}) collective-permute-start(bf16[352,256]{1,0:T(8,128)(2,1)S(1)} %get-tuple-element.38), channel_id=1, source_target_pairs={{0,0},{15,15},{1,2},{2,1},{3,4},{4,3},{5,6},{6,5},{7,8},{8,7},{9,1... | collective-permute-start | bytes 540680 | tf_op jit(solution)/shard_map/ppermute | solution.py:474
  25.6 0.6 middle.1
  26.2 1.1 %collective-permute-start.2 = (bf16[352,256]{1,0:T(8,128)(2,1)S(1)}, bf16[352,256]{1,0:T(8,128)(2,1)S(1)}, u32[]{:S(2)}, u32[]{:S(2)}) collective-permute-start(bf16[352,256]{1,0:T(8,128)(2,1)S(1)} %get-tuple-element.37), channel_id=1, source_target_pairs={{0,1},{1,0},{2,3},{3,2},{4,5},{5,4},{6,7},{7,6},{8,9},{9,8},{10,11... | collective-permute-start | bytes 540680 | tf_op jit(solution)/shard_map/ppermute | solution.py:467
  27.3 1.4 %order.1 = (s32[8,256]{1,0:T(8,128)S(1)}, bf16[2048,256]{1,0:T(8,128)(2,1)S(1)}, s32[16,2]{1,0:T(8,128)S(1)}, bf16[16,2048]{1,0:T(8,128)(2,1)S(1)}, f32[1,2048]{1,0:T(1,128)S(1)}) custom-call(s32[1,2048]{1,0:T(1,128)} %bitcast.9, s32[1,2048]{1,0:T(1,128)} %bitcast.10, f32[1,2048]{1,0:T(1,128)} %bitcast.11, f32[32,2048]{1,0:T(8,128)S(1)} %get-tuple-element.32.refs_0_.refs_3_), custom_call_target="tpu_custom_call" | custom-call | flops 1000000000 | bytes 286720 | tf_op jit(solution)/shard_map/order/pallas_call | solution.py:68
  28.7 1.1 %tails.1.refs_9_ = f32[16,8,128]{2,1,0:T(8,128)S(1)} custom-call(bf16[16,2048]{1,0:T(8,128)(2,1)S(1)} %get-tuple-element.40.refs_0_, s32[8,256]{1,0:T(8,128)S(1)} %get-tuple-element.41.refs_1_.refs_10_, bf16[2048,256]{1,0:T(8,128)(2,1)S(1)} %get-tuple-element.42.refs_2_.refs_11_, s32[16,2]{1,0:T(8,128)S(1)} %get-tuple-element.43.refs_3_.refs_12_), custom_call_target="tpu_custom_call" | custom-call | flops 1000000000 | bytes 1122432 | tf_op jit(solution)/shard_map/tails/pallas_call | solution.py:68
  29.8 0.0 collective-permute-done.3.refs_5_
  29.9 0.0 collective-permute-done.2.refs_4_
  29.9 2.8 %finish.1 = bf16[16,72,128]{2,1,0:T(8,128)(2,1)} custom-call(f32[32,2048]{1,0:T(8,128)S(1)} %get-tuple-element.32.refs_0_.refs_3_, f32[32,2048]{1,0:T(8,128)S(1)} %get-tuple-element.33.refs_1_, f32[32,2048]{1,0:T(8,128)S(1)} %get-tuple-element.35.refs_2_, f32[32,2048]{1,0:T(8,128)S(1)} %get-tuple-element.36.refs_3_, ...), custom_call_target="tpu_custom_call" | custom-call | bytes 4636800 | tf_op jit(solution)/shard_map/finish/pallas_call | solution.py:68
  32.6 6.2 %all-to-all-start.1 = ((bf16[16,72,128]{2,1,0:T(8,128)(2,1)}), bf16[16,72,128]{2,1,0:T(8,128)(2,1)S(1)}, u32[]{:S(2)}, u32[]{:S(2)}) async-start(bf16[16,72,128]{2,1,0:T(8,128)(2,1)} %finish.1), calls=%async_computation.1 | async-start | bytes 589824 | tf_op jit(solution)/shard_map/all_to_all | solution.py:595
  38.8 6.8 %couple.1 = (bf16[256,4096]{1,0:T(8,128)(2,1)S(1)}, bf16[8,32,256]{2,1,0:T(8,128)(2,1)S(1)}) custom-call(bf16[128,1024]{1,0:T(8,128)(2,1)} %refs_0_.5, s32[1,128]{1,0:T(1,128)} %bitcast.13, s32[1,128]{1,0:T(1,128)} %bitcast.15, s32[1,128]{1,0:T(1,128)} %bitcast.17, bf16[8,32,256]{2,1,0:T(8,128)(2,1)} %refs_4_.1), custom_call_target="tpu_custom_call" | custom-call | flops 10000000000 | bytes 394752 | tf_op jit(solution)/shard_map/couple/pallas_call | solution.py:68
  45.6 3.8 %all-to-all-done.1.refs_0_ = bf16[16,72,128]{2,1,0:T(8,128)(2,1)S(1)} async-done(((bf16[16,72,128]{2,1,0:T(8,128)(2,1)}), bf16[16,72,128]{2,1,0:T(8,128)(2,1)S(1)}, u32[]{:S(2)}, u32[]{:S(2)}) %all-to-all-start.1) | async-done | bytes 294944 | tf_op jit(solution)/shard_map/all_to_all | solution.py:595
  49.4 1.5 %gather.1 = (bf16[8,32,256]{2,1,0:T(8,128)(2,1)S(1)}, bf16[32,256]{1,0:T(8,128)(2,1)S(1)}, bf16[8,32,256]{2,1,0:T(8,128)(2,1)S(1)}) custom-call(bf16[16,72,128]{2,1,0:T(8,128)(2,1)S(1)} %all-to-all-done.1.refs_0_, bf16[8,32,256]{2,1,0:T(8,128)(2,1)S(1)} %get-tuple-element.44.refs_1_, bf16[256,4096]{1,0:T(8,128)(2,1)S(1)} %get-tuple-element.45.refs_2_.refs_1_), custom_call_target="tpu_custom_call" | custom-call | bytes 2523136 | tf_op jit(solution)/shard_map/gather/pallas_call | solution.py:68
  50.9 0.1 collective-permute-start.4
  51.0 0.3 own.1.refs_0_
  51.3 1.0 %collective-permute-done.4.refs_1_ = bf16[8,32,256]{2,1,0:T(8,128)(2,1)S(1)} collective-permute-done((bf16[8,32,256]{2,1,0:T(8,128)(2,1)S(1)}, bf16[8,32,256]{2,1,0:T(8,128)(2,1)S(1)}, u32[]{:S(2)}, u32[]{:S(2)}) %collective-permute-start.4) | collective-permute-done | bytes 131104 | tf_op jit(solution)/shard_map/ppermute | solution.py:619
  52.3 0.7 %merge.1 = bf16[8,32,256]{2,1,0:T(8,128)(2,1)} custom-call(f32[8,32,256]{2,1,0:T(8,128)S(1)} %own.1.refs_0_, bf16[8,32,256]{2,1,0:T(8,128)(2,1)S(1)} %collective-permute-done.4.refs_1_), custom_call_target="tpu_custom_call" | custom-call | bytes 393216 | tf_op jit(solution)/shard_map/merge/pallas_call | solution.py:68
  53.0 3.4 %all-to-all-start.2 = ((bf16[8,32,256]{2,1,0:T(8,128)(2,1)}), bf16[8,32,256]{2,1,0:T(8,128)(2,1)S(1)}, u32[]{:S(2)}, u32[]{:S(2)}) async-start(bf16[8,32,256]{2,1,0:T(8,128)(2,1)} %merge.1), calls=%async_computation.2 | async-start | bytes 262144 | tf_op jit(solution)/shard_map/all_to_all | solution.py:622
  56.4 1.6 %self_part.1 = (f32[32,2048]{1,0:T(8,128)S(1)}, bf16[8,32,256]{2,1,0:T(8,128)(2,1)S(1)}) custom-call(bf16[8,32,256]{2,1,0:T(8,128)(2,1)S(1)} %get-tuple-element.48.refs_0_, bf16[8,256,256]{2,1,0:T(8,128)(2,1)} %refs_1_.5, bf16[8,32,256]{2,1,0:T(8,128)(2,1)} %refs_2_.5), custom_call_target="tpu_custom_call" | custom-call | bytes 1310720 | tf_op jit(solution)/shard_map/self_part/pallas_call | solution.py:68
  58.0 5.9 %all-to-all-done.2.refs_0_ = bf16[8,32,256]{2,1,0:T(8,128)(2,1)S(1)} async-done(((bf16[8,32,256]{2,1,0:T(8,128)(2,1)}), bf16[8,32,256]{2,1,0:T(8,128)(2,1)S(1)}, u32[]{:S(2)}, u32[]{:S(2)}) %all-to-all-start.2) | async-done | bytes 131104 | tf_op jit(solution)/shard_map/all_to_all | solution.py:622
  63.9 0.8 %answer.1 = bf16[32,2048]{1,0:T(8,128)(2,1)} custom-call(bf16[8,32,256]{2,1,0:T(8,128)(2,1)S(1)} %all-to-all-done.2.refs_0_, f32[32,2048]{1,0:T(8,128)S(1)} %get-tuple-element.49.refs_1_, bf16[8,32,256]{2,1,0:T(8,128)(2,1)S(1)} %get-tuple-element.50.refs_2_), custom_call_target="tpu_custom_call" | custom-call | bytes 524288 | tf_op jit(solution)/shard_map/answer/pallas_call | solution.py:68
Async XLA Ops:
  0.0 14.0 %collective-permute-start = (bf16[32,2048]{1,0:T(8,128)(2,1)}, bf16[32,2048]{1,0:T(8,128)(2,1)S(1)}, u32[]{:S(2)}, u32[]{:S(2)}) collective-permute-start(bf16[32,2048]{1,0:T(8,128)(2,1)} %refs_2_.4), channel_id=1, source_target_pairs={{0,1},{1,0},{2,3},{3,2},{4,5},{5,4},{6,7},{7,6},{8,9},{9,8},{10,11... | collective-permute-start | bytes 393224 | tf_op jit(solution)/shard_map/ppermute | solution.py:467
  0.5 13.6 %collective-permute-start.1 = (bf16[32,2048]{1,0:T(8,128)(2,1)}, bf16[32,2048]{1,0:T(8,128)(2,1)S(1)}, u32[]{:S(2)}, u32[]{:S(2)}) collective-permute-start(bf16[32,2048]{1,0:T(8,128)(2,1)} %refs_2_.4), channel_id=1, source_target_pairs={{0,0},{15,15},{1,2},{2,1},{3,4},{4,3},{5,6},{6,5},{7,8},{8,7},{9,1... | collective-permute-start | bytes 393224 | tf_op jit(solution)/shard_map/ppermute | solution.py:474
  6.1 18.0 %all-to-all-start = ((bf16[16,8,1024]{2,1,0:T(8,128)(2,1)}), bf16[16,8,1024]{2,1,0:T(8,128)(2,1)S(1)}, u32[]{:S(2)}, u32[]{:S(2)}) async-start(bf16[16,8,1024]{2,1,0:T(8,128)(2,1)} %bitcast.3), calls=%async_computation | async-start | bytes 524288 | tf_op jit(solution)/shard_map/all_to_all | solution.py:480
  24.9 4.9 %collective-permute-start.3 = (bf16[352,256]{1,0:T(8,128)(2,1)S(1)}, bf16[352,256]{1,0:T(8,128)(2,1)S(1)}, u32[]{:S(2)}, u32[]{:S(2)}) collective-permute-start(bf16[352,256]{1,0:T(8,128)(2,1)S(1)} %get-tuple-element.38), channel_id=1, source_target_pairs={{0,0},{15,15},{1,2},{2,1},{3,4},{4,3},{5,6},{6,5},{7,8},{8,7},{9,1... | collective-permute-start | bytes 540680 | tf_op jit(solution)/shard_map/ppermute | solution.py:474
  26.2 3.7 %collective-permute-start.2 = (bf16[352,256]{1,0:T(8,128)(2,1)S(1)}, bf16[352,256]{1,0:T(8,128)(2,1)S(1)}, u32[]{:S(2)}, u32[]{:S(2)}) collective-permute-start(bf16[352,256]{1,0:T(8,128)(2,1)S(1)} %get-tuple-element.37), channel_id=1, source_target_pairs={{0,1},{1,0},{2,3},{3,2},{4,5},{5,4},{6,7},{7,6},{8,9},{9,8},{10,11... | collective-permute-start | bytes 540680 | tf_op jit(solution)/shard_map/ppermute | solution.py:467
  32.6 16.7 %all-to-all-start.1 = ((bf16[16,72,128]{2,1,0:T(8,128)(2,1)}), bf16[16,72,128]{2,1,0:T(8,128)(2,1)S(1)}, u32[]{:S(2)}, u32[]{:S(2)}) async-start(bf16[16,72,128]{2,1,0:T(8,128)(2,1)} %finish.1), calls=%async_computation.1 | async-start | bytes 589824 | tf_op jit(solution)/shard_map/all_to_all | solution.py:595
  50.9 1.4 %collective-permute-start.4 = (bf16[8,32,256]{2,1,0:T(8,128)(2,1)S(1)}, bf16[8,32,256]{2,1,0:T(8,128)(2,1)S(1)}, u32[]{:S(2)}, u32[]{:S(2)}) collective-permute-start(bf16[8,32,256]{2,1,0:T(8,128)(2,1)S(1)} %get-tuple-element.47), channel_id=1, source_target_pairs={{0,1},{1,0},{2,3},{3,2},{4,5},{5,4},{6,7},{7,6},{8,9},{9,8},{10,11... | collective-permute-start | bytes 393224 | tf_op jit(solution)/shard_map/ppermute | solution.py:619
  53.0 10.9 %all-to-all-start.2 = ((bf16[8,32,256]{2,1,0:T(8,128)(2,1)}), bf16[8,32,256]{2,1,0:T(8,128)(2,1)S(1)}, u32[]{:S(2)}, u32[]{:S(2)}) async-start(bf16[8,32,256]{2,1,0:T(8,128)(2,1)} %merge.1), calls=%async_computation.2 | async-start | bytes 262144 | tf_op jit(solution)/shard_map/all_to_all | solution.py:622

commit v13 on v12

--- a/solution.py
+++ b/solution.py
@@ -41,9 +41,15 @@
     return mask.astype(F32).astype(BF16)
 
 
-def call(body, outs, args, scratch=(), smem=(), held=(), far=(), small=(), streamed=(), flops=0, name=None):
+def call(body, outs, args, scratch=(), smem=(), held=(), far=(), loose=(), small=(), streamed=(), flops=0, name=None):
     spaces = [
-        pltpu.SMEM if k in smem else pltpu.HBM if k in held or k in far else pltpu.VMEM
+        pltpu.SMEM
+        if k in smem
+        else pl.ANY
+        if k in loose
+        else pltpu.HBM
+        if k in held or k in far
+        else pltpu.VMEM
         for k in range(len(args))
     ]
     size = sum(a.size * a.dtype.itemsize for a in args)
@@ -290,7 +296,7 @@
 
 def finish_body(
     start_ref, next_ref, second_ref, third_ref, inner_note, outer_note, lower_ref, upper_ref,
-    weight, tails_ref, high_ref, hot_ref, bounds_ref, send_ref,
+    weight, tails_ref, high_ref, hot_ref, bounds, send_ref,
     notes, spread, ordered, stage, sent,
 ):
     position = lax.axis_index("surf")
@@ -325,6 +331,7 @@
     put_in_order(ordered, spread, hot_ref)
     owners = send_ref.shape[0]
     pieces = (send_ref.shape[1] - TAIL) // INC
+    bounds_ref = ready(bounds)
     for o in range(owners):
         piece = owner_window(ordered, bounds_ref[o, 0], pieces)
         parts = [piece[:, j * LANES : (j + 1) * LANES] for j in range(pieces)]
@@ -589,7 +596,9 @@
             pltpu.SemaphoreType.DMA((surf_count,)),
         ],
         streamed=(0,),
-        smem=(12,),
+        held=(12,),
+        loose=(12,),
+        small=(12,),
         name="finish",
     )
     shares = lax.all_to_all(send, "surf", split_axis=0, concat_axis=0, tiled=True)

time: 65.2 us -> 65 us (level)
  transfers between devices with their start and end apart: 8 -> 8, of which waited for: 4 -> 4; matrix products, arithmetic and copies ran while one was open for 0% -> 0% of each run, Pallas kernels for 34% -> 35%
where the time goes in v13:
time: 65 us; the launch traced here: 64.5 us
  Pallas kernels  28.8 us (44%)
  starting transfers between devices  21.3 us (33%)
  waiting for transfers between devices  14.3 us (22%)
    pallas_call x13, Pallas kernels, call(): pl.pallas_call(wrapped, out_shape=outs, in_specs=[pl.BlockSpec(memory_spa...  28.8 us
    all_to_all x1, starting transfers between devices, exchange(): lax.all_to_all(array, 'surf', split_axis=0, concat_axis=0, tiled=True)  7.92 us
    all_to_all x1, starting transfers between devices, shards(): lax.all_to_all(send, 'surf', split_axis=0, concat_axis=0, tiled=True)  6.17 us
    all_to_all x1, waiting for transfers between devices, shards(): lax.all_to_all(merged, 'surf', split_axis=0, concat_axis=0, tiled=True, a...  5.89 us
    all_to_all x1, waiting for transfers between devices, shards(): lax.all_to_all(send, 'surf', split_axis=0, concat_axis=0, tiled=True)  3.83 us
    all_to_all x1, waiting for transfers between devices, exchange(): lax.all_to_all(array, 'surf', split_axis=0, concat_axis=0, tiled=True)  3.51 us
    all_to_all x1, starting transfers between devices, shards(): lax.all_to_all(merged, 'surf', split_axis=0, concat_axis=0, tiled=True, a...  3.37 us
    ppermute x2, starting transfers between devices, swap_outer(): return lax.ppermute(array, 'surf', pairs)  2.22 us
  transfers between devices with their start and end apart: 8, of which 4 were waited for; matrix products, arithmetic and copies ran while one was open for 0% of the time, Pallas kernels for 35%

profile of v13, /device:TPU:0, one launch (start us, length us, event | category | flops | bytes accessed | tf_op | source)
XLA Modules:
  0.0 64.5 jit_solution(8547154171251741806)
XLA Ops:
  0.0 0.5 collective-permute-start
  0.5 1.6 %collective-permute-start.1 = (bf16[32,2048]{1,0:T(8,128)(2,1)}, bf16[32,2048]{1,0:T(8,128)(2,1)S(1)}, u32[]{:S(2)}, u32[]{:S(2)}) collective-permute-start(bf16[32,2048]{1,0:T(8,128)(2,1)} %refs_2_.4), channel_id=1, source_target_pairs={{0,0},{15,15},{1,2},{2,1},{3,4},{4,3},{5,6},{6,5},{7,8},{8,7},{9,1... | collective-permute-start | bytes 393224 | tf_op jit(solution)/shard_map/ppermute | solution.py:481
  2.0 4.1 %far_up.1 = bf16[128,1024]{1,0:T(8,128)(2,1)} custom-call(bf16[32,2048]{1,0:T(8,128)(2,1)} %refs_2_.4, bf16[8,32,256]{2,1,0:T(8,128)(2,1)} %refs_1_.3, bf16[128,1024]{1,0:T(8,128)(2,1)} %refs_2_.3, s32[1,128]{1,0:T(1,128)} %bitcast.12, s32[1,128]{1,0:T(1,128)} %bitcast.14, s32[1,128]{1,0:T(1,128)} %bitcast.16), custom_call_target="tpu_custom_call" | custom-call | flops 99999997952 | bytes 525824 | tf_op jit(solution)/shard_map/far_up/pallas_call | solution.py:74
  6.1 7.9 %all-to-all-start = ((bf16[16,8,1024]{2,1,0:T(8,128)(2,1)}), bf16[16,8,1024]{2,1,0:T(8,128)(2,1)S(1)}, u32[]{:S(2)}, u32[]{:S(2)}) async-start(bf16[16,8,1024]{2,1,0:T(8,128)(2,1)} %bitcast.3), calls=%async_computation | async-start | bytes 524288 | tf_op jit(solution)/shard_map/all_to_all | solution.py:487
  14.0 0.0 collective-permute-done.refs_3_
  14.0 0.0 collective-permute-done.1.refs_4_
  14.0 6.5 %prepare.1 = (f32[32,2048]{1,0:T(8,128)S(1)}, bf16[8,256,256]{2,1,0:T(8,128)(2,1)S(1)}, bf16[8,256,256]{2,1,0:T(8,128)(2,1)S(1)}, bf16[8,32,256]{2,1,0:T(8,128)(2,1)S(1)}) custom-call(s32[48]{0:T(128)} %refs_0_.4, s32[48]{0:T(128)} %refs_1_.4, bf16[32,2048]{1,0:T(8,128)(2,1)} %refs_2_.4, bf16[32,2048]{1,0:T(8,128)(2,1)S(1)} %collective-permute-done.refs_3_, ...), custom_call_target="tpu_custom_call" | custom-call | flops 99999997952 | bytes 9961856 | tf_op jit(solution)/shard_map/prepare/pallas_call | solution.py:74
  20.5 3.5 %all-to-all-done = bf16[16,8,1024]{2,1,0:T(8,128)(2,1)S(1)} async-done(((bf16[16,8,1024]{2,1,0:T(8,128)(2,1)}), bf16[16,8,1024]{2,1,0:T(8,128)(2,1)S(1)}, u32[]{:S(2)}, u32[]{:S(2)}) %all-to-all-start) | async-done | bytes 262176 | tf_op jit(solution)/shard_map/all_to_all | solution.py:487
  24.1 0.9 %solve.1 = (f32[32,2048]{1,0:T(8,128)S(1)}, f32[32,2048]{1,0:T(8,128)S(1)}, bf16[352,256]{1,0:T(8,128)(2,1)S(1)}, bf16[352,256]{1,0:T(8,128)(2,1)S(1)}) custom-call(bf16[128,1024]{1,0:T(8,128)(2,1)S(1)} %bitcast.8, f32[32,2048]{1,0:T(8,128)S(1)} %get-tuple-element.28.refs_1_, bf16[8,32,256]{2,1,0:T(8,128)(2,1)S(1)} %get-tuple-element.29.refs_2_, ...), custom_call_target="tpu_custom_call" | custom-call | bytes 2752512 | tf_op jit(solution)/shard_map/solve/pallas_call | solution.py:74
  24.9 0.7 %collective-permute-start.3 = (bf16[352,256]{1,0:T(8,128)(2,1)S(1)}, bf16[352,256]{1,0:T(8,128)(2,1)S(1)}, u32[]{:S(2)}, u32[]{:S(2)}) collective-permute-start(bf16[352,256]{1,0:T(8,128)(2,1)S(1)} %get-tuple-element.38), channel_id=1, source_target_pairs={{0,0},{15,15},{1,2},{2,1},{3,4},{4,3},{5,6},{6,5},{7,8},{8,7},{9,1... | collective-permute-start | bytes 540680 | tf_op jit(solution)/shard_map/ppermute | solution.py:481
  25.6 0.6 middle.1
  26.2 1.1 %collective-permute-start.2 = (bf16[352,256]{1,0:T(8,128)(2,1)S(1)}, bf16[352,256]{1,0:T(8,128)(2,1)S(1)}, u32[]{:S(2)}, u32[]{:S(2)}) collective-permute-start(bf16[352,256]{1,0:T(8,128)(2,1)S(1)} %get-tuple-element.37), channel_id=1, source_target_pairs={{0,1},{1,0},{2,3},{3,2},{4,5},{5,4},{6,7},{7,6},{8,9},{9,8},{10,11... | collective-permute-start | bytes 540680 | tf_op jit(solution)/shard_map/ppermute | solution.py:474
  27.3 1.4 %order.1 = (s32[8,256]{1,0:T(8,128)S(1)}, bf16[2048,256]{1,0:T(8,128)(2,1)S(1)}, s32[16,2]{1,0:T(8,128)S(1)}, bf16[16,2048]{1,0:T(8,128)(2,1)S(1)}, f32[1,2048]{1,0:T(1,128)S(1)}) custom-call(s32[1,2048]{1,0:T(1,128)} %bitcast.9, s32[1,2048]{1,0:T(1,128)} %bitcast.10, f32[1,2048]{1,0:T(1,128)} %bitcast.11, f32[32,2048]{1,0:T(8,128)S(1)} %get-tuple-element.32.refs_0_.refs_3_), custom_call_target="tpu_custom_call" | custom-call | flops 1000000000 | bytes 286720 | tf_op jit(solution)/shard_map/order/pallas_call | solution.py:74
  28.7 1.1 %tails.1.refs_9_ = f32[16,8,128]{2,1,0:T(8,128)S(1)} custom-call(bf16[16,2048]{1,0:T(8,128)(2,1)S(1)} %get-tuple-element.40.refs_0_, s32[8,256]{1,0:T(8,128)S(1)} %get-tuple-element.41.refs_1_.refs_10_, bf16[2048,256]{1,0:T(8,128)(2,1)S(1)} %get-tuple-element.42.refs_2_.refs_11_, s32[16,2]{1,0:T(8,128)S(1)} %get-tuple-element.43.refs_3_.refs_12_), custom_call_target="tpu_custom_call" | custom-call | flops 1000000000 | bytes 1122432 | tf_op jit(solution)/shard_map/tails/pallas_call | solution.py:74
  29.8 0.0 collective-permute-done.3.refs_5_
  29.9 0.0 collective-permute-done.2.refs_4_
  29.9 2.6 %finish.1 = bf16[16,72,128]{2,1,0:T(8,128)(2,1)} custom-call(f32[32,2048]{1,0:T(8,128)S(1)} %get-tuple-element.32.refs_0_.refs_3_, f32[32,2048]{1,0:T(8,128)S(1)} %get-tuple-element.33.refs_1_, f32[32,2048]{1,0:T(8,128)S(1)} %get-tuple-element.35.refs_2_, f32[32,2048]{1,0:T(8,128)S(1)} %get-tuple-element.36.refs_3_, ...), custom_call_target="tpu_custom_call" | custom-call | bytes 4636800 | tf_op jit(solution)/shard_map/finish/pallas_call | solution.py:74
  32.5 6.2 %all-to-all-start.1 = ((bf16[16,72,128]{2,1,0:T(8,128)(2,1)}), bf16[16,72,128]{2,1,0:T(8,128)(2,1)S(1)}, u32[]{:S(2)}, u32[]{:S(2)}) async-start(bf16[16,72,128]{2,1,0:T(8,128)(2,1)} %finish.1), calls=%async_computation.1 | async-start | bytes 589824 | tf_op jit(solution)/shard_map/all_to_all | solution.py:604
  38.6 6.7 %couple.1 = (bf16[256,4096]{1,0:T(8,128)(2,1)S(1)}, bf16[8,32,256]{2,1,0:T(8,128)(2,1)S(1)}) custom-call(bf16[128,1024]{1,0:T(8,128)(2,1)} %refs_0_.5, s32[1,128]{1,0:T(1,128)} %bitcast.13, s32[1,128]{1,0:T(1,128)} %bitcast.15, s32[1,128]{1,0:T(1,128)} %bitcast.17, bf16[8,32,256]{2,1,0:T(8,128)(2,1)} %refs_4_.1), custom_call_target="tpu_custom_call" | custom-call | flops 10000000000 | bytes 394752 | tf_op jit(solution)/shard_map/couple/pallas_call | solution.py:74
  45.4 3.8 %all-to-all-done.1.refs_0_ = bf16[16,72,128]{2,1,0:T(8,128)(2,1)S(1)} async-done(((bf16[16,72,128]{2,1,0:T(8,128)(2,1)}), bf16[16,72,128]{2,1,0:T(8,128)(2,1)S(1)}, u32[]{:S(2)}, u32[]{:S(2)}) %all-to-all-start.1) | async-done | bytes 294944 | tf_op jit(solution)/shard_map/all_to_all | solution.py:604
  49.2 1.5 %gather.1 = (bf16[8,32,256]{2,1,0:T(8,128)(2,1)S(1)}, bf16[32,256]{1,0:T(8,128)(2,1)S(1)}, bf16[8,32,256]{2,1,0:T(8,128)(2,1)S(1)}) custom-call(bf16[16,72,128]{2,1,0:T(8,128)(2,1)S(1)} %all-to-all-done.1.refs_0_, bf16[8,32,256]{2,1,0:T(8,128)(2,1)S(1)} %get-tuple-element.44.refs_1_, bf16[256,4096]{1,0:T(8,128)(2,1)S(1)} %get-tuple-element.45.refs_2_.refs_1_), custom_call_target="tpu_custom_call" | custom-call | bytes 2523136 | tf_op jit(solution)/shard_map/gather/pallas_call | solution.py:74
  50.7 0.1 collective-permute-start.4
  50.8 0.3 own.1.refs_0_
  51.1 1.0 %collective-permute-done.4.refs_1_ = bf16[8,32,256]{2,1,0:T(8,128)(2,1)S(1)} collective-permute-done((bf16[8,32,256]{2,1,0:T(8,128)(2,1)S(1)}, bf16[8,32,256]{2,1,0:T(8,128)(2,1)S(1)}, u32[]{:S(2)}, u32[]{:S(2)}) %collective-permute-start.4) | collective-permute-done | bytes 131104 | tf_op jit(solution)/shard_map/ppermute | solution.py:628
  52.1 0.7 %merge.1 = bf16[8,32,256]{2,1,0:T(8,128)(2,1)} custom-call(f32[8,32,256]{2,1,0:T(8,128)S(1)} %own.1.refs_0_, bf16[8,32,256]{2,1,0:T(8,128)(2,1)S(1)} %collective-permute-done.4.refs_1_), custom_call_target="tpu_custom_call" | custom-call | bytes 393216 | tf_op jit(solution)/shard_map/merge/pallas_call | solution.py:74
  52.8 3.4 %all-to-all-start.2 = ((bf16[8,32,256]{2,1,0:T(8,128)(2,1)}), bf16[8,32,256]{2,1,0:T(8,128)(2,1)S(1)}, u32[]{:S(2)}, u32[]{:S(2)}) async-start(bf16[8,32,256]{2,1,0:T(8,128)(2,1)} %merge.1), calls=%async_computation.2 | async-start | bytes 262144 | tf_op jit(solution)/shard_map/all_to_all | solution.py:631
  56.2 1.6 %self_part.1 = (f32[32,2048]{1,0:T(8,128)S(1)}, bf16[8,32,256]{2,1,0:T(8,128)(2,1)S(1)}) custom-call(bf16[8,32,256]{2,1,0:T(8,128)(2,1)S(1)} %get-tuple-element.48.refs_0_, bf16[8,256,256]{2,1,0:T(8,128)(2,1)} %refs_1_.5, bf16[8,32,256]{2,1,0:T(8,128)(2,1)} %refs_2_.5), custom_call_target="tpu_custom_call" | custom-call | bytes 1310720 | tf_op jit(solution)/shard_map/self_part/pallas_call | solution.py:74
  57.8 5.9 %all-to-all-done.2.refs_0_ = bf16[8,32,256]{2,1,0:T(8,128)(2,1)S(1)} async-done(((bf16[8,32,256]{2,1,0:T(8,128)(2,1)}), bf16[8,32,256]{2,1,0:T(8,128)(2,1)S(1)}, u32[]{:S(2)}, u32[]{:S(2)}) %all-to-all-start.2) | async-done | bytes 131104 | tf_op jit(solution)/shard_map/all_to_all | solution.py:631
  63.7 0.8 %answer.1 = bf16[32,2048]{1,0:T(8,128)(2,1)} custom-call(bf16[8,32,256]{2,1,0:T(8,128)(2,1)S(1)} %all-to-all-done.2.refs_0_, f32[32,2048]{1,0:T(8,128)S(1)} %get-tuple-element.49.refs_1_, bf16[8,32,256]{2,1,0:T(8,128)(2,1)S(1)} %get-tuple-element.50.refs_2_), custom_call_target="tpu_custom_call" | custom-call | bytes 524288 | tf_op jit(solution)/shard_map/answer/pallas_call | solution.py:74
Async XLA Ops:
  0.0 14.0 %collective-permute-start = (bf16[32,2048]{1,0:T(8,128)(2,1)}, bf16[32,2048]{1,0:T(8,128)(2,1)S(1)}, u32[]{:S(2)}, u32[]{:S(2)}) collective-permute-start(bf16[32,2048]{1,0:T(8,128)(2,1)} %refs_2_.4), channel_id=1, source_target_pairs={{0,1},{1,0},{2,3},{3,2},{4,5},{5,4},{6,7},{7,6},{8,9},{9,8},{10,11... | collective-permute-start | bytes 393224 | tf_op jit(solution)/shard_map/ppermute | solution.py:474
  0.5 13.6 %collective-permute-start.1 = (bf16[32,2048]{1,0:T(8,128)(2,1)}, bf16[32,2048]{1,0:T(8,128)(2,1)S(1)}, u32[]{:S(2)}, u32[]{:S(2)}) collective-permute-start(bf16[32,2048]{1,0:T(8,128)(2,1)} %refs_2_.4), channel_id=1, source_target_pairs={{0,0},{15,15},{1,2},{2,1},{3,4},{4,3},{5,6},{6,5},{7,8},{8,7},{9,1... | collective-permute-start | bytes 393224 | tf_op jit(solution)/shard_map/ppermute | solution.py:481
  6.1 18.0 %all-to-all-start = ((bf16[16,8,1024]{2,1,0:T(8,128)(2,1)}), bf16[16,8,1024]{2,1,0:T(8,128)(2,1)S(1)}, u32[]{:S(2)}, u32[]{:S(2)}) async-start(bf16[16,8,1024]{2,1,0:T(8,128)(2,1)} %bitcast.3), calls=%async_computation | async-start | bytes 524288 | tf_op jit(solution)/shard_map/all_to_all | solution.py:487
  24.9 4.9 %collective-permute-start.3 = (bf16[352,256]{1,0:T(8,128)(2,1)S(1)}, bf16[352,256]{1,0:T(8,128)(2,1)S(1)}, u32[]{:S(2)}, u32[]{:S(2)}) collective-permute-start(bf16[352,256]{1,0:T(8,128)(2,1)S(1)} %get-tuple-element.38), channel_id=1, source_target_pairs={{0,0},{15,15},{1,2},{2,1},{3,4},{4,3},{5,6},{6,5},{7,8},{8,7},{9,1... | collective-permute-start | bytes 540680 | tf_op jit(solution)/shard_map/ppermute | solution.py:481
  26.2 3.7 %collective-permute-start.2 = (bf16[352,256]{1,0:T(8,128)(2,1)S(1)}, bf16[352,256]{1,0:T(8,128)(2,1)S(1)}, u32[]{:S(2)}, u32[]{:S(2)}) collective-permute-start(bf16[352,256]{1,0:T(8,128)(2,1)S(1)} %get-tuple-element.37), channel_id=1, source_target_pairs={{0,1},{1,0},{2,3},{3,2},{4,5},{5,4},{6,7},{7,6},{8,9},{9,8},{10,11... | collective-permute-start | bytes 540680 | tf_op jit(solution)/shard_map/ppermute | solution.py:474
  32.5 16.7 %all-to-all-start.1 = ((bf16[16,72,128]{2,1,0:T(8,128)(2,1)}), bf16[16,72,128]{2,1,0:T(8,128)(2,1)S(1)}, u32[]{:S(2)}, u32[]{:S(2)}) async-start(bf16[16,72,128]{2,1,0:T(8,128)(2,1)} %finish.1), calls=%async_computation.1 | async-start | bytes 589824 | tf_op jit(solution)/shard_map/all_to_all | solution.py:604
  50.7 1.4 %collective-permute-start.4 = (bf16[8,32,256]{2,1,0:T(8,128)(2,1)S(1)}, bf16[8,32,256]{2,1,0:T(8,128)(2,1)S(1)}, u32[]{:S(2)}, u32[]{:S(2)}) collective-permute-start(bf16[8,32,256]{2,1,0:T(8,128)(2,1)S(1)} %get-tuple-element.47), channel_id=1, source_target_pairs={{0,1},{1,0},{2,3},{3,2},{4,5},{5,4},{6,7},{7,6},{8,9},{9,8},{10,11... | collective-permute-start | bytes 393224 | tf_op jit(solution)/shard_map/ppermute | solution.py:628
  52.8 10.9 %all-to-all-start.2 = ((bf16[8,32,256]{2,1,0:T(8,128)(2,1)}), bf16[8,32,256]{2,1,0:T(8,128)(2,1)S(1)}, u32[]{:S(2)}, u32[]{:S(2)}) async-start(bf16[8,32,256]{2,1,0:T(8,128)(2,1)} %merge.1), calls=%async_computation.2 | async-start | bytes 262144 | tf_op jit(solution)/shard_map/all_to_all | solution.py:631

commit v14 on v13

--- a/solution.py
+++ b/solution.py
@@ -114,8 +114,6 @@
     value, compress, coupling, source, owner, place,
     out_ref, blocks, turned, spread, pick, terms,
 ):
-    coupling = ready(coupling)
-    turned[...] = coupling[...].astype(F32).T
     value, compress = ready(value), ready(compress)
     for s in range(BLK):
         blocks[s * INC : (s + 1) * INC, :] = block(value, s)
@@ -127,6 +125,9 @@
     source = ready(source)
     tiles = source.shape[1]
     pick[...] = dot(spread[...], as_hot((iota((width, tiles), 0) // RANK) == source[...]))
+
+    coupling = ready(coupling)
+    turned[...] = coupling[...].astype(F32).T
 
     def step(pair, carry):
         rows = pl.multiple_of(pair * (2 * RANK), 2 * RANK)
@@ -509,7 +510,7 @@
         [((targets, INC * RANK), BF16)],
         (currents, primal_compress, primal_coupling) + lists,
         scratch=far_scratch(tiles),
-        held=(2, 0, 1, 3, 4, 5),
+        held=(0, 1, 3, 2, 4, 5),
         flops=10**11,
         name="far_up",
     )

time: 65 us -> 65 us (level)
  no operation moved by 1% of the time
where the time goes in v14:
time: 65 us; the launch traced here: 64.5 us
  Pallas kernels  28.8 us (44%)
  starting transfers between devices  21.3 us (33%)
  waiting for transfers between devices  14.3 us (22%)
    pallas_call x13, Pallas kernels, call(): pl.pallas_call(wrapped, out_shape=outs, in_specs=[pl.BlockSpec(memory_spa...  28.8 us
    all_to_all x1, starting transfers between devices, exchange(): lax.all_to_all(array, 'surf', split_axis=0, concat_axis=0, tiled=True)  7.92 us
    all_to_all x1, starting transfers between devices, shards(): lax.all_to_all(send, 'surf', split_axis=0, concat_axis=0, tiled=True)  6.16 us
    all_to_all x1, waiting for transfers between devices, shards(): lax.all_to_all(merged, 'surf', split_axis=0, concat_axis=0, tiled=True, a...  5.89 us
    all_to_all x1, waiting for transfers between devices, shards(): lax.all_to_all(send, 'surf', split_axis=0, concat_axis=0, tiled=True)  3.82 us
    all_to_all x1, waiting for transfers between devices, exchange(): lax.all_to_all(array, 'surf', split_axis=0, concat_axis=0, tiled=True)  3.5 us
    all_to_all x1, starting transfers between devices, shards(): lax.all_to_all(merged, 'surf', split_axis=0, concat_axis=0, tiled=True, a...  3.37 us
    ppermute x2, starting transfers between devices, swap_outer(): return lax.ppermute(array, 'surf', pairs)  2.22 us
  transfers between devices with their start and end apart: 8, of which 4 were waited for; matrix products, arithmetic and copies ran while one was open for 0% of the time, Pallas kernels for 35%

profile of v14, /device:TPU:0, one launch (start us, length us, event | category | flops | bytes accessed | tf_op | source)
XLA Modules:
  0.0 64.5 jit_solution(7619439418341842585)
XLA Ops:
  0.0 0.5 collective-permute-start
  0.5 1.6 %collective-permute-start.1 = (bf16[32,2048]{1,0:T(8,128)(2,1)}, bf16[32,2048]{1,0:T(8,128)(2,1)S(1)}, u32[]{:S(2)}, u32[]{:S(2)}) collective-permute-start(bf16[32,2048]{1,0:T(8,128)(2,1)} %refs_2_.4), channel_id=1, source_target_pairs={{0,0},{15,15},{1,2},{2,1},{3,4},{4,3},{5,6},{6,5},{7,8},{8,7},{9,1... | collective-permute-start | bytes 393224 | tf_op jit(solution)/shard_map/ppermute | solution.py:482
  2.0 4.1 %far_up.1 = bf16[128,1024]{1,0:T(8,128)(2,1)} custom-call(bf16[32,2048]{1,0:T(8,128)(2,1)} %refs_2_.4, bf16[8,32,256]{2,1,0:T(8,128)(2,1)} %refs_1_.3, bf16[128,1024]{1,0:T(8,128)(2,1)} %refs_2_.3, s32[1,128]{1,0:T(1,128)} %bitcast.12, s32[1,128]{1,0:T(1,128)} %bitcast.14, s32[1,128]{1,0:T(1,128)} %bitcast.16), custom_call_target="tpu_custom_call" | custom-call | flops 99999997952 | bytes 525824 | tf_op jit(solution)/shard_map/far_up/pallas_call | solution.py:74
  6.1 7.9 %all-to-all-start = ((bf16[16,8,1024]{2,1,0:T(8,128)(2,1)}), bf16[16,8,1024]{2,1,0:T(8,128)(2,1)S(1)}, u32[]{:S(2)}, u32[]{:S(2)}) async-start(bf16[16,8,1024]{2,1,0:T(8,128)(2,1)} %bitcast.3), calls=%async_computation | async-start | bytes 524288 | tf_op jit(solution)/shard_map/all_to_all | solution.py:488
  14.0 0.0 collective-permute-done.refs_3_
  14.0 0.0 collective-permute-done.1.refs_4_
  14.0 6.5 %prepare.1 = (f32[32,2048]{1,0:T(8,128)S(1)}, bf16[8,256,256]{2,1,0:T(8,128)(2,1)S(1)}, bf16[8,256,256]{2,1,0:T(8,128)(2,1)S(1)}, bf16[8,32,256]{2,1,0:T(8,128)(2,1)S(1)}) custom-call(s32[48]{0:T(128)} %refs_0_.4, s32[48]{0:T(128)} %refs_1_.4, bf16[32,2048]{1,0:T(8,128)(2,1)} %refs_2_.4, bf16[32,2048]{1,0:T(8,128)(2,1)S(1)} %collective-permute-done.refs_3_, ...), custom_call_target="tpu_custom_call" | custom-call | flops 99999997952 | bytes 9961856 | tf_op jit(solution)/shard_map/prepare/pallas_call | solution.py:74
  20.5 3.5 %all-to-all-done = bf16[16,8,1024]{2,1,0:T(8,128)(2,1)S(1)} async-done(((bf16[16,8,1024]{2,1,0:T(8,128)(2,1)}), bf16[16,8,1024]{2,1,0:T(8,128)(2,1)S(1)}, u32[]{:S(2)}, u32[]{:S(2)}) %all-to-all-start) | async-done | bytes 262176 | tf_op jit(solution)/shard_map/all_to_all | solution.py:488
  24.0 0.9 %solve.1 = (f32[32,2048]{1,0:T(8,128)S(1)}, f32[32,2048]{1,0:T(8,128)S(1)}, bf16[352,256]{1,0:T(8,128)(2,1)S(1)}, bf16[352,256]{1,0:T(8,128)(2,1)S(1)}) custom-call(bf16[128,1024]{1,0:T(8,128)(2,1)S(1)} %bitcast.8, f32[32,2048]{1,0:T(8,128)S(1)} %get-tuple-element.28.refs_1_, bf16[8,32,256]{2,1,0:T(8,128)(2,1)S(1)} %get-tuple-element.29.refs_2_, ...), custom_call_target="tpu_custom_call" | custom-call | bytes 2752512 | tf_op jit(solution)/shard_map/solve/pallas_call | solution.py:74
  24.9 0.7 %collective-permute-start.3 = (bf16[352,256]{1,0:T(8,128)(2,1)S(1)}, bf16[352,256]{1,0:T(8,128)(2,1)S(1)}, u32[]{:S(2)}, u32[]{:S(2)}) collective-permute-start(bf16[352,256]{1,0:T(8,128)(2,1)S(1)} %get-tuple-element.38), channel_id=1, source_target_pairs={{0,0},{15,15},{1,2},{2,1},{3,4},{4,3},{5,6},{6,5},{7,8},{8,7},{9,1... | collective-permute-start | bytes 540680 | tf_op jit(solution)/shard_map/ppermute | solution.py:482
  25.6 0.6 middle.1
  26.2 1.1 %collective-permute-start.2 = (bf16[352,256]{1,0:T(8,128)(2,1)S(1)}, bf16[352,256]{1,0:T(8,128)(2,1)S(1)}, u32[]{:S(2)}, u32[]{:S(2)}) collective-permute-start(bf16[352,256]{1,0:T(8,128)(2,1)S(1)} %get-tuple-element.37), channel_id=1, source_target_pairs={{0,1},{1,0},{2,3},{3,2},{4,5},{5,4},{6,7},{7,6},{8,9},{9,8},{10,11... | collective-permute-start | bytes 540680 | tf_op jit(solution)/shard_map/ppermute | solution.py:475
  27.3 1.4 %order.1 = (s32[8,256]{1,0:T(8,128)S(1)}, bf16[2048,256]{1,0:T(8,128)(2,1)S(1)}, s32[16,2]{1,0:T(8,128)S(1)}, bf16[16,2048]{1,0:T(8,128)(2,1)S(1)}, f32[1,2048]{1,0:T(1,128)S(1)}) custom-call(s32[1,2048]{1,0:T(1,128)} %bitcast.9, s32[1,2048]{1,0:T(1,128)} %bitcast.10, f32[1,2048]{1,0:T(1,128)} %bitcast.11, f32[32,2048]{1,0:T(8,128)S(1)} %get-tuple-element.32.refs_0_.refs_3_), custom_call_target="tpu_custom_call" | custom-call | flops 1000000000 | bytes 286720 | tf_op jit(solution)/shard_map/order/pallas_call | solution.py:74
  28.7 1.1 %tails.1.refs_9_ = f32[16,8,128]{2,1,0:T(8,128)S(1)} custom-call(bf16[16,2048]{1,0:T(8,128)(2,1)S(1)} %get-tuple-element.40.refs_0_, s32[8,256]{1,0:T(8,128)S(1)} %get-tuple-element.41.refs_1_.refs_10_, bf16[2048,256]{1,0:T(8,128)(2,1)S(1)} %get-tuple-element.42.refs_2_.refs_11_, s32[16,2]{1,0:T(8,128)S(1)} %get-tuple-element.43.refs_3_.refs_12_), custom_call_target="tpu_custom_call" | custom-call | flops 1000000000 | bytes 1122432 | tf_op jit(solution)/shard_map/tails/pallas_call | solution.py:74
  29.8 0.0 collective-permute-done.3.refs_5_
  29.8 0.0 collective-permute-done.2.refs_4_
  29.9 2.6 %finish.1 = bf16[16,72,128]{2,1,0:T(8,128)(2,1)} custom-call(f32[32,2048]{1,0:T(8,128)S(1)} %get-tuple-element.32.refs_0_.refs_3_, f32[32,2048]{1,0:T(8,128)S(1)} %get-tuple-element.33.refs_1_, f32[32,2048]{1,0:T(8,128)S(1)} %get-tuple-element.35.refs_2_, f32[32,2048]{1,0:T(8,128)S(1)} %get-tuple-element.36.refs_3_, ...), custom_call_target="tpu_custom_call" | custom-call | bytes 4636800 | tf_op jit(solution)/shard_map/finish/pallas_call | solution.py:74
  32.4 6.2 %all-to-all-start.1 = ((bf16[16,72,128]{2,1,0:T(8,128)(2,1)}), bf16[16,72,128]{2,1,0:T(8,128)(2,1)S(1)}, u32[]{:S(2)}, u32[]{:S(2)}) async-start(bf16[16,72,128]{2,1,0:T(8,128)(2,1)} %finish.1), calls=%async_computation.1 | async-start | bytes 589824 | tf_op jit(solution)/shard_map/all_to_all | solution.py:605
  38.6 6.7 %couple.1 = (bf16[256,4096]{1,0:T(8,128)(2,1)S(1)}, bf16[8,32,256]{2,1,0:T(8,128)(2,1)S(1)}) custom-call(bf16[128,1024]{1,0:T(8,128)(2,1)} %refs_0_.5, s32[1,128]{1,0:T(1,128)} %bitcast.13, s32[1,128]{1,0:T(1,128)} %bitcast.15, s32[1,128]{1,0:T(1,128)} %bitcast.17, bf16[8,32,256]{2,1,0:T(8,128)(2,1)} %refs_4_.1), custom_call_target="tpu_custom_call" | custom-call | flops 10000000000 | bytes 394752 | tf_op jit(solution)/shard_map/couple/pallas_call | solution.py:74
  45.4 3.8 %all-to-all-done.1.refs_0_ = bf16[16,72,128]{2,1,0:T(8,128)(2,1)S(1)} async-done(((bf16[16,72,128]{2,1,0:T(8,128)(2,1)}), bf16[16,72,128]{2,1,0:T(8,128)(2,1)S(1)}, u32[]{:S(2)}, u32[]{:S(2)}) %all-to-all-start.1) | async-done | bytes 294944 | tf_op jit(solution)/shard_map/all_to_all | solution.py:605
  49.2 1.5 %gather.1 = (bf16[8,32,256]{2,1,0:T(8,128)(2,1)S(1)}, bf16[32,256]{1,0:T(8,128)(2,1)S(1)}, bf16[8,32,256]{2,1,0:T(8,128)(2,1)S(1)}) custom-call(bf16[16,72,128]{2,1,0:T(8,128)(2,1)S(1)} %all-to-all-done.1.refs_0_, bf16[8,32,256]{2,1,0:T(8,128)(2,1)S(1)} %get-tuple-element.44.refs_1_, bf16[256,4096]{1,0:T(8,128)(2,1)S(1)} %get-tuple-element.45.refs_2_.refs_1_), custom_call_target="tpu_custom_call" | custom-call | bytes 2523136 | tf_op jit(solution)/shard_map/gather/pallas_call | solution.py:74
  50.7 0.1 collective-permute-start.4
  50.7 0.3 own.1.refs_0_
  51.0 1.0 %collective-permute-done.4.refs_1_ = bf16[8,32,256]{2,1,0:T(8,128)(2,1)S(1)} collective-permute-done((bf16[8,32,256]{2,1,0:T(8,128)(2,1)S(1)}, bf16[8,32,256]{2,1,0:T(8,128)(2,1)S(1)}, u32[]{:S(2)}, u32[]{:S(2)}) %collective-permute-start.4) | collective-permute-done | bytes 131104 | tf_op jit(solution)/shard_map/ppermute | solution.py:629
  52.1 0.7 %merge.1 = bf16[8,32,256]{2,1,0:T(8,128)(2,1)} custom-call(f32[8,32,256]{2,1,0:T(8,128)S(1)} %own.1.refs_0_, bf16[8,32,256]{2,1,0:T(8,128)(2,1)S(1)} %collective-permute-done.4.refs_1_), custom_call_target="tpu_custom_call" | custom-call | bytes 393216 | tf_op jit(solution)/shard_map/merge/pallas_call | solution.py:74
  52.8 3.4 %all-to-all-start.2 = ((bf16[8,32,256]{2,1,0:T(8,128)(2,1)}), bf16[8,32,256]{2,1,0:T(8,128)(2,1)S(1)}, u32[]{:S(2)}, u32[]{:S(2)}) async-start(bf16[8,32,256]{2,1,0:T(8,128)(2,1)} %merge.1), calls=%async_computation.2 | async-start | bytes 262144 | tf_op jit(solution)/shard_map/all_to_all | solution.py:632
  56.1 1.6 %self_part.1 = (f32[32,2048]{1,0:T(8,128)S(1)}, bf16[8,32,256]{2,1,0:T(8,128)(2,1)S(1)}) custom-call(bf16[8,32,256]{2,1,0:T(8,128)(2,1)S(1)} %get-tuple-element.48.refs_0_, bf16[8,256,256]{2,1,0:T(8,128)(2,1)} %refs_1_.5, bf16[8,32,256]{2,1,0:T(8,128)(2,1)} %refs_2_.5), custom_call_target="tpu_custom_call" | custom-call | bytes 1310720 | tf_op jit(solution)/shard_map/self_part/pallas_call | solution.py:74
  57.8 5.9 %all-to-all-done.2.refs_0_ = bf16[8,32,256]{2,1,0:T(8,128)(2,1)S(1)} async-done(((bf16[8,32,256]{2,1,0:T(8,128)(2,1)}), bf16[8,32,256]{2,1,0:T(8,128)(2,1)S(1)}, u32[]{:S(2)}, u32[]{:S(2)}) %all-to-all-start.2) | async-done | bytes 131104 | tf_op jit(solution)/shard_map/all_to_all | solution.py:632
  63.7 0.8 %answer.1 = bf16[32,2048]{1,0:T(8,128)(2,1)} custom-call(bf16[8,32,256]{2,1,0:T(8,128)(2,1)S(1)} %all-to-all-done.2.refs_0_, f32[32,2048]{1,0:T(8,128)S(1)} %get-tuple-element.49.refs_1_, bf16[8,32,256]{2,1,0:T(8,128)(2,1)S(1)} %get-tuple-element.50.refs_2_), custom_call_target="tpu_custom_call" | custom-call | bytes 524288 | tf_op jit(solution)/shard_map/answer/pallas_call | solution.py:74
Async XLA Ops:
  0.0 14.0 %collective-permute-start = (bf16[32,2048]{1,0:T(8,128)(2,1)}, bf16[32,2048]{1,0:T(8,128)(2,1)S(1)}, u32[]{:S(2)}, u32[]{:S(2)}) collective-permute-start(bf16[32,2048]{1,0:T(8,128)(2,1)} %refs_2_.4), channel_id=1, source_target_pairs={{0,1},{1,0},{2,3},{3,2},{4,5},{5,4},{6,7},{7,6},{8,9},{9,8},{10,11... | collective-permute-start | bytes 393224 | tf_op jit(solution)/shard_map/ppermute | solution.py:475
  0.5 13.6 %collective-permute-start.1 = (bf16[32,2048]{1,0:T(8,128)(2,1)}, bf16[32,2048]{1,0:T(8,128)(2,1)S(1)}, u32[]{:S(2)}, u32[]{:S(2)}) collective-permute-start(bf16[32,2048]{1,0:T(8,128)(2,1)} %refs_2_.4), channel_id=1, source_target_pairs={{0,0},{15,15},{1,2},{2,1},{3,4},{4,3},{5,6},{6,5},{7,8},{8,7},{9,1... | collective-permute-start | bytes 393224 | tf_op jit(solution)/shard_map/ppermute | solution.py:482
  6.1 18.0 %all-to-all-start = ((bf16[16,8,1024]{2,1,0:T(8,128)(2,1)}), bf16[16,8,1024]{2,1,0:T(8,128)(2,1)S(1)}, u32[]{:S(2)}, u32[]{:S(2)}) async-start(bf16[16,8,1024]{2,1,0:T(8,128)(2,1)} %bitcast.3), calls=%async_computation | async-start | bytes 524288 | tf_op jit(solution)/shard_map/all_to_all | solution.py:488
  24.9 4.9 %collective-permute-start.3 = (bf16[352,256]{1,0:T(8,128)(2,1)S(1)}, bf16[352,256]{1,0:T(8,128)(2,1)S(1)}, u32[]{:S(2)}, u32[]{:S(2)}) collective-permute-start(bf16[352,256]{1,0:T(8,128)(2,1)S(1)} %get-tuple-element.38), channel_id=1, source_target_pairs={{0,0},{15,15},{1,2},{2,1},{3,4},{4,3},{5,6},{6,5},{7,8},{8,7},{9,1... | collective-permute-start | bytes 540680 | tf_op jit(solution)/shard_map/ppermute | solution.py:482
  26.2 3.7 %collective-permute-start.2 = (bf16[352,256]{1,0:T(8,128)(2,1)S(1)}, bf16[352,256]{1,0:T(8,128)(2,1)S(1)}, u32[]{:S(2)}, u32[]{:S(2)}) collective-permute-start(bf16[352,256]{1,0:T(8,128)(2,1)S(1)} %get-tuple-element.37), channel_id=1, source_target_pairs={{0,1},{1,0},{2,3},{3,2},{4,5},{5,4},{6,7},{7,6},{8,9},{9,8},{10,11... | collective-permute-start | bytes 540680 | tf_op jit(solution)/shard_map/ppermute | solution.py:475
  32.4 16.7 %all-to-all-start.1 = ((bf16[16,72,128]{2,1,0:T(8,128)(2,1)}), bf16[16,72,128]{2,1,0:T(8,128)(2,1)S(1)}, u32[]{:S(2)}, u32[]{:S(2)}) async-start(bf16[16,72,128]{2,1,0:T(8,128)(2,1)} %finish.1), calls=%async_computation.1 | async-start | bytes 589824 | tf_op jit(solution)/shard_map/all_to_all | solution.py:605
  50.7 1.4 %collective-permute-start.4 = (bf16[8,32,256]{2,1,0:T(8,128)(2,1)S(1)}, bf16[8,32,256]{2,1,0:T(8,128)(2,1)S(1)}, u32[]{:S(2)}, u32[]{:S(2)}) collective-permute-start(bf16[8,32,256]{2,1,0:T(8,128)(2,1)S(1)} %get-tuple-element.47), channel_id=1, source_target_pairs={{0,1},{1,0},{2,3},{3,2},{4,5},{5,4},{6,7},{7,6},{8,9},{9,8},{10,11... | collective-permute-start | bytes 393224 | tf_op jit(solution)/shard_map/ppermute | solution.py:629
  52.8 10.9 %all-to-all-start.2 = ((bf16[8,32,256]{2,1,0:T(8,128)(2,1)}), bf16[8,32,256]{2,1,0:T(8,128)(2,1)S(1)}, u32[]{:S(2)}, u32[]{:S(2)}) async-start(bf16[8,32,256]{2,1,0:T(8,128)(2,1)} %merge.1), calls=%async_computation.2 | async-start | bytes 262144 | tf_op jit(solution)/shard_map/all_to_all | solution.py:632
